TPU v7x, 32 devices: a whole 2x2x4 slice. The times are simulated.
32 devices in a mesh: ens: 2 (over y), row: 4 (over x, core), col: 4 (over z).
Axes of the slice: x: 2, y: 2, z: 4, core: 2. Of those that a mesh axis runs over, the one named last changes fastest.
Arguments:
- pair_state: bfloat16 [1024, 512, 128], P(('ens', 'row'), 'col'), parts along dimension 0, may hold values from -6 to 6
- pair_mask: int32 [1024, 512], P(('ens', 'row'), 'col'), parts along dimension 0, may hold values from 0 to 1, as said below
- norm_in_gain: float32 [2, 128], replicated, may hold values from 0.25 to 1.75
- norm_in_bias: float32 [2, 128], replicated, may hold values from -3 to 3
- proj_in: bfloat16 [2, 128, 256], replicated, may hold values from -0.5 to 0.5
- gate_in: bfloat16 [2, 128, 256], replicated, may hold values from -0.5 to 0.5
- norm_out_gain: float32 [2, 128], replicated, may hold values from 0.25 to 1.75
- norm_out_bias: float32 [2, 128], replicated, may hold values from -3 to 3
- proj_out: bfloat16 [2, 128, 128], replicated, may hold values from -0.5 to 0.5
- gate_out: bfloat16 [2, 128, 128], replicated, may hold values from -0.5 to 0.5
Outputs:
- pair_result: bfloat16 [1024, 512, 128], P(('ens', 'row'), 'col'), parts along dimension 0
There are 2 independent parts, one for each index of `ens`. A program takes and returns all parts, laid end to end along the dimension named above; an argument that names none is the same for every part. Nothing has to cross between parts.
Inputs may be any that keep to these rules, and one draw needn't show every extreme that they name: pair_mask[i, j] = t[i] * t[j] for a 0/1 token validity t: every token at or above one valid length, which lies between 448 and 511, is invalid, and some tokens below it may be invalid too.
All inputs are finite; a program needn't handle non-finite values.
Results may differ from a plain program's by a relative error of at most 0.0055.
Values may be sent and summed in bfloat16 or wider, within the bound.
No kernel may reach another device: no remote copies, remote signals or barrier semaphores. Data moves between devices by JAX's collectives and lax.ppermute only.
A program may use at most 128 MiB of HBM per device.

v0:
```python
import jax
import jax.numpy as jnp
from jax import lax
from jax.sharding import PartitionSpec as P

epsilon = 1e-05


def norm_last(values, norm_gain, norm_bias):
    centre = jnp.mean(values, axis=-1, keepdims=True)
    variance = jnp.mean(jnp.square(values - centre), axis=-1, keepdims=True)
    return (values - centre) * lax.rsqrt(variance + epsilon) * norm_gain + norm_bias


def norm_first(values, norm_gain, norm_bias):
    centre = jnp.mean(values, axis=0, keepdims=True)
    variance = jnp.mean(jnp.square(values - centre), axis=0, keepdims=True)
    return (values - centre) * lax.rsqrt(variance + epsilon) * norm_gain[:, None, None] + norm_bias[
        :, None, None
    ]


def alternate(matrix):
    in_width, out_width = matrix.shape
    half_width = out_width // 2
    return matrix.reshape(in_width, 2, half_width).transpose(0, 2, 1).reshape(in_width, out_width)


def spread(paired):
    arrived = lax.all_to_all(paired, ("row", "col"), split_axis=0, concat_axis=1, tiled=True)
    n_row = lax.axis_size("row")
    n_col = lax.axis_size("col")
    channels, stacked, tile_cols = arrived.shape
    tile_rows = stacked // (n_row * n_col)
    arrived = arrived.reshape(channels, n_row, n_col, tile_rows, tile_cols).transpose(0, 1, 3, 2, 4)
    return arrived.reshape(channels, n_row * tile_rows, n_col * tile_cols)


def gather_back(triangle_out):
    n_row = lax.axis_size("row")
    n_col = lax.axis_size("col")
    channels, total_rows, total_cols = triangle_out.shape
    tile_rows = total_rows // n_row
    tile_cols = total_cols // n_col
    pieces = triangle_out.reshape(channels, n_row, tile_rows, n_col, tile_cols).transpose(
        1, 3, 0, 2, 4
    )
    pieces = pieces.reshape(n_row * n_col * channels, tile_rows, tile_cols)
    return lax.all_to_all(pieces, ("row", "col"), split_axis=0, concat_axis=0, tiled=True)


def on_device(
    pair_state,
    pair_mask,
    norm_in_gain,
    norm_in_bias,
    proj_in,
    gate_in,
    norm_out_gain,
    norm_out_bias,
    proj_out,
    gate_out,
):
    mask_weight = pair_mask.astype(jnp.float32)[None]
    current = pair_state
    for update in range(2):
        normed = norm_last(
            current.astype(jnp.float32), norm_in_gain[update], norm_in_bias[update]
        ).astype(jnp.bfloat16)
        projected = jnp.einsum(
            "rcd,de->erc", normed, alternate(proj_in[update]), preferred_element_type=jnp.float32
        )
        gate_logit = jnp.einsum(
            "rcd,de->erc", normed, alternate(gate_in[update]), preferred_element_type=jnp.float32
        )
        paired = (projected * jax.nn.sigmoid(gate_logit) * mask_weight).astype(jnp.bfloat16)
        arrived = spread(paired)
        doubled, total_rows, total_cols = arrived.shape
        pair_count = doubled // 2
        arrived = arrived.reshape(pair_count, 2, total_rows, total_cols)
        left_side = arrived[:, 0]
        right_side = arrived[:, 1]
        pattern = "dik,djk->dij" if update == 0 else "dki,dkj->dij"
        triangle_out = jnp.einsum(
            pattern, left_side, right_side, preferred_element_type=jnp.float32
        ).astype(jnp.bfloat16)
        returned = gather_back(triangle_out)
        normed_out = norm_first(
            returned.astype(jnp.float32), norm_out_gain[update], norm_out_bias[update]
        ).astype(jnp.bfloat16)
        gate_value = jax.nn.sigmoid(
            jnp.einsum("rcd,df->rcf", normed, gate_out[update], preferred_element_type=jnp.float32)
        )
        change = (
            jnp.einsum(
                "erc,ef->rcf", normed_out, proj_out[update], preferred_element_type=jnp.float32
            )
            * gate_value
        )
        current = (current.astype(jnp.float32) + change).astype(jnp.bfloat16)
    return current


def solution(mesh):
    return jax.shard_map(
        on_device,
        mesh=mesh,
        in_specs=(
            P(("ens", "row"), "col", None),
            P(("ens", "row"), "col"),
            P(),
            P(),
            P(),
            P(),
            P(),
            P(),
            P(),
            P(),
        ),
        out_specs=P(("ens", "row"), "col", None),
        check_vma=False,
    )
```

profile of v0, /device:TPU:0, one launch (start us, length us, event | category | flops | bytes accessed | tf_op | source)
XLA Modules:
  0.0 769.4 jit_solution(7747783865300520052)
XLA Ops:
  0.0 6.4 copy.61
  6.4 3.4 convert_reduce_fusion.1
  9.9 3.9 fusion.12
  13.8 0.0 copy-done.4
  13.9 0.1 copy.65
  14.1 0.1 copy.62
  14.2 0.0 copy-start
  14.3 5.0 fusion.45
  19.2 0.0 copy-done
  19.2 8.3 %fusion.26 = bf16[256,128,128]{0,2,1:T(8,128)(2,1)} fusion(f32[128,128]{1,0:T(8,128)S(1)} %convert_element_type.49, f32[128,128,256]{2,1,0:T(8,128)S(1)} %fusion.45, bf16[128,256,1]{0,1,2:T(8,128)(2,1)S(1)} %bitcast.122, bf16[128,128,128]{1,2,0:T(8,128)(2,1)S(1)} %copy-done, f32[128]{0:T(128)S(1)} %get-tuple-element.16, f32[128]{0:T(128)S(1)} %get-tuple-element.19, ...), kind=kOutput, calls=%fused_computation.40 | convolution fusion | flops 1111490560 | bytes 29623296 | tf_op jit(solution)/shard_map/rcd,de->erc/dot_general | solution.py:70
  27.5 12.4 %copy.68 = bf16[256,128,128]{2,1,0:T(8,128)(2,1)} copy(bf16[256,128,128]{0,2,1:T(8,128)(2,1)} %fusion.26) | data formatting | bytes 16777216 | tf_op jit(solution)/shard_map/convert_element_type | solution.py:76
  39.9 191.8 %all_to_all.40 = bf16[256,128,128]{2,1,0:T(8,128)(2,1)S(1)} all-to-all(bf16[256,128,128]{2,1,0:T(8,128)(2,1)} %copy.68), channel_id=1, replica_groups=mesh['ens'=2,'row'=4,'col'=4] {'row','col'}, dimensions={0} | all-to-all | bytes 16777216 | tf_op jit(solution)/shard_map/all_to_all | solution.py:30
  231.8 8.0 %copy.122 = bf16[16,4,4,128,128]{4,2,3,1,0:T(4,128)(2,1)} copy(bf16[16,4,4,128,128]{4,3,0,2,1:T(8,128)(2,1)S(1)} %bitcast.112) | data formatting | bytes 16777216 | tf_op jit(solution)/shard_map/reshape | solution.py:35
  239.8 13.1 %reshape_reshape.6 = bf16[8,2,512,512]{3,2,1,0:T(8,128)(2,1)} reshape(bf16[16,4,128,4,128]{4,3,2,1,0:T(4,128)(2,1)} %bitcast.113) | data formatting | bytes 16777216 | tf_op jit(solution)/shard_map/reshape;reshape | solution.py:80
  252.9 7.8 %fusion.34 = bf16[8,512,512]{2,1,0:T(8,128)(2,1)} fusion(bf16[8,2,512,512]{3,2,1,0:T(8,128)(2,1)} %reshape_reshape.6), kind=kOutput, calls=%fused_computation.52 | convolution fusion | flops 2149580800 | bytes 12582912 | tf_op jit(solution)/shard_map/dik,djk->dij/dot_general | solution.py:84
  260.7 6.9 reshape.92
  267.6 5.3 copy.72
  272.9 4.8 all-to-all-start.1
  277.7 0.1 copy.80
  277.9 0.1 copy.77
  278.0 0.0 copy-start.6
  278.1 94.0 %all-to-all-done.1 = bf16[128,128,128]{2,1,0:T(8,128)(2,1)} async-done(((bf16[128,128,128]{2,1,0:T(8,128)(2,1)}), bf16[128,128,128]{2,1,0:T(8,128)(2,1)}, u32[]{:S(2)}, u32[]{:S(2)}) %all-to-all-start.1) | async-done | bytes 4194336 | tf_op jit(solution)/shard_map/all_to_all | solution.py:49
  372.1 2.8 convert_reduce_fusion.3
  374.9 3.3 fusion.20
  378.2 3.5 fusion.23
  381.7 0.0 copy-start.1
  381.7 0.0 copy-start.12
  381.8 3.2 fusion.32
  385.0 5.1 convert_reduce_fusion
  390.1 0.0 copy-start.2
  390.1 1.7 fusion.8
  391.9 2.6 fusion.49
  394.5 18.1 %fusion.27 = bf16[256,128,128]{0,2,1:T(8,128)(2,1)} fusion(f32[128,128]{1,0:T(8,128)S(1)} %convert_element_type.49, f32[128,128,256]{2,1,0:T(8,128)S(1)} %fusion.49, bf16[128,256,1]{0,1,2:T(8,128)(2,1)S(1)} %bitcast.121, bf16[128,128,128]{1,2,0:T(8,128)(2,1)S(1)} %get-tuple-element.18, f32[128]{0:T(128)S(1)} %get-tuple-element.15, ...), kind=kOutput, calls=%fused_computation.41 | convolution fusion | flops 1111490560 | bytes 29623296 | tf_op jit(solution)/shard_map/rcd,de->erc/dot_general | solution.py:70
  412.6 12.4 %copy.83 = bf16[256,128,128]{2,1,0:T(8,128)(2,1)} copy(bf16[256,128,128]{0,2,1:T(8,128)(2,1)} %fusion.27) | data formatting | bytes 16777216 | tf_op jit(solution)/shard_map/convert_element_type | solution.py:76
  425.1 188.2 %all_to_all.41 = bf16[256,128,128]{2,1,0:T(8,128)(2,1)S(1)} all-to-all(bf16[256,128,128]{2,1,0:T(8,128)(2,1)} %copy.83), channel_id=1, replica_groups=mesh['ens'=2,'row'=4,'col'=4] {'row','col'}, dimensions={0} | all-to-all | bytes 16777216 | tf_op jit(solution)/shard_map/all_to_all | solution.py:30
  613.3 8.0 %copy.121 = bf16[16,4,4,128,128]{4,2,3,1,0:T(4,128)(2,1)} copy(bf16[16,4,4,128,128]{4,3,0,2,1:T(8,128)(2,1)S(1)} %bitcast.114) | data formatting | bytes 16777216 | tf_op jit(solution)/shard_map/reshape | solution.py:35
  621.3 13.1 %reshape_reshape.7 = bf16[8,2,512,512]{3,2,1,0:T(8,128)(2,1)} reshape(bf16[16,4,128,4,128]{4,3,2,1,0:T(4,128)(2,1)} %bitcast.115) | data formatting | bytes 16777216 | tf_op jit(solution)/shard_map/reshape;reshape | solution.py:80
  634.4 7.8 %fusion.35 = bf16[8,512,512]{2,1,0:T(8,128)(2,1)} fusion(bf16[8,2,512,512]{3,2,1,0:T(8,128)(2,1)} %reshape_reshape.7), kind=kOutput, calls=%fused_computation.53 | convolution fusion | flops 2149580800 | bytes 12582912 | tf_op jit(solution)/shard_map/dki,dkj->dij/dot_general | solution.py:84
  642.2 6.9 reshape.97
  649.2 3.3 copy.87
  652.4 97.6 %all_to_all.42 = bf16[128,128,128]{2,1,0:T(8,128)(2,1)S(1)} all-to-all(bf16[128,128,128]{2,1,0:T(8,128)(2,1)S(1)} %bitcast.118), channel_id=1, replica_groups=mesh['ens'=2,'row'=4,'col'=4] {'row','col'}, dimensions={0} | all-to-all | bytes 8388608 | tf_op jit(solution)/shard_map/all_to_all | solution.py:49
  750.1 0.6 convert_reduce_fusion.2
  750.7 1.1 fusion.16
  751.9 2.0 fusion.19
  753.8 0.0 copy-start.3
  753.9 3.2 fusion.30
  757.1 5.8 fusion.25
  762.8 6.4 copy.92
  (35 shorter events, 0.3 us)
Async XLA Ops:
  0.0 13.8 %copy-start.4 = (bf16[2,128,256]{2,1,0:T(8,128)(2,1)S(1)}, bf16[2,128,256]{2,1,0:T(8,128)(2,1)}, u32[]{:S(2)}) copy-start(bf16[2,128,256]{2,1,0:T(8,128)(2,1)} %param.15) | copy-start | bytes 393220
  0.0 14.0 %copy-start.5 = (bf16[2,128,256]{2,1,0:T(8,128)(2,1)S(1)}, bf16[2,128,256]{2,1,0:T(8,128)(2,1)}, u32[]{:S(2)}) copy-start(bf16[2,128,256]{2,1,0:T(8,128)(2,1)} %param.14) | copy-start | bytes 393220
  0.0 14.2 %copy-start.7 = (s32[128,128]{1,0:T(8,128)S(1)}, s32[128,128]{1,0:T(8,128)}, u32[]{:S(2)}) copy-start(s32[128,128]{1,0:T(8,128)} %param.11) | copy-start | bytes 196612
  0.0 14.2 %copy-start.9 = (f32[2,128]{1,0:T(2,128)S(1)}, f32[2,128]{1,0:T(2,128)}, u32[]{:S(2)}) copy-start(f32[2,128]{1,0:T(2,128)} %param.12) | copy-start | bytes 3076
  0.0 14.2 %copy-start.8 = (f32[2,128]{1,0:T(2,128)S(1)}, f32[2,128]{1,0:T(2,128)}, u32[]{:S(2)}) copy-start(f32[2,128]{1,0:T(2,128)} %param.13) | copy-start | bytes 3076
  14.2 5.0 copy-start
  267.6 10.4 %copy-start.10 = (f32[2,128]{1,0:T(2,128)S(1)}, f32[2,128]{1,0:T(2,128)}, u32[]{:S(2)}) copy-start(f32[2,128]{1,0:T(2,128)} %param.17) | copy-start | bytes 3076
  267.6 10.4 %copy-start.11 = (f32[2,128]{1,0:T(2,128)S(1)}, f32[2,128]{1,0:T(2,128)}, u32[]{:S(2)}) copy-start(f32[2,128]{1,0:T(2,128)} %param.16) | copy-start | bytes 3076
  272.9 99.2 %all-to-all-start.1 = ((bf16[128,128,128]{2,1,0:T(8,128)(2,1)}), bf16[128,128,128]{2,1,0:T(8,128)(2,1)}, u32[]{:S(2)}, u32[]{:S(2)}) async-start(bf16[128,128,128]{2,1,0:T(8,128)(2,1)} %bitcast.116), calls=%async_computation.1 | async-start | bytes 8388608 | tf_op jit(solution)/shard_map/all_to_all | solution.py:49
  278.0 103.7 %copy-start.6 = (bf16[2,128,128]{2,1,0:T(8,128)(2,1)S(1)}, bf16[2,128,128]{2,1,0:T(8,128)(2,1)}, u32[]{:S(2)}) copy-start(bf16[2,128,128]{2,1,0:T(8,128)(2,1)} %param.18) | copy-start | bytes 196612
  381.7 3.2 copy-start.1
  381.7 3.2 copy-start.12
  390.1 4.4 copy-start.2
  753.8 3.2 copy-start.3
where the time goes:
time: 775 us; the launch traced here: 769 us
  blocking collectives  478 us (62%)
  local copies, waits for them, and re-layouts  103 us (13%)
  waiting for transfers between devices  94 us (12%)
  matrix products  66.9 us (9%)
  other arithmetic  22.5 us (3%)
    all_to_all x2, blocking collectives, spread(): lax.all_to_all(paired, ('row', 'col'), split_axis=0, concat_axis=1, tiled...  380 us
    all_to_all x1, blocking collectives, gather_back(): lax.all_to_all(pieces, ('row', 'col'), split_axis=0, concat_axis=0, tiled...  97.6 us
    all_to_all x1, waiting for transfers between devices, gather_back(): lax.all_to_all(pieces, ('row', 'col'), split_axis=0, concat_axis=0, tiled...  94 us
    dot_general x2, matrix products, on_device(): jnp.einsum('rcd,de->erc', normed, alternate(proj_in[update]), preferred_e...  26.4 us
    another operation x2, local copies, waits for them, and re-layouts, on_device(): arrived = arrived.reshape(pair_count, 2, total_rows, total_cols)  26.2 us
    convert_element_type x2, local copies, waits for them, and re-layouts, on_device(): (projected * jax.nn.sigmoid(gate_logit) * mask_weight).astype(jnp.bfloat16)  24.9 us
    reshape x3, local copies, waits for them, and re-layouts, gather_back(): triangle_out.reshape(channels, n_row, tile_rows, n_col, tile_cols)  17.1 us
    reshape x2, local copies, waits for them, and re-layouts, spread(): arrived.reshape(channels, n_row, n_col, tile_rows, tile_cols)  16 us
  transfers between devices with their start and end apart: 1, of which 1 were waited for; matrix products, arithmetic and copies ran while one was open for 0% of the time, Pallas kernels for 0%

commit v1 on v0

--- a/solution.py
+++ b/solution.py
@@ -1,6 +1,8 @@
 import jax
 import jax.numpy as jnp
 from jax import lax
+from jax.experimental import pallas as pl
+from jax.experimental.pallas import tpu as pltpu
 from jax.sharding import PartitionSpec as P
 
 epsilon = 1e-05
@@ -49,7 +51,468 @@
     return lax.all_to_all(pieces, ("row", "col"), split_axis=0, concat_axis=0, tiled=True)
 
 
-def on_device(
+TILE = 128
+SUB = 16
+BLOCKS = TILE // SUB
+VMEM_LIMIT = 40 * 1024 * 1024
+BOTH = ("row", "col")
+NT = (((1,), (1,)), ((), ()))
+TN = (((0,), (0,)), ((), ()))
+
+
+def norm_rows(rows, gain, bias):
+    average = jnp.full((TILE, TILE), 1.0 / TILE, jnp.bfloat16)
+    centre = jnp.dot(rows, average, preferred_element_type=jnp.float32)
+    apart = rows.astype(jnp.float32) - centre
+    spread_out = jnp.dot(
+        (apart * apart).astype(jnp.bfloat16), average, preferred_element_type=jnp.float32
+    )
+    return (apart * lax.rsqrt(spread_out + epsilon) * gain + bias).astype(jnp.bfloat16)
+
+
+def gated_pairs(normed, weights, mask_rows):
+    both = lax.dot_general(weights, normed, NT, preferred_element_type=jnp.float32)
+    half = both.shape[0] // 2
+    projected = both[:half]
+    paired = projected * jnp.tanh(both[half:]) + projected
+    mask_flat = jnp.concatenate([mask_rows[r : r + 1, :] for r in range(SUB)], axis=1)
+    paired = (paired * mask_flat).astype(jnp.bfloat16)
+    return paired.reshape(half, SUB, TILE)
+
+
+def changed_state(triangle, rows, normed, gain, bias, proj, gate):
+    centre = jnp.mean(triangle, axis=0, keepdims=True)
+    apart = triangle - centre
+    variance = jnp.mean(apart * apart, axis=0, keepdims=True)
+    wide_gain = jnp.concatenate([gain] * SUB, axis=1)
+    wide_bias = jnp.concatenate([bias] * SUB, axis=1)
+    normed_out = (apart * lax.rsqrt(variance + epsilon) * wide_gain + wide_bias).astype(jnp.bfloat16)
+    out = lax.dot_general(normed_out, proj, TN, preferred_element_type=jnp.float32)
+    gate_value = jnp.tanh(jnp.dot(normed, gate, preferred_element_type=jnp.float32))
+    return (rows.astype(jnp.float32) + (out * gate_value + out)).astype(jnp.bfloat16)
+
+
+def enter_kernel(at, own, sib, mask, gain, bias, weights, *rest):
+    state_out, left_out, right_out = rest[-3:]
+    step = pl.program_id(0)
+    use_own = (step == 1) == (at[4] == 1)
+    picked = jnp.where(use_own, own[...], sib[...])
+    rows = picked.reshape(SUB * TILE, TILE)
+    normed = norm_rows(rows, gain[...], bias[...])
+    paired = gated_pairs(normed, weights[...], mask[0, 0].astype(jnp.float32))
+    half = paired.shape[0] // 2
+    left_out[0] = paired[:half]
+    right_out[0] = paired[half:]
+
+    @pl.when(use_own)
+    def _():
+        state_out[0, 0] = picked
+
+
+def enter(own, sib, first_block, at, mask, gain, bias, weights, held):
+    n_block = own.shape[0] // SUB
+    full = pl.BlockSpec(memory_space=pl.ANY)
+
+    def core_of(step, at):
+        return jnp.where(step == 1, at[2], 1 - at[2])
+
+    def is_own(step, at):
+        return (step == 1) == (at[4] == 1)
+
+    def own_map(step, block, at):
+        return (jnp.where(is_own(step, at), block, jnp.where(step == 0, 0, n_block - 1)), 0, 0)
+
+    def sib_map(step, block, at):
+        return (jnp.where(is_own(step, at), jnp.where(step == 0, 0, n_block - 1), block), 0, 0)
+
+    def mask_map(step, block, at):
+        return (2 * at[0] + core_of(step, at), at[1], first_block + block, 0)
+
+    def state_map(step, block, at):
+        kept = jnp.where(is_own(step, at), block, jnp.where(step == 0, 0, n_block - 1))
+        return (at[0], at[1], first_block + kept, 0, 0)
+
+    def left_map(step, block, at):
+        return (at[1], 0, (2 * at[0] + core_of(step, at)) * BLOCKS + first_block + block, 0)
+
+    def right_map(step, block, at):
+        slot = jnp.where(at[3] == 1, core_of(step, at), 2)
+        return (at[1], 0, slot * BLOCKS + first_block + block, 0)
+
+    half = weights.shape[0] // 4
+    same = lambda step, block, at: (0, 0)
+    shapes = (
+        jax.ShapeDtypeStruct((2, 4, TILE, TILE, TILE), jnp.bfloat16),
+        jax.ShapeDtypeStruct((4, half, 4 * TILE, TILE), jnp.bfloat16),
+        jax.ShapeDtypeStruct((4, half, 3 * TILE, TILE), jnp.bfloat16),
+    )
+    in_specs = [
+        pl.BlockSpec((SUB, TILE, TILE), own_map),
+        pl.BlockSpec((SUB, TILE, TILE), sib_map),
+        pl.BlockSpec((1, 1, SUB, TILE), mask_map),
+        pl.BlockSpec((1, TILE), same),
+        pl.BlockSpec((1, TILE), same),
+        pl.BlockSpec((4 * half, TILE), same),
+    ]
+    operands = [own, sib, mask, gain, bias, weights]
+    aliases = {}
+    if held is not None:
+        aliases = {len(operands) + 1 + n: n for n in range(3)}
+        operands += list(held)
+        in_specs += [full] * 3
+    pairs = 2 * own.shape[0] * TILE
+    return pl.pallas_call(
+        enter_kernel,
+        grid_spec=pltpu.PrefetchScalarGridSpec(
+            num_scalar_prefetch=1,
+            grid=(2, n_block),
+            in_specs=in_specs,
+            out_specs=[
+                pl.BlockSpec((1, 1, SUB, TILE, TILE), state_map),
+                pl.BlockSpec((1, half, SUB, TILE), left_map),
+                pl.BlockSpec((1, half, SUB, TILE), right_map),
+            ],
+        ),
+        out_shape=shapes,
+        input_output_aliases=aliases,
+        compiler_params=pltpu.CompilerParams(
+            dimension_semantics=("arbitrary", "arbitrary"), vmem_limit_bytes=VMEM_LIMIT
+        ),
+        cost_estimate=pl.CostEstimate(
+            flops=pairs * TILE * 1024, bytes_accessed=pairs * 1024, transcendentals=pairs * TILE
+        ),
+        name="enter",
+    )(at, *operands)
+
+
+def outgoing_kernel(at, left, right, keep, send):
+    core = at[0]
+    third = pl.multiple_of(at[1] * TILE, TILE)
+
+    def wide(ref, start, count):
+        return jnp.concatenate([ref[k, 0, pl.ds(start, count), :] for k in range(4)], axis=1)
+
+    near = wide(right, 0, 2 * TILE)
+    far = wide(right, third, TILE)
+    for out, which in ((keep, core), (send, 1 - core)):
+        rows = jnp.concatenate(
+            [wide(left, pl.multiple_of((2 * x + which) * TILE, TILE), TILE) for x in range(2)], axis=0
+        )
+        first = lax.dot_general(rows, near, NT, preferred_element_type=jnp.float32)
+        out[0, 0] = first[:, :TILE].astype(jnp.bfloat16)
+        out[1, 0] = first[:, TILE:].astype(jnp.bfloat16)
+        out[2, 0] = lax.dot_general(rows, far, NT, preferred_element_type=jnp.float32).astype(
+            jnp.bfloat16
+        )
+
+
+def outgoing(at, left, right):
+    half = left.shape[1]
+    out = jax.ShapeDtypeStruct((3, half, 2 * TILE, TILE), jnp.bfloat16)
+    return pl.pallas_call(
+        outgoing_kernel,
+        grid_spec=pltpu.PrefetchScalarGridSpec(
+            num_scalar_prefetch=1,
+            grid=(half,),
+            in_specs=[
+                pl.BlockSpec((4, 1, 4 * TILE, TILE), lambda d, at: (0, d, 0, 0)),
+                pl.BlockSpec((4, 1, 3 * TILE, TILE), lambda d, at: (0, d, 0, 0)),
+            ],
+            out_specs=[pl.BlockSpec((3, 1, 2 * TILE, TILE), lambda d, at: (0, d, 0, 0))] * 2,
+        ),
+        out_shape=(out, out),
+        compiler_params=pltpu.CompilerParams(
+            dimension_semantics=("arbitrary",), vmem_limit_bytes=VMEM_LIMIT
+        ),
+        cost_estimate=pl.CostEstimate(
+            flops=half * 512 * 384 * 1024, bytes_accessed=half * 1300 * 1024, transcendentals=0
+        ),
+        name="outgoing",
+    )(at, left, right)
+
+
+def middle_kernel(
+    at, kept, got, state, mask, gain0, bias0, gain_out, bias_out, proj, gate, gain1, bias1, weights,
+    pairs_out, state_out,
+):
+    rows = state[0, 0].reshape(SUB * TILE, TILE)
+    normed = norm_rows(rows, gain0[...], bias0[...])
+    triangle = jnp.concatenate([kept[0], got[0]], axis=0).reshape(TILE, SUB * TILE)
+    changed = changed_state(
+        triangle.astype(jnp.float32), rows, normed, gain_out[...], bias_out[...], proj[...], gate[...]
+    )
+    normed1 = norm_rows(changed, gain1[...], bias1[...])
+    pairs_out[0] = gated_pairs(normed1, weights[0], mask[0, 0].astype(jnp.float32))
+    state_out[...] = changed.reshape(SUB, TILE, TILE)
+
+
+def middle(at, kept, got, states, mask, gain0, bias0, gain_out, bias_out, proj, gate, gain1, bias1, weights):
+    half = kept.shape[1]
+
+    def column(slot, at):
+        return jnp.where(slot == 2, at[2], 2 * at[1] + slot)
+
+    same = lambda slot, x, block, at: (0, 0)
+    row = pl.BlockSpec((1, TILE), same)
+    square = pl.BlockSpec((TILE, TILE), same)
+    tri = pl.BlockSpec((1, half, SUB, TILE), lambda slot, x, block, at: (slot, 0, x * BLOCKS + block, 0))
+    pairs = 6 * TILE * TILE
+    return pl.pallas_call(
+        middle_kernel,
+        grid_spec=pltpu.PrefetchScalarGridSpec(
+            num_scalar_prefetch=1,
+            grid=(3, 2, BLOCKS),
+            in_specs=[
+                tri,
+                tri,
+                pl.BlockSpec(
+                    (1, 1, SUB, TILE, TILE),
+                    lambda slot, x, block, at: (x, column(slot, at), block, 0, 0),
+                ),
+                pl.BlockSpec(
+                    (1, 1, SUB, TILE),
+                    lambda slot, x, block, at: (2 * x + at[0], column(slot, at), block, 0),
+                ),
+                row,
+                row,
+                square,
+                square,
+                square,
+                square,
+                row,
+                row,
+                pl.BlockSpec(
+                    (1, 2 * TILE, TILE),
+                    lambda slot, x, block, at: (jnp.where(slot == 2, 1, 0), 0, 0),
+                ),
+            ],
+            out_specs=[
+                pl.BlockSpec(
+                    (1, TILE, SUB, TILE), lambda slot, x, block, at: (slot, 0, x * BLOCKS + block, 0)
+                ),
+                pl.BlockSpec(
+                    (SUB, TILE, TILE),
+                    lambda slot, x, block, at: (
+                        jnp.where(slot == 2, x * BLOCKS + block, 2 * BLOCKS), 0, 0,
+                    ),
+                ),
+            ],
+        ),
+        out_shape=(
+            jax.ShapeDtypeStruct((3, TILE, 2 * TILE, TILE), jnp.bfloat16),
+            jax.ShapeDtypeStruct(((2 * BLOCKS + 1) * SUB, TILE, TILE), jnp.bfloat16),
+        ),
+        compiler_params=pltpu.CompilerParams(
+            dimension_semantics=("arbitrary",) * 3, vmem_limit_bytes=VMEM_LIMIT
+        ),
+        cost_estimate=pl.CostEstimate(
+            flops=pairs * TILE * 1024, bytes_accessed=pairs * 1024, transcendentals=pairs * TILE * 2
+        ),
+        name="middle",
+    )(at, kept, got, states, mask, gain0, bias0, gain_out, bias_out, proj, gate, gain1, bias1, weights)
+
+
+CHANNELS = 8
+
+
+def incoming_kernel(at, pairs, keep, send):
+    core = at[0]
+    for d in range(CHANNELS):
+        right = pairs[2, d]
+        keep[d] = lax.dot_general(pairs[core, d], right, TN, preferred_element_type=jnp.float32)
+        send[d] = lax.dot_general(
+            pairs[1 - core, d], right, TN, preferred_element_type=jnp.float32
+        ).astype(jnp.bfloat16)
+
+
+def incoming(at, pairs):
+    out_spec = pl.BlockSpec((CHANNELS, TILE, TILE), lambda d, at: (d, 0, 0))
+    return pl.pallas_call(
+        incoming_kernel,
+        grid_spec=pltpu.PrefetchScalarGridSpec(
+            num_scalar_prefetch=1,
+            grid=(TILE // CHANNELS,),
+            in_specs=[pl.BlockSpec((3, CHANNELS, 2 * TILE, TILE), lambda d, at: (0, d, 0, 0))],
+            out_specs=[out_spec, out_spec],
+        ),
+        out_shape=(
+            jax.ShapeDtypeStruct((TILE, TILE, TILE), jnp.float32),
+            jax.ShapeDtypeStruct((TILE, TILE, TILE), jnp.bfloat16),
+        ),
+        compiler_params=pltpu.CompilerParams(
+            dimension_semantics=("arbitrary",), vmem_limit_bytes=VMEM_LIMIT
+        ),
+        cost_estimate=pl.CostEstimate(
+            flops=TILE * 512 * 256 * TILE, bytes_accessed=36 * 2**20, transcendentals=0
+        ),
+        name="incoming",
+    )(at, pairs)
+
+
+def leave_kernel(at, kept, got, state, gain1, bias1, gain_out, bias_out, proj, gate, result):
+    rows = state[...].reshape(SUB * TILE, TILE)
+    normed = norm_rows(rows, gain1[...], bias1[...])
+    summed = (kept[...] + got[...].astype(jnp.float32)).astype(jnp.bfloat16)
+    triangle = summed.reshape(TILE, SUB * TILE).astype(jnp.float32)
+    changed = changed_state(triangle, rows, normed, gain_out[...], bias_out[...], proj[...], gate[...])
+    result[...] = changed.reshape(SUB, TILE, TILE)
+
+
+def leave(at, kept, got, states, gain1, bias1, gain_out, bias_out, proj, gate):
+    same = lambda block, at: (0, 0)
+    row = pl.BlockSpec((1, TILE), same)
+    square = pl.BlockSpec((TILE, TILE), same)
+    tri = pl.BlockSpec((TILE, SUB, TILE), lambda block, at: (0, block, 0))
+    return pl.pallas_call(
+        leave_kernel,
+        grid_spec=pltpu.PrefetchScalarGridSpec(
+            num_scalar_prefetch=1,
+            grid=(BLOCKS,),
+            in_specs=[
+                tri,
+                tri,
+                pl.BlockSpec((SUB, TILE, TILE), lambda block, at: (at[1] * BLOCKS + block, 0, 0)),
+                row,
+                row,
+                square,
+                square,
+                square,
+                square,
+            ],
+            out_specs=pl.BlockSpec((SUB, TILE, TILE), lambda block, at: (block, 0, 0)),
+        ),
+        out_shape=jax.ShapeDtypeStruct((TILE, TILE, TILE), jnp.bfloat16),
+        compiler_params=pltpu.CompilerParams(
+            dimension_semantics=("arbitrary",), vmem_limit_bytes=VMEM_LIMIT
+        ),
+        cost_estimate=pl.CostEstimate(
+            flops=TILE**3 * 512, bytes_accessed=20 * 2**20, transcendentals=TILE**3
+        ),
+        name="leave",
+    )(at, kept, got, states, gain1, bias1, gain_out, bias_out, proj, gate)
+
+
+def on_device_ring(
+    pair_state,
+    pair_mask,
+    norm_in_gain,
+    norm_in_bias,
+    proj_in,
+    gate_in,
+    norm_out_gain,
+    norm_out_bias,
+    proj_out,
+    gate_out,
+):
+    row = lax.axis_index("row")
+    z = lax.axis_index("col")
+    x, core = row // 2, row % 2
+    place = jnp.where(x == 0, z, 7 - z)
+
+    def device(position, which):
+        on_x, on_z = (0, position) if position < 4 else (1, 7 - position)
+        return (2 * on_x + which) * 4 + on_z
+
+    up = [(device(p, w), device((p + 1) % 8, w)) for p in range(8) for w in range(2)]
+    down = [(target, source) for source, target in up]
+    swap = [(device(p, w), device(p, 1 - w)) for p in range(8) for w in range(2)]
+
+    mask = lax.all_gather(pair_mask.astype(jnp.bfloat16), BOTH).reshape(4, 4, TILE, TILE)
+
+    half = TILE // 2
+    ours = core * half
+    theirs = half - ours
+
+    def halved(matrix, start, width):
+        return (0.5 * lax.dynamic_slice_in_dim(matrix, start, width, axis=1)).T
+
+    enter_weights = jnp.concatenate(
+        [halved(m[0], side + ours, half) for m in (proj_in, gate_in) for side in (0, TILE)], axis=0
+    )
+    middle_weights = jnp.stack(
+        [
+            jnp.concatenate([halved(m[1], side, TILE) for m in (proj_in, gate_in)], axis=0)
+            for side in (0, TILE)
+        ]
+    )
+    gain_in = [norm_in_gain[u].reshape(1, TILE) for u in range(2)]
+    bias_in = [norm_in_bias[u].reshape(1, TILE) for u in range(2)]
+
+    def reordered(values):
+        return jnp.concatenate(
+            [lax.dynamic_slice_in_dim(values, start, half, axis=0) for start in (ours, theirs)], axis=0
+        )
+
+    def columns(values):
+        return jnp.broadcast_to(values[:, None], (TILE, TILE))
+
+    def project(held, offset, own, sib, first_block):
+        there = lax.rem(place + offset, 8)
+        there_x = there // 4
+        there_z = jnp.where(there_x == 0, there, 7 - there)
+        last = lax.rem(z, 2)
+        at = jnp.stack(
+            [there_x, there_z, last, (there_x == x).astype(jnp.int32), (last == core).astype(jnp.int32)]
+        ).astype(jnp.int32)
+        return enter(own, sib, first_block, at, mask, gain_in[0], bias_in[0], enter_weights, held)
+
+    held = project(None, 0, pair_state, lax.ppermute(pair_state, BOTH, swap), 0)
+    from_below = lax.ppermute(pair_state, BOTH, up)
+    from_above = lax.ppermute(pair_state, BOTH, down)
+    for step in range(1, 4):
+        from_below, from_above, held = lax.optimization_barrier((from_below, from_above, held))
+        now_below, now_above = from_below, from_above
+        if step < 3:
+            from_below = lax.ppermute(now_below, BOTH, up)
+            from_above = lax.ppermute(now_above, BOTH, down)
+        else:
+            part = TILE // 2
+            from_below = lax.ppermute(now_below[:part], BOTH, up)
+            from_above = lax.ppermute(now_above[part:], BOTH, down)
+        held = project(held, 8 - step, now_below, lax.ppermute(now_below, BOTH, swap), 0)
+        held = project(held, step, now_above, lax.ppermute(now_above, BOTH, swap), 0)
+    from_below, from_above, held = lax.optimization_barrier((from_below, from_above, held))
+    held = project(held, 4, from_below, lax.ppermute(from_below, BOTH, swap), 0)
+    held = project(held, 4, from_above, lax.ppermute(from_above, BOTH, swap), part // SUB)
+    states, left, right = held
+
+    third = jnp.where(z // 2 == x, lax.rem(z, 2), 2)
+    kept, sent = outgoing(jnp.stack([core, third]).astype(jnp.int32), left, right)
+    got = lax.ppermute(sent, BOTH, swap)
+    at = jnp.stack([core, x, z]).astype(jnp.int32)
+    pairs, states1 = middle(
+        at,
+        kept,
+        got,
+        states,
+        mask,
+        gain_in[0],
+        bias_in[0],
+        columns(reordered(norm_out_gain[0])),
+        columns(reordered(norm_out_bias[0])),
+        0.5 * reordered(proj_out[0]),
+        0.5 * gate_out[0],
+        gain_in[1],
+        bias_in[1],
+        middle_weights,
+    )
+    kept1, sent1 = incoming(at, pairs)
+    got1 = lax.ppermute(sent1, BOTH, swap)
+    return leave(
+        at,
+        kept1,
+        got1,
+        states1,
+        gain_in[1],
+        bias_in[1],
+        columns(norm_out_gain[1]),
+        columns(norm_out_bias[1]),
+        0.5 * proj_out[1],
+        0.5 * gate_out[1],
+    )
+
+
+def on_device_exchange(
     pair_state,
     pair_mask,
     norm_in_gain,
@@ -101,6 +564,13 @@
     return current
 
 
+def on_device(pair_state, *others):
+    square = pair_state.shape == (TILE, TILE, TILE)
+    if square and lax.axis_size("row") == 4 and lax.axis_size("col") == 4:
+        return on_device_ring(pair_state, *others)
+    return on_device_exchange(pair_state, *others)
+
+
 def solution(mesh):
     return jax.shard_map(
         on_device,

time: 775 us -> 655 us (0.85)
  Pallas kernels: 0 us -> 365 us
  blocking collectives: 478 us -> 118 us
  local copies, waits for them, and re-layouts: 103 us -> 22.5 us
  matrix products: 66.9 us -> 0 us
  waiting for transfers between devices: 94 us -> 132 us
  other arithmetic: 22.5 us -> 1.33 us
    all_to_all x3 -> x0, blocking collectives: 478 us -> none  [the longest x2 380 us: spread(): lax.all_to_all(paired, ('row', 'col'), split_axis=0, concat_axis=1, tiled...]
    pallas_call x0 -> x13, Pallas kernels: none -> 365 us  [the longest x9 172 us: enter(): pl.pallas_call(enter_kernel, grid_spec=pltpu.PrefetchScalarGridSpec(num_s...]
    ppermute x0 -> x19, waiting for transfers between devices: none -> 132 us  [the longest x2 86.2 us: on_device_ring(): from_below = lax.ppermute(now_below, BOTH, up)]
    all_gather x0 -> x1, blocking collectives: none -> 118 us  [on_device_ring(): lax.all_gather(pair_mask.astype(jnp.bfloat16), BOTH)]
    all_to_all x1 -> x0, waiting for transfers between devices: 94 us -> none  [gather_back(): lax.all_to_all(pieces, ('row', 'col'), split_axis=0, concat_axis=0, tiled...]
    dot_general x10 -> x0, matrix products: 66.9 us -> none  [the longest x2 26.4 us: on_device(): jnp.einsum('rcd,de->erc', normed, alternate(proj_in[update]), preferred_e...]
    reshape x5 -> x0, local copies, waits for them, and re-layouts: 33.2 us -> none  [the longest x3 17.1 us: gather_back(): triangle_out.reshape(channels, n_row, tile_rows, n_col, tile_cols)]
    convert_element_type x3 -> x0, local copies, waits for them, and re-layouts: 31.2 us -> none  [the longest x2 24.9 us: on_device(): (projected * jax.nn.sigmoid(gate_logit) * mask_weight).astype(jnp.bfloat16)]
  transfers between devices with their start and end apart: 1 -> 19, of which waited for: 1 -> 9; matrix products, arithmetic and copies ran while one was open for 0% -> 2% of each run, Pallas kernels for 0% -> 25%
where the time goes in v1:
time: 655 us; the launch traced here: 650 us
  Pallas kernels  365 us (56%)
  waiting for transfers between devices  132 us (20%)
  blocking collectives  118 us (18%)
  local copies, waits for them, and re-layouts  22.5 us (3%)
  starting transfers between devices  11.8 us (2%)
    pallas_call x9, Pallas kernels, enter(): pl.pallas_call(enter_kernel, grid_spec=pltpu.PrefetchScalarGridSpec(num_s...  172 us
    all_gather x1, blocking collectives, on_device_ring(): lax.all_gather(pair_mask.astype(jnp.bfloat16), BOTH)  118 us
    pallas_call x1, Pallas kernels, middle(): pl.pallas_call(middle_kernel, grid_spec=pltpu.PrefetchScalarGridSpec(num_...  102 us
    ppermute x2, waiting for transfers between devices, on_device_ring(): from_below = lax.ppermute(now_below, BOTH, up)  86.2 us
    pallas_call x1, Pallas kernels, outgoing(): pl.pallas_call(outgoing_kernel, grid_spec=pltpu.PrefetchScalarGridSpec(nu...  58 us
    ppermute x1, waiting for transfers between devices, on_device_ring(): got = lax.ppermute(sent, BOTH, swap)  18 us
    pallas_call x1, Pallas kernels, incoming(): pl.pallas_call(incoming_kernel, grid_spec=pltpu.PrefetchScalarGridSpec(nu...  17 us
    pallas_call x1, Pallas kernels, leave(): pl.pallas_call(leave_kernel, grid_spec=pltpu.PrefetchScalarGridSpec(num_s...  16 us
  transfers between devices with their start and end apart: 19, of which 9 were waited for; matrix products, arithmetic and copies ran while one was open for 2% of the time, Pallas kernels for 25%

profile of v1, /device:TPU:0, one launch (start us, length us, event | category | flops | bytes accessed | tf_op | source)
XLA Modules:
  0.0 649.9 jit_solution(14140179218602183194)
XLA Ops:
  0.0 0.5 collective-permute-start.2
  0.5 2.6 collective-permute-start
  3.0 1.5 fusion.8
  4.5 1.5 fusion.9
  6.6 0.9 convert_element_type.2
  7.6 0.8 fusion.10
  8.3 117.7 %all-gather = bf16[2048,128]{1,0:T(8,128)(2,1)S(1)} all-gather(bf16[128,128]{1,0:T(8,128)(2,1)S(1)} %convert_element_type.2), channel_id=2, replica_groups=mesh['ens'=2,'row'=4,'col'=4] {'row','col'}, dimensions={0}, use_global_device_ids=true | all-gather | bytes 557056 | tf_op jit(solution)/shard_map/all_gather | solution.py:420
  126.0 2.2 copy-done.2
  128.2 20.2 %enter.9 = (bf16[2,4,128,128,128]{4,3,2,1,0:T(8,128)(2,1)}, bf16[4,64,512,128]{3,2,1,0:T(8,128)(2,1)}, bf16[4,64,384,128]{3,2,1,0:T(8,128)(2,1)}) custom-call(s32[5]{0:T(128)S(1)} %stack.195.at, bf16[128,128,128]{2,1,0:T(8,128)(2,1)S(1)} %copy-done.2, bf16[128,128,128]{2,1,0:T(8,128)(2,1)} %collective-permute-done.2.sib, ...), custom_call_target="tpu_custom_call" | custom-call | flops 4294967296 | bytes 33554432 | tf_op jit(solution)/shard_map/enter/pallas_call | solution.py:164
  148.5 0.5 collective-permute-start.5
  149.0 1.4 collective-permute-start.3
  150.4 0.6 collective-permute-start.4
  151.2 4.8 collective-permute-done.6.sib
  156.0 21.4 %enter.10 = (bf16[2,4,128,128,128]{4,3,2,1,0:T(8,128)(2,1)}, bf16[4,64,512,128]{3,2,1,0:T(8,128)(2,1)}, bf16[4,64,384,128]{3,2,1,0:T(8,128)(2,1)}) custom-call(s32[5]{0:T(128)S(1)} %stack.205.at, bf16[128,128,128]{2,1,0:T(8,128)(2,1)} %collective-permute-done.own, ...), custom_call_target="tpu_custom_call", output_to_operand_aliasing={{0}: (7, {}), {1}: (8, {}), {2}: (9, {})} | custom-call | flops 4294967296 | bytes 33554432 | tf_op jit(solution)/shard_map/enter/pallas_call | solution.py:164
  177.4 21.3 %enter.11 = (bf16[2,4,128,128,128]{4,3,2,1,0:T(8,128)(2,1)}, bf16[4,64,512,128]{3,2,1,0:T(8,128)(2,1)}, bf16[4,64,384,128]{3,2,1,0:T(8,128)(2,1)}) custom-call(s32[5]{0:T(128)S(1)} %stack.200.at, bf16[128,128,128]{2,1,0:T(8,128)(2,1)} %collective-permute-done.1.own, ...), custom_call_target="tpu_custom_call", output_to_operand_aliasing={{0}: (7, {}), {1}: (8, {}), {2}: (9, {})} | custom-call | flops 4294967296 | bytes 33554432 | tf_op jit(solution)/shard_map/enter/pallas_call | solution.py:164
  198.7 43.2 %collective-permute-done.3.own = bf16[128,128,128]{2,1,0:T(8,128)(2,1)} collective-permute-done((bf16[128,128,128]{2,1,0:T(8,128)(2,1)}, bf16[128,128,128]{2,1,0:T(8,128)(2,1)}, u32[]{:S(2)}, u32[]{:S(2)}) %collective-permute-start.3) | collective-permute-done | bytes 4194336 | tf_op jit(solution)/shard_map/ppermute | solution.py:466
  241.9 1.1 collective-permute-done.4.own
  243.0 0.5 collective-permute-start.9
  243.5 0.3 collective-permute-start.7
  243.8 1.7 collective-permute-start.8
  245.7 4.8 collective-permute-done.10.sib
  250.5 21.4 %enter.12 = (bf16[2,4,128,128,128]{4,3,2,1,0:T(8,128)(2,1)}, bf16[4,64,512,128]{3,2,1,0:T(8,128)(2,1)}, bf16[4,64,384,128]{3,2,1,0:T(8,128)(2,1)}) custom-call(s32[5]{0:T(128)S(1)} %stack.215.at, bf16[128,128,128]{2,1,0:T(8,128)(2,1)} %collective-permute-done.3.own, ...), custom_call_target="tpu_custom_call", output_to_operand_aliasing={{0}: (7, {}), {1}: (8, {}), {2}: (9, {})} | custom-call | flops 4294967296 | bytes 33554432 | tf_op jit(solution)/shard_map/enter/pallas_call | solution.py:164
  271.9 21.4 %enter.13 = (bf16[2,4,128,128,128]{4,3,2,1,0:T(8,128)(2,1)}, bf16[4,64,512,128]{3,2,1,0:T(8,128)(2,1)}, bf16[4,64,384,128]{3,2,1,0:T(8,128)(2,1)}) custom-call(s32[5]{0:T(128)S(1)} %stack.210.at, bf16[128,128,128]{2,1,0:T(8,128)(2,1)} %collective-permute-done.4.own, ...), custom_call_target="tpu_custom_call", output_to_operand_aliasing={{0}: (7, {}), {1}: (8, {}), {2}: (9, {})} | custom-call | flops 4294967296 | bytes 33554432 | tf_op jit(solution)/shard_map/enter/pallas_call | solution.py:164
  293.3 43.0 %collective-permute-done.7.own = bf16[128,128,128]{2,1,0:T(8,128)(2,1)} collective-permute-done((bf16[128,128,128]{2,1,0:T(8,128)(2,1)}, bf16[128,128,128]{2,1,0:T(8,128)(2,1)}, u32[]{:S(2)}, u32[]{:S(2)}) %collective-permute-start.7) | collective-permute-done | bytes 4194336 | tf_op jit(solution)/shard_map/ppermute | solution.py:466
  336.3 0.5 collective-permute-start.13
  336.8 3.2 slice.62
  340.0 3.2 slice.63
  343.2 0.3 collective-permute-start.11
  343.5 1.7 collective-permute-start.12
  345.4 21.3 %enter.14 = (bf16[2,4,128,128,128]{4,3,2,1,0:T(8,128)(2,1)}, bf16[4,64,512,128]{3,2,1,0:T(8,128)(2,1)}, bf16[4,64,384,128]{3,2,1,0:T(8,128)(2,1)}) custom-call(s32[5]{0:T(128)S(1)} %stack.225.at, bf16[128,128,128]{2,1,0:T(8,128)(2,1)} %collective-permute-done.7.own, ...), custom_call_target="tpu_custom_call", output_to_operand_aliasing={{0}: (7, {}), {1}: (8, {}), {2}: (9, {})} | custom-call | flops 4294967296 | bytes 33554432 | tf_op jit(solution)/shard_map/enter/pallas_call | solution.py:164
  366.7 21.3 %enter.15 = (bf16[2,4,128,128,128]{4,3,2,1,0:T(8,128)(2,1)}, bf16[4,64,512,128]{3,2,1,0:T(8,128)(2,1)}, bf16[4,64,384,128]{3,2,1,0:T(8,128)(2,1)}) custom-call(s32[5]{0:T(128)S(1)} %stack.220.at, bf16[128,128,128]{2,1,0:T(8,128)(2,1)} %collective-permute-done.8.own, ...), custom_call_target="tpu_custom_call", output_to_operand_aliasing={{0}: (7, {}), {1}: (8, {}), {2}: (9, {})} | custom-call | flops 4294967296 | bytes 33554432 | tf_op jit(solution)/shard_map/enter/pallas_call | solution.py:164
  388.0 3.0 collective-permute-done.11.own
  391.0 0.5 collective-permute-start.15
  391.7 6.8 %collective-permute-done.16.sib = bf16[64,128,128]{2,1,0:T(8,128)(2,1)} collective-permute-done((bf16[64,128,128]{2,1,0:T(8,128)(2,1)}, bf16[64,128,128]{2,1,0:T(8,128)(2,1)}, u32[]{:S(2)}, u32[]{:S(2)}) %collective-permute-start.16) | collective-permute-done | bytes 2097184 | tf_op jit(solution)/shard_map/ppermute | solution.py:475
  398.5 11.9 %enter.16 = (bf16[2,4,128,128,128]{4,3,2,1,0:T(8,128)(2,1)}, bf16[4,64,512,128]{3,2,1,0:T(8,128)(2,1)}, bf16[4,64,384,128]{3,2,1,0:T(8,128)(2,1)}) custom-call(s32[5]{0:T(128)S(1)} %stack.190.at, bf16[64,128,128]{2,1,0:T(8,128)(2,1)} %collective-permute-done.11.own, ...), custom_call_target="tpu_custom_call", output_to_operand_aliasing={{0}: (7, {}), {1}: (8, {}), {2}: (9, {})} | custom-call | flops 2147483648 | bytes 16777216 | tf_op jit(solution)/shard_map/enter/pallas_call | solution.py:164
  410.4 11.4 %enter.17 = (bf16[2,4,128,128,128]{4,3,2,1,0:T(8,128)(2,1)}, bf16[4,64,512,128]{3,2,1,0:T(8,128)(2,1)}, bf16[4,64,384,128]{3,2,1,0:T(8,128)(2,1)}) custom-call(s32[5]{0:T(128)S(1)} %stack.190.at, bf16[64,128,128]{2,1,0:T(8,128)(2,1)S(1)} %collective-permute-done.12.own, ...), custom_call_target="tpu_custom_call", output_to_operand_aliasing={{0}: (7, {}), {1}: (8, {}), {2}: (9, {})} | custom-call | flops 2147483648 | bytes 16777216 | tf_op jit(solution)/shard_map/enter/pallas_call | solution.py:164
  421.8 58.0 %outgoing.1 = (bf16[3,64,256,128]{3,2,1,0:T(8,128)(2,1)S(1)}, bf16[3,64,256,128]{3,2,1,0:T(8,128)(2,1)}) custom-call(s32[2]{0:T(128)S(1)} %pad_add_fusion.1.at, bf16[4,64,512,128]{3,2,1,0:T(8,128)(2,1)} %get-tuple-element.102.left, bf16[4,64,384,128]{3,2,1,0:T(8,128)(2,1)} %get-tuple-element.103.right), custom_call_target="tpu_custom_call" | custom-call | flops 12884901888 | bytes 85196800 | tf_op jit(solution)/shard_map/outgoing/pallas_call | solution.py:212
  479.8 4.5 copy-done
  484.3 0.3 collective-permute-start.17
  484.8 0.1 copy.38
  485.1 0.1 copy.48
  485.8 18.0 %collective-permute-done.17.got = bf16[3,64,256,128]{3,2,1,0:T(8,128)(2,1)} collective-permute-done((bf16[3,64,256,128]{3,2,1,0:T(8,128)(2,1)}, bf16[3,64,256,128]{3,2,1,0:T(8,128)(2,1)}, u32[]{:S(2)}, u32[]{:S(2)}) %collective-permute-start.17) | collective-permute-done | bytes 12582944 | tf_op jit(solution)/shard_map/ppermute | solution.py:481
  504.0 102.0 %middle.1 = (bf16[3,128,256,128]{3,2,1,0:T(8,128)(2,1)}, bf16[272,128,128]{2,1,0:T(8,128)(2,1)S(1)}) custom-call(s32[3]{0:T(128)S(1)} %pad_add_fusion.at, bf16[3,64,256,128]{3,2,1,0:T(8,128)(2,1)} %copy-done, bf16[3,64,256,128]{3,2,1,0:T(8,128)(2,1)} %collective-permute-done.17.got, bf16[2,4,128,128,128]{4,3,2,1,0:T(8,128)(2,1)} %get-tuple-element.106.state, ...), custom_call_target="tpu_custom_call" | custom-call | flops 12884901888 | bytes 100663296 | tf_op jit(solution)/shard_map/middle/pallas_call | solution.py:260
  606.0 3.5 copy-done.1
  609.5 17.0 %incoming.1 = (f32[128,128,128]{2,1,0:T(8,128)S(1)}, bf16[128,128,128]{2,1,0:T(8,128)(2,1)S(1)}) custom-call(s32[3]{0:T(128)S(1)} %pad_add_fusion.at, bf16[3,128,256,128]{3,2,1,0:T(8,128)(2,1)} %get-tuple-element.107.pairs), custom_call_target="tpu_custom_call" | custom-call | flops 2147483648 | bytes 37748736 | tf_op jit(solution)/shard_map/incoming/pallas_call | solution.py:330
  626.5 0.3 collective-permute-start.18
  626.8 6.9 %collective-permute-done.18.got = bf16[128,128,128]{2,1,0:T(8,128)(2,1)S(1)} collective-permute-done((bf16[128,128,128]{2,1,0:T(8,128)(2,1)S(1)}, bf16[128,128,128]{2,1,0:T(8,128)(2,1)S(1)}, u32[]{:S(2)}, u32[]{:S(2)}) %collective-permute-start.18) | collective-permute-done | bytes 4194336 | tf_op jit(solution)/shard_map/ppermute | solution.py:500
  633.9 16.0 %leave.1 = bf16[128,128,128]{2,1,0:T(8,128)(2,1)} custom-call(s32[3]{0:T(128)S(1)} %pad_add_fusion.at, f32[128,128,128]{2,1,0:T(8,128)S(1)} %get-tuple-element.108.kept, bf16[128,128,128]{2,1,0:T(8,128)(2,1)S(1)} %collective-permute-done.18.got, bf16[272,128,128]{2,1,0:T(8,128)(2,1)} %copy-done.1, f32[1,128]{1,0:T(1,128)S(1)} %get-tuple-element.144.gain1, ...), custom_call_target="tpu_custom_call" | custom-call | flops 1073741824 | bytes 20971520 | tf_op jit(solution)/shard_map/leave/pallas_call | solution.py:366
  (70 shorter events, 2.5 us)
Async XLA Ops:
  0.0 126.0 %collective-permute-start.2 = (bf16[128,128,128]{2,1,0:T(8,128)(2,1)}, bf16[128,128,128]{2,1,0:T(8,128)(2,1)}, u32[]{:S(2)}, u32[]{:S(2)}) collective-permute-start(bf16[128,128,128]{2,1,0:T(8,128)(2,1)} %own.1), channel_id=1, source_target_pairs={{0,4},{4,0},{1,5},{5,1},{2,6},{6,2},{3,7},{7,3},{11,15},{15,11},{1... | collective-permute-start | bytes 12582920 | tf_op jit(solution)/shard_map/ppermute | solution.py:459
  0.5 148.0 %collective-permute-start = (bf16[128,128,128]{2,1,0:T(8,128)(2,1)}, bf16[128,128,128]{2,1,0:T(8,128)(2,1)}, u32[]{:S(2)}, u32[]{:S(2)}) collective-permute-start(bf16[128,128,128]{2,1,0:T(8,128)(2,1)} %own.1), channel_id=1, source_target_pairs={{0,1},{4,5},{1,2},{5,6},{2,3},{6,7},{3,11},{7,15},{11,10},{15,14},... | collective-permute-start | bytes 12582920 | tf_op jit(solution)/shard_map/ppermute | solution.py:460
  3.0 145.4 %collective-permute-start.1 = (bf16[128,128,128]{2,1,0:T(8,128)(2,1)}, bf16[128,128,128]{2,1,0:T(8,128)(2,1)}, u32[]{:S(2)}, u32[]{:S(2)}) collective-permute-start(bf16[128,128,128]{2,1,0:T(8,128)(2,1)} %own.1), channel_id=1, source_target_pairs={{1,0},{5,4},{2,1},{6,5},{3,2},{7,6},{11,3},{15,7},{10,11},{14,15},... | collective-permute-start | bytes 12582920 | tf_op jit(solution)/shard_map/ppermute | solution.py:461
  126.0 2.2 copy-start.2
  148.5 7.6 %collective-permute-start.6 = (bf16[128,128,128]{2,1,0:T(8,128)(2,1)}, bf16[128,128,128]{2,1,0:T(8,128)(2,1)}, u32[]{:S(2)}, u32[]{:S(2)}) collective-permute-start(bf16[128,128,128]{2,1,0:T(8,128)(2,1)} %collective-permute-done.own), channel_id=1, source_target_pairs={{0,4},{4,0},{1,5},{5,1},{2,6},{6,2},{3,7},{7,3},{11,15},{15,11},{1... | collective-permute-start | bytes 12582920 | tf_op jit(solution)/shard_map/ppermute | solution.py:472
  148.5 28.9 %collective-permute-start.5 = (bf16[128,128,128]{2,1,0:T(8,128)(2,1)}, bf16[128,128,128]{2,1,0:T(8,128)(2,1)}, u32[]{:S(2)}, u32[]{:S(2)}) collective-permute-start(bf16[128,128,128]{2,1,0:T(8,128)(2,1)} %collective-permute-done.1.own), channel_id=1, source_target_pairs={{0,4},{4,0},{1,5},{5,1},{2,6},{6,2},{3,7},{7,3},{11,15},{15,11},{1... | collective-permute-start | bytes 12582920 | tf_op jit(solution)/shard_map/ppermute | solution.py:473
  149.0 92.9 %collective-permute-start.3 = (bf16[128,128,128]{2,1,0:T(8,128)(2,1)}, bf16[128,128,128]{2,1,0:T(8,128)(2,1)}, u32[]{:S(2)}, u32[]{:S(2)}) collective-permute-start(bf16[128,128,128]{2,1,0:T(8,128)(2,1)} %collective-permute-done.own), channel_id=1, source_target_pairs={{0,1},{4,5},{1,2},{5,6},{2,3},{6,7},{3,11},{7,15},{11,10},{15,14},... | collective-permute-start | bytes 12582920 | tf_op jit(solution)/shard_map/ppermute | solution.py:466
  150.4 92.6 %collective-permute-start.4 = (bf16[128,128,128]{2,1,0:T(8,128)(2,1)}, bf16[128,128,128]{2,1,0:T(8,128)(2,1)}, u32[]{:S(2)}, u32[]{:S(2)}) collective-permute-start(bf16[128,128,128]{2,1,0:T(8,128)(2,1)} %collective-permute-done.1.own), channel_id=1, source_target_pairs={{1,0},{5,4},{2,1},{6,5},{3,2},{7,6},{11,3},{15,7},{10,11},{14,15},... | collective-permute-start | bytes 12582920 | tf_op jit(solution)/shard_map/ppermute | solution.py:467
  243.0 7.5 %collective-permute-start.10 = (bf16[128,128,128]{2,1,0:T(8,128)(2,1)}, bf16[128,128,128]{2,1,0:T(8,128)(2,1)}, u32[]{:S(2)}, u32[]{:S(2)}) collective-permute-start(bf16[128,128,128]{2,1,0:T(8,128)(2,1)} %collective-permute-done.3.own), channel_id=1, source_target_pairs={{0,4},{4,0},{1,5},{5,1},{2,6},{6,2},{3,7},{7,3},{11,15},{15,11},{1... | collective-permute-start | bytes 12582920 | tf_op jit(solution)/shard_map/ppermute | solution.py:472
  243.0 28.9 %collective-permute-start.9 = (bf16[128,128,128]{2,1,0:T(8,128)(2,1)}, bf16[128,128,128]{2,1,0:T(8,128)(2,1)}, u32[]{:S(2)}, u32[]{:S(2)}) collective-permute-start(bf16[128,128,128]{2,1,0:T(8,128)(2,1)} %collective-permute-done.4.own), channel_id=1, source_target_pairs={{0,4},{4,0},{1,5},{5,1},{2,6},{6,2},{3,7},{7,3},{11,15},{15,11},{1... | collective-permute-start | bytes 12582920 | tf_op jit(solution)/shard_map/ppermute | solution.py:473
  243.5 92.8 %collective-permute-start.7 = (bf16[128,128,128]{2,1,0:T(8,128)(2,1)}, bf16[128,128,128]{2,1,0:T(8,128)(2,1)}, u32[]{:S(2)}, u32[]{:S(2)}) collective-permute-start(bf16[128,128,128]{2,1,0:T(8,128)(2,1)} %collective-permute-done.3.own), channel_id=1, source_target_pairs={{0,1},{4,5},{1,2},{5,6},{2,3},{6,7},{3,11},{7,15},{11,10},{15,14},... | collective-permute-start | bytes 12582920 | tf_op jit(solution)/shard_map/ppermute | solution.py:466
  243.8 92.5 %collective-permute-start.8 = (bf16[128,128,128]{2,1,0:T(8,128)(2,1)}, bf16[128,128,128]{2,1,0:T(8,128)(2,1)}, u32[]{:S(2)}, u32[]{:S(2)}) collective-permute-start(bf16[128,128,128]{2,1,0:T(8,128)(2,1)} %collective-permute-done.4.own), channel_id=1, source_target_pairs={{1,0},{5,4},{2,1},{6,5},{3,2},{7,6},{11,3},{15,7},{10,11},{14,15},... | collective-permute-start | bytes 12582920 | tf_op jit(solution)/shard_map/ppermute | solution.py:467
  336.3 9.1 %collective-permute-start.14 = (bf16[128,128,128]{2,1,0:T(8,128)(2,1)}, bf16[128,128,128]{2,1,0:T(8,128)(2,1)}, u32[]{:S(2)}, u32[]{:S(2)}) collective-permute-start(bf16[128,128,128]{2,1,0:T(8,128)(2,1)} %collective-permute-done.7.own), channel_id=1, source_target_pairs={{0,4},{4,0},{1,5},{5,1},{2,6},{6,2},{3,7},{7,3},{11,15},{15,11},{1... | collective-permute-start | bytes 12582920 | tf_op jit(solution)/shard_map/ppermute | solution.py:472
  336.3 30.4 %collective-permute-start.13 = (bf16[128,128,128]{2,1,0:T(8,128)(2,1)}, bf16[128,128,128]{2,1,0:T(8,128)(2,1)}, u32[]{:S(2)}, u32[]{:S(2)}) collective-permute-start(bf16[128,128,128]{2,1,0:T(8,128)(2,1)} %collective-permute-done.8.own), channel_id=1, source_target_pairs={{0,4},{4,0},{1,5},{5,1},{2,6},{6,2},{3,7},{7,3},{11,15},{15,11},{1... | collective-permute-start | bytes 12582920 | tf_op jit(solution)/shard_map/ppermute | solution.py:473
  343.2 47.9 %collective-permute-start.11 = (bf16[64,128,128]{2,1,0:T(8,128)(2,1)}, bf16[64,128,128]{2,1,0:T(8,128)(2,1)}, u32[]{:S(2)}, u32[]{:S(2)}) collective-permute-start(bf16[64,128,128]{2,1,0:T(8,128)(2,1)} %slice.62), channel_id=1, source_target_pairs={{0,1},{4,5},{1,2},{5,6},{2,3},{6,7},{3,11},{7,15},{11,10},{15,14},... | collective-permute-start | bytes 6291464 | tf_op jit(solution)/shard_map/ppermute | solution.py:470
  343.5 47.6 %collective-permute-start.12 = (bf16[64,128,128]{2,1,0:T(8,128)(2,1)}, bf16[64,128,128]{2,1,0:T(8,128)(2,1)S(1)}, u32[]{:S(2)}, u32[]{:S(2)}) collective-permute-start(bf16[64,128,128]{2,1,0:T(8,128)(2,1)} %slice.63), channel_id=1, source_target_pairs={{1,0},{5,4},{2,1},{6,5},{3,2},{7,6},{11,3},{15,7},{10,11},{14,15},... | collective-permute-start | bytes 6291464 | tf_op jit(solution)/shard_map/ppermute | solution.py:471
  391.0 7.5 %collective-permute-start.16 = (bf16[64,128,128]{2,1,0:T(8,128)(2,1)}, bf16[64,128,128]{2,1,0:T(8,128)(2,1)}, u32[]{:S(2)}, u32[]{:S(2)}) collective-permute-start(bf16[64,128,128]{2,1,0:T(8,128)(2,1)} %collective-permute-done.11.own), channel_id=1, source_target_pairs={{0,4},{4,0},{1,5},{5,1},{2,6},{6,2},{3,7},{7,3},{11,15},{15,11},{1... | collective-permute-start | bytes 6291464 | tf_op jit(solution)/shard_map/ppermute | solution.py:475
  391.0 19.3 %collective-permute-start.15 = (bf16[64,128,128]{2,1,0:T(8,128)(2,1)S(1)}, bf16[64,128,128]{2,1,0:T(8,128)(2,1)}, u32[]{:S(2)}, u32[]{:S(2)}) collective-permute-start(bf16[64,128,128]{2,1,0:T(8,128)(2,1)S(1)} %collective-permute-done.12.own), channel_id=1, source_target_pairs={{0,4},{4,0},{1,5},{5,1},{2,6},{6,2},{3,7},{7,3},{11,15},{15,11},{1... | collective-permute-start | bytes 6291464 | tf_op jit(solution)/shard_map/ppermute | solution.py:476
  421.8 62.8 %copy-start.5 = (bf16[2,128,128]{2,1,0:T(8,128)(2,1)S(1)}, bf16[2,128,128]{2,1,0:T(8,128)(2,1)}, u32[]{:S(2)}) copy-start(bf16[2,128,128]{2,1,0:T(8,128)(2,1)} %param.18) | copy-start | bytes 196612
  421.8 63.3 %copy-start.3 = (bf16[1,128,256]{2,1,0:T(8,128)(2,1)S(1)}, bf16[1,128,256]{2,1,0:T(8,128)(2,1)}, u32[]{:S(2)}) copy-start(bf16[1,128,256]{2,1,0:T(8,128)(2,1)} %get-tuple-element.111) | copy-start | bytes 196612
  421.8 63.5 %copy-start.4 = (bf16[1,128,256]{2,1,0:T(8,128)(2,1)S(1)}, bf16[1,128,256]{2,1,0:T(8,128)(2,1)}, u32[]{:S(2)}) copy-start(bf16[1,128,256]{2,1,0:T(8,128)(2,1)} %get-tuple-element.113) | copy-start | bytes 196612
  421.8 63.6 %copy-start.7 = (f32[2,128]{1,0:T(2,128)S(1)}, f32[2,128]{1,0:T(2,128)}, u32[]{:S(2)}) copy-start(f32[2,128]{1,0:T(2,128)} %param.17) | copy-start | bytes 3076
  421.8 63.6 %copy-start.8 = (f32[2,128]{1,0:T(2,128)S(1)}, f32[2,128]{1,0:T(2,128)}, u32[]{:S(2)}) copy-start(f32[2,128]{1,0:T(2,128)} %param.16) | copy-start | bytes 3076
  421.8 64.0 %copy-start.6 = (bf16[2,128,128]{2,1,0:T(8,128)(2,1)S(1)}, bf16[2,128,128]{2,1,0:T(8,128)(2,1)}, u32[]{:S(2)}) copy-start(bf16[2,128,128]{2,1,0:T(8,128)(2,1)} %param.19) | copy-start | bytes 196612
  479.8 4.5 copy-start
  484.3 19.5 %collective-permute-start.17 = (bf16[3,64,256,128]{3,2,1,0:T(8,128)(2,1)}, bf16[3,64,256,128]{3,2,1,0:T(8,128)(2,1)}, u32[]{:S(2)}, u32[]{:S(2)}) collective-permute-start(bf16[3,64,256,128]{3,2,1,0:T(8,128)(2,1)} %get-tuple-element.105), channel_id=1, source_target_pairs={{0,4},{4,0},{1,5},{5,1},{2,6},{6,2},{3,7},{7,3},{11,15},{15,11},{1... | collective-permute-start | bytes 37748744 | tf_op jit(solution)/shard_map/ppermute | solution.py:481
  606.0 3.5 copy-start.1
  626.5 7.2 %collective-permute-start.18 = (bf16[128,128,128]{2,1,0:T(8,128)(2,1)S(1)}, bf16[128,128,128]{2,1,0:T(8,128)(2,1)S(1)}, u32[]{:S(2)}, u32[]{:S(2)}) collective-permute-start(bf16[128,128,128]{2,1,0:T(8,128)(2,1)S(1)} %get-tuple-element.109), channel_id=1, source_target_pairs={{0,4},{4,0},{1,5},{5,1},{2,6},{6,2},{3,7},{7,3},{11,15},{15,11},{1... | collective-permute-start | bytes 12582920 | tf_op jit(solution)/shard_map/ppermute | solution.py:500

commit v2 on v1

--- a/solution.py
+++ b/solution.py
@@ -60,56 +60,59 @@
 TN = (((0,), (0,)), ((), ()))
 
 
-def norm_rows(rows, gain, bias):
-    average = jnp.full((TILE, TILE), 1.0 / TILE, jnp.bfloat16)
-    centre = jnp.dot(rows, average, preferred_element_type=jnp.float32)
-    apart = rows.astype(jnp.float32) - centre
-    spread_out = jnp.dot(
-        (apart * apart).astype(jnp.bfloat16), average, preferred_element_type=jnp.float32
-    )
-    return (apart * lax.rsqrt(spread_out + epsilon) * gain + bias).astype(jnp.bfloat16)
-
-
-def gated_pairs(normed, weights, mask_rows):
-    both = lax.dot_general(weights, normed, NT, preferred_element_type=jnp.float32)
-    half = both.shape[0] // 2
-    projected = both[:half]
-    paired = projected * jnp.tanh(both[half:]) + projected
-    mask_flat = jnp.concatenate([mask_rows[r : r + 1, :] for r in range(SUB)], axis=1)
-    paired = (paired * mask_flat).astype(jnp.bfloat16)
-    return paired.reshape(half, SUB, TILE)
-
-
-def changed_state(triangle, rows, normed, gain, bias, proj, gate):
-    centre = jnp.mean(triangle, axis=0, keepdims=True)
-    apart = triangle - centre
+def channels_first(rows, matrix):
+    return lax.dot_general(matrix, rows, NT, preferred_element_type=jnp.float32)
+
+
+def norm_apart(apart, gain, bias):
     variance = jnp.mean(apart * apart, axis=0, keepdims=True)
     wide_gain = jnp.concatenate([gain] * SUB, axis=1)
     wide_bias = jnp.concatenate([bias] * SUB, axis=1)
-    normed_out = (apart * lax.rsqrt(variance + epsilon) * wide_gain + wide_bias).astype(jnp.bfloat16)
-    out = lax.dot_general(normed_out, proj, TN, preferred_element_type=jnp.float32)
-    gate_value = jnp.tanh(jnp.dot(normed, gate, preferred_element_type=jnp.float32))
-    return (rows.astype(jnp.float32) + (out * gate_value + out)).astype(jnp.bfloat16)
-
-
-def enter_kernel(at, own, sib, mask, gain, bias, weights, *rest):
-    state_out, left_out, right_out = rest[-3:]
+    return (apart * lax.rsqrt(variance + epsilon) * wide_gain + wide_bias).astype(jnp.bfloat16)
+
+
+def norm_channels(values, gain, bias):
+    return norm_apart(values - jnp.mean(values, axis=0, keepdims=True), gain, bias)
+
+
+def gated(weights, normed):
+    both = jnp.dot(weights, normed, preferred_element_type=jnp.float32)
+    half = both.shape[0] // 2
+    return both[:half] * jnp.tanh(both[half:]) + both[:half]
+
+
+def masked_tiles(paired, mask_rows, turn):
+    channels = paired.shape[0]
+    for r in range(SUB):
+        turn[pl.ds(r, channels, stride=SUB), :] = (
+            paired[:, r * TILE : (r + 1) * TILE] * mask_rows[r : r + 1, :]
+        )
+    return turn[...].astype(jnp.bfloat16).reshape(channels, SUB, TILE)
+
+
+def flat_channels(turn):
+    return jnp.concatenate([turn[pl.ds(r, TILE, stride=SUB), :] for r in range(SUB)], axis=1)
+
+
+def enter_kernel(at, own, sib, mask, centre, gain, bias, weights, *rest):
+    state_out, left_out, right_out, mask_out, turn = rest[-5:]
     step = pl.program_id(0)
     use_own = (step == 1) == (at[4] == 1)
     picked = jnp.where(use_own, own[...], sib[...])
-    rows = picked.reshape(SUB * TILE, TILE)
-    normed = norm_rows(rows, gain[...], bias[...])
-    paired = gated_pairs(normed, weights[...], mask[0, 0].astype(jnp.float32))
+    apart = channels_first(picked.reshape(SUB * TILE, TILE), centre[...])
+    normed = norm_apart(apart, gain[...], bias[...])
+    paired = masked_tiles(gated(weights[...], normed), mask[0].astype(jnp.float32), turn)
     half = paired.shape[0] // 2
     left_out[0] = paired[:half]
     right_out[0] = paired[half:]
+    mask_out[0, 0] = mask[0]
 
     @pl.when(use_own)
     def _():
         state_out[0, 0] = picked
 
 
-def enter(own, sib, first_block, at, mask, gain, bias, weights, held):
+def enter(own, sib, first_block, at, mask, centre, gain, bias, weights, held):
     n_block = own.shape[0] // SUB
     full = pl.BlockSpec(memory_space=pl.ANY)
 
@@ -126,6 +129,9 @@
         return (jnp.where(is_own(step, at), jnp.where(step == 0, 0, n_block - 1), block), 0, 0)
 
     def mask_map(step, block, at):
+        return (core_of(step, at), first_block + block, 0)
+
+    def mask_out_map(step, block, at):
         return (2 * at[0] + core_of(step, at), at[1], first_block + block, 0)
 
     def state_map(step, block, at):
@@ -145,21 +151,23 @@
         jax.ShapeDtypeStruct((2, 4, TILE, TILE, TILE), jnp.bfloat16),
         jax.ShapeDtypeStruct((4, half, 4 * TILE, TILE), jnp.bfloat16),
         jax.ShapeDtypeStruct((4, half, 3 * TILE, TILE), jnp.bfloat16),
+        jax.ShapeDtypeStruct((4, 4, TILE, TILE), jnp.bfloat16),
     )
     in_specs = [
         pl.BlockSpec((SUB, TILE, TILE), own_map),
         pl.BlockSpec((SUB, TILE, TILE), sib_map),
-        pl.BlockSpec((1, 1, SUB, TILE), mask_map),
-        pl.BlockSpec((1, TILE), same),
-        pl.BlockSpec((1, TILE), same),
+        pl.BlockSpec((1, SUB, TILE), mask_map),
+        pl.BlockSpec((TILE, TILE), same),
+        pl.BlockSpec((TILE, TILE), same),
+        pl.BlockSpec((TILE, TILE), same),
         pl.BlockSpec((4 * half, TILE), same),
     ]
-    operands = [own, sib, mask, gain, bias, weights]
+    operands = [own, sib, mask, centre, gain, bias, weights]
     aliases = {}
     if held is not None:
-        aliases = {len(operands) + 1 + n: n for n in range(3)}
+        aliases = {len(operands) + 1 + n: n for n in range(4)}
         operands += list(held)
-        in_specs += [full] * 3
+        in_specs += [full] * 4
     pairs = 2 * own.shape[0] * TILE
     return pl.pallas_call(
         enter_kernel,
@@ -171,7 +179,9 @@
                 pl.BlockSpec((1, 1, SUB, TILE, TILE), state_map),
                 pl.BlockSpec((1, half, SUB, TILE), left_map),
                 pl.BlockSpec((1, half, SUB, TILE), right_map),
+                pl.BlockSpec((1, 1, SUB, TILE), mask_out_map),
             ],
+            scratch_shapes=[pltpu.VMEM((2 * half * SUB, TILE), jnp.float32)],
         ),
         out_shape=shapes,
         input_output_aliases=aliases,
@@ -192,31 +202,32 @@
     def wide(ref, start, count):
         return jnp.concatenate([ref[k, 0, pl.ds(start, count), :] for k in range(4)], axis=1)
 
-    near = wide(right, 0, 2 * TILE)
-    far = wide(right, third, TILE)
-    for out, which in ((keep, core), (send, 1 - core)):
-        rows = jnp.concatenate(
-            [wide(left, pl.multiple_of((2 * x + which) * TILE, TILE), TILE) for x in range(2)], axis=0
-        )
-        first = lax.dot_general(rows, near, NT, preferred_element_type=jnp.float32)
-        out[0, 0] = first[:, :TILE].astype(jnp.bfloat16)
-        out[1, 0] = first[:, TILE:].astype(jnp.bfloat16)
-        out[2, 0] = lax.dot_general(rows, far, NT, preferred_element_type=jnp.float32).astype(
-            jnp.bfloat16
-        )
-
-
-def outgoing(at, left, right):
-    half = left.shape[1]
-    out = jax.ShapeDtypeStruct((3, half, 2 * TILE, TILE), jnp.bfloat16)
+    columns = jnp.concatenate([wide(right, 0, 2 * TILE), wide(right, third, TILE)], axis=0)
+    blocks = [2 * x + which for which in (core, 1 - core) for x in range(2)]
+    rows = jnp.concatenate(
+        [wide(left, pl.multiple_of(block * TILE, TILE), TILE) for block in blocks], axis=0
+    )
+    sums = lax.dot_general(rows, columns, NT, preferred_element_type=jnp.float32).astype(jnp.bfloat16)
+    for slot in range(3):
+        keep[slot, 0] = sums[: 2 * TILE, slot * TILE : (slot + 1) * TILE]
+        send[slot, 0] = sums[2 * TILE :, slot * TILE : (slot + 1) * TILE]
+
+
+PARTS = 4
+
+
+def outgoing(at, left, right, part):
+    count = left.shape[1] // PARTS
+    first = part * count
+    out = jax.ShapeDtypeStruct((3, count, 2 * TILE, TILE), jnp.bfloat16)
     return pl.pallas_call(
         outgoing_kernel,
         grid_spec=pltpu.PrefetchScalarGridSpec(
             num_scalar_prefetch=1,
-            grid=(half,),
+            grid=(count,),
             in_specs=[
-                pl.BlockSpec((4, 1, 4 * TILE, TILE), lambda d, at: (0, d, 0, 0)),
-                pl.BlockSpec((4, 1, 3 * TILE, TILE), lambda d, at: (0, d, 0, 0)),
+                pl.BlockSpec((4, 1, 4 * TILE, TILE), lambda d, at: (0, first + d, 0, 0)),
+                pl.BlockSpec((4, 1, 3 * TILE, TILE), lambda d, at: (0, first + d, 0, 0)),
             ],
             out_specs=[pl.BlockSpec((3, 1, 2 * TILE, TILE), lambda d, at: (0, d, 0, 0))] * 2,
         ),
@@ -225,37 +236,38 @@
             dimension_semantics=("arbitrary",), vmem_limit_bytes=VMEM_LIMIT
         ),
         cost_estimate=pl.CostEstimate(
-            flops=half * 512 * 384 * 1024, bytes_accessed=half * 1300 * 1024, transcendentals=0
+            flops=count * 512 * 384 * 1024, bytes_accessed=count * 1300 * 1024, transcendentals=0
         ),
         name="outgoing",
     )(at, left, right)
 
 
 def middle_kernel(
-    at, kept, got, state, mask, gain0, bias0, gain_out, bias_out, proj, gate, gain1, bias1, weights,
-    pairs_out, state_out,
+    at, state, mask, both, gain0, bias0, gain_out, bias_out, proj, gate, gain1, bias1, weights, *rest
 ):
-    rows = state[0, 0].reshape(SUB * TILE, TILE)
-    normed = norm_rows(rows, gain0[...], bias0[...])
-    triangle = jnp.concatenate([kept[0], got[0]], axis=0).reshape(TILE, SUB * TILE)
-    changed = changed_state(
-        triangle.astype(jnp.float32), rows, normed, gain_out[...], bias_out[...], proj[...], gate[...]
-    )
-    normed1 = norm_rows(changed, gain1[...], bias1[...])
-    pairs_out[0] = gated_pairs(normed1, weights[0], mask[0, 0].astype(jnp.float32))
-    state_out[...] = changed.reshape(SUB, TILE, TILE)
-
-
-def middle(at, kept, got, states, mask, gain0, bias0, gain_out, bias_out, proj, gate, gain1, bias1, weights):
-    half = kept.shape[1]
-
+    parts, (pairs_out, state_out, turn) = rest[:-3], rest[-3:]
+    turned = channels_first(state[0, 0].reshape(SUB * TILE, TILE), both[...])
+    normed = norm_apart(turned[:TILE], gain0[...], bias0[...])
+    height = TILE * SUB // len(parts)
+    for n, part in enumerate(parts):
+        turn[n * height : (n + 1) * height, :] = part[0].reshape(height, TILE).astype(jnp.float32)
+    normed_out = norm_channels(flat_channels(turn), gain_out[...], bias_out[...])
+    out = jnp.dot(proj[...], normed_out, preferred_element_type=jnp.float32)
+    gate_value = jnp.tanh(jnp.dot(gate[...], normed, preferred_element_type=jnp.float32))
+    changed = (turned[TILE:] + (out * gate_value + out)).astype(jnp.bfloat16)
+    state_out[0] = changed
+    normed1 = norm_channels(changed.astype(jnp.float32), gain1[...], bias1[...])
+    pairs_out[0] = masked_tiles(gated(weights[0], normed1), mask[0, 0].astype(jnp.float32), turn)
+
+
+def middle(at, states, mask, both, gain0, bias0, gain_out, bias_out, proj, gate, gain1, bias1, weights, parts):
     def column(slot, at):
         return jnp.where(slot == 2, at[2], 2 * at[1] + slot)
 
-    same = lambda slot, x, block, at: (0, 0)
-    row = pl.BlockSpec((1, TILE), same)
-    square = pl.BlockSpec((TILE, TILE), same)
-    tri = pl.BlockSpec((1, half, SUB, TILE), lambda slot, x, block, at: (slot, 0, x * BLOCKS + block, 0))
+    square = pl.BlockSpec((TILE, TILE), lambda slot, x, block, at: (0, 0))
+    tri = pl.BlockSpec(
+        (1, parts[0].shape[1], SUB, TILE), lambda slot, x, block, at: (slot, 0, x * BLOCKS + block, 0)
+    )
     pairs = 6 * TILE * TILE
     return pl.pallas_call(
         middle_kernel,
@@ -263,8 +275,6 @@
             num_scalar_prefetch=1,
             grid=(3, 2, BLOCKS),
             in_specs=[
-                tri,
-                tri,
                 pl.BlockSpec(
                     (1, 1, SUB, TILE, TILE),
                     lambda slot, x, block, at: (x, column(slot, at), block, 0, 0),
@@ -273,34 +283,32 @@
                     (1, 1, SUB, TILE),
                     lambda slot, x, block, at: (2 * x + at[0], column(slot, at), block, 0),
                 ),
-                row,
-                row,
-                square,
-                square,
-                square,
-                square,
-                row,
-                row,
+                pl.BlockSpec((2 * TILE, TILE), lambda slot, x, block, at: (0, 0)),
+            ]
+            + [square] * 8
+            + [
                 pl.BlockSpec(
                     (1, 2 * TILE, TILE),
                     lambda slot, x, block, at: (jnp.where(slot == 2, 1, 0), 0, 0),
-                ),
-            ],
+                )
+            ]
+            + [tri] * len(parts),
             out_specs=[
                 pl.BlockSpec(
                     (1, TILE, SUB, TILE), lambda slot, x, block, at: (slot, 0, x * BLOCKS + block, 0)
                 ),
                 pl.BlockSpec(
-                    (SUB, TILE, TILE),
+                    (1, TILE, SUB * TILE),
                     lambda slot, x, block, at: (
                         jnp.where(slot == 2, x * BLOCKS + block, 2 * BLOCKS), 0, 0,
                     ),
                 ),
             ],
+            scratch_shapes=[pltpu.VMEM((TILE * SUB, TILE), jnp.float32)],
         ),
         out_shape=(
             jax.ShapeDtypeStruct((3, TILE, 2 * TILE, TILE), jnp.bfloat16),
-            jax.ShapeDtypeStruct(((2 * BLOCKS + 1) * SUB, TILE, TILE), jnp.bfloat16),
+            jax.ShapeDtypeStruct((2 * BLOCKS + 1, TILE, SUB * TILE), jnp.bfloat16),
         ),
         compiler_params=pltpu.CompilerParams(
             dimension_semantics=("arbitrary",) * 3, vmem_limit_bytes=VMEM_LIMIT
@@ -309,7 +317,7 @@
             flops=pairs * TILE * 1024, bytes_accessed=pairs * 1024, transcendentals=pairs * TILE * 2
         ),
         name="middle",
-    )(at, kept, got, states, mask, gain0, bias0, gain_out, bias_out, proj, gate, gain1, bias1, weights)
+    )(at, states, mask, both, gain0, bias0, gain_out, bias_out, proj, gate, gain1, bias1, weights, *parts)
 
 
 CHANNELS = 8
@@ -349,19 +357,20 @@
     )(at, pairs)
 
 
-def leave_kernel(at, kept, got, state, gain1, bias1, gain_out, bias_out, proj, gate, result):
-    rows = state[...].reshape(SUB * TILE, TILE)
-    normed = norm_rows(rows, gain1[...], bias1[...])
+def leave_kernel(at, kept, got, state, gain1, bias1, gain_out, bias_out, proj, gate, result, turn):
+    rows = state[0].astype(jnp.float32)
+    normed = norm_channels(rows, gain1[...], bias1[...])
     summed = (kept[...] + got[...].astype(jnp.float32)).astype(jnp.bfloat16)
-    triangle = summed.reshape(TILE, SUB * TILE).astype(jnp.float32)
-    changed = changed_state(triangle, rows, normed, gain_out[...], bias_out[...], proj[...], gate[...])
-    result[...] = changed.reshape(SUB, TILE, TILE)
-
-
-def leave(at, kept, got, states, gain1, bias1, gain_out, bias_out, proj, gate):
-    same = lambda block, at: (0, 0)
-    row = pl.BlockSpec((1, TILE), same)
-    square = pl.BlockSpec((TILE, TILE), same)
+    turn[...] = summed.astype(jnp.float32).reshape(TILE * SUB, TILE)
+    normed_out = norm_channels(flat_channels(turn), gain_out[...], bias_out[...])
+    out = jnp.dot(proj[...], normed_out, preferred_element_type=jnp.float32)
+    gate_value = jnp.tanh(jnp.dot(gate[...], normed, preferred_element_type=jnp.float32))
+    changed = (rows + (out * gate_value + out)).astype(jnp.bfloat16)
+    result[...] = changed.T.reshape(SUB, TILE, TILE)
+
+
+def leave(at, kept, got, states, *fixed):
+    square = pl.BlockSpec((TILE, TILE), lambda block, at: (0, 0))
     tri = pl.BlockSpec((TILE, SUB, TILE), lambda block, at: (0, block, 0))
     return pl.pallas_call(
         leave_kernel,
@@ -371,15 +380,11 @@
             in_specs=[
                 tri,
                 tri,
-                pl.BlockSpec((SUB, TILE, TILE), lambda block, at: (at[1] * BLOCKS + block, 0, 0)),
-                row,
-                row,
-                square,
-                square,
-                square,
-                square,
-            ],
+                pl.BlockSpec((1, TILE, SUB * TILE), lambda block, at: (at[1] * BLOCKS + block, 0, 0)),
+            ]
+            + [square] * 6,
             out_specs=pl.BlockSpec((SUB, TILE, TILE), lambda block, at: (block, 0, 0)),
+            scratch_shapes=[pltpu.VMEM((TILE * SUB, TILE), jnp.float32)],
         ),
         out_shape=jax.ShapeDtypeStruct((TILE, TILE, TILE), jnp.bfloat16),
         compiler_params=pltpu.CompilerParams(
@@ -389,7 +394,7 @@
             flops=TILE**3 * 512, bytes_accessed=20 * 2**20, transcendentals=TILE**3
         ),
         name="leave",
-    )(at, kept, got, states, gain1, bias1, gain_out, bias_out, proj, gate)
+    )(at, kept, got, states, *fixed)
 
 
 def on_device_ring(
@@ -417,7 +422,9 @@
     down = [(target, source) for source, target in up]
     swap = [(device(p, w), device(p, 1 - w)) for p in range(8) for w in range(2)]
 
-    mask = lax.all_gather(pair_mask.astype(jnp.bfloat16), BOTH).reshape(4, 4, TILE, TILE)
+    own_mask = pair_mask.astype(jnp.bfloat16)
+    sib_mask = lax.ppermute(own_mask, BOTH, swap)
+    masks = jnp.where(core == 0, jnp.stack([own_mask, sib_mask]), jnp.stack([sib_mask, own_mask]))
 
     half = TILE // 2
     ours = core * half
@@ -435,9 +442,8 @@
             for side in (0, TILE)
         ]
     )
-    gain_in = [norm_in_gain[u].reshape(1, TILE) for u in range(2)]
-    bias_in = [norm_in_bias[u].reshape(1, TILE) for u in range(2)]
-
+    identity = jnp.eye(TILE, dtype=jnp.bfloat16)
+    centre = identity - jnp.bfloat16(1.0 / TILE)
     def reordered(values):
         return jnp.concatenate(
             [lax.dynamic_slice_in_dim(values, start, half, axis=0) for start in (ours, theirs)], axis=0
@@ -446,7 +452,10 @@
     def columns(values):
         return jnp.broadcast_to(values[:, None], (TILE, TILE))
 
-    def project(held, offset, own, sib, first_block):
+    gain_in = [columns(norm_in_gain[u]) for u in range(2)]
+    bias_in = [columns(norm_in_bias[u]) for u in range(2)]
+
+    def project(held, offset, own, sib, mask, first_block):
         there = lax.rem(place + offset, 8)
         there_x = there // 4
         there_z = jnp.where(there_x == 0, there, 7 - there)
@@ -454,62 +463,68 @@
         at = jnp.stack(
             [there_x, there_z, last, (there_x == x).astype(jnp.int32), (last == core).astype(jnp.int32)]
         ).astype(jnp.int32)
-        return enter(own, sib, first_block, at, mask, gain_in[0], bias_in[0], enter_weights, held)
-
-    held = project(None, 0, pair_state, lax.ppermute(pair_state, BOTH, swap), 0)
-    from_below = lax.ppermute(pair_state, BOTH, up)
-    from_above = lax.ppermute(pair_state, BOTH, down)
-    for step in range(1, 4):
-        from_below, from_above, held = lax.optimization_barrier((from_below, from_above, held))
-        now_below, now_above = from_below, from_above
-        if step < 3:
-            from_below = lax.ppermute(now_below, BOTH, up)
-            from_above = lax.ppermute(now_above, BOTH, down)
-        else:
-            part = TILE // 2
-            from_below = lax.ppermute(now_below[:part], BOTH, up)
-            from_above = lax.ppermute(now_above[part:], BOTH, down)
-        held = project(held, 8 - step, now_below, lax.ppermute(now_below, BOTH, swap), 0)
-        held = project(held, step, now_above, lax.ppermute(now_above, BOTH, swap), 0)
-    from_below, from_above, held = lax.optimization_barrier((from_below, from_above, held))
-    held = project(held, 4, from_below, lax.ppermute(from_below, BOTH, swap), 0)
-    held = project(held, 4, from_above, lax.ppermute(from_above, BOTH, swap), part // SUB)
-    states, left, right = held
-
-    third = jnp.where(z // 2 == x, lax.rem(z, 2), 2)
-    kept, sent = outgoing(jnp.stack([core, third]).astype(jnp.int32), left, right)
-    got = lax.ppermute(sent, BOTH, swap)
-    at = jnp.stack([core, x, z]).astype(jnp.int32)
-    pairs, states1 = middle(
-        at,
-        kept,
-        got,
-        states,
-        mask,
+        return enter(own, sib, first_block, at, mask, centre, gain_in[0], bias_in[0], enter_weights, held)
+
+    def hop(values, pairs):
+        return [lax.ppermute(value, BOTH, pairs) for value in values]
+
+    held = project(None, 0, pair_state, lax.ppermute(pair_state, BOTH, swap), masks, 0)
+    below = hop([masks, pair_state], up)
+    above = hop([masks, pair_state], down)
+    part = TILE // 2
+    middle_fixed = [
+        jnp.concatenate([centre, identity], axis=0),
         gain_in[0],
         bias_in[0],
         columns(reordered(norm_out_gain[0])),
         columns(reordered(norm_out_bias[0])),
-        0.5 * reordered(proj_out[0]),
-        0.5 * gate_out[0],
+        0.5 * reordered(proj_out[0]).T,
+        0.5 * gate_out[0].T,
         gain_in[1],
         bias_in[1],
         middle_weights,
-    )
-    kept1, sent1 = incoming(at, pairs)
-    got1 = lax.ppermute(sent1, BOTH, swap)
-    return leave(
-        at,
-        kept1,
-        got1,
-        states1,
+    ]
+    leave_fixed = [
         gain_in[1],
         bias_in[1],
         columns(norm_out_gain[1]),
         columns(norm_out_bias[1]),
-        0.5 * proj_out[1],
-        0.5 * gate_out[1],
-    )
+        0.5 * proj_out[1].T,
+        0.5 * gate_out[1].T,
+    ]
+    for step in range(1, 4):
+        below, above, held, middle_fixed, leave_fixed = lax.optimization_barrier(
+            (below, above, held, middle_fixed, leave_fixed)
+        )
+        now_below, now_above = below, above
+        if step < 3:
+            below = hop(now_below, up)
+            above = hop(now_above, down)
+        else:
+            below = hop([now_below[0], now_below[1][:part]], up)
+            above = hop([now_above[1][part:]], down)
+        for offset, (mask, tile) in ((8 - step, now_below), (step, now_above)):
+            held = project(held, offset, tile, lax.ppermute(tile, BOTH, swap), mask, 0)
+    below, above, held = lax.optimization_barrier((below, above, held))
+    held = project(held, 4, below[1], lax.ppermute(below[1], BOTH, swap), below[0], 0)
+    held = project(held, 4, above[0], lax.ppermute(above[0], BOTH, swap), below[0], part // SUB)
+    states, left, right, mask = held
+
+    third = jnp.where(z // 2 == x, lax.rem(z, 2), 2)
+    at_tri = jnp.stack([core, third]).astype(jnp.int32)
+    kept, got = [], []
+    for n in range(PARTS):
+        if n >= 2:
+            at_tri, got[n - 2] = lax.optimization_barrier((at_tri, got[n - 2]))
+        stays, leaves = outgoing(at_tri, left, right, n)
+        kept.append(stays)
+        got.append(lax.ppermute(leaves, BOTH, swap))
+    parts = kept + got
+    at = jnp.stack([core, x, z]).astype(jnp.int32)
+    pairs, states1 = middle(at, states, mask, *middle_fixed, parts)
+    kept1, sent1 = incoming(at, pairs)
+    got1 = lax.ppermute(sent1, BOTH, swap)
+    return leave(at, kept1, got1, states1, *leave_fixed)
 
 
 def on_device_exchange(

time: 655 us -> 610 us (0.931)
  blocking collectives: 118 us -> 0 us
  waiting for transfers between devices: 132 us -> 183 us
  Pallas kernels: 365 us -> 378 us
  starting transfers between devices: 11.8 us -> 20.9 us
    all_gather x1 -> x0, blocking collectives: 118 us -> none  [on_device_ring(): lax.all_gather(pair_mask.astype(jnp.bfloat16), BOTH)]
    ppermute x18 -> x29, waiting for transfers between devices: 125 us -> 176 us  [the longest x15 154 us: hop(): return [lax.ppermute(value, BOTH, pairs) for value in values]]
    pallas_call x1, Pallas kernels: 102 us -> 118 us  [middle(): pl.pallas_call(middle_kernel, grid_spec=pltpu.PrefetchScalarGridSpec(num_...]
    ppermute x18 -> x29, starting transfers between devices: 11.5 us -> 20.3 us  [the longest x15 16.3 us: hop(): return [lax.ppermute(value, BOTH, pairs) for value in values]]
    pallas_call x1 -> x4, Pallas kernels: 58 us -> 58.7 us  [outgoing(): pl.pallas_call(outgoing_kernel, grid_spec=pltpu.PrefetchScalarGridSpec(nu...]
  transfers between devices with their start and end apart: 19 -> 30, of which waited for: 9 -> 13; matrix products, arithmetic and copies ran while one was open for 2% -> 3% of each run, Pallas kernels for 25% -> 31%
where the time goes in v2:
time: 610 us; the launch traced here: 605 us
  Pallas kernels  378 us (62%)
  waiting for transfers between devices  183 us (30%)
  starting transfers between devices  20.9 us (3%)
  local copies, waits for them, and re-layouts  20.1 us (3%)
    pallas_call x9, Pallas kernels, enter(): pl.pallas_call(enter_kernel, grid_spec=pltpu.PrefetchScalarGridSpec(num_s...  168 us
    ppermute x15, waiting for transfers between devices, hop(): return [lax.ppermute(value, BOTH, pairs) for value in values]  154 us
    pallas_call x1, Pallas kernels, middle(): pl.pallas_call(middle_kernel, grid_spec=pltpu.PrefetchScalarGridSpec(num_...  118 us
    pallas_call x4, Pallas kernels, outgoing(): pl.pallas_call(outgoing_kernel, grid_spec=pltpu.PrefetchScalarGridSpec(nu...  58.7 us
    pallas_call x1, Pallas kernels, incoming(): pl.pallas_call(incoming_kernel, grid_spec=pltpu.PrefetchScalarGridSpec(nu...  17 us
    ppermute x15, starting transfers between devices, hop(): return [lax.ppermute(value, BOTH, pairs) for value in values]  16.3 us
    pallas_call x1, Pallas kernels, leave(): pl.pallas_call(leave_kernel, grid_spec=pltpu.PrefetchScalarGridSpec(num_s...  15.7 us
  transfers between devices with their start and end apart: 30, of which 13 were waited for; matrix products, arithmetic and copies ran while one was open for 3% of the time, Pallas kernels for 31%

profile of v2, /device:TPU:0, one launch (start us, length us, event | category | flops | bytes accessed | tf_op | source)
XLA Modules:
  0.0 605.4 jit_solution(9564025459480987721)
XLA Ops:
  0.5 2.6 collective-permute-start.2
  3.0 0.8 convert_element_type.44
  4.1 0.9 fusion.10
  5.0 0.9 fusion.11
  6.4 0.8 fusion.13
  8.7 0.8 fusion.12
  12.9 0.8 convert_bitcast_fusion
  14.6 1.9 collective-permute-start.1
  16.8 2.2 copy-done.7
  19.0 19.7 %enter.9 = (bf16[2,4,128,128,128]{4,3,2,1,0:T(8,128)(2,1)}, bf16[4,64,512,128]{3,2,1,0:T(8,128)(2,1)}, bf16[4,64,384,128]{3,2,1,0:T(8,128)(2,1)}, bf16[4,4,128,128]{3,2,1,0:T(8,128)(2,1)S(1)}) custom-call(s32[5]{0:T(128)S(1)} %stack.211.at, bf16[128,128,128]{2,1,0:T(8,128)(2,1)S(1)} %copy-done.7, bf16[128,128,128]{2,1,0:T(8,128)(2,1)} %collective-permute-done.5.sib, ...), custom_call_target="tpu_custom_call" | custom-call | flops 4294967296 | bytes 33554432 | tf_op jit(solution)/shard_map/enter/pallas_call | solution.py:172
  38.7 57.1 %collective-permute-done.1.mask = bf16[2,128,128]{2,1,0:T(8,128)(2,1)S(1)} collective-permute-done((bf16[2,128,128]{2,1,0:T(8,128)(2,1)S(1)}, bf16[2,128,128]{2,1,0:T(8,128)(2,1)S(1)}, u32[]{:S(2)}, u32[]{:S(2)}) %collective-permute-start.1) | collective-permute-done | bytes 65568 | tf_op jit(solution)/shard_map/ppermute | solution.py:469
  95.8 1.5 collective-permute-done.3.mask
  98.4 1.6 collective-permute-start.7
  100.6 1.6 collective-permute-start.6
  102.2 3.2 collective-permute-done.11.sib
  105.7 20.9 %enter.10 = (bf16[2,4,128,128,128]{4,3,2,1,0:T(8,128)(2,1)}, bf16[4,64,512,128]{3,2,1,0:T(8,128)(2,1)}, bf16[4,64,384,128]{3,2,1,0:T(8,128)(2,1)}, bf16[4,4,128,128]{3,2,1,0:T(8,128)(2,1)S(1)}) custom-call(s32[5]{0:T(128)S(1)} %stack.224.at, ...), custom_call_target="tpu_custom_call", output_to_operand_aliasing={{0}: (8, {}), {1}: (9, {}), {2}: (10, {}), {3}: (11, {})} | custom-call | flops 4294967296 | bytes 33554432 | tf_op jit(solution)/shard_map/enter/pallas_call | solution.py:172
  126.7 20.9 %enter.11 = (bf16[2,4,128,128,128]{4,3,2,1,0:T(8,128)(2,1)}, bf16[4,64,512,128]{3,2,1,0:T(8,128)(2,1)}, bf16[4,64,384,128]{3,2,1,0:T(8,128)(2,1)}, bf16[4,4,128,128]{3,2,1,0:T(8,128)(2,1)S(1)}) custom-call(s32[5]{0:T(128)S(1)} %stack.219.at, ...), custom_call_target="tpu_custom_call", output_to_operand_aliasing={{0}: (8, {}), {1}: (9, {}), {2}: (10, {}), {3}: (11, {})} | custom-call | flops 4294967296 | bytes 33554432 | tf_op jit(solution)/shard_map/enter/pallas_call | solution.py:172
  147.6 45.0 %collective-permute-done.6.mask = bf16[2,128,128]{2,1,0:T(8,128)(2,1)S(1)} collective-permute-done((bf16[2,128,128]{2,1,0:T(8,128)(2,1)S(1)}, bf16[2,128,128]{2,1,0:T(8,128)(2,1)S(1)}, u32[]{:S(2)}, u32[]{:S(2)}) %collective-permute-start.6) | collective-permute-done | bytes 65568 | tf_op jit(solution)/shard_map/ppermute | solution.py:469
  192.6 1.3 collective-permute-done.8.mask
  194.4 1.6 collective-permute-start.13
  196.6 1.6 collective-permute-start.12
  198.2 3.2 collective-permute-done.17.sib
  201.8 20.9 %enter.12 = (bf16[2,4,128,128,128]{4,3,2,1,0:T(8,128)(2,1)}, bf16[4,64,512,128]{3,2,1,0:T(8,128)(2,1)}, bf16[4,64,384,128]{3,2,1,0:T(8,128)(2,1)}, bf16[4,4,128,128]{3,2,1,0:T(8,128)(2,1)S(1)}) custom-call(s32[5]{0:T(128)S(1)} %stack.234.at, ...), custom_call_target="tpu_custom_call", output_to_operand_aliasing={{0}: (8, {}), {1}: (9, {}), {2}: (10, {}), {3}: (11, {})} | custom-call | flops 4294967296 | bytes 33554432 | tf_op jit(solution)/shard_map/enter/pallas_call | solution.py:172
  222.8 21.0 %enter.13 = (bf16[2,4,128,128,128]{4,3,2,1,0:T(8,128)(2,1)}, bf16[4,64,512,128]{3,2,1,0:T(8,128)(2,1)}, bf16[4,64,384,128]{3,2,1,0:T(8,128)(2,1)}, bf16[4,4,128,128]{3,2,1,0:T(8,128)(2,1)S(1)}) custom-call(s32[5]{0:T(128)S(1)} %stack.229.at, ...), custom_call_target="tpu_custom_call", output_to_operand_aliasing={{0}: (8, {}), {1}: (9, {}), {2}: (10, {}), {3}: (11, {})} | custom-call | flops 4294967296 | bytes 33554432 | tf_op jit(solution)/shard_map/enter/pallas_call | solution.py:172
  243.8 44.8 %collective-permute-done.12.mask = bf16[2,128,128]{2,1,0:T(8,128)(2,1)S(1)} collective-permute-done((bf16[2,128,128]{2,1,0:T(8,128)(2,1)S(1)}, bf16[2,128,128]{2,1,0:T(8,128)(2,1)S(1)}, u32[]{:S(2)}, u32[]{:S(2)}) %collective-permute-start.12) | collective-permute-done | bytes 65568 | tf_op jit(solution)/shard_map/ppermute | solution.py:469
  288.6 1.3 collective-permute-done.14.mask
  290.4 3.2 slice.74
  293.6 3.2 slice.75
  296.8 1.5 collective-permute-start.19
  299.0 1.7 collective-permute-start.18
  300.6 0.9 copy-done.4
  301.5 21.0 %enter.14 = (bf16[2,4,128,128,128]{4,3,2,1,0:T(8,128)(2,1)}, bf16[4,64,512,128]{3,2,1,0:T(8,128)(2,1)}, bf16[4,64,384,128]{3,2,1,0:T(8,128)(2,1)}, bf16[4,4,128,128]{3,2,1,0:T(8,128)(2,1)S(1)}) custom-call(s32[5]{0:T(128)S(1)} %stack.244.at, ...), custom_call_target="tpu_custom_call", output_to_operand_aliasing={{0}: (8, {}), {1}: (9, {}), {2}: (10, {}), {3}: (11, {})} | custom-call | flops 4294967296 | bytes 33554432 | tf_op jit(solution)/shard_map/enter/pallas_call | solution.py:172
  322.4 20.9 %enter.15 = (bf16[2,4,128,128,128]{4,3,2,1,0:T(8,128)(2,1)}, bf16[4,64,512,128]{3,2,1,0:T(8,128)(2,1)}, bf16[4,64,384,128]{3,2,1,0:T(8,128)(2,1)}, bf16[4,4,128,128]{3,2,1,0:T(8,128)(2,1)S(1)}) custom-call(s32[5]{0:T(128)S(1)} %stack.239.at, ...), custom_call_target="tpu_custom_call", output_to_operand_aliasing={{0}: (8, {}), {1}: (9, {}), {2}: (10, {}), {3}: (11, {})} | custom-call | flops 4294967296 | bytes 33554432 | tf_op jit(solution)/shard_map/enter/pallas_call | solution.py:172
  343.4 2.6 collective-permute-done.18.mask
  346.7 6.1 %collective-permute-done.24.sib = bf16[64,128,128]{2,1,0:T(8,128)(2,1)} collective-permute-done((bf16[64,128,128]{2,1,0:T(8,128)(2,1)}, bf16[64,128,128]{2,1,0:T(8,128)(2,1)}, u32[]{:S(2)}, u32[]{:S(2)}) %collective-permute-start.24) | collective-permute-done | bytes 2097184 | tf_op jit(solution)/shard_map/ppermute | solution.py:509
  352.8 11.6 %enter.16 = (bf16[2,4,128,128,128]{4,3,2,1,0:T(8,128)(2,1)}, bf16[4,64,512,128]{3,2,1,0:T(8,128)(2,1)}, bf16[4,64,384,128]{3,2,1,0:T(8,128)(2,1)}, bf16[4,4,128,128]{3,2,1,0:T(8,128)(2,1)S(1)}) custom-call(s32[5]{0:T(128)S(1)} %stack.202.at, ...), custom_call_target="tpu_custom_call", output_to_operand_aliasing={{0}: (8, {}), {1}: (9, {}), {2}: (10, {}), {3}: (11, {})} | custom-call | flops 2147483648 | bytes 16777216 | tf_op jit(solution)/shard_map/enter/pallas_call | solution.py:172
  364.4 11.1 %enter.17 = (bf16[2,4,128,128,128]{4,3,2,1,0:T(8,128)(2,1)}, bf16[4,64,512,128]{3,2,1,0:T(8,128)(2,1)}, bf16[4,64,384,128]{3,2,1,0:T(8,128)(2,1)}, bf16[4,4,128,128]{3,2,1,0:T(8,128)(2,1)S(1)}) custom-call(s32[5]{0:T(128)S(1)} %stack.202.at, ...), custom_call_target="tpu_custom_call", output_to_operand_aliasing={{0}: (8, {}), {1}: (9, {}), {2}: (10, {}), {3}: (11, {})} | custom-call | flops 2147483648 | bytes 16777216 | tf_op jit(solution)/shard_map/enter/pallas_call | solution.py:172
  375.5 14.6 %outgoing.4 = (bf16[3,16,256,128]{3,2,1,0:T(8,128)(2,1)S(1)}, bf16[3,16,256,128]{3,2,1,0:T(8,128)(2,1)S(1)}) custom-call(s32[2]{0:T(128)S(1)} %pad_add_fusion.1.at, bf16[4,64,512,128]{3,2,1,0:T(8,128)(2,1)} %get-tuple-element.243.left, bf16[4,64,384,128]{3,2,1,0:T(8,128)(2,1)} %get-tuple-element.244.right), custom_call_target="tpu_custom_call" | custom-call | flops 3221225472 | bytes 21299200 | tf_op jit(solution)/shard_map/outgoing/pallas_call | solution.py:223
  390.6 14.7 %outgoing.5 = (bf16[3,16,256,128]{3,2,1,0:T(8,128)(2,1)S(1)}, bf16[3,16,256,128]{3,2,1,0:T(8,128)(2,1)S(1)}) custom-call(s32[2]{0:T(128)S(1)} %pad_add_fusion.1.at, bf16[4,64,512,128]{3,2,1,0:T(8,128)(2,1)} %get-tuple-element.243.left, bf16[4,64,384,128]{3,2,1,0:T(8,128)(2,1)} %get-tuple-element.244.right), custom_call_target="tpu_custom_call" | custom-call | flops 3221225472 | bytes 21299200 | tf_op jit(solution)/shard_map/outgoing/pallas_call | solution.py:223
  405.5 14.7 %outgoing.6 = (bf16[3,16,256,128]{3,2,1,0:T(8,128)(2,1)S(1)}, bf16[3,16,256,128]{3,2,1,0:T(8,128)(2,1)S(1)}) custom-call(s32[2]{0:T(128)S(1)} %pad_add_fusion.1.at, bf16[4,64,512,128]{3,2,1,0:T(8,128)(2,1)} %get-tuple-element.243.left, bf16[4,64,384,128]{3,2,1,0:T(8,128)(2,1)} %get-tuple-element.244.right), custom_call_target="tpu_custom_call" | custom-call | flops 3221225472 | bytes 21299200 | tf_op jit(solution)/shard_map/outgoing/pallas_call | solution.py:223
  420.2 14.7 %outgoing.7 = (bf16[3,16,256,128]{3,2,1,0:T(8,128)(2,1)S(1)}, bf16[3,16,256,128]{3,2,1,0:T(8,128)(2,1)S(1)}) custom-call(s32[2]{0:T(128)S(1)} %pad_add_fusion.1.at, bf16[4,64,512,128]{3,2,1,0:T(8,128)(2,1)} %get-tuple-element.243.left, bf16[4,64,384,128]{3,2,1,0:T(8,128)(2,1)} %get-tuple-element.244.right), custom_call_target="tpu_custom_call" | custom-call | flops 3221225472 | bytes 21299200 | tf_op jit(solution)/shard_map/outgoing/pallas_call | solution.py:223
  435.6 5.1 collective-permute-done.28.rest_7_
  440.7 4.5 collective-permute-done.27.rest_6_
  445.2 1.7 copy-done.9
  446.8 118.4 %middle.1 = (bf16[3,128,256,128]{3,2,1,0:T(8,128)(2,1)}, bf16[17,128,2048]{2,1,0:T(8,128)(2,1)}) custom-call(s32[3]{0:T(128)S(1)} %pad_add_fusion.at, bf16[2,4,128,128,128]{4,3,2,1,0:T(8,128)(2,1)} %get-tuple-element.231.state, bf16[4,4,128,128]{3,2,1,0:T(8,128)(2,1)S(1)} %get-tuple-element.232.mask, bf16[256,128]{1,0:T(8,128)(2,1)S(1)} %pad_maximum_fusion.2.both, ...), custom_call_target="tpu_custom_call" | custom-call | flops 12884901888 | bytes 100663296 | tf_op jit(solution)/shard_map/middle/pallas_call | solution.py:272
  565.3 17.0 %incoming.1 = (f32[128,128,128]{2,1,0:T(8,128)S(1)}, bf16[128,128,128]{2,1,0:T(8,128)(2,1)S(1)}) custom-call(s32[3]{0:T(128)S(1)} %pad_add_fusion.at, bf16[3,128,256,128]{3,2,1,0:T(8,128)(2,1)} %get-tuple-element.257.pairs), custom_call_target="tpu_custom_call" | custom-call | flops 2147483648 | bytes 37748736 | tf_op jit(solution)/shard_map/incoming/pallas_call | solution.py:338
  582.9 6.8 %collective-permute-done.29.got = bf16[128,128,128]{2,1,0:T(8,128)(2,1)S(1)} collective-permute-done((bf16[128,128,128]{2,1,0:T(8,128)(2,1)S(1)}, bf16[128,128,128]{2,1,0:T(8,128)(2,1)S(1)}, u32[]{:S(2)}, u32[]{:S(2)}) %collective-permute-start.29) | collective-permute-done | bytes 4194336 | tf_op jit(solution)/shard_map/ppermute | solution.py:526
  589.7 15.7 %leave.1 = bf16[128,128,128]{2,1,0:T(8,128)(2,1)} custom-call(s32[3]{0:T(128)S(1)} %pad_add_fusion.at, f32[128,128,128]{2,1,0:T(8,128)S(1)} %get-tuple-element.258.kept, bf16[128,128,128]{2,1,0:T(8,128)(2,1)S(1)} %collective-permute-done.29.got, bf16[17,128,2048]{2,1,0:T(8,128)(2,1)} %get-tuple-element.260.state, f32[128,128]{1,0:T(8,128)S(1)} %broadcast_in_dim.61.gain1, ...), custom_call_target="tpu_custom_call" | custom-call | flops 1073741824 | bytes 20971520 | tf_op jit(solution)/shard_map/leave/pallas_call | solution.py:375
  (110 shorter events, 14.5 us)
Async XLA Ops:
  0.0 16.6 %collective-permute-start.5 = (bf16[128,128,128]{2,1,0:T(8,128)(2,1)}, bf16[128,128,128]{2,1,0:T(8,128)(2,1)}, u32[]{:S(2)}, u32[]{:S(2)}) collective-permute-start(bf16[128,128,128]{2,1,0:T(8,128)(2,1)} %own.1), channel_id=1, source_target_pairs={{0,4},{4,0},{1,5},{5,1},{2,6},{6,2},{3,7},{7,3},{11,15},{15,11},{1... | collective-permute-start | bytes 12582920 | tf_op jit(solution)/shard_map/ppermute | solution.py:471
  0.5 96.9 %collective-permute-start.2 = (bf16[128,128,128]{2,1,0:T(8,128)(2,1)}, bf16[128,128,128]{2,1,0:T(8,128)(2,1)}, u32[]{:S(2)}, u32[]{:S(2)}) collective-permute-start(bf16[128,128,128]{2,1,0:T(8,128)(2,1)} %own.1), channel_id=1, source_target_pairs={{0,1},{4,5},{1,2},{5,6},{2,3},{6,7},{3,11},{7,15},{11,10},{15,14},... | collective-permute-start | bytes 12582920 | tf_op jit(solution)/shard_map/ppermute | solution.py:469
  3.0 94.3 %collective-permute-start.4 = (bf16[128,128,128]{2,1,0:T(8,128)(2,1)}, bf16[128,128,128]{2,1,0:T(8,128)(2,1)}, u32[]{:S(2)}, u32[]{:S(2)}) collective-permute-start(bf16[128,128,128]{2,1,0:T(8,128)(2,1)} %own.1), channel_id=1, source_target_pairs={{1,0},{5,4},{2,1},{6,5},{3,2},{7,6},{11,3},{15,7},{10,11},{14,15},... | collective-permute-start | bytes 12582920 | tf_op jit(solution)/shard_map/ppermute | solution.py:469
  3.9 10.7 %collective-permute-start = (bf16[128,128]{1,0:T(8,128)(2,1)S(1)}, bf16[128,128]{1,0:T(8,128)(2,1)S(1)}, u32[]{:S(2)}, u32[]{:S(2)}) collective-permute-start(bf16[128,128]{1,0:T(8,128)(2,1)S(1)} %convert_element_type.44), channel_id=1, source_target_pairs={{0,4},{4,0},{1,5},{5,1},{2,6},{6,2},{3,7},{7,3},{11,15},{15,11},{1... | collective-permute-start | bytes 98312 | tf_op jit(solution)/shard_map/ppermute | solution.py:426
  14.6 81.2 %collective-permute-start.1 = (bf16[2,128,128]{2,1,0:T(8,128)(2,1)S(1)}, bf16[2,128,128]{2,1,0:T(8,128)(2,1)S(1)}, u32[]{:S(2)}, u32[]{:S(2)}) collective-permute-start(bf16[2,128,128]{2,1,0:T(8,128)(2,1)S(1)} %maximum_select_fusion.mask), channel_id=1, source_target_pairs={{0,1},{4,5},{1,2},{5,6},{2,3},{6,7},{3,11},{7,15},{11,10},{15,14},... | collective-permute-start | bytes 196616 | tf_op jit(solution)/shard_map/ppermute | solution.py:469
  16.4 80.9 %collective-permute-start.3 = (bf16[2,128,128]{2,1,0:T(8,128)(2,1)S(1)}, bf16[2,128,128]{2,1,0:T(8,128)(2,1)S(1)}, u32[]{:S(2)}, u32[]{:S(2)}) collective-permute-start(bf16[2,128,128]{2,1,0:T(8,128)(2,1)S(1)} %maximum_select_fusion.mask), channel_id=1, source_target_pairs={{1,0},{5,4},{2,1},{6,5},{3,2},{7,6},{11,3},{15,7},{10,11},{14,15},... | collective-permute-start | bytes 196616 | tf_op jit(solution)/shard_map/ppermute | solution.py:469
  16.8 2.2 copy-start.7
  97.8 7.5 %collective-permute-start.11 = (bf16[128,128,128]{2,1,0:T(8,128)(2,1)}, bf16[128,128,128]{2,1,0:T(8,128)(2,1)}, u32[]{:S(2)}, u32[]{:S(2)}) collective-permute-start(bf16[128,128,128]{2,1,0:T(8,128)(2,1)} %collective-permute-done.2.own), channel_id=1, source_target_pairs={{0,4},{4,0},{1,5},{5,1},{2,6},{6,2},{3,7},{7,3},{11,15},{15,11},{1... | collective-permute-start | bytes 12582920 | tf_op jit(solution)/shard_map/ppermute | solution.py:507
  97.9 28.8 %collective-permute-start.10 = (bf16[128,128,128]{2,1,0:T(8,128)(2,1)}, bf16[128,128,128]{2,1,0:T(8,128)(2,1)}, u32[]{:S(2)}, u32[]{:S(2)}) collective-permute-start(bf16[128,128,128]{2,1,0:T(8,128)(2,1)} %collective-permute-done.4.own), channel_id=1, source_target_pairs={{0,4},{4,0},{1,5},{5,1},{2,6},{6,2},{3,7},{7,3},{11,15},{15,11},{1... | collective-permute-start | bytes 12582920 | tf_op jit(solution)/shard_map/ppermute | solution.py:507
  98.4 95.5 %collective-permute-start.7 = (bf16[128,128,128]{2,1,0:T(8,128)(2,1)}, bf16[128,128,128]{2,1,0:T(8,128)(2,1)}, u32[]{:S(2)}, u32[]{:S(2)}) collective-permute-start(bf16[128,128,128]{2,1,0:T(8,128)(2,1)} %collective-permute-done.2.own), channel_id=1, source_target_pairs={{0,1},{4,5},{1,2},{5,6},{2,3},{6,7},{3,11},{7,15},{11,10},{15,14},... | collective-permute-start | bytes 12582920 | tf_op jit(solution)/shard_map/ppermute | solution.py:469
  100.0 93.9 %collective-permute-start.9 = (bf16[128,128,128]{2,1,0:T(8,128)(2,1)}, bf16[128,128,128]{2,1,0:T(8,128)(2,1)}, u32[]{:S(2)}, u32[]{:S(2)}) collective-permute-start(bf16[128,128,128]{2,1,0:T(8,128)(2,1)} %collective-permute-done.4.own), channel_id=1, source_target_pairs={{1,0},{5,4},{2,1},{6,5},{3,2},{7,6},{11,3},{15,7},{10,11},{14,15},... | collective-permute-start | bytes 12582920 | tf_op jit(solution)/shard_map/ppermute | solution.py:469
  100.6 92.0 %collective-permute-start.6 = (bf16[2,128,128]{2,1,0:T(8,128)(2,1)S(1)}, bf16[2,128,128]{2,1,0:T(8,128)(2,1)S(1)}, u32[]{:S(2)}, u32[]{:S(2)}) collective-permute-start(bf16[2,128,128]{2,1,0:T(8,128)(2,1)S(1)} %collective-permute-done.1.mask), channel_id=1, source_target_pairs={{0,1},{4,5},{1,2},{5,6},{2,3},{6,7},{3,11},{7,15},{11,10},{15,14},... | collective-permute-start | bytes 196616 | tf_op jit(solution)/shard_map/ppermute | solution.py:469
  105.4 88.5 %collective-permute-start.8 = (bf16[2,128,128]{2,1,0:T(8,128)(2,1)S(1)}, bf16[2,128,128]{2,1,0:T(8,128)(2,1)S(1)}, u32[]{:S(2)}, u32[]{:S(2)}) collective-permute-start(bf16[2,128,128]{2,1,0:T(8,128)(2,1)S(1)} %collective-permute-done.3.mask), channel_id=1, source_target_pairs={{1,0},{5,4},{2,1},{6,5},{3,2},{7,6},{11,3},{15,7},{10,11},{14,15},... | collective-permute-start | bytes 196616 | tf_op jit(solution)/shard_map/ppermute | solution.py:469
  193.9 7.5 %collective-permute-start.17 = (bf16[128,128,128]{2,1,0:T(8,128)(2,1)}, bf16[128,128,128]{2,1,0:T(8,128)(2,1)}, u32[]{:S(2)}, u32[]{:S(2)}) collective-permute-start(bf16[128,128,128]{2,1,0:T(8,128)(2,1)} %collective-permute-done.7.own), channel_id=1, source_target_pairs={{0,4},{4,0},{1,5},{5,1},{2,6},{6,2},{3,7},{7,3},{11,15},{15,11},{1... | collective-permute-start | bytes 12582920 | tf_op jit(solution)/shard_map/ppermute | solution.py:507
  193.9 28.9 %collective-permute-start.16 = (bf16[128,128,128]{2,1,0:T(8,128)(2,1)}, bf16[128,128,128]{2,1,0:T(8,128)(2,1)}, u32[]{:S(2)}, u32[]{:S(2)}) collective-permute-start(bf16[128,128,128]{2,1,0:T(8,128)(2,1)} %collective-permute-done.9.own), channel_id=1, source_target_pairs={{0,4},{4,0},{1,5},{5,1},{2,6},{6,2},{3,7},{7,3},{11,15},{15,11},{1... | collective-permute-start | bytes 12582920 | tf_op jit(solution)/shard_map/ppermute | solution.py:507
  194.4 95.5 %collective-permute-start.13 = (bf16[128,128,128]{2,1,0:T(8,128)(2,1)}, bf16[128,128,128]{2,1,0:T(8,128)(2,1)}, u32[]{:S(2)}, u32[]{:S(2)}) collective-permute-start(bf16[128,128,128]{2,1,0:T(8,128)(2,1)} %collective-permute-done.7.own), channel_id=1, source_target_pairs={{0,1},{4,5},{1,2},{5,6},{2,3},{6,7},{3,11},{7,15},{11,10},{15,14},... | collective-permute-start | bytes 12582920 | tf_op jit(solution)/shard_map/ppermute | solution.py:469
  196.0 93.9 %collective-permute-start.15 = (bf16[128,128,128]{2,1,0:T(8,128)(2,1)}, bf16[128,128,128]{2,1,0:T(8,128)(2,1)}, u32[]{:S(2)}, u32[]{:S(2)}) collective-permute-start(bf16[128,128,128]{2,1,0:T(8,128)(2,1)} %collective-permute-done.9.own), channel_id=1, source_target_pairs={{1,0},{5,4},{2,1},{6,5},{3,2},{7,6},{11,3},{15,7},{10,11},{14,15},... | collective-permute-start | bytes 12582920 | tf_op jit(solution)/shard_map/ppermute | solution.py:469
  196.6 92.0 %collective-permute-start.12 = (bf16[2,128,128]{2,1,0:T(8,128)(2,1)S(1)}, bf16[2,128,128]{2,1,0:T(8,128)(2,1)S(1)}, u32[]{:S(2)}, u32[]{:S(2)}) collective-permute-start(bf16[2,128,128]{2,1,0:T(8,128)(2,1)S(1)} %collective-permute-done.6.mask), channel_id=1, source_target_pairs={{0,1},{4,5},{1,2},{5,6},{2,3},{6,7},{3,11},{7,15},{11,10},{15,14},... | collective-permute-start | bytes 196616 | tf_op jit(solution)/shard_map/ppermute | solution.py:469
  201.4 88.5 %collective-permute-start.14 = (bf16[2,128,128]{2,1,0:T(8,128)(2,1)S(1)}, bf16[2,128,128]{2,1,0:T(8,128)(2,1)S(1)}, u32[]{:S(2)}, u32[]{:S(2)}) collective-permute-start(bf16[2,128,128]{2,1,0:T(8,128)(2,1)S(1)} %collective-permute-done.8.mask), channel_id=1, source_target_pairs={{1,0},{5,4},{2,1},{6,5},{3,2},{7,6},{11,3},{15,7},{10,11},{14,15},... | collective-permute-start | bytes 196616 | tf_op jit(solution)/shard_map/ppermute | solution.py:469
  288.6 8.2 %copy-start.3 = (bf16[2,128,128]{2,1,0:T(8,128)(2,1)}, bf16[2,128,128]{2,1,0:T(8,128)(2,1)S(1)}, u32[]{:S(2)}) copy-start(bf16[2,128,128]{2,1,0:T(8,128)(2,1)S(1)} %collective-permute-done.12.mask) | copy-start | bytes 196612
  289.9 6.9 %copy-start.5 = (bf16[2,128,128]{2,1,0:T(8,128)(2,1)}, bf16[2,128,128]{2,1,0:T(8,128)(2,1)S(1)}, u32[]{:S(2)}) copy-start(bf16[2,128,128]{2,1,0:T(8,128)(2,1)S(1)} %collective-permute-done.14.mask) | copy-start | bytes 196612
  289.9 10.7 %collective-permute-start.22 = (bf16[128,128,128]{2,1,0:T(8,128)(2,1)}, bf16[128,128,128]{2,1,0:T(8,128)(2,1)}, u32[]{:S(2)}, u32[]{:S(2)}) collective-permute-start(bf16[128,128,128]{2,1,0:T(8,128)(2,1)} %collective-permute-done.13.own), channel_id=1, source_target_pairs={{0,4},{4,0},{1,5},{5,1},{2,6},{6,2},{3,7},{7,3},{11,15},{15,11},{1... | collective-permute-start | bytes 12582920 | tf_op jit(solution)/shard_map/ppermute | solution.py:507
  289.9 32.5 %collective-permute-start.21 = (bf16[128,128,128]{2,1,0:T(8,128)(2,1)}, bf16[128,128,128]{2,1,0:T(8,128)(2,1)}, u32[]{:S(2)}, u32[]{:S(2)}) collective-permute-start(bf16[128,128,128]{2,1,0:T(8,128)(2,1)} %collective-permute-done.15.own), channel_id=1, source_target_pairs={{0,4},{4,0},{1,5},{5,1},{2,6},{6,2},{3,7},{7,3},{11,15},{15,11},{1... | collective-permute-start | bytes 12582920 | tf_op jit(solution)/shard_map/ppermute | solution.py:507
  296.8 49.2 %collective-permute-start.19 = (bf16[64,128,128]{2,1,0:T(8,128)(2,1)}, bf16[64,128,128]{2,1,0:T(8,128)(2,1)}, u32[]{:S(2)}, u32[]{:S(2)}) collective-permute-start(bf16[64,128,128]{2,1,0:T(8,128)(2,1)} %slice.74), channel_id=1, source_target_pairs={{0,1},{4,5},{1,2},{5,6},{2,3},{6,7},{3,11},{7,15},{11,10},{15,14},... | collective-permute-start | bytes 6291464 | tf_op jit(solution)/shard_map/ppermute | solution.py:469
  298.2 47.7 %collective-permute-start.20 = (bf16[64,128,128]{2,1,0:T(8,128)(2,1)}, bf16[64,128,128]{2,1,0:T(8,128)(2,1)S(1)}, u32[]{:S(2)}, u32[]{:S(2)}) collective-permute-start(bf16[64,128,128]{2,1,0:T(8,128)(2,1)} %slice.75), channel_id=1, source_target_pairs={{1,0},{5,4},{2,1},{6,5},{3,2},{7,6},{11,3},{15,7},{10,11},{14,15},... | collective-permute-start | bytes 6291464 | tf_op jit(solution)/shard_map/ppermute | solution.py:469
  299.0 47.0 %collective-permute-start.18 = (bf16[2,128,128]{2,1,0:T(8,128)(2,1)}, bf16[2,128,128]{2,1,0:T(8,128)(2,1)S(1)}, u32[]{:S(2)}, u32[]{:S(2)}) collective-permute-start(bf16[2,128,128]{2,1,0:T(8,128)(2,1)} %copy-done.3), channel_id=1, source_target_pairs={{0,1},{4,5},{1,2},{5,6},{2,3},{6,7},{3,11},{7,15},{11,10},{15,14},... | collective-permute-start | bytes 196616 | tf_op jit(solution)/shard_map/ppermute | solution.py:469
  300.6 0.9 copy-start.4
  301.5 21.0 %copy-start.6 = (bf16[2,128,128]{2,1,0:T(8,128)(2,1)S(1)}, bf16[2,128,128]{2,1,0:T(8,128)(2,1)}, u32[]{:S(2)}) copy-start(bf16[2,128,128]{2,1,0:T(8,128)(2,1)} %copy-done.5) | copy-start | bytes 196612
  346.0 6.8 %collective-permute-start.24 = (bf16[64,128,128]{2,1,0:T(8,128)(2,1)}, bf16[64,128,128]{2,1,0:T(8,128)(2,1)}, u32[]{:S(2)}, u32[]{:S(2)}) collective-permute-start(bf16[64,128,128]{2,1,0:T(8,128)(2,1)} %collective-permute-done.19.own), channel_id=1, source_target_pairs={{0,4},{4,0},{1,5},{5,1},{2,6},{6,2},{3,7},{7,3},{11,15},{15,11},{1... | collective-permute-start | bytes 6291464 | tf_op jit(solution)/shard_map/ppermute | solution.py:509
  346.0 18.4 %collective-permute-start.23 = (bf16[64,128,128]{2,1,0:T(8,128)(2,1)S(1)}, bf16[64,128,128]{2,1,0:T(8,128)(2,1)}, u32[]{:S(2)}, u32[]{:S(2)}) collective-permute-start(bf16[64,128,128]{2,1,0:T(8,128)(2,1)S(1)} %collective-permute-done.20.own), channel_id=1, source_target_pairs={{0,4},{4,0},{1,5},{5,1},{2,6},{6,2},{3,7},{7,3},{11,15},{15,11},{1... | collective-permute-start | bytes 6291464 | tf_op jit(solution)/shard_map/ppermute | solution.py:510
  390.2 15.3 %collective-permute-start.25 = (bf16[3,16,256,128]{3,2,1,0:T(8,128)(2,1)S(1)}, bf16[3,16,256,128]{3,2,1,0:T(8,128)(2,1)}, u32[]{:S(2)}, u32[]{:S(2)}) collective-permute-start(bf16[3,16,256,128]{3,2,1,0:T(8,128)(2,1)S(1)} %get-tuple-element.247), channel_id=1, source_target_pairs={{0,4},{4,0},{1,5},{5,1},{2,6},{6,2},{3,7},{7,3},{11,15},{15,11},{1... | collective-permute-start | bytes 9437192 | tf_op jit(solution)/shard_map/ppermute | solution.py:521
  405.3 15.0 %collective-permute-start.26 = (bf16[3,16,256,128]{3,2,1,0:T(8,128)(2,1)S(1)}, bf16[3,16,256,128]{3,2,1,0:T(8,128)(2,1)}, u32[]{:S(2)}, u32[]{:S(2)}) collective-permute-start(bf16[3,16,256,128]{3,2,1,0:T(8,128)(2,1)S(1)} %get-tuple-element.250), channel_id=1, source_target_pairs={{0,4},{4,0},{1,5},{5,1},{2,6},{6,2},{3,7},{7,3},{11,15},{15,11},{1... | collective-permute-start | bytes 9437192 | tf_op jit(solution)/shard_map/ppermute | solution.py:521
  420.2 26.6 %copy-start = (bf16[128,128]{1,0:T(8,128)(2,1)S(1)}, bf16[128,128]{1,0:T(8,128)(2,1)}, u32[]{:S(2)}) copy-start(bf16[128,128]{1,0:T(8,128)(2,1)} %multiply_bitcast_fusion.2.gate) | copy-start | bytes 98308
  434.9 5.7 collective-permute-start.28
  435.3 9.8 %collective-permute-start.27 = (bf16[3,16,256,128]{3,2,1,0:T(8,128)(2,1)S(1)}, bf16[3,16,256,128]{3,2,1,0:T(8,128)(2,1)S(1)}, u32[]{:S(2)}, u32[]{:S(2)}) collective-permute-start(bf16[3,16,256,128]{3,2,1,0:T(8,128)(2,1)S(1)} %get-tuple-element.255), channel_id=1, source_target_pairs={{0,4},{4,0},{1,5},{5,1},{2,6},{6,2},{3,7},{7,3},{11,15},{15,11},{1... | collective-permute-start | bytes 9437192 | tf_op jit(solution)/shard_map/ppermute | solution.py:521
  440.7 4.5 copy-start.8
  445.2 1.7 copy-start.9
  565.3 24.4 %copy-start.1 = (bf16[128,128]{1,0:T(8,128)(2,1)S(1)}, bf16[128,128]{1,0:T(8,128)(2,1)}, u32[]{:S(2)}) copy-start(bf16[128,128]{1,0:T(8,128)(2,1)} %get-tuple-element.266.gate) | copy-start | bytes 98308
  565.3 24.4 %copy-start.2 = (bf16[128,128]{1,0:T(8,128)(2,1)S(1)}, bf16[128,128]{1,0:T(8,128)(2,1)}, u32[]{:S(2)}) copy-start(bf16[128,128]{1,0:T(8,128)(2,1)} %get-tuple-element.265.proj) | copy-start | bytes 98308
  582.3 7.4 %collective-permute-start.29 = (bf16[128,128,128]{2,1,0:T(8,128)(2,1)S(1)}, bf16[128,128,128]{2,1,0:T(8,128)(2,1)S(1)}, u32[]{:S(2)}, u32[]{:S(2)}) collective-permute-start(bf16[128,128,128]{2,1,0:T(8,128)(2,1)S(1)} %get-tuple-element.259), channel_id=1, source_target_pairs={{0,4},{4,0},{1,5},{5,1},{2,6},{6,2},{3,7},{7,3},{11,15},{15,11},{1... | collective-permute-start | bytes 12582920 | tf_op jit(solution)/shard_map/ppermute | solution.py:526

commit v3 on v2

--- a/solution.py
+++ b/solution.py
@@ -54,6 +54,8 @@
 TILE = 128
 SUB = 16
 BLOCKS = TILE // SUB
+CHUNK = 2
+STATE_BLOCKS = 6 * BLOCKS
 VMEM_LIMIT = 40 * 1024 * 1024
 BOTH = ("row", "col")
 NT = (((1,), (1,)), ((), ()))
@@ -66,8 +68,8 @@
 
 def norm_apart(apart, gain, bias):
     variance = jnp.mean(apart * apart, axis=0, keepdims=True)
-    wide_gain = jnp.concatenate([gain] * SUB, axis=1)
-    wide_bias = jnp.concatenate([bias] * SUB, axis=1)
+    wide_gain = jnp.concatenate([gain[...]] * CHUNK, axis=1)
+    wide_bias = jnp.concatenate([bias[...]] * CHUNK, axis=1)
     return (apart * lax.rsqrt(variance + epsilon) * wide_gain + wide_bias).astype(jnp.bfloat16)
 
 
@@ -75,44 +77,54 @@
     return norm_apart(values - jnp.mean(values, axis=0, keepdims=True), gain, bias)
 
 
-def gated(weights, normed):
-    both = jnp.dot(weights, normed, preferred_element_type=jnp.float32)
+def product(matrix, values):
+    return jnp.dot(matrix, values, preferred_element_type=jnp.float32)
+
+
+def gated_store(weights, normed, mask_rows, first, turn):
+    both = product(weights, normed)
     half = both.shape[0] // 2
-    return both[:half] * jnp.tanh(both[half:]) + both[:half]
-
-
-def masked_tiles(paired, mask_rows, turn):
-    channels = paired.shape[0]
-    for r in range(SUB):
-        turn[pl.ds(r, channels, stride=SUB), :] = (
-            paired[:, r * TILE : (r + 1) * TILE] * mask_rows[r : r + 1, :]
-        )
-    return turn[...].astype(jnp.bfloat16).reshape(channels, SUB, TILE)
-
-
-def flat_channels(turn):
-    return jnp.concatenate([turn[pl.ds(r, TILE, stride=SUB), :] for r in range(SUB)], axis=1)
-
-
-def enter_kernel(at, own, sib, mask, centre, gain, bias, weights, *rest):
-    state_out, left_out, right_out, mask_out, turn = rest[-5:]
+    paired = both[:half] * jnp.tanh(both[half:]) + both[:half]
+    for r in range(CHUNK):
+        turn[pl.ds(first + r, half, stride=SUB), :] = (
+            paired[:, r * TILE : (r + 1) * TILE] * mask_rows[first + r : first + r + 1, :]
+        )
+
+
+def chunk_of(turn, first):
+    return jnp.concatenate([turn[pl.ds(first + r, TILE, stride=SUB), :] for r in range(CHUNK)], axis=1)
+
+
+def enter_kernel(at, own, sib, mask, both, gain, bias, weights, *rest):
+    state_out, left_low, left_high, right_out, mask_out, turn = rest[-6:]
     step = pl.program_id(0)
     use_own = (step == 1) == (at[4] == 1)
-    picked = jnp.where(use_own, own[...], sib[...])
-    apart = channels_first(picked.reshape(SUB * TILE, TILE), centre[...])
-    normed = norm_apart(apart, gain[...], bias[...])
-    paired = masked_tiles(gated(weights[...], normed), mask[0].astype(jnp.float32), turn)
-    half = paired.shape[0] // 2
-    left_out[0] = paired[:half]
-    right_out[0] = paired[half:]
+    mask_rows = mask[0].astype(jnp.float32)
     mask_out[0, 0] = mask[0]
 
     @pl.when(use_own)
     def _():
-        state_out[0, 0] = picked
-
-
-def enter(own, sib, first_block, at, mask, centre, gain, bias, weights, held):
+        for first in range(0, SUB, CHUNK):
+            turned = channels_first(own[first : first + CHUNK].reshape(CHUNK * TILE, TILE), both[...])
+            normed = norm_apart(turned[:TILE], gain, bias)
+            lanes = slice(first * TILE, (first + CHUNK) * TILE)
+            state_out[0, :, lanes] = turned[TILE:].astype(jnp.bfloat16)
+            gated_store(weights[...], normed, mask_rows, first, turn)
+
+    @pl.when(jnp.logical_not(use_own))
+    def _():
+        for first in range(0, SUB, CHUNK):
+            apart = channels_first(sib[first : first + CHUNK].reshape(CHUNK * TILE, TILE), both[:TILE])
+            gated_store(weights[...], norm_apart(apart, gain, bias), mask_rows, first, turn)
+
+    start = 0
+    for out in (left_low, left_high, right_out):
+        stop = start + out.shape[1] * SUB
+        out[0] = turn[start:stop, :].astype(jnp.bfloat16).reshape(out.shape[1], SUB, TILE)
+        start = stop
+
+
+def enter(own, sib, first_block, at, mask, both, gain, bias, weights, held):
     n_block = own.shape[0] // SUB
     full = pl.BlockSpec(memory_space=pl.ANY)
 
@@ -136,7 +148,7 @@
 
     def state_map(step, block, at):
         kept = jnp.where(is_own(step, at), block, jnp.where(step == 0, 0, n_block - 1))
-        return (at[0], at[1], first_block + kept, 0, 0)
+        return (jnp.where(at[5] < 0, STATE_BLOCKS, at[5] + first_block + kept), 0, 0)
 
     def left_map(step, block, at):
         return (at[1], 0, (2 * at[0] + core_of(step, at)) * BLOCKS + first_block + block, 0)
@@ -148,8 +160,9 @@
     half = weights.shape[0] // 4
     same = lambda step, block, at: (0, 0)
     shapes = (
-        jax.ShapeDtypeStruct((2, 4, TILE, TILE, TILE), jnp.bfloat16),
-        jax.ShapeDtypeStruct((4, half, 4 * TILE, TILE), jnp.bfloat16),
+        jax.ShapeDtypeStruct((STATE_BLOCKS + 1, TILE, SUB * TILE), jnp.bfloat16),
+        jax.ShapeDtypeStruct((4, half // 2, 4 * TILE, TILE), jnp.bfloat16),
+        jax.ShapeDtypeStruct((4, half // 2, 4 * TILE, TILE), jnp.bfloat16),
         jax.ShapeDtypeStruct((4, half, 3 * TILE, TILE), jnp.bfloat16),
         jax.ShapeDtypeStruct((4, 4, TILE, TILE), jnp.bfloat16),
     )
@@ -157,17 +170,17 @@
         pl.BlockSpec((SUB, TILE, TILE), own_map),
         pl.BlockSpec((SUB, TILE, TILE), sib_map),
         pl.BlockSpec((1, SUB, TILE), mask_map),
-        pl.BlockSpec((TILE, TILE), same),
+        pl.BlockSpec((2 * TILE, TILE), same),
         pl.BlockSpec((TILE, TILE), same),
         pl.BlockSpec((TILE, TILE), same),
         pl.BlockSpec((4 * half, TILE), same),
     ]
-    operands = [own, sib, mask, centre, gain, bias, weights]
+    operands = [own, sib, mask, both, gain, bias, weights]
     aliases = {}
     if held is not None:
-        aliases = {len(operands) + 1 + n: n for n in range(4)}
+        aliases = {len(operands) + 1 + n: n for n in range(5)}
         operands += list(held)
-        in_specs += [full] * 4
+        in_specs += [full] * 5
     pairs = 2 * own.shape[0] * TILE
     return pl.pallas_call(
         enter_kernel,
@@ -176,8 +189,9 @@
             grid=(2, n_block),
             in_specs=in_specs,
             out_specs=[
-                pl.BlockSpec((1, 1, SUB, TILE, TILE), state_map),
-                pl.BlockSpec((1, half, SUB, TILE), left_map),
+                pl.BlockSpec((1, TILE, SUB * TILE), state_map),
+                pl.BlockSpec((1, half // 2, SUB, TILE), left_map),
+                pl.BlockSpec((1, half // 2, SUB, TILE), left_map),
                 pl.BlockSpec((1, half, SUB, TILE), right_map),
                 pl.BlockSpec((1, 1, SUB, TILE), mask_out_map),
             ],
@@ -199,37 +213,45 @@
     core = at[0]
     third = pl.multiple_of(at[1] * TILE, TILE)
 
-    def wide(ref, start, count):
-        return jnp.concatenate([ref[k, 0, pl.ds(start, count), :] for k in range(4)], axis=1)
-
-    columns = jnp.concatenate([wide(right, 0, 2 * TILE), wide(right, third, TILE)], axis=0)
+    def wide(ref, d, start, count):
+        return jnp.concatenate([ref[k, d, pl.ds(start, count), :] for k in range(4)], axis=1)
+
     blocks = [2 * x + which for which in (core, 1 - core) for x in range(2)]
-    rows = jnp.concatenate(
-        [wide(left, pl.multiple_of(block * TILE, TILE), TILE) for block in blocks], axis=0
-    )
-    sums = lax.dot_general(rows, columns, NT, preferred_element_type=jnp.float32).astype(jnp.bfloat16)
-    for slot in range(3):
-        keep[slot, 0] = sums[: 2 * TILE, slot * TILE : (slot + 1) * TILE]
-        send[slot, 0] = sums[2 * TILE :, slot * TILE : (slot + 1) * TILE]
-
-
+    for d in range(TOGETHER):
+        columns = jnp.concatenate(
+            [wide(right, d, 0, 2 * TILE), wide(right, d, third, TILE)], axis=0
+        )
+        rows = jnp.concatenate(
+            [wide(left, d, pl.multiple_of(block * TILE, TILE), TILE) for block in blocks], axis=0
+        )
+        sums = lax.dot_general(rows, columns, NT, preferred_element_type=jnp.float32)
+        for slot in range(3):
+            lanes = slice(slot * TILE, (slot + 1) * TILE)
+            keep[slot, d] = sums[: 2 * TILE, lanes].astype(jnp.bfloat16)
+            send[slot, d] = sums[2 * TILE :, lanes].astype(jnp.bfloat16)
+
+
+TOGETHER = 2
 PARTS = 4
 
 
-def outgoing(at, left, right, part):
-    count = left.shape[1] // PARTS
-    first = part * count
+def outgoing(at, lefts, right, part):
+    count = right.shape[1] // PARTS
+    steps = count // TOGETHER
+    first = part * steps
+    left = lefts[part * len(lefts) // PARTS]
+    left_first = part % (PARTS // len(lefts)) * steps
     out = jax.ShapeDtypeStruct((3, count, 2 * TILE, TILE), jnp.bfloat16)
     return pl.pallas_call(
         outgoing_kernel,
         grid_spec=pltpu.PrefetchScalarGridSpec(
             num_scalar_prefetch=1,
-            grid=(count,),
+            grid=(steps,),
             in_specs=[
-                pl.BlockSpec((4, 1, 4 * TILE, TILE), lambda d, at: (0, first + d, 0, 0)),
-                pl.BlockSpec((4, 1, 3 * TILE, TILE), lambda d, at: (0, first + d, 0, 0)),
+                pl.BlockSpec((4, TOGETHER, 4 * TILE, TILE), lambda d, at: (0, left_first + d, 0, 0)),
+                pl.BlockSpec((4, TOGETHER, 3 * TILE, TILE), lambda d, at: (0, first + d, 0, 0)),
             ],
-            out_specs=[pl.BlockSpec((3, 1, 2 * TILE, TILE), lambda d, at: (0, d, 0, 0))] * 2,
+            out_specs=[pl.BlockSpec((3, TOGETHER, 2 * TILE, TILE), lambda d, at: (0, d, 0, 0))] * 2,
         ),
         out_shape=(out, out),
         compiler_params=pltpu.CompilerParams(
@@ -243,30 +265,37 @@
 
 
 def middle_kernel(
-    at, state, mask, both, gain0, bias0, gain_out, bias_out, proj, gate, gain1, bias1, weights, *rest
+    at, state, mask, gain0, bias0, gain_out, bias_out, proj, gate, gain1, bias1, weights, *rest
 ):
-    parts, (pairs_out, state_out, turn) = rest[:-3], rest[-3:]
-    turned = channels_first(state[0, 0].reshape(SUB * TILE, TILE), both[...])
-    normed = norm_apart(turned[:TILE], gain0[...], bias0[...])
+    parts, (pairs_out, state_out, turn, turn_out) = rest[:-4], rest[-4:]
     height = TILE * SUB // len(parts)
     for n, part in enumerate(parts):
         turn[n * height : (n + 1) * height, :] = part[0].reshape(height, TILE).astype(jnp.float32)
-    normed_out = norm_channels(flat_channels(turn), gain_out[...], bias_out[...])
-    out = jnp.dot(proj[...], normed_out, preferred_element_type=jnp.float32)
-    gate_value = jnp.tanh(jnp.dot(gate[...], normed, preferred_element_type=jnp.float32))
-    changed = (turned[TILE:] + (out * gate_value + out)).astype(jnp.bfloat16)
-    state_out[0] = changed
-    normed1 = norm_channels(changed.astype(jnp.float32), gain1[...], bias1[...])
-    pairs_out[0] = masked_tiles(gated(weights[0], normed1), mask[0, 0].astype(jnp.float32), turn)
-
-
-def middle(at, states, mask, both, gain0, bias0, gain_out, bias_out, proj, gate, gain1, bias1, weights, parts):
+    mask_rows = mask[0, 0].astype(jnp.float32)
+    for first in range(0, SUB, CHUNK):
+        lanes = slice(first * TILE, (first + CHUNK) * TILE)
+        normed_out = norm_channels(chunk_of(turn, first), gain_out, bias_out)
+        out = product(proj[...], normed_out)
+        before = state[0, :, lanes].astype(jnp.float32)
+        gate_value = jnp.tanh(product(gate[...], norm_channels(before, gain0, bias0)))
+        changed = (before + (out * gate_value + out)).astype(jnp.bfloat16)
+        state_out[0, :, lanes] = changed
+        normed1 = norm_channels(changed.astype(jnp.float32), gain1, bias1)
+        gated_store(weights[0], normed1, mask_rows, first, turn_out)
+    pairs_out[0] = turn_out[...].astype(jnp.bfloat16).reshape(TILE, SUB, TILE)
+
+
+def middle(at, states, mask, fixed, parts):
     def column(slot, at):
         return jnp.where(slot == 2, at[2], 2 * at[1] + slot)
 
     square = pl.BlockSpec((TILE, TILE), lambda slot, x, block, at: (0, 0))
     tri = pl.BlockSpec(
         (1, parts[0].shape[1], SUB, TILE), lambda slot, x, block, at: (slot, 0, x * BLOCKS + block, 0)
+    )
+    state_spec = pl.BlockSpec(
+        (1, TILE, SUB * TILE),
+        lambda slot, x, block, at: ((x * 3 + jnp.where(slot == 2, at[3], slot)) * BLOCKS + block, 0, 0),
     )
     pairs = 6 * TILE * TILE
     return pl.pallas_call(
@@ -275,15 +304,11 @@
             num_scalar_prefetch=1,
             grid=(3, 2, BLOCKS),
             in_specs=[
-                pl.BlockSpec(
-                    (1, 1, SUB, TILE, TILE),
-                    lambda slot, x, block, at: (x, column(slot, at), block, 0, 0),
-                ),
+                state_spec,
                 pl.BlockSpec(
                     (1, 1, SUB, TILE),
                     lambda slot, x, block, at: (2 * x + at[0], column(slot, at), block, 0),
                 ),
-                pl.BlockSpec((2 * TILE, TILE), lambda slot, x, block, at: (0, 0)),
             ]
             + [square] * 8
             + [
@@ -304,7 +329,7 @@
                     ),
                 ),
             ],
-            scratch_shapes=[pltpu.VMEM((TILE * SUB, TILE), jnp.float32)],
+            scratch_shapes=[pltpu.VMEM((TILE * SUB, TILE), jnp.float32)] * 2,
         ),
         out_shape=(
             jax.ShapeDtypeStruct((3, TILE, 2 * TILE, TILE), jnp.bfloat16),
@@ -317,7 +342,7 @@
             flops=pairs * TILE * 1024, bytes_accessed=pairs * 1024, transcendentals=pairs * TILE * 2
         ),
         name="middle",
-    )(at, states, mask, both, gain0, bias0, gain_out, bias_out, proj, gate, gain1, bias1, weights, *parts)
+    )(at, states, mask, *fixed, *parts)
 
 
 CHANNELS = 8
@@ -358,15 +383,15 @@
 
 
 def leave_kernel(at, kept, got, state, gain1, bias1, gain_out, bias_out, proj, gate, result, turn):
-    rows = state[0].astype(jnp.float32)
-    normed = norm_channels(rows, gain1[...], bias1[...])
     summed = (kept[...] + got[...].astype(jnp.float32)).astype(jnp.bfloat16)
     turn[...] = summed.astype(jnp.float32).reshape(TILE * SUB, TILE)
-    normed_out = norm_channels(flat_channels(turn), gain_out[...], bias_out[...])
-    out = jnp.dot(proj[...], normed_out, preferred_element_type=jnp.float32)
-    gate_value = jnp.tanh(jnp.dot(gate[...], normed, preferred_element_type=jnp.float32))
-    changed = (rows + (out * gate_value + out)).astype(jnp.bfloat16)
-    result[...] = changed.T.reshape(SUB, TILE, TILE)
+    for first in range(0, SUB, CHUNK):
+        before = state[0, :, first * TILE : (first + CHUNK) * TILE].astype(jnp.float32)
+        normed = norm_channels(before, gain1, bias1)
+        out = product(proj[...], norm_channels(chunk_of(turn, first), gain_out, bias_out))
+        gate_value = jnp.tanh(product(gate[...], normed))
+        changed = (before + (out * gate_value + out)).astype(jnp.bfloat16)
+        result[first : first + CHUNK] = changed.T.reshape(CHUNK, TILE, TILE)
 
 
 def leave(at, kept, got, states, *fixed):
@@ -443,7 +468,7 @@
         ]
     )
     identity = jnp.eye(TILE, dtype=jnp.bfloat16)
-    centre = identity - jnp.bfloat16(1.0 / TILE)
+    both = jnp.concatenate([identity - jnp.bfloat16(1.0 / TILE), identity], axis=0)
     def reordered(values):
         return jnp.concatenate(
             [lax.dynamic_slice_in_dim(values, start, half, axis=0) for start in (ours, theirs)], axis=0
@@ -460,10 +485,19 @@
         there_x = there // 4
         there_z = jnp.where(there_x == 0, there, 7 - there)
         last = lax.rem(z, 2)
+        slot = jnp.where(there_z // 2 == x, lax.rem(there_z, 2), jnp.where(there_z == z, 2, -1))
         at = jnp.stack(
-            [there_x, there_z, last, (there_x == x).astype(jnp.int32), (last == core).astype(jnp.int32)]
+            [
+                there_x,
+                there_z,
+                last,
+                (there_x == x).astype(jnp.int32),
+                (last == core).astype(jnp.int32),
+                jnp.where(slot < 0, -1, (3 * there_x + slot) * BLOCKS),
+            ]
         ).astype(jnp.int32)
-        return enter(own, sib, first_block, at, mask, centre, gain_in[0], bias_in[0], enter_weights, held)
+        fixed = (both, gain_in[0], bias_in[0], enter_weights)
+        return enter(own, sib, first_block, at, mask, *fixed, held)
 
     def hop(values, pairs):
         return [lax.ppermute(value, BOTH, pairs) for value in values]
@@ -473,7 +507,6 @@
     above = hop([masks, pair_state], down)
     part = TILE // 2
     middle_fixed = [
-        jnp.concatenate([centre, identity], axis=0),
         gain_in[0],
         bias_in[0],
         columns(reordered(norm_out_gain[0])),
@@ -508,7 +541,7 @@
     below, above, held = lax.optimization_barrier((below, above, held))
     held = project(held, 4, below[1], lax.ppermute(below[1], BOTH, swap), below[0], 0)
     held = project(held, 4, above[0], lax.ppermute(above[0], BOTH, swap), below[0], part // SUB)
-    states, left, right, mask = held
+    states, *lefts, right, mask = held
 
     third = jnp.where(z // 2 == x, lax.rem(z, 2), 2)
     at_tri = jnp.stack([core, third]).astype(jnp.int32)
@@ -516,12 +549,12 @@
     for n in range(PARTS):
         if n >= 2:
             at_tri, got[n - 2] = lax.optimization_barrier((at_tri, got[n - 2]))
-        stays, leaves = outgoing(at_tri, left, right, n)
+        stays, leaves = outgoing(at_tri, lefts, right, n)
         kept.append(stays)
         got.append(lax.ppermute(leaves, BOTH, swap))
     parts = kept + got
-    at = jnp.stack([core, x, z]).astype(jnp.int32)
-    pairs, states1 = middle(at, states, mask, *middle_fixed, parts)
+    at = jnp.stack([core, x, z, third]).astype(jnp.int32)
+    pairs, states1 = middle(at, states, mask, middle_fixed, parts)
     kept1, sent1 = incoming(at, pairs)
     got1 = lax.ppermute(sent1, BOTH, swap)
     return leave(at, kept1, got1, states1, *leave_fixed)

time: 610 us -> 603 us (0.989)
  waiting for transfers between devices: 183 us -> 162 us
  Pallas kernels: 378 us -> 393 us
    pallas_call x9, Pallas kernels: 168 us -> 205 us  [enter(): pl.pallas_call(enter_kernel, grid_spec=pltpu.PrefetchScalarGridSpec(num_s...]
    ppermute x15, waiting for transfers between devices: 154 us -> 128 us  [hop(): return [lax.ppermute(value, BOTH, pairs) for value in values]]
    pallas_call x4, Pallas kernels: 58.7 us -> 42.4 us  [outgoing(): pl.pallas_call(outgoing_kernel, grid_spec=pltpu.PrefetchScalarGridSpec(nu...]
    pallas_call x1, Pallas kernels: 118 us -> 112 us  [middle(): pl.pallas_call(middle_kernel, grid_spec=pltpu.PrefetchScalarGridSpec(num_...]
  transfers between devices with their start and end apart: 30 -> 30, of which waited for: 13 -> 13; matrix products, arithmetic and copies ran while one was open for 3% -> 3% of each run, Pallas kernels for 31% -> 33%
where the time goes in v3:
time: 603 us; the launch traced here: 602 us
  Pallas kernels  393 us (65%)
  waiting for transfers between devices  162 us (27%)
  local copies, waits for them, and re-layouts  21.8 us (4%)
  starting transfers between devices  20.7 us (3%)
    pallas_call x9, Pallas kernels, enter(): pl.pallas_call(enter_kernel, grid_spec=pltpu.PrefetchScalarGridSpec(num_s...  205 us
    ppermute x15, waiting for transfers between devices, hop(): return [lax.ppermute(value, BOTH, pairs) for value in values]  128 us
    pallas_call x1, Pallas kernels, middle(): pl.pallas_call(middle_kernel, grid_spec=pltpu.PrefetchScalarGridSpec(num_...  112 us
    pallas_call x4, Pallas kernels, outgoing(): pl.pallas_call(outgoing_kernel, grid_spec=pltpu.PrefetchScalarGridSpec(nu...  42.4 us
    pallas_call x1, Pallas kernels, incoming(): pl.pallas_call(incoming_kernel, grid_spec=pltpu.PrefetchScalarGridSpec(nu...  17 us
    pallas_call x1, Pallas kernels, leave(): pl.pallas_call(leave_kernel, grid_spec=pltpu.PrefetchScalarGridSpec(num_s...  16.7 us
    ppermute x15, starting transfers between devices, hop(): return [lax.ppermute(value, BOTH, pairs) for value in values]  16.2 us
    ppermute x4, waiting for transfers between devices, on_device_ring(): got.append(lax.ppermute(leaves, BOTH, swap))  14.9 us
  transfers between devices with their start and end apart: 30, of which 13 were waited for; matrix products, arithmetic and copies ran while one was open for 3% of the time, Pallas kernels for 33%

profile of v3, /device:TPU:0, one launch (start us, length us, event | category | flops | bytes accessed | tf_op | source)
XLA Modules:
  0.0 601.6 jit_solution(2047746228318999401)
XLA Ops:
  0.5 2.6 collective-permute-start.2
  3.0 0.8 convert_element_type.6
  4.1 0.9 fusion.10
  5.0 0.9 fusion.11
  6.4 0.8 fusion.13
  13.5 0.8 convert_bitcast_fusion
  14.6 1.9 collective-permute-start.1
  16.8 2.2 copy-done.6
  19.0 25.0 %enter.9 = (bf16[49,128,2048]{2,1,0:T(8,128)(2,1)}, bf16[4,32,512,128]{3,2,1,0:T(8,128)(2,1)}, bf16[4,32,512,128]{3,2,1,0:T(8,128)(2,1)}, bf16[4,64,384,128]{3,2,1,0:T(8,128)(2,1)}, bf16[4,4,128,128]{3,2,1,0:T(8,128)(2,1)S(1)}) custom-call(s32[6]{0:T(128)S(1)} %stack.240.at, bf16[128,128,128]{2,1,0:T(8,128)(2,1)S(1)} %copy-done.6, ...), custom_call_target="tpu_custom_call" | custom-call | flops 4294967296 | bytes 33554432 | tf_op jit(solution)/shard_map/enter/pallas_call | solution.py:185
  44.0 51.8 %collective-permute-done.1.mask = bf16[2,128,128]{2,1,0:T(8,128)(2,1)S(1)} collective-permute-done((bf16[2,128,128]{2,1,0:T(8,128)(2,1)S(1)}, bf16[2,128,128]{2,1,0:T(8,128)(2,1)S(1)}, u32[]{:S(2)}, u32[]{:S(2)}) %collective-permute-start.1) | collective-permute-done | bytes 65568 | tf_op jit(solution)/shard_map/ppermute | solution.py:503
  95.8 1.5 collective-permute-done.3.mask
  98.4 1.6 collective-permute-start.7
  100.6 1.6 collective-permute-start.6
  102.2 3.2 collective-permute-done.11.sib
  105.7 25.3 %enter.10 = (bf16[49,128,2048]{2,1,0:T(8,128)(2,1)}, bf16[4,32,512,128]{3,2,1,0:T(8,128)(2,1)}, bf16[4,32,512,128]{3,2,1,0:T(8,128)(2,1)}, bf16[4,64,384,128]{3,2,1,0:T(8,128)(2,1)}, bf16[4,4,128,128]{3,2,1,0:T(8,128)(2,1)S(1)}) custom-call(s32[6]{0:T(128)S(1)} %stack.255.at, ...), custom_call_target="tpu_custom_call", output_to_operand_aliasing={{0}: (8, {}), {1}: (9, {}), {2}: (10, {}), {3}: (11, {}), {... | custom-call | flops 4294967296 | bytes 33554432 | tf_op jit(solution)/shard_map/enter/pallas_call | solution.py:185
  131.0 25.3 %enter.11 = (bf16[49,128,2048]{2,1,0:T(8,128)(2,1)}, bf16[4,32,512,128]{3,2,1,0:T(8,128)(2,1)}, bf16[4,32,512,128]{3,2,1,0:T(8,128)(2,1)}, bf16[4,64,384,128]{3,2,1,0:T(8,128)(2,1)}, bf16[4,4,128,128]{3,2,1,0:T(8,128)(2,1)S(1)}) custom-call(s32[6]{0:T(128)S(1)} %stack.249.at, ...), custom_call_target="tpu_custom_call", output_to_operand_aliasing={{0}: (8, {}), {1}: (9, {}), {2}: (10, {}), {3}: (11, {}), {... | custom-call | flops 4294967296 | bytes 33554432 | tf_op jit(solution)/shard_map/enter/pallas_call | solution.py:185
  156.3 36.2 %collective-permute-done.6.mask = bf16[2,128,128]{2,1,0:T(8,128)(2,1)S(1)} collective-permute-done((bf16[2,128,128]{2,1,0:T(8,128)(2,1)S(1)}, bf16[2,128,128]{2,1,0:T(8,128)(2,1)S(1)}, u32[]{:S(2)}, u32[]{:S(2)}) %collective-permute-start.6) | collective-permute-done | bytes 65568 | tf_op jit(solution)/shard_map/ppermute | solution.py:503
  192.6 1.3 collective-permute-done.8.mask
  194.4 1.6 collective-permute-start.13
  196.6 1.6 collective-permute-start.12
  198.2 3.2 collective-permute-done.17.sib
  201.8 25.3 %enter.12 = (bf16[49,128,2048]{2,1,0:T(8,128)(2,1)}, bf16[4,32,512,128]{3,2,1,0:T(8,128)(2,1)}, bf16[4,32,512,128]{3,2,1,0:T(8,128)(2,1)}, bf16[4,64,384,128]{3,2,1,0:T(8,128)(2,1)}, bf16[4,4,128,128]{3,2,1,0:T(8,128)(2,1)S(1)}) custom-call(s32[6]{0:T(128)S(1)} %stack.267.at, ...), custom_call_target="tpu_custom_call", output_to_operand_aliasing={{0}: (8, {}), {1}: (9, {}), {2}: (10, {}), {3}: (11, {}), {... | custom-call | flops 4294967296 | bytes 33554432 | tf_op jit(solution)/shard_map/enter/pallas_call | solution.py:185
  227.2 25.3 %enter.13 = (bf16[49,128,2048]{2,1,0:T(8,128)(2,1)}, bf16[4,32,512,128]{3,2,1,0:T(8,128)(2,1)}, bf16[4,32,512,128]{3,2,1,0:T(8,128)(2,1)}, bf16[4,64,384,128]{3,2,1,0:T(8,128)(2,1)}, bf16[4,4,128,128]{3,2,1,0:T(8,128)(2,1)S(1)}) custom-call(s32[6]{0:T(128)S(1)} %stack.261.at, ...), custom_call_target="tpu_custom_call", output_to_operand_aliasing={{0}: (8, {}), {1}: (9, {}), {2}: (10, {}), {3}: (11, {}), {... | custom-call | flops 4294967296 | bytes 33554432 | tf_op jit(solution)/shard_map/enter/pallas_call | solution.py:185
  252.5 36.1 %collective-permute-done.12.mask = bf16[2,128,128]{2,1,0:T(8,128)(2,1)S(1)} collective-permute-done((bf16[2,128,128]{2,1,0:T(8,128)(2,1)S(1)}, bf16[2,128,128]{2,1,0:T(8,128)(2,1)S(1)}, u32[]{:S(2)}, u32[]{:S(2)}) %collective-permute-start.12) | collective-permute-done | bytes 65568 | tf_op jit(solution)/shard_map/ppermute | solution.py:503
  288.6 1.3 collective-permute-done.14.mask
  290.4 3.1 slice.74
  293.6 3.2 slice.75
  296.7 1.5 collective-permute-start.19
  298.9 1.5 collective-permute-start.18
  300.4 0.9 copy-done.3
  301.3 25.3 %enter.14 = (bf16[49,128,2048]{2,1,0:T(8,128)(2,1)}, bf16[4,32,512,128]{3,2,1,0:T(8,128)(2,1)}, bf16[4,32,512,128]{3,2,1,0:T(8,128)(2,1)}, bf16[4,64,384,128]{3,2,1,0:T(8,128)(2,1)}, bf16[4,4,128,128]{3,2,1,0:T(8,128)(2,1)S(1)}) custom-call(s32[6]{0:T(128)S(1)} %stack.279.at, ...), custom_call_target="tpu_custom_call", output_to_operand_aliasing={{0}: (8, {}), {1}: (9, {}), {2}: (10, {}), {3}: (11, {}), {... | custom-call | flops 4294967296 | bytes 33554432 | tf_op jit(solution)/shard_map/enter/pallas_call | solution.py:185
  326.7 25.3 %enter.15 = (bf16[49,128,2048]{2,1,0:T(8,128)(2,1)}, bf16[4,32,512,128]{3,2,1,0:T(8,128)(2,1)}, bf16[4,32,512,128]{3,2,1,0:T(8,128)(2,1)}, bf16[4,64,384,128]{3,2,1,0:T(8,128)(2,1)}, bf16[4,4,128,128]{3,2,1,0:T(8,128)(2,1)S(1)}) custom-call(s32[6]{0:T(128)S(1)} %stack.273.at, ...), custom_call_target="tpu_custom_call", output_to_operand_aliasing={{0}: (8, {}), {1}: (9, {}), {2}: (10, {}), {3}: (11, {}), {... | custom-call | flops 4294967296 | bytes 33554432 | tf_op jit(solution)/shard_map/enter/pallas_call | solution.py:185
  352.7 6.0 %collective-permute-done.24.sib = bf16[64,128,128]{2,1,0:T(8,128)(2,1)} collective-permute-done((bf16[64,128,128]{2,1,0:T(8,128)(2,1)}, bf16[64,128,128]{2,1,0:T(8,128)(2,1)}, u32[]{:S(2)}, u32[]{:S(2)}) %collective-permute-start.24) | collective-permute-done | bytes 2097184 | tf_op jit(solution)/shard_map/ppermute | solution.py:542
  358.7 14.0 %enter.16 = (bf16[49,128,2048]{2,1,0:T(8,128)(2,1)}, bf16[4,32,512,128]{3,2,1,0:T(8,128)(2,1)}, bf16[4,32,512,128]{3,2,1,0:T(8,128)(2,1)}, bf16[4,64,384,128]{3,2,1,0:T(8,128)(2,1)}, bf16[4,4,128,128]{3,2,1,0:T(8,128)(2,1)S(1)}) custom-call(s32[6]{0:T(128)S(1)} %stack.230.at, ...), custom_call_target="tpu_custom_call", output_to_operand_aliasing={{0}: (8, {}), {1}: (9, {}), {2}: (10, {}), {3}: (11, {}), {... | custom-call | flops 2147483648 | bytes 16777216 | tf_op jit(solution)/shard_map/enter/pallas_call | solution.py:185
  372.8 13.8 %enter.17 = (bf16[49,128,2048]{2,1,0:T(8,128)(2,1)}, bf16[4,32,512,128]{3,2,1,0:T(8,128)(2,1)}, bf16[4,32,512,128]{3,2,1,0:T(8,128)(2,1)}, bf16[4,64,384,128]{3,2,1,0:T(8,128)(2,1)}, bf16[4,4,128,128]{3,2,1,0:T(8,128)(2,1)S(1)}) custom-call(s32[6]{0:T(128)S(1)} %stack.230.at, ...), custom_call_target="tpu_custom_call", output_to_operand_aliasing={{0}: (8, {}), {1}: (9, {}), {2}: (10, {}), {3}: (11, {}), {... | custom-call | flops 2147483648 | bytes 16777216 | tf_op jit(solution)/shard_map/enter/pallas_call | solution.py:185
  386.5 10.6 %outgoing.4 = (bf16[3,16,256,128]{3,2,1,0:T(8,128)(2,1)S(1)}, bf16[3,16,256,128]{3,2,1,0:T(8,128)(2,1)S(1)}) custom-call(s32[2]{0:T(128)S(1)} %pad_add_fusion.1.at, bf16[4,32,512,128]{3,2,1,0:T(8,128)(2,1)} %get-tuple-element.262.left, bf16[4,64,384,128]{3,2,1,0:T(8,128)(2,1)} %get-tuple-element.263.right), custom_call_target="tpu_custom_call" | custom-call | flops 3221225472 | bytes 21299200 | tf_op jit(solution)/shard_map/outgoing/pallas_call | solution.py:245
  397.3 10.6 %outgoing.5 = (bf16[3,16,256,128]{3,2,1,0:T(8,128)(2,1)S(1)}, bf16[3,16,256,128]{3,2,1,0:T(8,128)(2,1)S(1)}) custom-call(s32[2]{0:T(128)S(1)} %pad_add_fusion.1.at, bf16[4,32,512,128]{3,2,1,0:T(8,128)(2,1)} %get-tuple-element.262.left, bf16[4,64,384,128]{3,2,1,0:T(8,128)(2,1)} %get-tuple-element.263.right), custom_call_target="tpu_custom_call" | custom-call | flops 3221225472 | bytes 21299200 | tf_op jit(solution)/shard_map/outgoing/pallas_call | solution.py:245
  408.4 5.3 collective-permute-done.26.rest_5_
  413.6 1.7 copy-done.8
  415.4 10.6 %outgoing.6 = (bf16[3,16,256,128]{3,2,1,0:T(8,128)(2,1)S(1)}, bf16[3,16,256,128]{3,2,1,0:T(8,128)(2,1)S(1)}) custom-call(s32[2]{0:T(128)S(1)} %pad_add_fusion.1.at, bf16[4,32,512,128]{3,2,1,0:T(8,128)(2,1)} %get-tuple-element.268.left, bf16[4,64,384,128]{3,2,1,0:T(8,128)(2,1)} %get-tuple-element.263.right), custom_call_target="tpu_custom_call" | custom-call | flops 3221225472 | bytes 21299200 | tf_op jit(solution)/shard_map/outgoing/pallas_call | solution.py:245
  426.0 10.6 %outgoing.7 = (bf16[3,16,256,128]{3,2,1,0:T(8,128)(2,1)S(1)}, bf16[3,16,256,128]{3,2,1,0:T(8,128)(2,1)S(1)}) custom-call(s32[2]{0:T(128)S(1)} %pad_add_fusion.1.at, bf16[4,32,512,128]{3,2,1,0:T(8,128)(2,1)} %get-tuple-element.268.left, bf16[4,64,384,128]{3,2,1,0:T(8,128)(2,1)} %get-tuple-element.263.right), custom_call_target="tpu_custom_call" | custom-call | flops 3221225472 | bytes 21299200 | tf_op jit(solution)/shard_map/outgoing/pallas_call | solution.py:245
  437.3 5.1 collective-permute-done.28.rest_7_
  442.4 4.5 collective-permute-done.27.rest_6_
  446.9 1.6 copy-done.10
  448.5 112.1 %middle.1 = (bf16[3,128,256,128]{3,2,1,0:T(8,128)(2,1)}, bf16[17,128,2048]{2,1,0:T(8,128)(2,1)}) custom-call(s32[4]{0:T(128)S(1)} %pad_add_fusion.at, bf16[49,128,2048]{2,1,0:T(8,128)(2,1)} %get-tuple-element.251.state, bf16[4,4,128,128]{3,2,1,0:T(8,128)(2,1)S(1)} %get-tuple-element.252.mask, f32[128,128]{1,0:T(8,128)S(1)} %broadcast_in_dim.55.gain.gain0, ...), custom_call_target="tpu_custom_call" | custom-call | flops 12884901888 | bytes 100663296 | tf_op jit(solution)/shard_map/middle/pallas_call | solution.py:301
  560.6 17.0 %incoming.1 = (f32[128,128,128]{2,1,0:T(8,128)S(1)}, bf16[128,128,128]{2,1,0:T(8,128)(2,1)S(1)}) custom-call(s32[4]{0:T(128)S(1)} %pad_add_fusion.at, bf16[3,128,256,128]{3,2,1,0:T(8,128)(2,1)} %get-tuple-element.277.pairs), custom_call_target="tpu_custom_call" | custom-call | flops 2147483648 | bytes 37748736 | tf_op jit(solution)/shard_map/incoming/pallas_call | solution.py:363
  578.1 6.8 %collective-permute-done.29.got = bf16[128,128,128]{2,1,0:T(8,128)(2,1)S(1)} collective-permute-done((bf16[128,128,128]{2,1,0:T(8,128)(2,1)S(1)}, bf16[128,128,128]{2,1,0:T(8,128)(2,1)S(1)}, u32[]{:S(2)}, u32[]{:S(2)}) %collective-permute-start.29) | collective-permute-done | bytes 4194336 | tf_op jit(solution)/shard_map/ppermute | solution.py:559
  584.9 16.7 %leave.1 = bf16[128,128,128]{2,1,0:T(8,128)(2,1)} custom-call(s32[4]{0:T(128)S(1)} %pad_add_fusion.at, f32[128,128,128]{2,1,0:T(8,128)S(1)} %get-tuple-element.278.kept, bf16[128,128,128]{2,1,0:T(8,128)(2,1)S(1)} %collective-permute-done.29.got, bf16[17,128,2048]{2,1,0:T(8,128)(2,1)} %get-tuple-element.280.state, f32[128,128]{1,0:T(8,128)S(1)} %broadcast_in_dim.61.gain1, ...), custom_call_target="tpu_custom_call" | custom-call | flops 1073741824 | bytes 20971520 | tf_op jit(solution)/shard_map/leave/pallas_call | solution.py:400
  (112 shorter events, 15.2 us)
Async XLA Ops:
  0.0 16.7 %collective-permute-start.5 = (bf16[128,128,128]{2,1,0:T(8,128)(2,1)}, bf16[128,128,128]{2,1,0:T(8,128)(2,1)}, u32[]{:S(2)}, u32[]{:S(2)}) collective-permute-start(bf16[128,128,128]{2,1,0:T(8,128)(2,1)} %own.1), channel_id=1, source_target_pairs={{0,4},{4,0},{1,5},{5,1},{2,6},{6,2},{3,7},{7,3},{11,15},{15,11},{1... | collective-permute-start | bytes 12582920 | tf_op jit(solution)/shard_map/ppermute | solution.py:505
  0.5 96.9 %collective-permute-start.2 = (bf16[128,128,128]{2,1,0:T(8,128)(2,1)}, bf16[128,128,128]{2,1,0:T(8,128)(2,1)}, u32[]{:S(2)}, u32[]{:S(2)}) collective-permute-start(bf16[128,128,128]{2,1,0:T(8,128)(2,1)} %own.1), channel_id=1, source_target_pairs={{0,1},{4,5},{1,2},{5,6},{2,3},{6,7},{3,11},{7,15},{11,10},{15,14},... | collective-permute-start | bytes 12582920 | tf_op jit(solution)/shard_map/ppermute | solution.py:503
  3.0 94.3 %collective-permute-start.4 = (bf16[128,128,128]{2,1,0:T(8,128)(2,1)}, bf16[128,128,128]{2,1,0:T(8,128)(2,1)}, u32[]{:S(2)}, u32[]{:S(2)}) collective-permute-start(bf16[128,128,128]{2,1,0:T(8,128)(2,1)} %own.1), channel_id=1, source_target_pairs={{1,0},{5,4},{2,1},{6,5},{3,2},{7,6},{11,3},{15,7},{10,11},{14,15},... | collective-permute-start | bytes 12582920 | tf_op jit(solution)/shard_map/ppermute | solution.py:503
  3.9 10.7 %collective-permute-start = (bf16[128,128]{1,0:T(8,128)(2,1)S(1)}, bf16[128,128]{1,0:T(8,128)(2,1)S(1)}, u32[]{:S(2)}, u32[]{:S(2)}) collective-permute-start(bf16[128,128]{1,0:T(8,128)(2,1)S(1)} %convert_element_type.6), channel_id=1, source_target_pairs={{0,4},{4,0},{1,5},{5,1},{2,6},{6,2},{3,7},{7,3},{11,15},{15,11},{1... | collective-permute-start | bytes 98312 | tf_op jit(solution)/shard_map/ppermute | solution.py:451
  14.6 81.2 %collective-permute-start.1 = (bf16[2,128,128]{2,1,0:T(8,128)(2,1)S(1)}, bf16[2,128,128]{2,1,0:T(8,128)(2,1)S(1)}, u32[]{:S(2)}, u32[]{:S(2)}) collective-permute-start(bf16[2,128,128]{2,1,0:T(8,128)(2,1)S(1)} %maximum_select_fusion.mask), channel_id=1, source_target_pairs={{0,1},{4,5},{1,2},{5,6},{2,3},{6,7},{3,11},{7,15},{11,10},{15,14},... | collective-permute-start | bytes 196616 | tf_op jit(solution)/shard_map/ppermute | solution.py:503
  16.5 80.9 %collective-permute-start.3 = (bf16[2,128,128]{2,1,0:T(8,128)(2,1)S(1)}, bf16[2,128,128]{2,1,0:T(8,128)(2,1)S(1)}, u32[]{:S(2)}, u32[]{:S(2)}) collective-permute-start(bf16[2,128,128]{2,1,0:T(8,128)(2,1)S(1)} %maximum_select_fusion.mask), channel_id=1, source_target_pairs={{1,0},{5,4},{2,1},{6,5},{3,2},{7,6},{11,3},{15,7},{10,11},{14,15},... | collective-permute-start | bytes 196616 | tf_op jit(solution)/shard_map/ppermute | solution.py:503
  16.8 2.2 copy-start.6
  97.8 7.5 %collective-permute-start.11 = (bf16[128,128,128]{2,1,0:T(8,128)(2,1)}, bf16[128,128,128]{2,1,0:T(8,128)(2,1)}, u32[]{:S(2)}, u32[]{:S(2)}) collective-permute-start(bf16[128,128,128]{2,1,0:T(8,128)(2,1)} %collective-permute-done.2.own), channel_id=1, source_target_pairs={{0,4},{4,0},{1,5},{5,1},{2,6},{6,2},{3,7},{7,3},{11,15},{15,11},{1... | collective-permute-start | bytes 12582920 | tf_op jit(solution)/shard_map/ppermute | solution.py:540
  97.9 33.1 %collective-permute-start.10 = (bf16[128,128,128]{2,1,0:T(8,128)(2,1)}, bf16[128,128,128]{2,1,0:T(8,128)(2,1)}, u32[]{:S(2)}, u32[]{:S(2)}) collective-permute-start(bf16[128,128,128]{2,1,0:T(8,128)(2,1)} %collective-permute-done.4.own), channel_id=1, source_target_pairs={{0,4},{4,0},{1,5},{5,1},{2,6},{6,2},{3,7},{7,3},{11,15},{15,11},{1... | collective-permute-start | bytes 12582920 | tf_op jit(solution)/shard_map/ppermute | solution.py:540
  98.4 95.5 %collective-permute-start.7 = (bf16[128,128,128]{2,1,0:T(8,128)(2,1)}, bf16[128,128,128]{2,1,0:T(8,128)(2,1)}, u32[]{:S(2)}, u32[]{:S(2)}) collective-permute-start(bf16[128,128,128]{2,1,0:T(8,128)(2,1)} %collective-permute-done.2.own), channel_id=1, source_target_pairs={{0,1},{4,5},{1,2},{5,6},{2,3},{6,7},{3,11},{7,15},{11,10},{15,14},... | collective-permute-start | bytes 12582920 | tf_op jit(solution)/shard_map/ppermute | solution.py:503
  100.0 93.9 %collective-permute-start.9 = (bf16[128,128,128]{2,1,0:T(8,128)(2,1)}, bf16[128,128,128]{2,1,0:T(8,128)(2,1)}, u32[]{:S(2)}, u32[]{:S(2)}) collective-permute-start(bf16[128,128,128]{2,1,0:T(8,128)(2,1)} %collective-permute-done.4.own), channel_id=1, source_target_pairs={{1,0},{5,4},{2,1},{6,5},{3,2},{7,6},{11,3},{15,7},{10,11},{14,15},... | collective-permute-start | bytes 12582920 | tf_op jit(solution)/shard_map/ppermute | solution.py:503
  100.6 92.0 %collective-permute-start.6 = (bf16[2,128,128]{2,1,0:T(8,128)(2,1)S(1)}, bf16[2,128,128]{2,1,0:T(8,128)(2,1)S(1)}, u32[]{:S(2)}, u32[]{:S(2)}) collective-permute-start(bf16[2,128,128]{2,1,0:T(8,128)(2,1)S(1)} %collective-permute-done.1.mask), channel_id=1, source_target_pairs={{0,1},{4,5},{1,2},{5,6},{2,3},{6,7},{3,11},{7,15},{11,10},{15,14},... | collective-permute-start | bytes 196616 | tf_op jit(solution)/shard_map/ppermute | solution.py:503
  105.4 88.5 %collective-permute-start.8 = (bf16[2,128,128]{2,1,0:T(8,128)(2,1)S(1)}, bf16[2,128,128]{2,1,0:T(8,128)(2,1)S(1)}, u32[]{:S(2)}, u32[]{:S(2)}) collective-permute-start(bf16[2,128,128]{2,1,0:T(8,128)(2,1)S(1)} %collective-permute-done.3.mask), channel_id=1, source_target_pairs={{1,0},{5,4},{2,1},{6,5},{3,2},{7,6},{11,3},{15,7},{10,11},{14,15},... | collective-permute-start | bytes 196616 | tf_op jit(solution)/shard_map/ppermute | solution.py:503
  193.9 7.5 %collective-permute-start.17 = (bf16[128,128,128]{2,1,0:T(8,128)(2,1)}, bf16[128,128,128]{2,1,0:T(8,128)(2,1)}, u32[]{:S(2)}, u32[]{:S(2)}) collective-permute-start(bf16[128,128,128]{2,1,0:T(8,128)(2,1)} %collective-permute-done.7.own), channel_id=1, source_target_pairs={{0,4},{4,0},{1,5},{5,1},{2,6},{6,2},{3,7},{7,3},{11,15},{15,11},{1... | collective-permute-start | bytes 12582920 | tf_op jit(solution)/shard_map/ppermute | solution.py:540
  193.9 33.3 %collective-permute-start.16 = (bf16[128,128,128]{2,1,0:T(8,128)(2,1)}, bf16[128,128,128]{2,1,0:T(8,128)(2,1)}, u32[]{:S(2)}, u32[]{:S(2)}) collective-permute-start(bf16[128,128,128]{2,1,0:T(8,128)(2,1)} %collective-permute-done.9.own), channel_id=1, source_target_pairs={{0,4},{4,0},{1,5},{5,1},{2,6},{6,2},{3,7},{7,3},{11,15},{15,11},{1... | collective-permute-start | bytes 12582920 | tf_op jit(solution)/shard_map/ppermute | solution.py:540
  194.4 95.5 %collective-permute-start.13 = (bf16[128,128,128]{2,1,0:T(8,128)(2,1)}, bf16[128,128,128]{2,1,0:T(8,128)(2,1)}, u32[]{:S(2)}, u32[]{:S(2)}) collective-permute-start(bf16[128,128,128]{2,1,0:T(8,128)(2,1)} %collective-permute-done.7.own), channel_id=1, source_target_pairs={{0,1},{4,5},{1,2},{5,6},{2,3},{6,7},{3,11},{7,15},{11,10},{15,14},... | collective-permute-start | bytes 12582920 | tf_op jit(solution)/shard_map/ppermute | solution.py:503
  196.0 93.9 %collective-permute-start.15 = (bf16[128,128,128]{2,1,0:T(8,128)(2,1)}, bf16[128,128,128]{2,1,0:T(8,128)(2,1)}, u32[]{:S(2)}, u32[]{:S(2)}) collective-permute-start(bf16[128,128,128]{2,1,0:T(8,128)(2,1)} %collective-permute-done.9.own), channel_id=1, source_target_pairs={{1,0},{5,4},{2,1},{6,5},{3,2},{7,6},{11,3},{15,7},{10,11},{14,15},... | collective-permute-start | bytes 12582920 | tf_op jit(solution)/shard_map/ppermute | solution.py:503
  196.6 92.0 %collective-permute-start.12 = (bf16[2,128,128]{2,1,0:T(8,128)(2,1)S(1)}, bf16[2,128,128]{2,1,0:T(8,128)(2,1)S(1)}, u32[]{:S(2)}, u32[]{:S(2)}) collective-permute-start(bf16[2,128,128]{2,1,0:T(8,128)(2,1)S(1)} %collective-permute-done.6.mask), channel_id=1, source_target_pairs={{0,1},{4,5},{1,2},{5,6},{2,3},{6,7},{3,11},{7,15},{11,10},{15,14},... | collective-permute-start | bytes 196616 | tf_op jit(solution)/shard_map/ppermute | solution.py:503
  201.4 88.5 %collective-permute-start.14 = (bf16[2,128,128]{2,1,0:T(8,128)(2,1)S(1)}, bf16[2,128,128]{2,1,0:T(8,128)(2,1)S(1)}, u32[]{:S(2)}, u32[]{:S(2)}) collective-permute-start(bf16[2,128,128]{2,1,0:T(8,128)(2,1)S(1)} %collective-permute-done.8.mask), channel_id=1, source_target_pairs={{1,0},{5,4},{2,1},{6,5},{3,2},{7,6},{11,3},{15,7},{10,11},{14,15},... | collective-permute-start | bytes 196616 | tf_op jit(solution)/shard_map/ppermute | solution.py:503
  288.6 8.2 %copy-start.2 = (bf16[2,128,128]{2,1,0:T(8,128)(2,1)}, bf16[2,128,128]{2,1,0:T(8,128)(2,1)S(1)}, u32[]{:S(2)}) copy-start(bf16[2,128,128]{2,1,0:T(8,128)(2,1)S(1)} %collective-permute-done.12.mask) | copy-start | bytes 196612
  289.9 8.4 %copy-start.4 = (bf16[2,128,128]{2,1,0:T(8,128)(2,1)}, bf16[2,128,128]{2,1,0:T(8,128)(2,1)S(1)}, u32[]{:S(2)}) copy-start(bf16[2,128,128]{2,1,0:T(8,128)(2,1)S(1)} %collective-permute-done.14.mask) | copy-start | bytes 196612
  289.9 10.6 %collective-permute-start.22 = (bf16[128,128,128]{2,1,0:T(8,128)(2,1)}, bf16[128,128,128]{2,1,0:T(8,128)(2,1)}, u32[]{:S(2)}, u32[]{:S(2)}) collective-permute-start(bf16[128,128,128]{2,1,0:T(8,128)(2,1)} %collective-permute-done.13.own), channel_id=1, source_target_pairs={{0,4},{4,0},{1,5},{5,1},{2,6},{6,2},{3,7},{7,3},{11,15},{15,11},{1... | collective-permute-start | bytes 12582920 | tf_op jit(solution)/shard_map/ppermute | solution.py:540
  289.9 36.7 %collective-permute-start.21 = (bf16[128,128,128]{2,1,0:T(8,128)(2,1)}, bf16[128,128,128]{2,1,0:T(8,128)(2,1)}, u32[]{:S(2)}, u32[]{:S(2)}) collective-permute-start(bf16[128,128,128]{2,1,0:T(8,128)(2,1)} %collective-permute-done.15.own), channel_id=1, source_target_pairs={{0,4},{4,0},{1,5},{5,1},{2,6},{6,2},{3,7},{7,3},{11,15},{15,11},{1... | collective-permute-start | bytes 12582920 | tf_op jit(solution)/shard_map/ppermute | solution.py:540
  296.7 55.2 %collective-permute-start.19 = (bf16[64,128,128]{2,1,0:T(8,128)(2,1)}, bf16[64,128,128]{2,1,0:T(8,128)(2,1)}, u32[]{:S(2)}, u32[]{:S(2)}) collective-permute-start(bf16[64,128,128]{2,1,0:T(8,128)(2,1)} %slice.74), channel_id=1, source_target_pairs={{0,1},{4,5},{1,2},{5,6},{2,3},{6,7},{3,11},{7,15},{11,10},{15,14},... | collective-permute-start | bytes 6291464 | tf_op jit(solution)/shard_map/ppermute | solution.py:503
  298.2 53.7 %collective-permute-start.20 = (bf16[64,128,128]{2,1,0:T(8,128)(2,1)}, bf16[64,128,128]{2,1,0:T(8,128)(2,1)S(1)}, u32[]{:S(2)}, u32[]{:S(2)}) collective-permute-start(bf16[64,128,128]{2,1,0:T(8,128)(2,1)} %slice.75), channel_id=1, source_target_pairs={{1,0},{5,4},{2,1},{6,5},{3,2},{7,6},{11,3},{15,7},{10,11},{14,15},... | collective-permute-start | bytes 6291464 | tf_op jit(solution)/shard_map/ppermute | solution.py:503
  298.9 53.0 %collective-permute-start.18 = (bf16[2,128,128]{2,1,0:T(8,128)(2,1)}, bf16[2,128,128]{2,1,0:T(8,128)(2,1)S(1)}, u32[]{:S(2)}, u32[]{:S(2)}) collective-permute-start(bf16[2,128,128]{2,1,0:T(8,128)(2,1)} %copy-done.2), channel_id=1, source_target_pairs={{0,1},{4,5},{1,2},{5,6},{2,3},{6,7},{3,11},{7,15},{11,10},{15,14},... | collective-permute-start | bytes 196616 | tf_op jit(solution)/shard_map/ppermute | solution.py:503
  300.4 0.9 copy-start.3
  301.3 25.3 %copy-start.5 = (bf16[2,128,128]{2,1,0:T(8,128)(2,1)S(1)}, bf16[2,128,128]{2,1,0:T(8,128)(2,1)}, u32[]{:S(2)}) copy-start(bf16[2,128,128]{2,1,0:T(8,128)(2,1)} %copy-done.4) | copy-start | bytes 196612
  352.0 6.8 %collective-permute-start.24 = (bf16[64,128,128]{2,1,0:T(8,128)(2,1)}, bf16[64,128,128]{2,1,0:T(8,128)(2,1)}, u32[]{:S(2)}, u32[]{:S(2)}) collective-permute-start(bf16[64,128,128]{2,1,0:T(8,128)(2,1)} %collective-permute-done.19.own), channel_id=1, source_target_pairs={{0,4},{4,0},{1,5},{5,1},{2,6},{6,2},{3,7},{7,3},{11,15},{15,11},{1... | collective-permute-start | bytes 6291464 | tf_op jit(solution)/shard_map/ppermute | solution.py:542
  352.0 20.7 %collective-permute-start.23 = (bf16[64,128,128]{2,1,0:T(8,128)(2,1)S(1)}, bf16[64,128,128]{2,1,0:T(8,128)(2,1)}, u32[]{:S(2)}, u32[]{:S(2)}) collective-permute-start(bf16[64,128,128]{2,1,0:T(8,128)(2,1)S(1)} %collective-permute-done.20.own), channel_id=1, source_target_pairs={{0,4},{4,0},{1,5},{5,1},{2,6},{6,2},{3,7},{7,3},{11,15},{15,11},{1... | collective-permute-start | bytes 6291464 | tf_op jit(solution)/shard_map/ppermute | solution.py:543
  397.1 11.2 %collective-permute-start.25 = (bf16[3,16,256,128]{3,2,1,0:T(8,128)(2,1)S(1)}, bf16[3,16,256,128]{3,2,1,0:T(8,128)(2,1)S(1)}, u32[]{:S(2)}, u32[]{:S(2)}) collective-permute-start(bf16[3,16,256,128]{3,2,1,0:T(8,128)(2,1)S(1)} %get-tuple-element.266), channel_id=1, source_target_pairs={{0,4},{4,0},{1,5},{5,1},{2,6},{6,2},{3,7},{7,3},{11,15},{15,11},{1... | collective-permute-start | bytes 9437192 | tf_op jit(solution)/shard_map/ppermute | solution.py:554
  407.9 5.7 collective-permute-start.26
  408.4 17.6 %copy-start.7 = (bf16[3,16,256,128]{3,2,1,0:T(8,128)(2,1)}, bf16[3,16,256,128]{3,2,1,0:T(8,128)(2,1)S(1)}, u32[]{:S(2)}) copy-start(bf16[3,16,256,128]{3,2,1,0:T(8,128)(2,1)S(1)} %collective-permute-done.25.rest_4_) | copy-start | bytes 9437188
  413.6 1.7 copy-start.8
  426.0 22.5 %copy-start = (bf16[128,128]{1,0:T(8,128)(2,1)S(1)}, bf16[128,128]{1,0:T(8,128)(2,1)}, u32[]{:S(2)}) copy-start(bf16[128,128]{1,0:T(8,128)(2,1)} %fusion.5.proj) | copy-start | bytes 98308
  426.0 22.5 %copy-start.1 = (bf16[128,128]{1,0:T(8,128)(2,1)S(1)}, bf16[128,128]{1,0:T(8,128)(2,1)}, u32[]{:S(2)}) copy-start(bf16[128,128]{1,0:T(8,128)(2,1)} %multiply_bitcast_fusion.2.gate) | copy-start | bytes 98308
  436.6 5.7 collective-permute-start.28
  437.1 9.8 %collective-permute-start.27 = (bf16[3,16,256,128]{3,2,1,0:T(8,128)(2,1)S(1)}, bf16[3,16,256,128]{3,2,1,0:T(8,128)(2,1)S(1)}, u32[]{:S(2)}, u32[]{:S(2)}) collective-permute-start(bf16[3,16,256,128]{3,2,1,0:T(8,128)(2,1)S(1)} %get-tuple-element.275), channel_id=1, source_target_pairs={{0,4},{4,0},{1,5},{5,1},{2,6},{6,2},{3,7},{7,3},{11,15},{15,11},{1... | collective-permute-start | bytes 9437192 | tf_op jit(solution)/shard_map/ppermute | solution.py:554
  442.4 6.1 %copy-start.9 = (bf16[3,16,256,128]{3,2,1,0:T(8,128)(2,1)}, bf16[3,16,256,128]{3,2,1,0:T(8,128)(2,1)S(1)}, u32[]{:S(2)}) copy-start(bf16[3,16,256,128]{3,2,1,0:T(8,128)(2,1)S(1)} %collective-permute-done.28.rest_7_) | copy-start | bytes 9437188
  446.9 1.6 copy-start.10
  577.7 7.2 %collective-permute-start.29 = (bf16[128,128,128]{2,1,0:T(8,128)(2,1)S(1)}, bf16[128,128,128]{2,1,0:T(8,128)(2,1)S(1)}, u32[]{:S(2)}, u32[]{:S(2)}) collective-permute-start(bf16[128,128,128]{2,1,0:T(8,128)(2,1)S(1)} %get-tuple-element.279), channel_id=1, source_target_pairs={{0,4},{4,0},{1,5},{5,1},{2,6},{6,2},{3,7},{7,3},{11,15},{15,11},{1... | collective-permute-start | bytes 12582920 | tf_op jit(solution)/shard_map/ppermute | solution.py:559

commit v4 on v3

--- a/solution.py
+++ b/solution.py
@@ -55,7 +55,8 @@
 SUB = 16
 BLOCKS = TILE // SUB
 CHUNK = 2
-STATE_BLOCKS = 6 * BLOCKS
+GROUPS = 2
+MIDDLE_GROUPS = 4
 VMEM_LIMIT = 40 * 1024 * 1024
 BOTH = ("row", "col")
 NT = (((1,), (1,)), ((), ()))
@@ -81,51 +82,71 @@
     return jnp.dot(matrix, values, preferred_element_type=jnp.float32)
 
 
-def gated_store(weights, normed, mask_rows, first, turn):
+def gated(weights, normed):
     both = product(weights, normed)
     half = both.shape[0] // 2
-    paired = both[:half] * jnp.tanh(both[half:]) + both[:half]
-    for r in range(CHUNK):
-        turn[pl.ds(first + r, half, stride=SUB), :] = (
-            paired[:, r * TILE : (r + 1) * TILE] * mask_rows[first + r : first + r + 1, :]
-        )
+    return both[:half] * jnp.tanh(both[half:]) + both[:half]
+
+
+def turn_masked(chunks, mask_rows, turn):
+    count = chunks[0].shape[0]
+    for r in range(SUB):
+        lanes = slice(r % CHUNK * TILE, (r % CHUNK + 1) * TILE)
+        turn[pl.ds(r, count, stride=SUB), :] = chunks[r // CHUNK][:, lanes] * mask_rows[r : r + 1, :]
 
 
 def chunk_of(turn, first):
     return jnp.concatenate([turn[pl.ds(first + r, TILE, stride=SUB), :] for r in range(CHUNK)], axis=1)
+
+
+def rows_of(group):
+    return pl.ds(pl.multiple_of(group * SUB, SUB), SUB)
 
 
 def enter_kernel(at, own, sib, mask, both, gain, bias, weights, *rest):
     state_out, left_low, left_high, right_out, mask_out, turn = rest[-6:]
     step = pl.program_id(0)
     use_own = (step == 1) == (at[4] == 1)
-    mask_rows = mask[0].astype(jnp.float32)
     mask_out[0, 0] = mask[0]
+
+    def finish(group, paired):
+        turn_masked(paired, mask[0, rows_of(group), :].astype(jnp.float32), turn)
+        start = 0
+        for out in (left_low, left_high, right_out):
+            stop = start + out.shape[1] * SUB
+            out[0, :, rows_of(group), :] = (
+                turn[start:stop, :].astype(jnp.bfloat16).reshape(out.shape[1], SUB, TILE)
+            )
+            start = stop
+
+    def turned_chunks(tile, group, matrix):
+        rows = tile[rows_of(group)].reshape(SUB * TILE, TILE)
+        size = CHUNK * TILE
+        return [channels_first(rows[n * size : (n + 1) * size], matrix) for n in range(SUB // CHUNK)]
 
     @pl.when(use_own)
     def _():
-        for first in range(0, SUB, CHUNK):
-            turned = channels_first(own[first : first + CHUNK].reshape(CHUNK * TILE, TILE), both[...])
-            normed = norm_apart(turned[:TILE], gain, bias)
-            lanes = slice(first * TILE, (first + CHUNK) * TILE)
-            state_out[0, :, lanes] = turned[TILE:].astype(jnp.bfloat16)
-            gated_store(weights[...], normed, mask_rows, first, turn)
+        @pl.loop(0, GROUPS)
+        def _(group):
+            chunks = turned_chunks(own, group, both[...])
+            paired = [gated(weights[...], norm_apart(chunk[:TILE], gain, bias)) for chunk in chunks]
+            state_out[group] = jnp.concatenate(
+                [chunk[TILE:].astype(jnp.bfloat16) for chunk in chunks], axis=1
+            )
+            finish(group, paired)
 
     @pl.when(jnp.logical_not(use_own))
     def _():
-        for first in range(0, SUB, CHUNK):
-            apart = channels_first(sib[first : first + CHUNK].reshape(CHUNK * TILE, TILE), both[:TILE])
-            gated_store(weights[...], norm_apart(apart, gain, bias), mask_rows, first, turn)
-
-    start = 0
-    for out in (left_low, left_high, right_out):
-        stop = start + out.shape[1] * SUB
-        out[0] = turn[start:stop, :].astype(jnp.bfloat16).reshape(out.shape[1], SUB, TILE)
-        start = stop
+        @pl.loop(0, GROUPS)
+        def _(group):
+            chunks = turned_chunks(sib, group, both[:TILE])
+            finish(group, [gated(weights[...], norm_apart(chunk, gain, bias)) for chunk in chunks])
 
 
 def enter(own, sib, first_block, at, mask, both, gain, bias, weights, held):
-    n_block = own.shape[0] // SUB
+    n_block = own.shape[0] // (GROUPS * SUB)
+    blocks = TILE // (GROUPS * SUB)
+    high = GROUPS * SUB
     full = pl.BlockSpec(memory_space=pl.ANY)
 
     def core_of(step, at):
@@ -148,28 +169,28 @@
 
     def state_map(step, block, at):
         kept = jnp.where(is_own(step, at), block, jnp.where(step == 0, 0, n_block - 1))
-        return (jnp.where(at[5] < 0, STATE_BLOCKS, at[5] + first_block + kept), 0, 0)
+        return (jnp.where(at[5] < 0, 6 * blocks, at[5] * blocks + first_block + kept), 0, 0)
 
     def left_map(step, block, at):
-        return (at[1], 0, (2 * at[0] + core_of(step, at)) * BLOCKS + first_block + block, 0)
+        return (at[1], 0, (2 * at[0] + core_of(step, at)) * blocks + first_block + block, 0)
 
     def right_map(step, block, at):
         slot = jnp.where(at[3] == 1, core_of(step, at), 2)
-        return (at[1], 0, slot * BLOCKS + first_block + block, 0)
+        return (at[1], 0, slot * blocks + first_block + block, 0)
 
     half = weights.shape[0] // 4
     same = lambda step, block, at: (0, 0)
     shapes = (
-        jax.ShapeDtypeStruct((STATE_BLOCKS + 1, TILE, SUB * TILE), jnp.bfloat16),
+        jax.ShapeDtypeStruct((6 * BLOCKS + GROUPS, TILE, SUB * TILE), jnp.bfloat16),
         jax.ShapeDtypeStruct((4, half // 2, 4 * TILE, TILE), jnp.bfloat16),
         jax.ShapeDtypeStruct((4, half // 2, 4 * TILE, TILE), jnp.bfloat16),
         jax.ShapeDtypeStruct((4, half, 3 * TILE, TILE), jnp.bfloat16),
         jax.ShapeDtypeStruct((4, 4, TILE, TILE), jnp.bfloat16),
     )
     in_specs = [
-        pl.BlockSpec((SUB, TILE, TILE), own_map),
-        pl.BlockSpec((SUB, TILE, TILE), sib_map),
-        pl.BlockSpec((1, SUB, TILE), mask_map),
+        pl.BlockSpec((high, TILE, TILE), own_map),
+        pl.BlockSpec((high, TILE, TILE), sib_map),
+        pl.BlockSpec((1, high, TILE), mask_map),
         pl.BlockSpec((2 * TILE, TILE), same),
         pl.BlockSpec((TILE, TILE), same),
         pl.BlockSpec((TILE, TILE), same),
@@ -189,11 +210,11 @@
             grid=(2, n_block),
             in_specs=in_specs,
             out_specs=[
-                pl.BlockSpec((1, TILE, SUB * TILE), state_map),
-                pl.BlockSpec((1, half // 2, SUB, TILE), left_map),
-                pl.BlockSpec((1, half // 2, SUB, TILE), left_map),
-                pl.BlockSpec((1, half, SUB, TILE), right_map),
-                pl.BlockSpec((1, 1, SUB, TILE), mask_out_map),
+                pl.BlockSpec((GROUPS, TILE, SUB * TILE), state_map),
+                pl.BlockSpec((1, half // 2, high, TILE), left_map),
+                pl.BlockSpec((1, half // 2, high, TILE), left_map),
+                pl.BlockSpec((1, half, high, TILE), right_map),
+                pl.BlockSpec((1, 1, high, TILE), mask_out_map),
             ],
             scratch_shapes=[pltpu.VMEM((2 * half * SUB, TILE), jnp.float32)],
         ),
@@ -269,44 +290,52 @@
 ):
     parts, (pairs_out, state_out, turn, turn_out) = rest[:-4], rest[-4:]
     height = TILE * SUB // len(parts)
-    for n, part in enumerate(parts):
-        turn[n * height : (n + 1) * height, :] = part[0].reshape(height, TILE).astype(jnp.float32)
-    mask_rows = mask[0, 0].astype(jnp.float32)
-    for first in range(0, SUB, CHUNK):
-        lanes = slice(first * TILE, (first + CHUNK) * TILE)
-        normed_out = norm_channels(chunk_of(turn, first), gain_out, bias_out)
-        out = product(proj[...], normed_out)
-        before = state[0, :, lanes].astype(jnp.float32)
-        gate_value = jnp.tanh(product(gate[...], norm_channels(before, gain0, bias0)))
-        changed = (before + (out * gate_value + out)).astype(jnp.bfloat16)
-        state_out[0, :, lanes] = changed
-        normed1 = norm_channels(changed.astype(jnp.float32), gain1, bias1)
-        gated_store(weights[0], normed1, mask_rows, first, turn_out)
-    pairs_out[0] = turn_out[...].astype(jnp.bfloat16).reshape(TILE, SUB, TILE)
+
+    @pl.loop(0, MIDDLE_GROUPS)
+    def _(group):
+        for n, part in enumerate(parts):
+            turn[n * height : (n + 1) * height, :] = (
+                part[0, :, rows_of(group), :].reshape(height, TILE).astype(jnp.float32)
+            )
+        changed, paired = [], []
+        for first in range(0, SUB, CHUNK):
+            before = state[group, :, first * TILE : (first + CHUNK) * TILE].astype(jnp.float32)
+            gate_value = jnp.tanh(product(gate[...], norm_channels(before, gain0, bias0)))
+            out = product(proj[...], norm_channels(chunk_of(turn, first), gain_out, bias_out))
+            changed.append((before + (out * gate_value + out)).astype(jnp.bfloat16))
+            normed1 = norm_channels(changed[-1].astype(jnp.float32), gain1, bias1)
+            paired.append(gated(weights[0], normed1))
+        state_out[group] = jnp.concatenate(changed, axis=1)
+        turn_masked(paired, mask[0, 0, rows_of(group), :].astype(jnp.float32), turn_out)
+        pairs_out[0, :, rows_of(group), :] = (
+            turn_out[...].astype(jnp.bfloat16).reshape(TILE, SUB, TILE)
+        )
 
 
 def middle(at, states, mask, fixed, parts):
     def column(slot, at):
         return jnp.where(slot == 2, at[2], 2 * at[1] + slot)
 
+    blocks = BLOCKS // MIDDLE_GROUPS
+    high = MIDDLE_GROUPS * SUB
     square = pl.BlockSpec((TILE, TILE), lambda slot, x, block, at: (0, 0))
     tri = pl.BlockSpec(
-        (1, parts[0].shape[1], SUB, TILE), lambda slot, x, block, at: (slot, 0, x * BLOCKS + block, 0)
+        (1, parts[0].shape[1], high, TILE), lambda slot, x, block, at: (slot, 0, x * blocks + block, 0)
     )
     state_spec = pl.BlockSpec(
-        (1, TILE, SUB * TILE),
-        lambda slot, x, block, at: ((x * 3 + jnp.where(slot == 2, at[3], slot)) * BLOCKS + block, 0, 0),
+        (MIDDLE_GROUPS, TILE, SUB * TILE),
+        lambda slot, x, block, at: ((x * 3 + jnp.where(slot == 2, at[3], slot)) * blocks + block, 0, 0),
     )
     pairs = 6 * TILE * TILE
     return pl.pallas_call(
         middle_kernel,
         grid_spec=pltpu.PrefetchScalarGridSpec(
             num_scalar_prefetch=1,
-            grid=(3, 2, BLOCKS),
+            grid=(3, 2, blocks),
             in_specs=[
                 state_spec,
                 pl.BlockSpec(
-                    (1, 1, SUB, TILE),
+                    (1, 1, high, TILE),
                     lambda slot, x, block, at: (2 * x + at[0], column(slot, at), block, 0),
                 ),
             ]
@@ -320,12 +349,12 @@
             + [tri] * len(parts),
             out_specs=[
                 pl.BlockSpec(
-                    (1, TILE, SUB, TILE), lambda slot, x, block, at: (slot, 0, x * BLOCKS + block, 0)
+                    (1, TILE, high, TILE), lambda slot, x, block, at: (slot, 0, x * blocks + block, 0)
                 ),
                 pl.BlockSpec(
-                    (1, TILE, SUB * TILE),
+                    (MIDDLE_GROUPS, TILE, SUB * TILE),
                     lambda slot, x, block, at: (
-                        jnp.where(slot == 2, x * BLOCKS + block, 2 * BLOCKS), 0, 0,
+                        jnp.where(slot == 2, x * blocks + block, 2 * blocks), 0, 0,
                     ),
                 ),
             ],
@@ -333,7 +362,7 @@
         ),
         out_shape=(
             jax.ShapeDtypeStruct((3, TILE, 2 * TILE, TILE), jnp.bfloat16),
-            jax.ShapeDtypeStruct((2 * BLOCKS + 1, TILE, SUB * TILE), jnp.bfloat16),
+            jax.ShapeDtypeStruct((2 * BLOCKS + MIDDLE_GROUPS, TILE, SUB * TILE), jnp.bfloat16),
         ),
         compiler_params=pltpu.CompilerParams(
             dimension_semantics=("arbitrary",) * 3, vmem_limit_bytes=VMEM_LIMIT
@@ -383,32 +412,37 @@
 
 
 def leave_kernel(at, kept, got, state, gain1, bias1, gain_out, bias_out, proj, gate, result, turn):
-    summed = (kept[...] + got[...].astype(jnp.float32)).astype(jnp.bfloat16)
-    turn[...] = summed.astype(jnp.float32).reshape(TILE * SUB, TILE)
-    for first in range(0, SUB, CHUNK):
-        before = state[0, :, first * TILE : (first + CHUNK) * TILE].astype(jnp.float32)
-        normed = norm_channels(before, gain1, bias1)
-        out = product(proj[...], norm_channels(chunk_of(turn, first), gain_out, bias_out))
-        gate_value = jnp.tanh(product(gate[...], normed))
-        changed = (before + (out * gate_value + out)).astype(jnp.bfloat16)
-        result[first : first + CHUNK] = changed.T.reshape(CHUNK, TILE, TILE)
+    @pl.loop(0, GROUPS)
+    def _(group):
+        summed = kept[:, rows_of(group), :] + got[:, rows_of(group), :].astype(jnp.float32)
+        turn[...] = summed.astype(jnp.bfloat16).astype(jnp.float32).reshape(TILE * SUB, TILE)
+        changed = []
+        for first in range(0, SUB, CHUNK):
+            before = state[group, :, first * TILE : (first + CHUNK) * TILE].astype(jnp.float32)
+            gate_value = jnp.tanh(product(gate[...], norm_channels(before, gain1, bias1)))
+            out = product(proj[...], norm_channels(chunk_of(turn, first), gain_out, bias_out))
+            changed.append((before + (out * gate_value + out)).astype(jnp.bfloat16))
+        result[rows_of(group)] = jnp.concatenate([chunk.T for chunk in changed], axis=0).reshape(
+            SUB, TILE, TILE
+        )
 
 
 def leave(at, kept, got, states, *fixed):
+    blocks = BLOCKS // GROUPS
     square = pl.BlockSpec((TILE, TILE), lambda block, at: (0, 0))
-    tri = pl.BlockSpec((TILE, SUB, TILE), lambda block, at: (0, block, 0))
+    tri = pl.BlockSpec((TILE, GROUPS * SUB, TILE), lambda block, at: (0, block, 0))
     return pl.pallas_call(
         leave_kernel,
         grid_spec=pltpu.PrefetchScalarGridSpec(
             num_scalar_prefetch=1,
-            grid=(BLOCKS,),
+            grid=(blocks,),
             in_specs=[
                 tri,
                 tri,
-                pl.BlockSpec((1, TILE, SUB * TILE), lambda block, at: (at[1] * BLOCKS + block, 0, 0)),
+                pl.BlockSpec((GROUPS, TILE, SUB * TILE), lambda block, at: (at[1] * blocks + block, 0, 0)),
             ]
             + [square] * 6,
-            out_specs=pl.BlockSpec((SUB, TILE, TILE), lambda block, at: (block, 0, 0)),
+            out_specs=pl.BlockSpec((GROUPS * SUB, TILE, TILE), lambda block, at: (block, 0, 0)),
             scratch_shapes=[pltpu.VMEM((TILE * SUB, TILE), jnp.float32)],
         ),
         out_shape=jax.ShapeDtypeStruct((TILE, TILE, TILE), jnp.bfloat16),
@@ -493,7 +527,7 @@
                 last,
                 (there_x == x).astype(jnp.int32),
                 (last == core).astype(jnp.int32),
-                jnp.where(slot < 0, -1, (3 * there_x + slot) * BLOCKS),
+                jnp.where(slot < 0, -1, 3 * there_x + slot),
             ]
         ).astype(jnp.int32)
         fixed = (both, gain_in[0], bias_in[0], enter_weights)
@@ -540,7 +574,7 @@
             held = project(held, offset, tile, lax.ppermute(tile, BOTH, swap), mask, 0)
     below, above, held = lax.optimization_barrier((below, above, held))
     held = project(held, 4, below[1], lax.ppermute(below[1], BOTH, swap), below[0], 0)
-    held = project(held, 4, above[0], lax.ppermute(above[0], BOTH, swap), below[0], part // SUB)
+    held = project(held, 4, above[0], lax.ppermute(above[0], BOTH, swap), below[0], part // (GROUPS * SUB))
     states, *lefts, right, mask = held
 
     third = jnp.where(z // 2 == x, lax.rem(z, 2), 2)

time: 603 us -> 594 us (0.985)
  Pallas kernels: 393 us -> 346 us
  waiting for transfers between devices: 162 us -> 200 us
    pallas_call x9, Pallas kernels: 205 us -> 156 us  [enter(): pl.pallas_call(enter_kernel, grid_spec=pltpu.PrefetchScalarGridSpec(num_s...]
    ppermute x15, waiting for transfers between devices: 128 us -> 166 us  [hop(): return [lax.ppermute(value, BOTH, pairs) for value in values]]
  transfers between devices with their start and end apart: 30 -> 30, of which waited for: 13 -> 14; matrix products, arithmetic and copies ran while one was open for 3% -> 3% of each run, Pallas kernels for 33% -> 26%
where the time goes in v4:
time: 594 us; the launch traced here: 592 us
  Pallas kernels  346 us (58%)
  waiting for transfers between devices  200 us (34%)
  local copies, waits for them, and re-layouts  21.8 us (4%)
  starting transfers between devices  20.6 us (3%)
    ppermute x15, waiting for transfers between devices, hop(): return [lax.ppermute(value, BOTH, pairs) for value in values]  166 us
    pallas_call x9, Pallas kernels, enter(): pl.pallas_call(enter_kernel, grid_spec=pltpu.PrefetchScalarGridSpec(num_s...  156 us
    pallas_call x1, Pallas kernels, middle(): pl.pallas_call(middle_kernel, grid_spec=pltpu.PrefetchScalarGridSpec(num_...  115 us
    pallas_call x4, Pallas kernels, outgoing(): pl.pallas_call(outgoing_kernel, grid_spec=pltpu.PrefetchScalarGridSpec(nu...  42.4 us
    pallas_call x1, Pallas kernels, incoming(): pl.pallas_call(incoming_kernel, grid_spec=pltpu.PrefetchScalarGridSpec(nu...  17 us
    pallas_call x1, Pallas kernels, leave(): pl.pallas_call(leave_kernel, grid_spec=pltpu.PrefetchScalarGridSpec(num_s...  16.4 us
    ppermute x15, starting transfers between devices, hop(): return [lax.ppermute(value, BOTH, pairs) for value in values]  16.2 us
    ppermute x4, waiting for transfers between devices, on_device_ring(): got.append(lax.ppermute(leaves, BOTH, swap))  14.9 us
  transfers between devices with their start and end apart: 30, of which 14 were waited for; matrix products, arithmetic and copies ran while one was open for 3% of the time, Pallas kernels for 26%

profile of v4, /device:TPU:0, one launch (start us, length us, event | category | flops | bytes accessed | tf_op | source)
XLA Modules:
  0.0 592.2 jit_solution(5996758058282866828)
XLA Ops:
  0.5 2.6 collective-permute-start.2
  3.0 0.8 convert_element_type.6
  4.1 0.9 fusion.10
  5.0 0.9 fusion.11
  13.5 0.8 convert_bitcast_fusion
  14.6 1.9 collective-permute-start.1
  16.8 2.2 copy-done.6
  19.0 18.6 %enter.9 = (bf16[50,128,2048]{2,1,0:T(8,128)(2,1)}, bf16[4,32,512,128]{3,2,1,0:T(8,128)(2,1)}, bf16[4,32,512,128]{3,2,1,0:T(8,128)(2,1)}, bf16[4,64,384,128]{3,2,1,0:T(8,128)(2,1)}, bf16[4,4,128,128]{3,2,1,0:T(8,128)(2,1)S(1)}) custom-call(s32[6]{0:T(128)S(1)} %stack.240.at, bf16[128,128,128]{2,1,0:T(8,128)(2,1)S(1)} %copy-done.6, ...), custom_call_target="tpu_custom_call" | custom-call | flops 4294967296 | bytes 33554432 | tf_op jit(solution)/shard_map/enter/pallas_call | solution.py:206
  37.7 58.1 %collective-permute-done.1.mask = bf16[2,128,128]{2,1,0:T(8,128)(2,1)S(1)} collective-permute-done((bf16[2,128,128]{2,1,0:T(8,128)(2,1)S(1)}, bf16[2,128,128]{2,1,0:T(8,128)(2,1)S(1)}, u32[]{:S(2)}, u32[]{:S(2)}) %collective-permute-start.1) | collective-permute-done | bytes 65568 | tf_op jit(solution)/shard_map/ppermute | solution.py:537
  95.8 1.5 collective-permute-done.3.mask
  98.4 1.6 collective-permute-start.7
  100.6 1.6 collective-permute-start.6
  102.2 3.2 collective-permute-done.11.sib
  105.7 19.1 %enter.10 = (bf16[50,128,2048]{2,1,0:T(8,128)(2,1)}, bf16[4,32,512,128]{3,2,1,0:T(8,128)(2,1)}, bf16[4,32,512,128]{3,2,1,0:T(8,128)(2,1)}, bf16[4,64,384,128]{3,2,1,0:T(8,128)(2,1)}, bf16[4,4,128,128]{3,2,1,0:T(8,128)(2,1)S(1)}) custom-call(s32[6]{0:T(128)S(1)} %stack.255.at, ...), custom_call_target="tpu_custom_call", output_to_operand_aliasing={{0}: (8, {}), {1}: (9, {}), {2}: (10, {}), {3}: (11, {}), {... | custom-call | flops 4294967296 | bytes 33554432 | tf_op jit(solution)/shard_map/enter/pallas_call | solution.py:206
  124.8 19.1 %enter.11 = (bf16[50,128,2048]{2,1,0:T(8,128)(2,1)}, bf16[4,32,512,128]{3,2,1,0:T(8,128)(2,1)}, bf16[4,32,512,128]{3,2,1,0:T(8,128)(2,1)}, bf16[4,64,384,128]{3,2,1,0:T(8,128)(2,1)}, bf16[4,4,128,128]{3,2,1,0:T(8,128)(2,1)S(1)}) custom-call(s32[6]{0:T(128)S(1)} %stack.249.at, ...), custom_call_target="tpu_custom_call", output_to_operand_aliasing={{0}: (8, {}), {1}: (9, {}), {2}: (10, {}), {3}: (11, {}), {... | custom-call | flops 4294967296 | bytes 33554432 | tf_op jit(solution)/shard_map/enter/pallas_call | solution.py:206
  144.0 48.6 %collective-permute-done.6.mask = bf16[2,128,128]{2,1,0:T(8,128)(2,1)S(1)} collective-permute-done((bf16[2,128,128]{2,1,0:T(8,128)(2,1)S(1)}, bf16[2,128,128]{2,1,0:T(8,128)(2,1)S(1)}, u32[]{:S(2)}, u32[]{:S(2)}) %collective-permute-start.6) | collective-permute-done | bytes 65568 | tf_op jit(solution)/shard_map/ppermute | solution.py:537
  192.6 1.3 collective-permute-done.8.mask
  194.4 1.6 collective-permute-start.13
  196.6 1.6 collective-permute-start.12
  198.2 3.2 collective-permute-done.17.sib
  201.8 19.1 %enter.12 = (bf16[50,128,2048]{2,1,0:T(8,128)(2,1)}, bf16[4,32,512,128]{3,2,1,0:T(8,128)(2,1)}, bf16[4,32,512,128]{3,2,1,0:T(8,128)(2,1)}, bf16[4,64,384,128]{3,2,1,0:T(8,128)(2,1)}, bf16[4,4,128,128]{3,2,1,0:T(8,128)(2,1)S(1)}) custom-call(s32[6]{0:T(128)S(1)} %stack.267.at, ...), custom_call_target="tpu_custom_call", output_to_operand_aliasing={{0}: (8, {}), {1}: (9, {}), {2}: (10, {}), {3}: (11, {}), {... | custom-call | flops 4294967296 | bytes 33554432 | tf_op jit(solution)/shard_map/enter/pallas_call | solution.py:206
  220.9 19.1 %enter.13 = (bf16[50,128,2048]{2,1,0:T(8,128)(2,1)}, bf16[4,32,512,128]{3,2,1,0:T(8,128)(2,1)}, bf16[4,32,512,128]{3,2,1,0:T(8,128)(2,1)}, bf16[4,64,384,128]{3,2,1,0:T(8,128)(2,1)}, bf16[4,4,128,128]{3,2,1,0:T(8,128)(2,1)S(1)}) custom-call(s32[6]{0:T(128)S(1)} %stack.261.at, ...), custom_call_target="tpu_custom_call", output_to_operand_aliasing={{0}: (8, {}), {1}: (9, {}), {2}: (10, {}), {3}: (11, {}), {... | custom-call | flops 4294967296 | bytes 33554432 | tf_op jit(solution)/shard_map/enter/pallas_call | solution.py:206
  240.1 48.5 %collective-permute-done.12.mask = bf16[2,128,128]{2,1,0:T(8,128)(2,1)S(1)} collective-permute-done((bf16[2,128,128]{2,1,0:T(8,128)(2,1)S(1)}, bf16[2,128,128]{2,1,0:T(8,128)(2,1)S(1)}, u32[]{:S(2)}, u32[]{:S(2)}) %collective-permute-start.12) | collective-permute-done | bytes 65568 | tf_op jit(solution)/shard_map/ppermute | solution.py:537
  288.6 1.3 collective-permute-done.14.mask
  290.4 3.2 slice.74
  293.6 3.2 slice.75
  296.8 1.5 collective-permute-start.19
  299.0 1.5 collective-permute-start.18
  300.5 0.9 copy-done.3
  301.3 19.1 %enter.14 = (bf16[50,128,2048]{2,1,0:T(8,128)(2,1)}, bf16[4,32,512,128]{3,2,1,0:T(8,128)(2,1)}, bf16[4,32,512,128]{3,2,1,0:T(8,128)(2,1)}, bf16[4,64,384,128]{3,2,1,0:T(8,128)(2,1)}, bf16[4,4,128,128]{3,2,1,0:T(8,128)(2,1)S(1)}) custom-call(s32[6]{0:T(128)S(1)} %stack.279.at, ...), custom_call_target="tpu_custom_call", output_to_operand_aliasing={{0}: (8, {}), {1}: (9, {}), {2}: (10, {}), {3}: (11, {}), {... | custom-call | flops 4294967296 | bytes 33554432 | tf_op jit(solution)/shard_map/enter/pallas_call | solution.py:206
  320.5 19.2 %enter.15 = (bf16[50,128,2048]{2,1,0:T(8,128)(2,1)}, bf16[4,32,512,128]{3,2,1,0:T(8,128)(2,1)}, bf16[4,32,512,128]{3,2,1,0:T(8,128)(2,1)}, bf16[4,64,384,128]{3,2,1,0:T(8,128)(2,1)}, bf16[4,4,128,128]{3,2,1,0:T(8,128)(2,1)S(1)}) custom-call(s32[6]{0:T(128)S(1)} %stack.273.at, ...), custom_call_target="tpu_custom_call", output_to_operand_aliasing={{0}: (8, {}), {1}: (9, {}), {2}: (10, {}), {3}: (11, {}), {... | custom-call | flops 4294967296 | bytes 33554432 | tf_op jit(solution)/shard_map/enter/pallas_call | solution.py:206
  339.6 6.4 %collective-permute-done.18.mask = bf16[2,128,128]{2,1,0:T(8,128)(2,1)S(1)} collective-permute-done((bf16[2,128,128]{2,1,0:T(8,128)(2,1)}, bf16[2,128,128]{2,1,0:T(8,128)(2,1)S(1)}, u32[]{:S(2)}, u32[]{:S(2)}) %collective-permute-start.18) | collective-permute-done | bytes 65568 | tf_op jit(solution)/shard_map/ppermute | solution.py:537
  346.7 6.1 %collective-permute-done.24.sib = bf16[64,128,128]{2,1,0:T(8,128)(2,1)} collective-permute-done((bf16[64,128,128]{2,1,0:T(8,128)(2,1)}, bf16[64,128,128]{2,1,0:T(8,128)(2,1)}, u32[]{:S(2)}, u32[]{:S(2)}) %collective-permute-start.24) | collective-permute-done | bytes 2097184 | tf_op jit(solution)/shard_map/ppermute | solution.py:576
  352.8 11.2 %enter.16 = (bf16[50,128,2048]{2,1,0:T(8,128)(2,1)}, bf16[4,32,512,128]{3,2,1,0:T(8,128)(2,1)}, bf16[4,32,512,128]{3,2,1,0:T(8,128)(2,1)}, bf16[4,64,384,128]{3,2,1,0:T(8,128)(2,1)}, bf16[4,4,128,128]{3,2,1,0:T(8,128)(2,1)S(1)}) custom-call(s32[6]{0:T(128)S(1)} %stack.230.at, ...), custom_call_target="tpu_custom_call", output_to_operand_aliasing={{0}: (8, {}), {1}: (9, {}), {2}: (10, {}), {3}: (11, {}), {... | custom-call | flops 2147483648 | bytes 16777216 | tf_op jit(solution)/shard_map/enter/pallas_call | solution.py:206
  364.0 10.9 %enter.17 = (bf16[50,128,2048]{2,1,0:T(8,128)(2,1)}, bf16[4,32,512,128]{3,2,1,0:T(8,128)(2,1)}, bf16[4,32,512,128]{3,2,1,0:T(8,128)(2,1)}, bf16[4,64,384,128]{3,2,1,0:T(8,128)(2,1)}, bf16[4,4,128,128]{3,2,1,0:T(8,128)(2,1)S(1)}) custom-call(s32[6]{0:T(128)S(1)} %stack.230.at, ...), custom_call_target="tpu_custom_call", output_to_operand_aliasing={{0}: (8, {}), {1}: (9, {}), {2}: (10, {}), {3}: (11, {}), {... | custom-call | flops 2147483648 | bytes 16777216 | tf_op jit(solution)/shard_map/enter/pallas_call | solution.py:206
  374.9 10.6 %outgoing.4 = (bf16[3,16,256,128]{3,2,1,0:T(8,128)(2,1)S(1)}, bf16[3,16,256,128]{3,2,1,0:T(8,128)(2,1)S(1)}) custom-call(s32[2]{0:T(128)S(1)} %pad_add_fusion.1.at, bf16[4,32,512,128]{3,2,1,0:T(8,128)(2,1)} %get-tuple-element.262.left, bf16[4,64,384,128]{3,2,1,0:T(8,128)(2,1)} %get-tuple-element.263.right), custom_call_target="tpu_custom_call" | custom-call | flops 3221225472 | bytes 21299200 | tf_op jit(solution)/shard_map/outgoing/pallas_call | solution.py:266
  385.7 10.6 %outgoing.5 = (bf16[3,16,256,128]{3,2,1,0:T(8,128)(2,1)S(1)}, bf16[3,16,256,128]{3,2,1,0:T(8,128)(2,1)S(1)}) custom-call(s32[2]{0:T(128)S(1)} %pad_add_fusion.1.at, bf16[4,32,512,128]{3,2,1,0:T(8,128)(2,1)} %get-tuple-element.262.left, bf16[4,64,384,128]{3,2,1,0:T(8,128)(2,1)} %get-tuple-element.263.right), custom_call_target="tpu_custom_call" | custom-call | flops 3221225472 | bytes 21299200 | tf_op jit(solution)/shard_map/outgoing/pallas_call | solution.py:266
  396.7 5.3 collective-permute-done.26.rest_5_
  402.0 1.6 copy-done.8
  403.7 10.6 %outgoing.6 = (bf16[3,16,256,128]{3,2,1,0:T(8,128)(2,1)S(1)}, bf16[3,16,256,128]{3,2,1,0:T(8,128)(2,1)S(1)}) custom-call(s32[2]{0:T(128)S(1)} %pad_add_fusion.1.at, bf16[4,32,512,128]{3,2,1,0:T(8,128)(2,1)} %get-tuple-element.268.left, bf16[4,64,384,128]{3,2,1,0:T(8,128)(2,1)} %get-tuple-element.263.right), custom_call_target="tpu_custom_call" | custom-call | flops 3221225472 | bytes 21299200 | tf_op jit(solution)/shard_map/outgoing/pallas_call | solution.py:266
  414.3 10.6 %outgoing.7 = (bf16[3,16,256,128]{3,2,1,0:T(8,128)(2,1)S(1)}, bf16[3,16,256,128]{3,2,1,0:T(8,128)(2,1)S(1)}) custom-call(s32[2]{0:T(128)S(1)} %pad_add_fusion.1.at, bf16[4,32,512,128]{3,2,1,0:T(8,128)(2,1)} %get-tuple-element.268.left, bf16[4,64,384,128]{3,2,1,0:T(8,128)(2,1)} %get-tuple-element.263.right), custom_call_target="tpu_custom_call" | custom-call | flops 3221225472 | bytes 21299200 | tf_op jit(solution)/shard_map/outgoing/pallas_call | solution.py:266
  425.6 5.1 collective-permute-done.28.rest_7_
  430.7 4.5 collective-permute-done.27.rest_6_
  435.2 1.6 copy-done.10
  436.8 114.7 %middle.1 = (bf16[3,128,256,128]{3,2,1,0:T(8,128)(2,1)}, bf16[20,128,2048]{2,1,0:T(8,128)(2,1)}) custom-call(s32[4]{0:T(128)S(1)} %pad_add_fusion.at, bf16[50,128,2048]{2,1,0:T(8,128)(2,1)} %get-tuple-element.251.state, bf16[4,4,128,128]{3,2,1,0:T(8,128)(2,1)S(1)} %get-tuple-element.252.mask, f32[128,128]{1,0:T(8,128)S(1)} %broadcast_in_dim.55.gain.gain0, ...), custom_call_target="tpu_custom_call" | custom-call | flops 12884901888 | bytes 100663296 | tf_op jit(solution)/shard_map/middle/pallas_call | solution.py:330
  551.5 17.0 %incoming.1 = (f32[128,128,128]{2,1,0:T(8,128)S(1)}, bf16[128,128,128]{2,1,0:T(8,128)(2,1)S(1)}) custom-call(s32[4]{0:T(128)S(1)} %pad_add_fusion.at, bf16[3,128,256,128]{3,2,1,0:T(8,128)(2,1)} %get-tuple-element.277.pairs), custom_call_target="tpu_custom_call" | custom-call | flops 2147483648 | bytes 37748736 | tf_op jit(solution)/shard_map/incoming/pallas_call | solution.py:392
  569.0 6.8 %collective-permute-done.29.got = bf16[128,128,128]{2,1,0:T(8,128)(2,1)S(1)} collective-permute-done((bf16[128,128,128]{2,1,0:T(8,128)(2,1)S(1)}, bf16[128,128,128]{2,1,0:T(8,128)(2,1)S(1)}, u32[]{:S(2)}, u32[]{:S(2)}) %collective-permute-start.29) | collective-permute-done | bytes 4194336 | tf_op jit(solution)/shard_map/ppermute | solution.py:593
  575.8 16.4 %leave.1 = bf16[128,128,128]{2,1,0:T(8,128)(2,1)} custom-call(s32[4]{0:T(128)S(1)} %pad_add_fusion.at, f32[128,128,128]{2,1,0:T(8,128)S(1)} %get-tuple-element.278.kept, bf16[128,128,128]{2,1,0:T(8,128)(2,1)S(1)} %collective-permute-done.29.got, bf16[20,128,2048]{2,1,0:T(8,128)(2,1)} %get-tuple-element.280.state, f32[128,128]{1,0:T(8,128)S(1)} %broadcast_in_dim.61.gain1, ...), custom_call_target="tpu_custom_call" | custom-call | flops 1073741824 | bytes 20971520 | tf_op jit(solution)/shard_map/leave/pallas_call | solution.py:434
  (112 shorter events, 15.9 us)
Async XLA Ops:
  0.0 16.7 %collective-permute-start.5 = (bf16[128,128,128]{2,1,0:T(8,128)(2,1)}, bf16[128,128,128]{2,1,0:T(8,128)(2,1)}, u32[]{:S(2)}, u32[]{:S(2)}) collective-permute-start(bf16[128,128,128]{2,1,0:T(8,128)(2,1)} %own.1), channel_id=1, source_target_pairs={{0,4},{4,0},{1,5},{5,1},{2,6},{6,2},{3,7},{7,3},{11,15},{15,11},{1... | collective-permute-start | bytes 12582920 | tf_op jit(solution)/shard_map/ppermute | solution.py:539
  0.5 96.9 %collective-permute-start.2 = (bf16[128,128,128]{2,1,0:T(8,128)(2,1)}, bf16[128,128,128]{2,1,0:T(8,128)(2,1)}, u32[]{:S(2)}, u32[]{:S(2)}) collective-permute-start(bf16[128,128,128]{2,1,0:T(8,128)(2,1)} %own.1), channel_id=1, source_target_pairs={{0,1},{4,5},{1,2},{5,6},{2,3},{6,7},{3,11},{7,15},{11,10},{15,14},... | collective-permute-start | bytes 12582920 | tf_op jit(solution)/shard_map/ppermute | solution.py:537
  3.0 94.3 %collective-permute-start.4 = (bf16[128,128,128]{2,1,0:T(8,128)(2,1)}, bf16[128,128,128]{2,1,0:T(8,128)(2,1)}, u32[]{:S(2)}, u32[]{:S(2)}) collective-permute-start(bf16[128,128,128]{2,1,0:T(8,128)(2,1)} %own.1), channel_id=1, source_target_pairs={{1,0},{5,4},{2,1},{6,5},{3,2},{7,6},{11,3},{15,7},{10,11},{14,15},... | collective-permute-start | bytes 12582920 | tf_op jit(solution)/shard_map/ppermute | solution.py:537
  3.9 10.7 %collective-permute-start = (bf16[128,128]{1,0:T(8,128)(2,1)S(1)}, bf16[128,128]{1,0:T(8,128)(2,1)S(1)}, u32[]{:S(2)}, u32[]{:S(2)}) collective-permute-start(bf16[128,128]{1,0:T(8,128)(2,1)S(1)} %convert_element_type.6), channel_id=1, source_target_pairs={{0,4},{4,0},{1,5},{5,1},{2,6},{6,2},{3,7},{7,3},{11,15},{15,11},{1... | collective-permute-start | bytes 98312 | tf_op jit(solution)/shard_map/ppermute | solution.py:485
  14.6 81.2 %collective-permute-start.1 = (bf16[2,128,128]{2,1,0:T(8,128)(2,1)S(1)}, bf16[2,128,128]{2,1,0:T(8,128)(2,1)S(1)}, u32[]{:S(2)}, u32[]{:S(2)}) collective-permute-start(bf16[2,128,128]{2,1,0:T(8,128)(2,1)S(1)} %maximum_select_fusion.mask), channel_id=1, source_target_pairs={{0,1},{4,5},{1,2},{5,6},{2,3},{6,7},{3,11},{7,15},{11,10},{15,14},... | collective-permute-start | bytes 196616 | tf_op jit(solution)/shard_map/ppermute | solution.py:537
  16.5 80.9 %collective-permute-start.3 = (bf16[2,128,128]{2,1,0:T(8,128)(2,1)S(1)}, bf16[2,128,128]{2,1,0:T(8,128)(2,1)S(1)}, u32[]{:S(2)}, u32[]{:S(2)}) collective-permute-start(bf16[2,128,128]{2,1,0:T(8,128)(2,1)S(1)} %maximum_select_fusion.mask), channel_id=1, source_target_pairs={{1,0},{5,4},{2,1},{6,5},{3,2},{7,6},{11,3},{15,7},{10,11},{14,15},... | collective-permute-start | bytes 196616 | tf_op jit(solution)/shard_map/ppermute | solution.py:537
  16.8 2.2 copy-start.6
  97.8 7.5 %collective-permute-start.11 = (bf16[128,128,128]{2,1,0:T(8,128)(2,1)}, bf16[128,128,128]{2,1,0:T(8,128)(2,1)}, u32[]{:S(2)}, u32[]{:S(2)}) collective-permute-start(bf16[128,128,128]{2,1,0:T(8,128)(2,1)} %collective-permute-done.2.own), channel_id=1, source_target_pairs={{0,4},{4,0},{1,5},{5,1},{2,6},{6,2},{3,7},{7,3},{11,15},{15,11},{1... | collective-permute-start | bytes 12582920 | tf_op jit(solution)/shard_map/ppermute | solution.py:574
  97.9 26.9 %collective-permute-start.10 = (bf16[128,128,128]{2,1,0:T(8,128)(2,1)}, bf16[128,128,128]{2,1,0:T(8,128)(2,1)}, u32[]{:S(2)}, u32[]{:S(2)}) collective-permute-start(bf16[128,128,128]{2,1,0:T(8,128)(2,1)} %collective-permute-done.4.own), channel_id=1, source_target_pairs={{0,4},{4,0},{1,5},{5,1},{2,6},{6,2},{3,7},{7,3},{11,15},{15,11},{1... | collective-permute-start | bytes 12582920 | tf_op jit(solution)/shard_map/ppermute | solution.py:574
  98.4 95.5 %collective-permute-start.7 = (bf16[128,128,128]{2,1,0:T(8,128)(2,1)}, bf16[128,128,128]{2,1,0:T(8,128)(2,1)}, u32[]{:S(2)}, u32[]{:S(2)}) collective-permute-start(bf16[128,128,128]{2,1,0:T(8,128)(2,1)} %collective-permute-done.2.own), channel_id=1, source_target_pairs={{0,1},{4,5},{1,2},{5,6},{2,3},{6,7},{3,11},{7,15},{11,10},{15,14},... | collective-permute-start | bytes 12582920 | tf_op jit(solution)/shard_map/ppermute | solution.py:537
  100.0 93.9 %collective-permute-start.9 = (bf16[128,128,128]{2,1,0:T(8,128)(2,1)}, bf16[128,128,128]{2,1,0:T(8,128)(2,1)}, u32[]{:S(2)}, u32[]{:S(2)}) collective-permute-start(bf16[128,128,128]{2,1,0:T(8,128)(2,1)} %collective-permute-done.4.own), channel_id=1, source_target_pairs={{1,0},{5,4},{2,1},{6,5},{3,2},{7,6},{11,3},{15,7},{10,11},{14,15},... | collective-permute-start | bytes 12582920 | tf_op jit(solution)/shard_map/ppermute | solution.py:537
  100.6 92.0 %collective-permute-start.6 = (bf16[2,128,128]{2,1,0:T(8,128)(2,1)S(1)}, bf16[2,128,128]{2,1,0:T(8,128)(2,1)S(1)}, u32[]{:S(2)}, u32[]{:S(2)}) collective-permute-start(bf16[2,128,128]{2,1,0:T(8,128)(2,1)S(1)} %collective-permute-done.1.mask), channel_id=1, source_target_pairs={{0,1},{4,5},{1,2},{5,6},{2,3},{6,7},{3,11},{7,15},{11,10},{15,14},... | collective-permute-start | bytes 196616 | tf_op jit(solution)/shard_map/ppermute | solution.py:537
  105.4 88.5 %collective-permute-start.8 = (bf16[2,128,128]{2,1,0:T(8,128)(2,1)S(1)}, bf16[2,128,128]{2,1,0:T(8,128)(2,1)S(1)}, u32[]{:S(2)}, u32[]{:S(2)}) collective-permute-start(bf16[2,128,128]{2,1,0:T(8,128)(2,1)S(1)} %collective-permute-done.3.mask), channel_id=1, source_target_pairs={{1,0},{5,4},{2,1},{6,5},{3,2},{7,6},{11,3},{15,7},{10,11},{14,15},... | collective-permute-start | bytes 196616 | tf_op jit(solution)/shard_map/ppermute | solution.py:537
  193.9 7.5 %collective-permute-start.17 = (bf16[128,128,128]{2,1,0:T(8,128)(2,1)}, bf16[128,128,128]{2,1,0:T(8,128)(2,1)}, u32[]{:S(2)}, u32[]{:S(2)}) collective-permute-start(bf16[128,128,128]{2,1,0:T(8,128)(2,1)} %collective-permute-done.7.own), channel_id=1, source_target_pairs={{0,4},{4,0},{1,5},{5,1},{2,6},{6,2},{3,7},{7,3},{11,15},{15,11},{1... | collective-permute-start | bytes 12582920 | tf_op jit(solution)/shard_map/ppermute | solution.py:574
  193.9 27.0 %collective-permute-start.16 = (bf16[128,128,128]{2,1,0:T(8,128)(2,1)}, bf16[128,128,128]{2,1,0:T(8,128)(2,1)}, u32[]{:S(2)}, u32[]{:S(2)}) collective-permute-start(bf16[128,128,128]{2,1,0:T(8,128)(2,1)} %collective-permute-done.9.own), channel_id=1, source_target_pairs={{0,4},{4,0},{1,5},{5,1},{2,6},{6,2},{3,7},{7,3},{11,15},{15,11},{1... | collective-permute-start | bytes 12582920 | tf_op jit(solution)/shard_map/ppermute | solution.py:574
  194.4 95.5 %collective-permute-start.13 = (bf16[128,128,128]{2,1,0:T(8,128)(2,1)}, bf16[128,128,128]{2,1,0:T(8,128)(2,1)}, u32[]{:S(2)}, u32[]{:S(2)}) collective-permute-start(bf16[128,128,128]{2,1,0:T(8,128)(2,1)} %collective-permute-done.7.own), channel_id=1, source_target_pairs={{0,1},{4,5},{1,2},{5,6},{2,3},{6,7},{3,11},{7,15},{11,10},{15,14},... | collective-permute-start | bytes 12582920 | tf_op jit(solution)/shard_map/ppermute | solution.py:537
  196.0 93.9 %collective-permute-start.15 = (bf16[128,128,128]{2,1,0:T(8,128)(2,1)}, bf16[128,128,128]{2,1,0:T(8,128)(2,1)}, u32[]{:S(2)}, u32[]{:S(2)}) collective-permute-start(bf16[128,128,128]{2,1,0:T(8,128)(2,1)} %collective-permute-done.9.own), channel_id=1, source_target_pairs={{1,0},{5,4},{2,1},{6,5},{3,2},{7,6},{11,3},{15,7},{10,11},{14,15},... | collective-permute-start | bytes 12582920 | tf_op jit(solution)/shard_map/ppermute | solution.py:537
  196.6 92.0 %collective-permute-start.12 = (bf16[2,128,128]{2,1,0:T(8,128)(2,1)S(1)}, bf16[2,128,128]{2,1,0:T(8,128)(2,1)S(1)}, u32[]{:S(2)}, u32[]{:S(2)}) collective-permute-start(bf16[2,128,128]{2,1,0:T(8,128)(2,1)S(1)} %collective-permute-done.6.mask), channel_id=1, source_target_pairs={{0,1},{4,5},{1,2},{5,6},{2,3},{6,7},{3,11},{7,15},{11,10},{15,14},... | collective-permute-start | bytes 196616 | tf_op jit(solution)/shard_map/ppermute | solution.py:537
  201.4 88.5 %collective-permute-start.14 = (bf16[2,128,128]{2,1,0:T(8,128)(2,1)S(1)}, bf16[2,128,128]{2,1,0:T(8,128)(2,1)S(1)}, u32[]{:S(2)}, u32[]{:S(2)}) collective-permute-start(bf16[2,128,128]{2,1,0:T(8,128)(2,1)S(1)} %collective-permute-done.8.mask), channel_id=1, source_target_pairs={{1,0},{5,4},{2,1},{6,5},{3,2},{7,6},{11,3},{15,7},{10,11},{14,15},... | collective-permute-start | bytes 196616 | tf_op jit(solution)/shard_map/ppermute | solution.py:537
  288.6 8.2 %copy-start.2 = (bf16[2,128,128]{2,1,0:T(8,128)(2,1)}, bf16[2,128,128]{2,1,0:T(8,128)(2,1)S(1)}, u32[]{:S(2)}) copy-start(bf16[2,128,128]{2,1,0:T(8,128)(2,1)S(1)} %collective-permute-done.12.mask) | copy-start | bytes 196612
  289.9 8.4 %copy-start.4 = (bf16[2,128,128]{2,1,0:T(8,128)(2,1)}, bf16[2,128,128]{2,1,0:T(8,128)(2,1)S(1)}, u32[]{:S(2)}) copy-start(bf16[2,128,128]{2,1,0:T(8,128)(2,1)S(1)} %collective-permute-done.14.mask) | copy-start | bytes 196612
  289.9 10.6 %collective-permute-start.22 = (bf16[128,128,128]{2,1,0:T(8,128)(2,1)}, bf16[128,128,128]{2,1,0:T(8,128)(2,1)}, u32[]{:S(2)}, u32[]{:S(2)}) collective-permute-start(bf16[128,128,128]{2,1,0:T(8,128)(2,1)} %collective-permute-done.13.own), channel_id=1, source_target_pairs={{0,4},{4,0},{1,5},{5,1},{2,6},{6,2},{3,7},{7,3},{11,15},{15,11},{1... | collective-permute-start | bytes 12582920 | tf_op jit(solution)/shard_map/ppermute | solution.py:574
  289.9 30.5 %collective-permute-start.21 = (bf16[128,128,128]{2,1,0:T(8,128)(2,1)}, bf16[128,128,128]{2,1,0:T(8,128)(2,1)}, u32[]{:S(2)}, u32[]{:S(2)}) collective-permute-start(bf16[128,128,128]{2,1,0:T(8,128)(2,1)} %collective-permute-done.15.own), channel_id=1, source_target_pairs={{0,4},{4,0},{1,5},{5,1},{2,6},{6,2},{3,7},{7,3},{11,15},{15,11},{1... | collective-permute-start | bytes 12582920 | tf_op jit(solution)/shard_map/ppermute | solution.py:574
  296.8 49.2 %collective-permute-start.19 = (bf16[64,128,128]{2,1,0:T(8,128)(2,1)}, bf16[64,128,128]{2,1,0:T(8,128)(2,1)}, u32[]{:S(2)}, u32[]{:S(2)}) collective-permute-start(bf16[64,128,128]{2,1,0:T(8,128)(2,1)} %slice.74), channel_id=1, source_target_pairs={{0,1},{4,5},{1,2},{5,6},{2,3},{6,7},{3,11},{7,15},{11,10},{15,14},... | collective-permute-start | bytes 6291464 | tf_op jit(solution)/shard_map/ppermute | solution.py:537
  298.3 47.7 %collective-permute-start.20 = (bf16[64,128,128]{2,1,0:T(8,128)(2,1)}, bf16[64,128,128]{2,1,0:T(8,128)(2,1)S(1)}, u32[]{:S(2)}, u32[]{:S(2)}) collective-permute-start(bf16[64,128,128]{2,1,0:T(8,128)(2,1)} %slice.75), channel_id=1, source_target_pairs={{1,0},{5,4},{2,1},{6,5},{3,2},{7,6},{11,3},{15,7},{10,11},{14,15},... | collective-permute-start | bytes 6291464 | tf_op jit(solution)/shard_map/ppermute | solution.py:537
  299.0 47.0 %collective-permute-start.18 = (bf16[2,128,128]{2,1,0:T(8,128)(2,1)}, bf16[2,128,128]{2,1,0:T(8,128)(2,1)S(1)}, u32[]{:S(2)}, u32[]{:S(2)}) collective-permute-start(bf16[2,128,128]{2,1,0:T(8,128)(2,1)} %copy-done.2), channel_id=1, source_target_pairs={{0,1},{4,5},{1,2},{5,6},{2,3},{6,7},{3,11},{7,15},{11,10},{15,14},... | collective-permute-start | bytes 196616 | tf_op jit(solution)/shard_map/ppermute | solution.py:537
  300.5 0.9 copy-start.3
  301.3 19.1 %copy-start.5 = (bf16[2,128,128]{2,1,0:T(8,128)(2,1)S(1)}, bf16[2,128,128]{2,1,0:T(8,128)(2,1)}, u32[]{:S(2)}) copy-start(bf16[2,128,128]{2,1,0:T(8,128)(2,1)} %copy-done.4) | copy-start | bytes 196612
  346.0 6.8 %collective-permute-start.24 = (bf16[64,128,128]{2,1,0:T(8,128)(2,1)}, bf16[64,128,128]{2,1,0:T(8,128)(2,1)}, u32[]{:S(2)}, u32[]{:S(2)}) collective-permute-start(bf16[64,128,128]{2,1,0:T(8,128)(2,1)} %collective-permute-done.19.own), channel_id=1, source_target_pairs={{0,4},{4,0},{1,5},{5,1},{2,6},{6,2},{3,7},{7,3},{11,15},{15,11},{1... | collective-permute-start | bytes 6291464 | tf_op jit(solution)/shard_map/ppermute | solution.py:576
  346.0 18.0 %collective-permute-start.23 = (bf16[64,128,128]{2,1,0:T(8,128)(2,1)S(1)}, bf16[64,128,128]{2,1,0:T(8,128)(2,1)}, u32[]{:S(2)}, u32[]{:S(2)}) collective-permute-start(bf16[64,128,128]{2,1,0:T(8,128)(2,1)S(1)} %collective-permute-done.20.own), channel_id=1, source_target_pairs={{0,4},{4,0},{1,5},{5,1},{2,6},{6,2},{3,7},{7,3},{11,15},{15,11},{1... | collective-permute-start | bytes 6291464 | tf_op jit(solution)/shard_map/ppermute | solution.py:577
  385.5 11.2 %collective-permute-start.25 = (bf16[3,16,256,128]{3,2,1,0:T(8,128)(2,1)S(1)}, bf16[3,16,256,128]{3,2,1,0:T(8,128)(2,1)S(1)}, u32[]{:S(2)}, u32[]{:S(2)}) collective-permute-start(bf16[3,16,256,128]{3,2,1,0:T(8,128)(2,1)S(1)} %get-tuple-element.266), channel_id=1, source_target_pairs={{0,4},{4,0},{1,5},{5,1},{2,6},{6,2},{3,7},{7,3},{11,15},{15,11},{1... | collective-permute-start | bytes 9437192 | tf_op jit(solution)/shard_map/ppermute | solution.py:588
  396.3 5.7 collective-permute-start.26
  396.7 17.5 %copy-start.7 = (bf16[3,16,256,128]{3,2,1,0:T(8,128)(2,1)}, bf16[3,16,256,128]{3,2,1,0:T(8,128)(2,1)S(1)}, u32[]{:S(2)}) copy-start(bf16[3,16,256,128]{3,2,1,0:T(8,128)(2,1)S(1)} %collective-permute-done.25.rest_4_) | copy-start | bytes 9437188
  402.0 1.6 copy-start.8
  414.3 22.5 %copy-start = (bf16[128,128]{1,0:T(8,128)(2,1)S(1)}, bf16[128,128]{1,0:T(8,128)(2,1)}, u32[]{:S(2)}) copy-start(bf16[128,128]{1,0:T(8,128)(2,1)} %fusion.5.proj) | copy-start | bytes 98308
  414.3 22.5 %copy-start.1 = (bf16[128,128]{1,0:T(8,128)(2,1)S(1)}, bf16[128,128]{1,0:T(8,128)(2,1)}, u32[]{:S(2)}) copy-start(bf16[128,128]{1,0:T(8,128)(2,1)} %multiply_bitcast_fusion.2.gate) | copy-start | bytes 98308
  425.0 5.7 collective-permute-start.28
  425.4 9.8 %collective-permute-start.27 = (bf16[3,16,256,128]{3,2,1,0:T(8,128)(2,1)S(1)}, bf16[3,16,256,128]{3,2,1,0:T(8,128)(2,1)S(1)}, u32[]{:S(2)}, u32[]{:S(2)}) collective-permute-start(bf16[3,16,256,128]{3,2,1,0:T(8,128)(2,1)S(1)} %get-tuple-element.275), channel_id=1, source_target_pairs={{0,4},{4,0},{1,5},{5,1},{2,6},{6,2},{3,7},{7,3},{11,15},{15,11},{1... | collective-permute-start | bytes 9437192 | tf_op jit(solution)/shard_map/ppermute | solution.py:588
  430.7 6.1 %copy-start.9 = (bf16[3,16,256,128]{3,2,1,0:T(8,128)(2,1)}, bf16[3,16,256,128]{3,2,1,0:T(8,128)(2,1)S(1)}, u32[]{:S(2)}) copy-start(bf16[3,16,256,128]{3,2,1,0:T(8,128)(2,1)S(1)} %collective-permute-done.28.rest_7_) | copy-start | bytes 9437188
  435.2 1.6 copy-start.10
  568.6 7.2 %collective-permute-start.29 = (bf16[128,128,128]{2,1,0:T(8,128)(2,1)S(1)}, bf16[128,128,128]{2,1,0:T(8,128)(2,1)S(1)}, u32[]{:S(2)}, u32[]{:S(2)}) collective-permute-start(bf16[128,128,128]{2,1,0:T(8,128)(2,1)S(1)} %get-tuple-element.279), channel_id=1, source_target_pairs={{0,4},{4,0},{1,5},{5,1},{2,6},{6,2},{3,7},{7,3},{11,15},{15,11},{1... | collective-permute-start | bytes 12582920 | tf_op jit(solution)/shard_map/ppermute | solution.py:593

commit v5 on v4

--- a/solution.py
+++ b/solution.py
@@ -55,6 +55,7 @@
 SUB = 16
 BLOCKS = TILE // SUB
 CHUNK = 2
+PITCH = SUB + 1
 GROUPS = 2
 MIDDLE_GROUPS = 4
 VMEM_LIMIT = 40 * 1024 * 1024
@@ -92,15 +93,20 @@
     count = chunks[0].shape[0]
     for r in range(SUB):
         lanes = slice(r % CHUNK * TILE, (r % CHUNK + 1) * TILE)
-        turn[pl.ds(r, count, stride=SUB), :] = chunks[r // CHUNK][:, lanes] * mask_rows[r : r + 1, :]
+        turn[pl.ds(r, count, stride=PITCH), :] = chunks[r // CHUNK][:, lanes] * mask_rows[r : r + 1, :]
 
 
 def chunk_of(turn, first):
-    return jnp.concatenate([turn[pl.ds(first + r, TILE, stride=SUB), :] for r in range(CHUNK)], axis=1)
+    return jnp.concatenate([turn[pl.ds(first + r, TILE, stride=PITCH), :] for r in range(CHUNK)], axis=1)
 
 
 def rows_of(group):
     return pl.ds(pl.multiple_of(group * SUB, SUB), SUB)
+
+
+def unturn(turn, places, group):
+    for n, (out, d) in enumerate(places):
+        out[0, d, rows_of(group), :] = turn[n * PITCH : n * PITCH + SUB, :].astype(jnp.bfloat16)
 
 
 def enter_kernel(at, own, sib, mask, both, gain, bias, weights, *rest):
@@ -111,13 +117,7 @@
 
     def finish(group, paired):
         turn_masked(paired, mask[0, rows_of(group), :].astype(jnp.float32), turn)
-        start = 0
-        for out in (left_low, left_high, right_out):
-            stop = start + out.shape[1] * SUB
-            out[0, :, rows_of(group), :] = (
-                turn[start:stop, :].astype(jnp.bfloat16).reshape(out.shape[1], SUB, TILE)
-            )
-            start = stop
+        unturn(turn, [(out, d) for out in (left_low, left_high, right_out) for d in range(out.shape[1])], group)
 
     def turned_chunks(tile, group, matrix):
         rows = tile[rows_of(group)].reshape(SUB * TILE, TILE)
@@ -216,7 +216,7 @@
                 pl.BlockSpec((1, half, high, TILE), right_map),
                 pl.BlockSpec((1, 1, high, TILE), mask_out_map),
             ],
-            scratch_shapes=[pltpu.VMEM((2 * half * SUB, TILE), jnp.float32)],
+            scratch_shapes=[pltpu.VMEM((2 * half * PITCH, TILE), jnp.float32)],
         ),
         out_shape=shapes,
         input_output_aliases=aliases,
@@ -253,7 +253,7 @@
 
 
 TOGETHER = 2
-PARTS = 4
+PARTS = 2
 
 
 def outgoing(at, lefts, right, part):
@@ -289,14 +289,11 @@
     at, state, mask, gain0, bias0, gain_out, bias_out, proj, gate, gain1, bias1, weights, *rest
 ):
     parts, (pairs_out, state_out, turn, turn_out) = rest[:-4], rest[-4:]
-    height = TILE * SUB // len(parts)
 
     @pl.loop(0, MIDDLE_GROUPS)
     def _(group):
-        for n, part in enumerate(parts):
-            turn[n * height : (n + 1) * height, :] = (
-                part[0, :, rows_of(group), :].reshape(height, TILE).astype(jnp.float32)
-            )
+        for n, (part, d) in enumerate((part, d) for part in parts for d in range(part.shape[1])):
+            turn[n * PITCH : n * PITCH + SUB, :] = part[0, d, rows_of(group), :].astype(jnp.float32)
         changed, paired = [], []
         for first in range(0, SUB, CHUNK):
             before = state[group, :, first * TILE : (first + CHUNK) * TILE].astype(jnp.float32)
@@ -307,9 +304,7 @@
             paired.append(gated(weights[0], normed1))
         state_out[group] = jnp.concatenate(changed, axis=1)
         turn_masked(paired, mask[0, 0, rows_of(group), :].astype(jnp.float32), turn_out)
-        pairs_out[0, :, rows_of(group), :] = (
-            turn_out[...].astype(jnp.bfloat16).reshape(TILE, SUB, TILE)
-        )
+        unturn(turn_out, [(pairs_out, d) for d in range(TILE)], group)
 
 
 def middle(at, states, mask, fixed, parts):
@@ -358,7 +353,7 @@
                     ),
                 ),
             ],
-            scratch_shapes=[pltpu.VMEM((TILE * SUB, TILE), jnp.float32)] * 2,
+            scratch_shapes=[pltpu.VMEM((TILE * PITCH, TILE), jnp.float32)] * 2,
         ),
         out_shape=(
             jax.ShapeDtypeStruct((3, TILE, 2 * TILE, TILE), jnp.bfloat16),
@@ -381,7 +376,9 @@
     core = at[0]
     for d in range(CHANNELS):
         right = pairs[2, d]
-        keep[d] = lax.dot_general(pairs[core, d], right, TN, preferred_element_type=jnp.float32)
+        keep[d] = lax.dot_general(
+            pairs[core, d], right, TN, preferred_element_type=jnp.float32
+        ).astype(jnp.bfloat16)
         send[d] = lax.dot_general(
             pairs[1 - core, d], right, TN, preferred_element_type=jnp.float32
         ).astype(jnp.bfloat16)
@@ -398,7 +395,7 @@
             out_specs=[out_spec, out_spec],
         ),
         out_shape=(
-            jax.ShapeDtypeStruct((TILE, TILE, TILE), jnp.float32),
+            jax.ShapeDtypeStruct((TILE, TILE, TILE), jnp.bfloat16),
             jax.ShapeDtypeStruct((TILE, TILE, TILE), jnp.bfloat16),
         ),
         compiler_params=pltpu.CompilerParams(
@@ -414,8 +411,10 @@
 def leave_kernel(at, kept, got, state, gain1, bias1, gain_out, bias_out, proj, gate, result, turn):
     @pl.loop(0, GROUPS)
     def _(group):
-        summed = kept[:, rows_of(group), :] + got[:, rows_of(group), :].astype(jnp.float32)
-        turn[...] = summed.astype(jnp.bfloat16).astype(jnp.float32).reshape(TILE * SUB, TILE)
+        for d in range(TILE):
+            turn[d * PITCH : d * PITCH + SUB, :] = kept[d, rows_of(group), :].astype(jnp.float32) + got[
+                d, rows_of(group), :
+            ].astype(jnp.float32)
         changed = []
         for first in range(0, SUB, CHUNK):
             before = state[group, :, first * TILE : (first + CHUNK) * TILE].astype(jnp.float32)
@@ -443,7 +442,7 @@
             ]
             + [square] * 6,
             out_specs=pl.BlockSpec((GROUPS * SUB, TILE, TILE), lambda block, at: (block, 0, 0)),
-            scratch_shapes=[pltpu.VMEM((TILE * SUB, TILE), jnp.float32)],
+            scratch_shapes=[pltpu.VMEM((TILE * PITCH, TILE), jnp.float32)],
         ),
         out_shape=jax.ShapeDtypeStruct((TILE, TILE, TILE), jnp.bfloat16),
         compiler_params=pltpu.CompilerParams(

time: 594 us -> 557 us (0.938)
  Pallas kernels: 346 us -> 299 us
  waiting for transfers between devices: 200 us -> 211 us
    pallas_call x1, Pallas kernels: 115 us -> 91.7 us  [middle(): pl.pallas_call(middle_kernel, grid_spec=pltpu.PrefetchScalarGridSpec(num_...]
    pallas_call x9, Pallas kernels: 156 us -> 136 us  [enter(): pl.pallas_call(enter_kernel, grid_spec=pltpu.PrefetchScalarGridSpec(num_s...]
    ppermute x15, waiting for transfers between devices: 166 us -> 182 us  [hop(): return [lax.ppermute(value, BOTH, pairs) for value in values]]
    ppermute x4 -> x2, waiting for transfers between devices: 14.9 us -> 9.71 us  [on_device_ring(): got.append(lax.ppermute(leaves, BOTH, swap))]
    pallas_call x4 -> x2, Pallas kernels: 42.4 us -> 41.4 us  [outgoing(): pl.pallas_call(outgoing_kernel, grid_spec=pltpu.PrefetchScalarGridSpec(nu...]
  transfers between devices with their start and end apart: 30 -> 28, of which waited for: 14 -> 12; matrix products, arithmetic and copies ran while one was open for 3% -> 3% of each run, Pallas kernels for 26% -> 26%
where the time goes in v5:
time: 557 us; the launch traced here: 555 us
  Pallas kernels  299 us (54%)
  waiting for transfers between devices  211 us (38%)
  local copies, waits for them, and re-layouts  21.1 us (4%)
  starting transfers between devices  20.1 us (4%)
    ppermute x15, waiting for transfers between devices, hop(): return [lax.ppermute(value, BOTH, pairs) for value in values]  182 us
    pallas_call x9, Pallas kernels, enter(): pl.pallas_call(enter_kernel, grid_spec=pltpu.PrefetchScalarGridSpec(num_s...  136 us
    pallas_call x1, Pallas kernels, middle(): pl.pallas_call(middle_kernel, grid_spec=pltpu.PrefetchScalarGridSpec(num_...  91.7 us
    pallas_call x2, Pallas kernels, outgoing(): pl.pallas_call(outgoing_kernel, grid_spec=pltpu.PrefetchScalarGridSpec(nu...  41.4 us
    pallas_call x1, Pallas kernels, incoming(): pl.pallas_call(incoming_kernel, grid_spec=pltpu.PrefetchScalarGridSpec(nu...  17.1 us
    ppermute x15, starting transfers between devices, hop(): return [lax.ppermute(value, BOTH, pairs) for value in values]  16.3 us
    pallas_call x1, Pallas kernels, leave(): pl.pallas_call(leave_kernel, grid_spec=pltpu.PrefetchScalarGridSpec(num_s...  12.4 us
  transfers between devices with their start and end apart: 28, of which 12 were waited for; matrix products, arithmetic and copies ran while one was open for 3% of the time, Pallas kernels for 26%

profile of v5, /device:TPU:0, one launch (start us, length us, event | category | flops | bytes accessed | tf_op | source)
XLA Modules:
  0.0 555.2 jit_solution(16308110895520342647)
XLA Ops:
  0.5 2.6 collective-permute-start.2
  3.0 0.8 convert_element_type.6
  4.1 0.9 fusion.10
  5.0 0.9 fusion.11
  6.4 0.8 fusion.13
  7.2 0.8 slice_bitcast_fusion
  8.7 0.8 fusion.12
  11.4 0.8 slice_bitcast_fusion.3
  12.1 0.8 slice_bitcast_fusion.2
  13.5 0.8 convert_bitcast_fusion
  14.6 1.9 collective-permute-start.1
  16.8 2.2 copy-done.6
  19.0 16.3 %enter.9 = (bf16[50,128,2048]{2,1,0:T(8,128)(2,1)}, bf16[4,32,512,128]{3,2,1,0:T(8,128)(2,1)}, bf16[4,32,512,128]{3,2,1,0:T(8,128)(2,1)}, bf16[4,64,384,128]{3,2,1,0:T(8,128)(2,1)}, bf16[4,4,128,128]{3,2,1,0:T(8,128)(2,1)S(1)}) custom-call(s32[6]{0:T(128)S(1)} %stack.240.at, bf16[128,128,128]{2,1,0:T(8,128)(2,1)S(1)} %copy-done.6, ...), custom_call_target="tpu_custom_call" | custom-call | flops 4294967296 | bytes 33554432 | tf_op jit(solution)/shard_map/enter/pallas_call | solution.py:206
  35.3 60.5 %collective-permute-done.1.mask = bf16[2,128,128]{2,1,0:T(8,128)(2,1)S(1)} collective-permute-done((bf16[2,128,128]{2,1,0:T(8,128)(2,1)S(1)}, bf16[2,128,128]{2,1,0:T(8,128)(2,1)S(1)}, u32[]{:S(2)}, u32[]{:S(2)}) %collective-permute-start.1) | collective-permute-done | bytes 65568 | tf_op jit(solution)/shard_map/ppermute | solution.py:536
  95.8 1.5 collective-permute-done.3.mask
  98.4 1.6 collective-permute-start.7
  100.6 1.6 collective-permute-start.6
  102.2 3.2 collective-permute-done.11.sib
  105.7 16.9 %enter.10 = (bf16[50,128,2048]{2,1,0:T(8,128)(2,1)}, bf16[4,32,512,128]{3,2,1,0:T(8,128)(2,1)}, bf16[4,32,512,128]{3,2,1,0:T(8,128)(2,1)}, bf16[4,64,384,128]{3,2,1,0:T(8,128)(2,1)}, bf16[4,4,128,128]{3,2,1,0:T(8,128)(2,1)S(1)}) custom-call(s32[6]{0:T(128)S(1)} %stack.255.at, ...), custom_call_target="tpu_custom_call", output_to_operand_aliasing={{0}: (8, {}), {1}: (9, {}), {2}: (10, {}), {3}: (11, {}), {... | custom-call | flops 4294967296 | bytes 33554432 | tf_op jit(solution)/shard_map/enter/pallas_call | solution.py:206
  122.6 16.9 %enter.11 = (bf16[50,128,2048]{2,1,0:T(8,128)(2,1)}, bf16[4,32,512,128]{3,2,1,0:T(8,128)(2,1)}, bf16[4,32,512,128]{3,2,1,0:T(8,128)(2,1)}, bf16[4,64,384,128]{3,2,1,0:T(8,128)(2,1)}, bf16[4,4,128,128]{3,2,1,0:T(8,128)(2,1)S(1)}) custom-call(s32[6]{0:T(128)S(1)} %stack.249.at, ...), custom_call_target="tpu_custom_call", output_to_operand_aliasing={{0}: (8, {}), {1}: (9, {}), {2}: (10, {}), {3}: (11, {}), {... | custom-call | flops 4294967296 | bytes 33554432 | tf_op jit(solution)/shard_map/enter/pallas_call | solution.py:206
  139.4 53.1 %collective-permute-done.6.mask = bf16[2,128,128]{2,1,0:T(8,128)(2,1)S(1)} collective-permute-done((bf16[2,128,128]{2,1,0:T(8,128)(2,1)S(1)}, bf16[2,128,128]{2,1,0:T(8,128)(2,1)S(1)}, u32[]{:S(2)}, u32[]{:S(2)}) %collective-permute-start.6) | collective-permute-done | bytes 65568 | tf_op jit(solution)/shard_map/ppermute | solution.py:536
  192.6 1.3 collective-permute-done.8.mask
  194.4 1.6 collective-permute-start.13
  196.6 1.6 collective-permute-start.12
  198.2 3.2 collective-permute-done.17.sib
  201.8 16.8 %enter.12 = (bf16[50,128,2048]{2,1,0:T(8,128)(2,1)}, bf16[4,32,512,128]{3,2,1,0:T(8,128)(2,1)}, bf16[4,32,512,128]{3,2,1,0:T(8,128)(2,1)}, bf16[4,64,384,128]{3,2,1,0:T(8,128)(2,1)}, bf16[4,4,128,128]{3,2,1,0:T(8,128)(2,1)S(1)}) custom-call(s32[6]{0:T(128)S(1)} %stack.267.at, ...), custom_call_target="tpu_custom_call", output_to_operand_aliasing={{0}: (8, {}), {1}: (9, {}), {2}: (10, {}), {3}: (11, {}), {... | custom-call | flops 4294967296 | bytes 33554432 | tf_op jit(solution)/shard_map/enter/pallas_call | solution.py:206
  218.7 16.6 %enter.13 = (bf16[50,128,2048]{2,1,0:T(8,128)(2,1)}, bf16[4,32,512,128]{3,2,1,0:T(8,128)(2,1)}, bf16[4,32,512,128]{3,2,1,0:T(8,128)(2,1)}, bf16[4,64,384,128]{3,2,1,0:T(8,128)(2,1)}, bf16[4,4,128,128]{3,2,1,0:T(8,128)(2,1)S(1)}) custom-call(s32[6]{0:T(128)S(1)} %stack.261.at, ...), custom_call_target="tpu_custom_call", output_to_operand_aliasing={{0}: (8, {}), {1}: (9, {}), {2}: (10, {}), {3}: (11, {}), {... | custom-call | flops 4294967296 | bytes 33554432 | tf_op jit(solution)/shard_map/enter/pallas_call | solution.py:206
  235.3 53.2 %collective-permute-done.12.mask = bf16[2,128,128]{2,1,0:T(8,128)(2,1)S(1)} collective-permute-done((bf16[2,128,128]{2,1,0:T(8,128)(2,1)S(1)}, bf16[2,128,128]{2,1,0:T(8,128)(2,1)S(1)}, u32[]{:S(2)}, u32[]{:S(2)}) %collective-permute-start.12) | collective-permute-done | bytes 65568 | tf_op jit(solution)/shard_map/ppermute | solution.py:536
  288.6 1.3 collective-permute-done.14.mask
  290.4 3.2 slice.74
  293.6 3.2 slice.75
  296.8 1.5 collective-permute-start.19
  299.0 1.7 collective-permute-start.18
  300.6 0.9 copy-done.3
  301.5 16.7 %enter.14 = (bf16[50,128,2048]{2,1,0:T(8,128)(2,1)}, bf16[4,32,512,128]{3,2,1,0:T(8,128)(2,1)}, bf16[4,32,512,128]{3,2,1,0:T(8,128)(2,1)}, bf16[4,64,384,128]{3,2,1,0:T(8,128)(2,1)}, bf16[4,4,128,128]{3,2,1,0:T(8,128)(2,1)S(1)}) custom-call(s32[6]{0:T(128)S(1)} %stack.279.at, ...), custom_call_target="tpu_custom_call", output_to_operand_aliasing={{0}: (8, {}), {1}: (9, {}), {2}: (10, {}), {3}: (11, {}), {... | custom-call | flops 4294967296 | bytes 33554432 | tf_op jit(solution)/shard_map/enter/pallas_call | solution.py:206
  318.2 16.7 %enter.15 = (bf16[50,128,2048]{2,1,0:T(8,128)(2,1)}, bf16[4,32,512,128]{3,2,1,0:T(8,128)(2,1)}, bf16[4,32,512,128]{3,2,1,0:T(8,128)(2,1)}, bf16[4,64,384,128]{3,2,1,0:T(8,128)(2,1)}, bf16[4,4,128,128]{3,2,1,0:T(8,128)(2,1)S(1)}) custom-call(s32[6]{0:T(128)S(1)} %stack.273.at, ...), custom_call_target="tpu_custom_call", output_to_operand_aliasing={{0}: (8, {}), {1}: (9, {}), {2}: (10, {}), {3}: (11, {}), {... | custom-call | flops 4294967296 | bytes 33554432 | tf_op jit(solution)/shard_map/enter/pallas_call | solution.py:206
  334.9 11.1 %collective-permute-done.18.mask = bf16[2,128,128]{2,1,0:T(8,128)(2,1)S(1)} collective-permute-done((bf16[2,128,128]{2,1,0:T(8,128)(2,1)}, bf16[2,128,128]{2,1,0:T(8,128)(2,1)S(1)}, u32[]{:S(2)}, u32[]{:S(2)}) %collective-permute-start.18) | collective-permute-done | bytes 65568 | tf_op jit(solution)/shard_map/ppermute | solution.py:536
  346.7 6.1 %collective-permute-done.24.sib = bf16[64,128,128]{2,1,0:T(8,128)(2,1)} collective-permute-done((bf16[64,128,128]{2,1,0:T(8,128)(2,1)}, bf16[64,128,128]{2,1,0:T(8,128)(2,1)}, u32[]{:S(2)}, u32[]{:S(2)}) %collective-permute-start.24) | collective-permute-done | bytes 2097184 | tf_op jit(solution)/shard_map/ppermute | solution.py:575
  352.8 10.0 %enter.16 = (bf16[50,128,2048]{2,1,0:T(8,128)(2,1)}, bf16[4,32,512,128]{3,2,1,0:T(8,128)(2,1)}, bf16[4,32,512,128]{3,2,1,0:T(8,128)(2,1)}, bf16[4,64,384,128]{3,2,1,0:T(8,128)(2,1)}, bf16[4,4,128,128]{3,2,1,0:T(8,128)(2,1)S(1)}) custom-call(s32[6]{0:T(128)S(1)} %stack.230.at, ...), custom_call_target="tpu_custom_call", output_to_operand_aliasing={{0}: (8, {}), {1}: (9, {}), {2}: (10, {}), {3}: (11, {}), {... | custom-call | flops 2147483648 | bytes 16777216 | tf_op jit(solution)/shard_map/enter/pallas_call | solution.py:206
  362.7 9.6 %enter.17 = (bf16[50,128,2048]{2,1,0:T(8,128)(2,1)}, bf16[4,32,512,128]{3,2,1,0:T(8,128)(2,1)}, bf16[4,32,512,128]{3,2,1,0:T(8,128)(2,1)}, bf16[4,64,384,128]{3,2,1,0:T(8,128)(2,1)}, bf16[4,4,128,128]{3,2,1,0:T(8,128)(2,1)S(1)}) custom-call(s32[6]{0:T(128)S(1)} %stack.230.at, ...), custom_call_target="tpu_custom_call", output_to_operand_aliasing={{0}: (8, {}), {1}: (9, {}), {2}: (10, {}), {3}: (11, {}), {... | custom-call | flops 2147483648 | bytes 16777216 | tf_op jit(solution)/shard_map/enter/pallas_call | solution.py:206
  372.3 21.5 %outgoing.3 = (bf16[3,32,256,128]{3,2,1,0:T(8,128)(2,1)S(1)}, bf16[3,32,256,128]{3,2,1,0:T(8,128)(2,1)}) custom-call(s32[2]{0:T(128)S(1)} %pad_add_fusion.1.at, bf16[4,32,512,128]{3,2,1,0:T(8,128)(2,1)} %get-tuple-element.257.left, bf16[4,64,384,128]{3,2,1,0:T(8,128)(2,1)} %get-tuple-element.255.right), custom_call_target="tpu_custom_call" | custom-call | flops 6442450944 | bytes 42598400 | tf_op jit(solution)/shard_map/outgoing/pallas_call | solution.py:266
  394.0 19.8 %outgoing.2 = (bf16[3,32,256,128]{3,2,1,0:T(8,128)(2,1)S(1)}, bf16[3,32,256,128]{3,2,1,0:T(8,128)(2,1)S(1)}) custom-call(s32[2]{0:T(128)S(1)} %pad_add_fusion.1.at, bf16[4,32,512,128]{3,2,1,0:T(8,128)(2,1)} %get-tuple-element.254.left, bf16[4,64,384,128]{3,2,1,0:T(8,128)(2,1)} %get-tuple-element.255.right), custom_call_target="tpu_custom_call" | custom-call | flops 6442450944 | bytes 42598400 | tf_op jit(solution)/shard_map/outgoing/pallas_call | solution.py:266
  414.4 9.7 %collective-permute-done.25.rest_2_ = bf16[3,32,256,128]{3,2,1,0:T(8,128)(2,1)S(1)} collective-permute-done((bf16[3,32,256,128]{3,2,1,0:T(8,128)(2,1)S(1)}, bf16[3,32,256,128]{3,2,1,0:T(8,128)(2,1)S(1)}, u32[]{:S(2)}, u32[]{:S(2)}) %collective-permute-start.25) | collective-permute-done | bytes 6291488 | tf_op jit(solution)/shard_map/ppermute | solution.py:587
  424.1 2.6 copy-done.7
  426.7 91.7 %middle.1 = (bf16[3,128,256,128]{3,2,1,0:T(8,128)(2,1)}, bf16[20,128,2048]{2,1,0:T(8,128)(2,1)}) custom-call(s32[4]{0:T(128)S(1)} %pad_add_fusion.at, bf16[50,128,2048]{2,1,0:T(8,128)(2,1)} %get-tuple-element.243.state, bf16[4,4,128,128]{3,2,1,0:T(8,128)(2,1)S(1)} %get-tuple-element.244.mask, f32[128,128]{1,0:T(8,128)S(1)} %broadcast_in_dim.55.gain.gain0, ...), custom_call_target="tpu_custom_call" | custom-call | flops 12884901888 | bytes 100663296 | tf_op jit(solution)/shard_map/middle/pallas_call | solution.py:325
  518.4 17.1 %incoming.1 = (bf16[128,128,128]{2,1,0:T(8,128)(2,1)S(1)}, bf16[128,128,128]{2,1,0:T(8,128)(2,1)S(1)}) custom-call(s32[4]{0:T(128)S(1)} %pad_add_fusion.at, bf16[3,128,256,128]{3,2,1,0:T(8,128)(2,1)} %get-tuple-element.261.pairs), custom_call_target="tpu_custom_call" | custom-call | flops 2147483648 | bytes 37748736 | tf_op jit(solution)/shard_map/incoming/pallas_call | solution.py:389
  536.0 6.8 %collective-permute-done.27.got = bf16[128,128,128]{2,1,0:T(8,128)(2,1)S(1)} collective-permute-done((bf16[128,128,128]{2,1,0:T(8,128)(2,1)S(1)}, bf16[128,128,128]{2,1,0:T(8,128)(2,1)S(1)}, u32[]{:S(2)}, u32[]{:S(2)}) %collective-permute-start.27) | collective-permute-done | bytes 4194336 | tf_op jit(solution)/shard_map/ppermute | solution.py:592
  542.8 12.4 %leave.1 = bf16[128,128,128]{2,1,0:T(8,128)(2,1)} custom-call(s32[4]{0:T(128)S(1)} %pad_add_fusion.at, bf16[128,128,128]{2,1,0:T(8,128)(2,1)S(1)} %get-tuple-element.262.kept, bf16[128,128,128]{2,1,0:T(8,128)(2,1)S(1)} %collective-permute-done.27.got, bf16[20,128,2048]{2,1,0:T(8,128)(2,1)} %get-tuple-element.264.state, ...), custom_call_target="tpu_custom_call" | custom-call | flops 1073741824 | bytes 20971520 | tf_op jit(solution)/shard_map/leave/pallas_call | solution.py:433
  (100 shorter events, 11.5 us)
Async XLA Ops:
  0.0 16.7 %collective-permute-start.5 = (bf16[128,128,128]{2,1,0:T(8,128)(2,1)}, bf16[128,128,128]{2,1,0:T(8,128)(2,1)}, u32[]{:S(2)}, u32[]{:S(2)}) collective-permute-start(bf16[128,128,128]{2,1,0:T(8,128)(2,1)} %own.1), channel_id=1, source_target_pairs={{0,4},{4,0},{1,5},{5,1},{2,6},{6,2},{3,7},{7,3},{11,15},{15,11},{1... | collective-permute-start | bytes 12582920 | tf_op jit(solution)/shard_map/ppermute | solution.py:538
  0.5 96.9 %collective-permute-start.2 = (bf16[128,128,128]{2,1,0:T(8,128)(2,1)}, bf16[128,128,128]{2,1,0:T(8,128)(2,1)}, u32[]{:S(2)}, u32[]{:S(2)}) collective-permute-start(bf16[128,128,128]{2,1,0:T(8,128)(2,1)} %own.1), channel_id=1, source_target_pairs={{0,1},{4,5},{1,2},{5,6},{2,3},{6,7},{3,11},{7,15},{11,10},{15,14},... | collective-permute-start | bytes 12582920 | tf_op jit(solution)/shard_map/ppermute | solution.py:536
  3.0 94.3 %collective-permute-start.4 = (bf16[128,128,128]{2,1,0:T(8,128)(2,1)}, bf16[128,128,128]{2,1,0:T(8,128)(2,1)}, u32[]{:S(2)}, u32[]{:S(2)}) collective-permute-start(bf16[128,128,128]{2,1,0:T(8,128)(2,1)} %own.1), channel_id=1, source_target_pairs={{1,0},{5,4},{2,1},{6,5},{3,2},{7,6},{11,3},{15,7},{10,11},{14,15},... | collective-permute-start | bytes 12582920 | tf_op jit(solution)/shard_map/ppermute | solution.py:536
  3.9 10.7 %collective-permute-start = (bf16[128,128]{1,0:T(8,128)(2,1)S(1)}, bf16[128,128]{1,0:T(8,128)(2,1)S(1)}, u32[]{:S(2)}, u32[]{:S(2)}) collective-permute-start(bf16[128,128]{1,0:T(8,128)(2,1)S(1)} %convert_element_type.6), channel_id=1, source_target_pairs={{0,4},{4,0},{1,5},{5,1},{2,6},{6,2},{3,7},{7,3},{11,15},{15,11},{1... | collective-permute-start | bytes 98312 | tf_op jit(solution)/shard_map/ppermute | solution.py:484
  14.6 81.2 %collective-permute-start.1 = (bf16[2,128,128]{2,1,0:T(8,128)(2,1)S(1)}, bf16[2,128,128]{2,1,0:T(8,128)(2,1)S(1)}, u32[]{:S(2)}, u32[]{:S(2)}) collective-permute-start(bf16[2,128,128]{2,1,0:T(8,128)(2,1)S(1)} %maximum_select_fusion.mask), channel_id=1, source_target_pairs={{0,1},{4,5},{1,2},{5,6},{2,3},{6,7},{3,11},{7,15},{11,10},{15,14},... | collective-permute-start | bytes 196616 | tf_op jit(solution)/shard_map/ppermute | solution.py:536
  16.5 80.9 %collective-permute-start.3 = (bf16[2,128,128]{2,1,0:T(8,128)(2,1)S(1)}, bf16[2,128,128]{2,1,0:T(8,128)(2,1)S(1)}, u32[]{:S(2)}, u32[]{:S(2)}) collective-permute-start(bf16[2,128,128]{2,1,0:T(8,128)(2,1)S(1)} %maximum_select_fusion.mask), channel_id=1, source_target_pairs={{1,0},{5,4},{2,1},{6,5},{3,2},{7,6},{11,3},{15,7},{10,11},{14,15},... | collective-permute-start | bytes 196616 | tf_op jit(solution)/shard_map/ppermute | solution.py:536
  16.8 2.2 copy-start.6
  97.8 7.5 %collective-permute-start.11 = (bf16[128,128,128]{2,1,0:T(8,128)(2,1)}, bf16[128,128,128]{2,1,0:T(8,128)(2,1)}, u32[]{:S(2)}, u32[]{:S(2)}) collective-permute-start(bf16[128,128,128]{2,1,0:T(8,128)(2,1)} %collective-permute-done.2.own), channel_id=1, source_target_pairs={{0,4},{4,0},{1,5},{5,1},{2,6},{6,2},{3,7},{7,3},{11,15},{15,11},{1... | collective-permute-start | bytes 12582920 | tf_op jit(solution)/shard_map/ppermute | solution.py:573
  97.9 24.7 %collective-permute-start.10 = (bf16[128,128,128]{2,1,0:T(8,128)(2,1)}, bf16[128,128,128]{2,1,0:T(8,128)(2,1)}, u32[]{:S(2)}, u32[]{:S(2)}) collective-permute-start(bf16[128,128,128]{2,1,0:T(8,128)(2,1)} %collective-permute-done.4.own), channel_id=1, source_target_pairs={{0,4},{4,0},{1,5},{5,1},{2,6},{6,2},{3,7},{7,3},{11,15},{15,11},{1... | collective-permute-start | bytes 12582920 | tf_op jit(solution)/shard_map/ppermute | solution.py:573
  98.4 95.5 %collective-permute-start.7 = (bf16[128,128,128]{2,1,0:T(8,128)(2,1)}, bf16[128,128,128]{2,1,0:T(8,128)(2,1)}, u32[]{:S(2)}, u32[]{:S(2)}) collective-permute-start(bf16[128,128,128]{2,1,0:T(8,128)(2,1)} %collective-permute-done.2.own), channel_id=1, source_target_pairs={{0,1},{4,5},{1,2},{5,6},{2,3},{6,7},{3,11},{7,15},{11,10},{15,14},... | collective-permute-start | bytes 12582920 | tf_op jit(solution)/shard_map/ppermute | solution.py:536
  100.0 93.9 %collective-permute-start.9 = (bf16[128,128,128]{2,1,0:T(8,128)(2,1)}, bf16[128,128,128]{2,1,0:T(8,128)(2,1)}, u32[]{:S(2)}, u32[]{:S(2)}) collective-permute-start(bf16[128,128,128]{2,1,0:T(8,128)(2,1)} %collective-permute-done.4.own), channel_id=1, source_target_pairs={{1,0},{5,4},{2,1},{6,5},{3,2},{7,6},{11,3},{15,7},{10,11},{14,15},... | collective-permute-start | bytes 12582920 | tf_op jit(solution)/shard_map/ppermute | solution.py:536
  100.6 92.0 %collective-permute-start.6 = (bf16[2,128,128]{2,1,0:T(8,128)(2,1)S(1)}, bf16[2,128,128]{2,1,0:T(8,128)(2,1)S(1)}, u32[]{:S(2)}, u32[]{:S(2)}) collective-permute-start(bf16[2,128,128]{2,1,0:T(8,128)(2,1)S(1)} %collective-permute-done.1.mask), channel_id=1, source_target_pairs={{0,1},{4,5},{1,2},{5,6},{2,3},{6,7},{3,11},{7,15},{11,10},{15,14},... | collective-permute-start | bytes 196616 | tf_op jit(solution)/shard_map/ppermute | solution.py:536
  105.4 88.5 %collective-permute-start.8 = (bf16[2,128,128]{2,1,0:T(8,128)(2,1)S(1)}, bf16[2,128,128]{2,1,0:T(8,128)(2,1)S(1)}, u32[]{:S(2)}, u32[]{:S(2)}) collective-permute-start(bf16[2,128,128]{2,1,0:T(8,128)(2,1)S(1)} %collective-permute-done.3.mask), channel_id=1, source_target_pairs={{1,0},{5,4},{2,1},{6,5},{3,2},{7,6},{11,3},{15,7},{10,11},{14,15},... | collective-permute-start | bytes 196616 | tf_op jit(solution)/shard_map/ppermute | solution.py:536
  193.9 7.5 %collective-permute-start.17 = (bf16[128,128,128]{2,1,0:T(8,128)(2,1)}, bf16[128,128,128]{2,1,0:T(8,128)(2,1)}, u32[]{:S(2)}, u32[]{:S(2)}) collective-permute-start(bf16[128,128,128]{2,1,0:T(8,128)(2,1)} %collective-permute-done.7.own), channel_id=1, source_target_pairs={{0,4},{4,0},{1,5},{5,1},{2,6},{6,2},{3,7},{7,3},{11,15},{15,11},{1... | collective-permute-start | bytes 12582920 | tf_op jit(solution)/shard_map/ppermute | solution.py:573
  193.9 24.8 %collective-permute-start.16 = (bf16[128,128,128]{2,1,0:T(8,128)(2,1)}, bf16[128,128,128]{2,1,0:T(8,128)(2,1)}, u32[]{:S(2)}, u32[]{:S(2)}) collective-permute-start(bf16[128,128,128]{2,1,0:T(8,128)(2,1)} %collective-permute-done.9.own), channel_id=1, source_target_pairs={{0,4},{4,0},{1,5},{5,1},{2,6},{6,2},{3,7},{7,3},{11,15},{15,11},{1... | collective-permute-start | bytes 12582920 | tf_op jit(solution)/shard_map/ppermute | solution.py:573
  194.4 95.5 %collective-permute-start.13 = (bf16[128,128,128]{2,1,0:T(8,128)(2,1)}, bf16[128,128,128]{2,1,0:T(8,128)(2,1)}, u32[]{:S(2)}, u32[]{:S(2)}) collective-permute-start(bf16[128,128,128]{2,1,0:T(8,128)(2,1)} %collective-permute-done.7.own), channel_id=1, source_target_pairs={{0,1},{4,5},{1,2},{5,6},{2,3},{6,7},{3,11},{7,15},{11,10},{15,14},... | collective-permute-start | bytes 12582920 | tf_op jit(solution)/shard_map/ppermute | solution.py:536
  196.0 93.9 %collective-permute-start.15 = (bf16[128,128,128]{2,1,0:T(8,128)(2,1)}, bf16[128,128,128]{2,1,0:T(8,128)(2,1)}, u32[]{:S(2)}, u32[]{:S(2)}) collective-permute-start(bf16[128,128,128]{2,1,0:T(8,128)(2,1)} %collective-permute-done.9.own), channel_id=1, source_target_pairs={{1,0},{5,4},{2,1},{6,5},{3,2},{7,6},{11,3},{15,7},{10,11},{14,15},... | collective-permute-start | bytes 12582920 | tf_op jit(solution)/shard_map/ppermute | solution.py:536
  196.6 92.0 %collective-permute-start.12 = (bf16[2,128,128]{2,1,0:T(8,128)(2,1)S(1)}, bf16[2,128,128]{2,1,0:T(8,128)(2,1)S(1)}, u32[]{:S(2)}, u32[]{:S(2)}) collective-permute-start(bf16[2,128,128]{2,1,0:T(8,128)(2,1)S(1)} %collective-permute-done.6.mask), channel_id=1, source_target_pairs={{0,1},{4,5},{1,2},{5,6},{2,3},{6,7},{3,11},{7,15},{11,10},{15,14},... | collective-permute-start | bytes 196616 | tf_op jit(solution)/shard_map/ppermute | solution.py:536
  201.4 88.5 %collective-permute-start.14 = (bf16[2,128,128]{2,1,0:T(8,128)(2,1)S(1)}, bf16[2,128,128]{2,1,0:T(8,128)(2,1)S(1)}, u32[]{:S(2)}, u32[]{:S(2)}) collective-permute-start(bf16[2,128,128]{2,1,0:T(8,128)(2,1)S(1)} %collective-permute-done.8.mask), channel_id=1, source_target_pairs={{1,0},{5,4},{2,1},{6,5},{3,2},{7,6},{11,3},{15,7},{10,11},{14,15},... | collective-permute-start | bytes 196616 | tf_op jit(solution)/shard_map/ppermute | solution.py:536
  288.6 8.2 %copy-start.2 = (bf16[2,128,128]{2,1,0:T(8,128)(2,1)}, bf16[2,128,128]{2,1,0:T(8,128)(2,1)S(1)}, u32[]{:S(2)}) copy-start(bf16[2,128,128]{2,1,0:T(8,128)(2,1)S(1)} %collective-permute-done.12.mask) | copy-start | bytes 196612
  289.9 8.4 %copy-start.4 = (bf16[2,128,128]{2,1,0:T(8,128)(2,1)}, bf16[2,128,128]{2,1,0:T(8,128)(2,1)S(1)}, u32[]{:S(2)}) copy-start(bf16[2,128,128]{2,1,0:T(8,128)(2,1)S(1)} %collective-permute-done.14.mask) | copy-start | bytes 196612
  289.9 10.7 %collective-permute-start.22 = (bf16[128,128,128]{2,1,0:T(8,128)(2,1)}, bf16[128,128,128]{2,1,0:T(8,128)(2,1)}, u32[]{:S(2)}, u32[]{:S(2)}) collective-permute-start(bf16[128,128,128]{2,1,0:T(8,128)(2,1)} %collective-permute-done.13.own), channel_id=1, source_target_pairs={{0,4},{4,0},{1,5},{5,1},{2,6},{6,2},{3,7},{7,3},{11,15},{15,11},{1... | collective-permute-start | bytes 12582920 | tf_op jit(solution)/shard_map/ppermute | solution.py:573
  289.9 28.2 %collective-permute-start.21 = (bf16[128,128,128]{2,1,0:T(8,128)(2,1)}, bf16[128,128,128]{2,1,0:T(8,128)(2,1)}, u32[]{:S(2)}, u32[]{:S(2)}) collective-permute-start(bf16[128,128,128]{2,1,0:T(8,128)(2,1)} %collective-permute-done.15.own), channel_id=1, source_target_pairs={{0,4},{4,0},{1,5},{5,1},{2,6},{6,2},{3,7},{7,3},{11,15},{15,11},{1... | collective-permute-start | bytes 12582920 | tf_op jit(solution)/shard_map/ppermute | solution.py:573
  296.8 49.2 %collective-permute-start.19 = (bf16[64,128,128]{2,1,0:T(8,128)(2,1)}, bf16[64,128,128]{2,1,0:T(8,128)(2,1)}, u32[]{:S(2)}, u32[]{:S(2)}) collective-permute-start(bf16[64,128,128]{2,1,0:T(8,128)(2,1)} %slice.74), channel_id=1, source_target_pairs={{0,1},{4,5},{1,2},{5,6},{2,3},{6,7},{3,11},{7,15},{11,10},{15,14},... | collective-permute-start | bytes 6291464 | tf_op jit(solution)/shard_map/ppermute | solution.py:536
  298.2 47.7 %collective-permute-start.20 = (bf16[64,128,128]{2,1,0:T(8,128)(2,1)}, bf16[64,128,128]{2,1,0:T(8,128)(2,1)S(1)}, u32[]{:S(2)}, u32[]{:S(2)}) collective-permute-start(bf16[64,128,128]{2,1,0:T(8,128)(2,1)} %slice.75), channel_id=1, source_target_pairs={{1,0},{5,4},{2,1},{6,5},{3,2},{7,6},{11,3},{15,7},{10,11},{14,15},... | collective-permute-start | bytes 6291464 | tf_op jit(solution)/shard_map/ppermute | solution.py:536
  299.0 47.0 %collective-permute-start.18 = (bf16[2,128,128]{2,1,0:T(8,128)(2,1)}, bf16[2,128,128]{2,1,0:T(8,128)(2,1)S(1)}, u32[]{:S(2)}, u32[]{:S(2)}) collective-permute-start(bf16[2,128,128]{2,1,0:T(8,128)(2,1)} %copy-done.2), channel_id=1, source_target_pairs={{0,1},{4,5},{1,2},{5,6},{2,3},{6,7},{3,11},{7,15},{11,10},{15,14},... | collective-permute-start | bytes 196616 | tf_op jit(solution)/shard_map/ppermute | solution.py:536
  300.6 0.9 copy-start.3
  301.5 16.7 %copy-start.5 = (bf16[2,128,128]{2,1,0:T(8,128)(2,1)S(1)}, bf16[2,128,128]{2,1,0:T(8,128)(2,1)}, u32[]{:S(2)}) copy-start(bf16[2,128,128]{2,1,0:T(8,128)(2,1)} %copy-done.4) | copy-start | bytes 196612
  346.0 6.8 %collective-permute-start.24 = (bf16[64,128,128]{2,1,0:T(8,128)(2,1)}, bf16[64,128,128]{2,1,0:T(8,128)(2,1)}, u32[]{:S(2)}, u32[]{:S(2)}) collective-permute-start(bf16[64,128,128]{2,1,0:T(8,128)(2,1)} %collective-permute-done.19.own), channel_id=1, source_target_pairs={{0,4},{4,0},{1,5},{5,1},{2,6},{6,2},{3,7},{7,3},{11,15},{15,11},{1... | collective-permute-start | bytes 6291464 | tf_op jit(solution)/shard_map/ppermute | solution.py:575
  346.0 16.7 %collective-permute-start.23 = (bf16[64,128,128]{2,1,0:T(8,128)(2,1)S(1)}, bf16[64,128,128]{2,1,0:T(8,128)(2,1)}, u32[]{:S(2)}, u32[]{:S(2)}) collective-permute-start(bf16[64,128,128]{2,1,0:T(8,128)(2,1)S(1)} %collective-permute-done.20.own), channel_id=1, source_target_pairs={{0,4},{4,0},{1,5},{5,1},{2,6},{6,2},{3,7},{7,3},{11,15},{15,11},{1... | collective-permute-start | bytes 6291464 | tf_op jit(solution)/shard_map/ppermute | solution.py:576
  393.9 20.5 %collective-permute-start.26 = (bf16[3,32,256,128]{3,2,1,0:T(8,128)(2,1)}, bf16[3,32,256,128]{3,2,1,0:T(8,128)(2,1)}, u32[]{:S(2)}, u32[]{:S(2)}) collective-permute-start(bf16[3,32,256,128]{3,2,1,0:T(8,128)(2,1)} %get-tuple-element.260), channel_id=1, source_target_pairs={{0,4},{4,0},{1,5},{5,1},{2,6},{6,2},{3,7},{7,3},{11,15},{15,11},{1... | collective-permute-start | bytes 18874376 | tf_op jit(solution)/shard_map/ppermute | solution.py:587
  394.0 32.7 %copy-start = (bf16[128,128]{1,0:T(8,128)(2,1)S(1)}, bf16[128,128]{1,0:T(8,128)(2,1)}, u32[]{:S(2)}) copy-start(bf16[128,128]{1,0:T(8,128)(2,1)} %fusion.5.proj) | copy-start | bytes 98308
  394.0 32.7 %copy-start.1 = (bf16[128,128]{1,0:T(8,128)(2,1)S(1)}, bf16[128,128]{1,0:T(8,128)(2,1)}, u32[]{:S(2)}) copy-start(bf16[128,128]{1,0:T(8,128)(2,1)} %multiply_bitcast_fusion.2.gate) | copy-start | bytes 98308
  413.8 10.2 %collective-permute-start.25 = (bf16[3,32,256,128]{3,2,1,0:T(8,128)(2,1)S(1)}, bf16[3,32,256,128]{3,2,1,0:T(8,128)(2,1)S(1)}, u32[]{:S(2)}, u32[]{:S(2)}) collective-permute-start(bf16[3,32,256,128]{3,2,1,0:T(8,128)(2,1)S(1)} %get-tuple-element.259), channel_id=1, source_target_pairs={{0,4},{4,0},{1,5},{5,1},{2,6},{6,2},{3,7},{7,3},{11,15},{15,11},{1... | collective-permute-start | bytes 18874376 | tf_op jit(solution)/shard_map/ppermute | solution.py:587
  424.1 2.6 copy-start.7
  535.6 7.2 %collective-permute-start.27 = (bf16[128,128,128]{2,1,0:T(8,128)(2,1)S(1)}, bf16[128,128,128]{2,1,0:T(8,128)(2,1)S(1)}, u32[]{:S(2)}, u32[]{:S(2)}) collective-permute-start(bf16[128,128,128]{2,1,0:T(8,128)(2,1)S(1)} %get-tuple-element.263), channel_id=1, source_target_pairs={{0,4},{4,0},{1,5},{5,1},{2,6},{6,2},{3,7},{7,3},{11,15},{15,11},{1... | collective-permute-start | bytes 12582920 | tf_op jit(solution)/shard_map/ppermute | solution.py:592

commit v6 on v5

--- a/solution.py
+++ b/solution.py
@@ -75,8 +75,8 @@
     return (apart * lax.rsqrt(variance + epsilon) * wide_gain + wide_bias).astype(jnp.bfloat16)
 
 
-def norm_channels(values, gain, bias):
-    return norm_apart(values - jnp.mean(values, axis=0, keepdims=True), gain, bias)
+def norm_channels(values, centre, gain, bias):
+    return norm_apart(product(centre[...], values), gain, bias)
 
 
 def product(matrix, values):
@@ -286,7 +286,7 @@
 
 
 def middle_kernel(
-    at, state, mask, gain0, bias0, gain_out, bias_out, proj, gate, gain1, bias1, weights, *rest
+    at, state, mask, centre, gain0, bias0, gain_out, bias_out, proj, gate, gain1, bias1, weights, *rest
 ):
     parts, (pairs_out, state_out, turn, turn_out) = rest[:-4], rest[-4:]
 
@@ -296,11 +296,14 @@
             turn[n * PITCH : n * PITCH + SUB, :] = part[0, d, rows_of(group), :].astype(jnp.float32)
         changed, paired = [], []
         for first in range(0, SUB, CHUNK):
-            before = state[group, :, first * TILE : (first + CHUNK) * TILE].astype(jnp.float32)
-            gate_value = jnp.tanh(product(gate[...], norm_channels(before, gain0, bias0)))
-            out = product(proj[...], norm_channels(chunk_of(turn, first), gain_out, bias_out))
-            changed.append((before + (out * gate_value + out)).astype(jnp.bfloat16))
-            normed1 = norm_channels(changed[-1].astype(jnp.float32), gain1, bias1)
+            before = state[group, :, first * TILE : (first + CHUNK) * TILE]
+            gate_value = jnp.tanh(product(gate[...], norm_channels(before, centre, gain0, bias0)))
+            triangle = chunk_of(turn, first).astype(jnp.bfloat16)
+            out = product(proj[...], norm_channels(triangle, centre, gain_out, bias_out))
+            changed.append(
+                (before.astype(jnp.float32) + (out * gate_value + out)).astype(jnp.bfloat16)
+            )
+            normed1 = norm_channels(changed[-1], centre, gain1, bias1)
             paired.append(gated(weights[0], normed1))
         state_out[group] = jnp.concatenate(changed, axis=1)
         turn_masked(paired, mask[0, 0, rows_of(group), :].astype(jnp.float32), turn_out)
@@ -334,7 +337,7 @@
                     lambda slot, x, block, at: (2 * x + at[0], column(slot, at), block, 0),
                 ),
             ]
-            + [square] * 8
+            + [square] * 9
             + [
                 pl.BlockSpec(
                     (1, 2 * TILE, TILE),
@@ -408,7 +411,7 @@
     )(at, pairs)
 
 
-def leave_kernel(at, kept, got, state, gain1, bias1, gain_out, bias_out, proj, gate, result, turn):
+def leave_kernel(at, kept, got, state, centre, gain1, bias1, gain_out, bias_out, proj, gate, result, turn):
     @pl.loop(0, GROUPS)
     def _(group):
         for d in range(TILE):
@@ -417,10 +420,13 @@
             ].astype(jnp.float32)
         changed = []
         for first in range(0, SUB, CHUNK):
-            before = state[group, :, first * TILE : (first + CHUNK) * TILE].astype(jnp.float32)
-            gate_value = jnp.tanh(product(gate[...], norm_channels(before, gain1, bias1)))
-            out = product(proj[...], norm_channels(chunk_of(turn, first), gain_out, bias_out))
-            changed.append((before + (out * gate_value + out)).astype(jnp.bfloat16))
+            before = state[group, :, first * TILE : (first + CHUNK) * TILE]
+            gate_value = jnp.tanh(product(gate[...], norm_channels(before, centre, gain1, bias1)))
+            triangle = chunk_of(turn, first).astype(jnp.bfloat16)
+            out = product(proj[...], norm_channels(triangle, centre, gain_out, bias_out))
+            changed.append(
+                (before.astype(jnp.float32) + (out * gate_value + out)).astype(jnp.bfloat16)
+            )
         result[rows_of(group)] = jnp.concatenate([chunk.T for chunk in changed], axis=0).reshape(
             SUB, TILE, TILE
         )
@@ -440,7 +446,7 @@
                 tri,
                 pl.BlockSpec((GROUPS, TILE, SUB * TILE), lambda block, at: (at[1] * blocks + block, 0, 0)),
             ]
-            + [square] * 6,
+            + [square] * 7,
             out_specs=pl.BlockSpec((GROUPS * SUB, TILE, TILE), lambda block, at: (block, 0, 0)),
             scratch_shapes=[pltpu.VMEM((TILE * PITCH, TILE), jnp.float32)],
         ),
@@ -540,6 +546,7 @@
     above = hop([masks, pair_state], down)
     part = TILE // 2
     middle_fixed = [
+        both[:TILE],
         gain_in[0],
         bias_in[0],
         columns(reordered(norm_out_gain[0])),
@@ -551,6 +558,7 @@
         middle_weights,
     ]
     leave_fixed = [
+        both[:TILE],
         gain_in[1],
         bias_in[1],
         columns(norm_out_gain[1]),

time: 557 us -> 714 us (1.28)
  Pallas kernels: 299 us -> 456 us
    pallas_call x1, Pallas kernels: 91.7 us -> 249 us  [middle(): pl.pallas_call(middle_kernel, grid_spec=pltpu.PrefetchScalarGridSpec(num_...]
  transfers between devices with their start and end apart: 28 -> 28, of which waited for: 12 -> 12; matrix products, arithmetic and copies ran while one was open for 3% -> 2% of each run, Pallas kernels for 26% -> 21%
where the time goes in v6:
time: 714 us; the launch traced here: 712 us
  Pallas kernels  456 us (64%)
  waiting for transfers between devices  212 us (30%)
  local copies, waits for them, and re-layouts  21.4 us (3%)
  starting transfers between devices  20.1 us (3%)
    pallas_call x1, Pallas kernels, middle(): pl.pallas_call(middle_kernel, grid_spec=pltpu.PrefetchScalarGridSpec(num_...  249 us
    ppermute x15, waiting for transfers between devices, hop(): return [lax.ppermute(value, BOTH, pairs) for value in values]  183 us
    pallas_call x9, Pallas kernels, enter(): pl.pallas_call(enter_kernel, grid_spec=pltpu.PrefetchScalarGridSpec(num_s...  136 us
    pallas_call x2, Pallas kernels, outgoing(): pl.pallas_call(outgoing_kernel, grid_spec=pltpu.PrefetchScalarGridSpec(nu...  41.4 us
    pallas_call x1, Pallas kernels, incoming(): pl.pallas_call(incoming_kernel, grid_spec=pltpu.PrefetchScalarGridSpec(nu...  17.1 us
    ppermute x15, starting transfers between devices, hop(): return [lax.ppermute(value, BOTH, pairs) for value in values]  16.3 us
  transfers between devices with their start and end apart: 28, of which 12 were waited for; matrix products, arithmetic and copies ran while one was open for 2% of the time, Pallas kernels for 21%

profile of v6, /device:TPU:0, one launch (start us, length us, event | category | flops | bytes accessed | tf_op | source)
XLA Modules:
  0.0 712.2 jit_solution(17412469188997371337)
XLA Ops:
  0.5 2.6 collective-permute-start.2
  3.0 0.8 convert_element_type.10
  4.1 0.9 fusion.10
  5.0 0.9 fusion.11
  6.4 0.8 fusion.13
  7.2 0.8 slice_bitcast_fusion
  7.9 0.8 slice_bitcast_fusion.1
  8.7 0.8 fusion.12
  11.2 0.8 slice_bitcast_fusion.3
  12.7 0.8 convert_bitcast_fusion
  14.4 1.9 collective-permute-start.1
  16.6 2.2 copy-done.8
  18.8 16.3 %enter.9 = (bf16[50,128,2048]{2,1,0:T(8,128)(2,1)}, bf16[4,32,512,128]{3,2,1,0:T(8,128)(2,1)}, bf16[4,32,512,128]{3,2,1,0:T(8,128)(2,1)}, bf16[4,64,384,128]{3,2,1,0:T(8,128)(2,1)}, bf16[4,4,128,128]{3,2,1,0:T(8,128)(2,1)S(1)}) custom-call(s32[6]{0:T(128)S(1)} %stack.240.at, bf16[128,128,128]{2,1,0:T(8,128)(2,1)S(1)} %copy-done.8, ...), custom_call_target="tpu_custom_call" | custom-call | flops 4294967296 | bytes 33554432 | tf_op jit(solution)/shard_map/enter/pallas_call | solution.py:206
  35.1 60.7 %collective-permute-done.1.mask = bf16[2,128,128]{2,1,0:T(8,128)(2,1)S(1)} collective-permute-done((bf16[2,128,128]{2,1,0:T(8,128)(2,1)S(1)}, bf16[2,128,128]{2,1,0:T(8,128)(2,1)S(1)}, u32[]{:S(2)}, u32[]{:S(2)}) %collective-permute-start.1) | collective-permute-done | bytes 65568 | tf_op jit(solution)/shard_map/ppermute | solution.py:542
  95.8 1.5 collective-permute-done.3.mask
  98.4 1.6 collective-permute-start.7
  100.6 1.6 collective-permute-start.6
  102.2 3.2 collective-permute-done.11.sib
  105.7 16.8 %enter.10 = (bf16[50,128,2048]{2,1,0:T(8,128)(2,1)}, bf16[4,32,512,128]{3,2,1,0:T(8,128)(2,1)}, bf16[4,32,512,128]{3,2,1,0:T(8,128)(2,1)}, bf16[4,64,384,128]{3,2,1,0:T(8,128)(2,1)}, bf16[4,4,128,128]{3,2,1,0:T(8,128)(2,1)S(1)}) custom-call(s32[6]{0:T(128)S(1)} %stack.255.at, ...), custom_call_target="tpu_custom_call", output_to_operand_aliasing={{0}: (8, {}), {1}: (9, {}), {2}: (10, {}), {3}: (11, {}), {... | custom-call | flops 4294967296 | bytes 33554432 | tf_op jit(solution)/shard_map/enter/pallas_call | solution.py:206
  122.5 16.8 %enter.11 = (bf16[50,128,2048]{2,1,0:T(8,128)(2,1)}, bf16[4,32,512,128]{3,2,1,0:T(8,128)(2,1)}, bf16[4,32,512,128]{3,2,1,0:T(8,128)(2,1)}, bf16[4,64,384,128]{3,2,1,0:T(8,128)(2,1)}, bf16[4,4,128,128]{3,2,1,0:T(8,128)(2,1)S(1)}) custom-call(s32[6]{0:T(128)S(1)} %stack.249.at, ...), custom_call_target="tpu_custom_call", output_to_operand_aliasing={{0}: (8, {}), {1}: (9, {}), {2}: (10, {}), {3}: (11, {}), {... | custom-call | flops 4294967296 | bytes 33554432 | tf_op jit(solution)/shard_map/enter/pallas_call | solution.py:206
  139.4 53.2 %collective-permute-done.6.mask = bf16[2,128,128]{2,1,0:T(8,128)(2,1)S(1)} collective-permute-done((bf16[2,128,128]{2,1,0:T(8,128)(2,1)S(1)}, bf16[2,128,128]{2,1,0:T(8,128)(2,1)S(1)}, u32[]{:S(2)}, u32[]{:S(2)}) %collective-permute-start.6) | collective-permute-done | bytes 65568 | tf_op jit(solution)/shard_map/ppermute | solution.py:542
  192.6 1.3 collective-permute-done.8.mask
  194.4 1.6 collective-permute-start.13
  196.6 1.6 collective-permute-start.12
  198.2 3.2 collective-permute-done.17.sib
  201.8 16.8 %enter.12 = (bf16[50,128,2048]{2,1,0:T(8,128)(2,1)}, bf16[4,32,512,128]{3,2,1,0:T(8,128)(2,1)}, bf16[4,32,512,128]{3,2,1,0:T(8,128)(2,1)}, bf16[4,64,384,128]{3,2,1,0:T(8,128)(2,1)}, bf16[4,4,128,128]{3,2,1,0:T(8,128)(2,1)S(1)}) custom-call(s32[6]{0:T(128)S(1)} %stack.267.at, ...), custom_call_target="tpu_custom_call", output_to_operand_aliasing={{0}: (8, {}), {1}: (9, {}), {2}: (10, {}), {3}: (11, {}), {... | custom-call | flops 4294967296 | bytes 33554432 | tf_op jit(solution)/shard_map/enter/pallas_call | solution.py:206
  218.7 16.6 %enter.13 = (bf16[50,128,2048]{2,1,0:T(8,128)(2,1)}, bf16[4,32,512,128]{3,2,1,0:T(8,128)(2,1)}, bf16[4,32,512,128]{3,2,1,0:T(8,128)(2,1)}, bf16[4,64,384,128]{3,2,1,0:T(8,128)(2,1)}, bf16[4,4,128,128]{3,2,1,0:T(8,128)(2,1)S(1)}) custom-call(s32[6]{0:T(128)S(1)} %stack.261.at, ...), custom_call_target="tpu_custom_call", output_to_operand_aliasing={{0}: (8, {}), {1}: (9, {}), {2}: (10, {}), {3}: (11, {}), {... | custom-call | flops 4294967296 | bytes 33554432 | tf_op jit(solution)/shard_map/enter/pallas_call | solution.py:206
  235.3 53.3 %collective-permute-done.12.mask = bf16[2,128,128]{2,1,0:T(8,128)(2,1)S(1)} collective-permute-done((bf16[2,128,128]{2,1,0:T(8,128)(2,1)S(1)}, bf16[2,128,128]{2,1,0:T(8,128)(2,1)S(1)}, u32[]{:S(2)}, u32[]{:S(2)}) %collective-permute-start.12) | collective-permute-done | bytes 65568 | tf_op jit(solution)/shard_map/ppermute | solution.py:542
  288.6 1.3 collective-permute-done.14.mask
  290.4 3.2 slice.74
  293.6 3.2 slice.75
  296.8 1.5 collective-permute-start.19
  298.9 1.7 collective-permute-start.18
  300.6 0.9 copy-done.5
  301.5 16.6 %enter.14 = (bf16[50,128,2048]{2,1,0:T(8,128)(2,1)}, bf16[4,32,512,128]{3,2,1,0:T(8,128)(2,1)}, bf16[4,32,512,128]{3,2,1,0:T(8,128)(2,1)}, bf16[4,64,384,128]{3,2,1,0:T(8,128)(2,1)}, bf16[4,4,128,128]{3,2,1,0:T(8,128)(2,1)S(1)}) custom-call(s32[6]{0:T(128)S(1)} %stack.279.at, ...), custom_call_target="tpu_custom_call", output_to_operand_aliasing={{0}: (8, {}), {1}: (9, {}), {2}: (10, {}), {3}: (11, {}), {... | custom-call | flops 4294967296 | bytes 33554432 | tf_op jit(solution)/shard_map/enter/pallas_call | solution.py:206
  318.1 16.7 %enter.15 = (bf16[50,128,2048]{2,1,0:T(8,128)(2,1)}, bf16[4,32,512,128]{3,2,1,0:T(8,128)(2,1)}, bf16[4,32,512,128]{3,2,1,0:T(8,128)(2,1)}, bf16[4,64,384,128]{3,2,1,0:T(8,128)(2,1)}, bf16[4,4,128,128]{3,2,1,0:T(8,128)(2,1)S(1)}) custom-call(s32[6]{0:T(128)S(1)} %stack.273.at, ...), custom_call_target="tpu_custom_call", output_to_operand_aliasing={{0}: (8, {}), {1}: (9, {}), {2}: (10, {}), {3}: (11, {}), {... | custom-call | flops 4294967296 | bytes 33554432 | tf_op jit(solution)/shard_map/enter/pallas_call | solution.py:206
  334.7 11.2 %collective-permute-done.18.mask = bf16[2,128,128]{2,1,0:T(8,128)(2,1)S(1)} collective-permute-done((bf16[2,128,128]{2,1,0:T(8,128)(2,1)}, bf16[2,128,128]{2,1,0:T(8,128)(2,1)S(1)}, u32[]{:S(2)}, u32[]{:S(2)}) %collective-permute-start.18) | collective-permute-done | bytes 65568 | tf_op jit(solution)/shard_map/ppermute | solution.py:542
  346.7 6.1 collective-permute-done.24.sib
  352.8 10.0 %enter.16 = (bf16[50,128,2048]{2,1,0:T(8,128)(2,1)}, bf16[4,32,512,128]{3,2,1,0:T(8,128)(2,1)}, bf16[4,32,512,128]{3,2,1,0:T(8,128)(2,1)}, bf16[4,64,384,128]{3,2,1,0:T(8,128)(2,1)}, bf16[4,4,128,128]{3,2,1,0:T(8,128)(2,1)S(1)}) custom-call(s32[6]{0:T(128)S(1)} %stack.230.at, ...), custom_call_target="tpu_custom_call", output_to_operand_aliasing={{0}: (8, {}), {1}: (9, {}), {2}: (10, {}), {3}: (11, {}), {... | custom-call | flops 2147483648 | bytes 16777216 | tf_op jit(solution)/shard_map/enter/pallas_call | solution.py:206
  362.7 9.7 %enter.17 = (bf16[50,128,2048]{2,1,0:T(8,128)(2,1)}, bf16[4,32,512,128]{3,2,1,0:T(8,128)(2,1)}, bf16[4,32,512,128]{3,2,1,0:T(8,128)(2,1)}, bf16[4,64,384,128]{3,2,1,0:T(8,128)(2,1)}, bf16[4,4,128,128]{3,2,1,0:T(8,128)(2,1)S(1)}) custom-call(s32[6]{0:T(128)S(1)} %stack.230.at, ...), custom_call_target="tpu_custom_call", output_to_operand_aliasing={{0}: (8, {}), {1}: (9, {}), {2}: (10, {}), {3}: (11, {}), {... | custom-call | flops 2147483648 | bytes 16777216 | tf_op jit(solution)/shard_map/enter/pallas_call | solution.py:206
  372.4 21.5 %outgoing.3 = (bf16[3,32,256,128]{3,2,1,0:T(8,128)(2,1)S(1)}, bf16[3,32,256,128]{3,2,1,0:T(8,128)(2,1)}) custom-call(s32[2]{0:T(128)S(1)} %pad_add_fusion.1.at, bf16[4,32,512,128]{3,2,1,0:T(8,128)(2,1)} %get-tuple-element.268.left, bf16[4,64,384,128]{3,2,1,0:T(8,128)(2,1)} %get-tuple-element.266.right), custom_call_target="tpu_custom_call" | custom-call | flops 6442450944 | bytes 42598400 | tf_op jit(solution)/shard_map/outgoing/pallas_call | solution.py:266
  394.1 19.8 %outgoing.2 = (bf16[3,32,256,128]{3,2,1,0:T(8,128)(2,1)S(1)}, bf16[3,32,256,128]{3,2,1,0:T(8,128)(2,1)S(1)}) custom-call(s32[2]{0:T(128)S(1)} %pad_add_fusion.1.at, bf16[4,32,512,128]{3,2,1,0:T(8,128)(2,1)} %get-tuple-element.265.left, bf16[4,64,384,128]{3,2,1,0:T(8,128)(2,1)} %get-tuple-element.266.right), custom_call_target="tpu_custom_call" | custom-call | flops 6442450944 | bytes 42598400 | tf_op jit(solution)/shard_map/outgoing/pallas_call | solution.py:266
  414.4 9.7 %collective-permute-done.25.rest_2_ = bf16[3,32,256,128]{3,2,1,0:T(8,128)(2,1)S(1)} collective-permute-done((bf16[3,32,256,128]{3,2,1,0:T(8,128)(2,1)S(1)}, bf16[3,32,256,128]{3,2,1,0:T(8,128)(2,1)S(1)}, u32[]{:S(2)}, u32[]{:S(2)}) %collective-permute-start.25) | collective-permute-done | bytes 6291488 | tf_op jit(solution)/shard_map/ppermute | solution.py:595
  424.1 2.6 copy-done.9
  426.8 248.6 %middle.1 = (bf16[3,128,256,128]{3,2,1,0:T(8,128)(2,1)}, bf16[20,128,2048]{2,1,0:T(8,128)(2,1)}) custom-call(s32[4]{0:T(128)S(1)} %pad_add_fusion.at, bf16[50,128,2048]{2,1,0:T(8,128)(2,1)} %get-tuple-element.253.state, bf16[4,4,128,128]{3,2,1,0:T(8,128)(2,1)S(1)} %get-tuple-element.254.mask, bf16[128,128]{1,0:T(8,128)(2,1)S(1)} %copy-done.1, ...), custom_call_target="tpu_custom_call" | custom-call | flops 12884901888 | bytes 100663296 | tf_op jit(solution)/shard_map/middle/pallas_call | solution.py:328
  675.4 17.1 %incoming.1 = (bf16[128,128,128]{2,1,0:T(8,128)(2,1)S(1)}, bf16[128,128,128]{2,1,0:T(8,128)(2,1)S(1)}) custom-call(s32[4]{0:T(128)S(1)} %pad_add_fusion.at, bf16[3,128,256,128]{3,2,1,0:T(8,128)(2,1)} %get-tuple-element.272.pairs), custom_call_target="tpu_custom_call" | custom-call | flops 2147483648 | bytes 37748736 | tf_op jit(solution)/shard_map/incoming/pallas_call | solution.py:392
  692.9 6.8 collective-permute-done.27.got
  699.7 12.5 %leave.1 = bf16[128,128,128]{2,1,0:T(8,128)(2,1)} custom-call(s32[4]{0:T(128)S(1)} %pad_add_fusion.at, bf16[128,128,128]{2,1,0:T(8,128)(2,1)S(1)} %get-tuple-element.273.kept, bf16[128,128,128]{2,1,0:T(8,128)(2,1)S(1)} %collective-permute-done.27.got, bf16[20,128,2048]{2,1,0:T(8,128)(2,1)} %get-tuple-element.275.state, bf16[128,128]{1,0:T(8,128)(2,1)S(1)} %copy-done.1, ...), custom_call_target="tpu_custom_call" | custom-call | flops 1073741824 | bytes 20971520 | tf_op jit(solution)/shard_map/leave/pallas_call | solution.py:439
  (104 shorter events, 11.2 us)
Async XLA Ops:
  0.0 16.4 %collective-permute-start.5 = (bf16[128,128,128]{2,1,0:T(8,128)(2,1)}, bf16[128,128,128]{2,1,0:T(8,128)(2,1)}, u32[]{:S(2)}, u32[]{:S(2)}) collective-permute-start(bf16[128,128,128]{2,1,0:T(8,128)(2,1)} %own.1), channel_id=1, source_target_pairs={{0,4},{4,0},{1,5},{5,1},{2,6},{6,2},{3,7},{7,3},{11,15},{15,11},{1... | collective-permute-start | bytes 12582920 | tf_op jit(solution)/shard_map/ppermute | solution.py:544
  0.5 96.9 %collective-permute-start.2 = (bf16[128,128,128]{2,1,0:T(8,128)(2,1)}, bf16[128,128,128]{2,1,0:T(8,128)(2,1)}, u32[]{:S(2)}, u32[]{:S(2)}) collective-permute-start(bf16[128,128,128]{2,1,0:T(8,128)(2,1)} %own.1), channel_id=1, source_target_pairs={{0,1},{4,5},{1,2},{5,6},{2,3},{6,7},{3,11},{7,15},{11,10},{15,14},... | collective-permute-start | bytes 12582920 | tf_op jit(solution)/shard_map/ppermute | solution.py:542
  3.0 94.3 %collective-permute-start.4 = (bf16[128,128,128]{2,1,0:T(8,128)(2,1)}, bf16[128,128,128]{2,1,0:T(8,128)(2,1)}, u32[]{:S(2)}, u32[]{:S(2)}) collective-permute-start(bf16[128,128,128]{2,1,0:T(8,128)(2,1)} %own.1), channel_id=1, source_target_pairs={{1,0},{5,4},{2,1},{6,5},{3,2},{7,6},{11,3},{15,7},{10,11},{14,15},... | collective-permute-start | bytes 12582920 | tf_op jit(solution)/shard_map/ppermute | solution.py:542
  3.9 10.5 %collective-permute-start = (bf16[128,128]{1,0:T(8,128)(2,1)S(1)}, bf16[128,128]{1,0:T(8,128)(2,1)S(1)}, u32[]{:S(2)}, u32[]{:S(2)}) collective-permute-start(bf16[128,128]{1,0:T(8,128)(2,1)S(1)} %convert_element_type.10), channel_id=1, source_target_pairs={{0,4},{4,0},{1,5},{5,1},{2,6},{6,2},{3,7},{7,3},{11,15},{15,11},{1... | collective-permute-start | bytes 98312 | tf_op jit(solution)/shard_map/ppermute | solution.py:490
  10.5 0.6 copy-start
  14.4 81.4 %collective-permute-start.1 = (bf16[2,128,128]{2,1,0:T(8,128)(2,1)S(1)}, bf16[2,128,128]{2,1,0:T(8,128)(2,1)S(1)}, u32[]{:S(2)}, u32[]{:S(2)}) collective-permute-start(bf16[2,128,128]{2,1,0:T(8,128)(2,1)S(1)} %maximum_select_fusion.mask), channel_id=1, source_target_pairs={{0,1},{4,5},{1,2},{5,6},{2,3},{6,7},{3,11},{7,15},{11,10},{15,14},... | collective-permute-start | bytes 196616 | tf_op jit(solution)/shard_map/ppermute | solution.py:542
  16.2 81.1 %collective-permute-start.3 = (bf16[2,128,128]{2,1,0:T(8,128)(2,1)S(1)}, bf16[2,128,128]{2,1,0:T(8,128)(2,1)S(1)}, u32[]{:S(2)}, u32[]{:S(2)}) collective-permute-start(bf16[2,128,128]{2,1,0:T(8,128)(2,1)S(1)} %maximum_select_fusion.mask), channel_id=1, source_target_pairs={{1,0},{5,4},{2,1},{6,5},{3,2},{7,6},{11,3},{15,7},{10,11},{14,15},... | collective-permute-start | bytes 196616 | tf_op jit(solution)/shard_map/ppermute | solution.py:542
  16.6 2.2 copy-start.8
  97.8 7.5 %collective-permute-start.11 = (bf16[128,128,128]{2,1,0:T(8,128)(2,1)}, bf16[128,128,128]{2,1,0:T(8,128)(2,1)}, u32[]{:S(2)}, u32[]{:S(2)}) collective-permute-start(bf16[128,128,128]{2,1,0:T(8,128)(2,1)} %collective-permute-done.2.own), channel_id=1, source_target_pairs={{0,4},{4,0},{1,5},{5,1},{2,6},{6,2},{3,7},{7,3},{11,15},{15,11},{1... | collective-permute-start | bytes 12582920 | tf_op jit(solution)/shard_map/ppermute | solution.py:581
  97.9 24.6 %collective-permute-start.10 = (bf16[128,128,128]{2,1,0:T(8,128)(2,1)}, bf16[128,128,128]{2,1,0:T(8,128)(2,1)}, u32[]{:S(2)}, u32[]{:S(2)}) collective-permute-start(bf16[128,128,128]{2,1,0:T(8,128)(2,1)} %collective-permute-done.4.own), channel_id=1, source_target_pairs={{0,4},{4,0},{1,5},{5,1},{2,6},{6,2},{3,7},{7,3},{11,15},{15,11},{1... | collective-permute-start | bytes 12582920 | tf_op jit(solution)/shard_map/ppermute | solution.py:581
  98.4 95.5 %collective-permute-start.7 = (bf16[128,128,128]{2,1,0:T(8,128)(2,1)}, bf16[128,128,128]{2,1,0:T(8,128)(2,1)}, u32[]{:S(2)}, u32[]{:S(2)}) collective-permute-start(bf16[128,128,128]{2,1,0:T(8,128)(2,1)} %collective-permute-done.2.own), channel_id=1, source_target_pairs={{0,1},{4,5},{1,2},{5,6},{2,3},{6,7},{3,11},{7,15},{11,10},{15,14},... | collective-permute-start | bytes 12582920 | tf_op jit(solution)/shard_map/ppermute | solution.py:542
  100.0 93.9 %collective-permute-start.9 = (bf16[128,128,128]{2,1,0:T(8,128)(2,1)}, bf16[128,128,128]{2,1,0:T(8,128)(2,1)}, u32[]{:S(2)}, u32[]{:S(2)}) collective-permute-start(bf16[128,128,128]{2,1,0:T(8,128)(2,1)} %collective-permute-done.4.own), channel_id=1, source_target_pairs={{1,0},{5,4},{2,1},{6,5},{3,2},{7,6},{11,3},{15,7},{10,11},{14,15},... | collective-permute-start | bytes 12582920 | tf_op jit(solution)/shard_map/ppermute | solution.py:542
  100.6 92.0 %collective-permute-start.6 = (bf16[2,128,128]{2,1,0:T(8,128)(2,1)S(1)}, bf16[2,128,128]{2,1,0:T(8,128)(2,1)S(1)}, u32[]{:S(2)}, u32[]{:S(2)}) collective-permute-start(bf16[2,128,128]{2,1,0:T(8,128)(2,1)S(1)} %collective-permute-done.1.mask), channel_id=1, source_target_pairs={{0,1},{4,5},{1,2},{5,6},{2,3},{6,7},{3,11},{7,15},{11,10},{15,14},... | collective-permute-start | bytes 196616 | tf_op jit(solution)/shard_map/ppermute | solution.py:542
  105.4 88.5 %collective-permute-start.8 = (bf16[2,128,128]{2,1,0:T(8,128)(2,1)S(1)}, bf16[2,128,128]{2,1,0:T(8,128)(2,1)S(1)}, u32[]{:S(2)}, u32[]{:S(2)}) collective-permute-start(bf16[2,128,128]{2,1,0:T(8,128)(2,1)S(1)} %collective-permute-done.3.mask), channel_id=1, source_target_pairs={{1,0},{5,4},{2,1},{6,5},{3,2},{7,6},{11,3},{15,7},{10,11},{14,15},... | collective-permute-start | bytes 196616 | tf_op jit(solution)/shard_map/ppermute | solution.py:542
  193.9 7.5 %collective-permute-start.17 = (bf16[128,128,128]{2,1,0:T(8,128)(2,1)}, bf16[128,128,128]{2,1,0:T(8,128)(2,1)}, u32[]{:S(2)}, u32[]{:S(2)}) collective-permute-start(bf16[128,128,128]{2,1,0:T(8,128)(2,1)} %collective-permute-done.7.own), channel_id=1, source_target_pairs={{0,4},{4,0},{1,5},{5,1},{2,6},{6,2},{3,7},{7,3},{11,15},{15,11},{1... | collective-permute-start | bytes 12582920 | tf_op jit(solution)/shard_map/ppermute | solution.py:581
  193.9 24.8 %collective-permute-start.16 = (bf16[128,128,128]{2,1,0:T(8,128)(2,1)}, bf16[128,128,128]{2,1,0:T(8,128)(2,1)}, u32[]{:S(2)}, u32[]{:S(2)}) collective-permute-start(bf16[128,128,128]{2,1,0:T(8,128)(2,1)} %collective-permute-done.9.own), channel_id=1, source_target_pairs={{0,4},{4,0},{1,5},{5,1},{2,6},{6,2},{3,7},{7,3},{11,15},{15,11},{1... | collective-permute-start | bytes 12582920 | tf_op jit(solution)/shard_map/ppermute | solution.py:581
  194.4 95.5 %collective-permute-start.13 = (bf16[128,128,128]{2,1,0:T(8,128)(2,1)}, bf16[128,128,128]{2,1,0:T(8,128)(2,1)}, u32[]{:S(2)}, u32[]{:S(2)}) collective-permute-start(bf16[128,128,128]{2,1,0:T(8,128)(2,1)} %collective-permute-done.7.own), channel_id=1, source_target_pairs={{0,1},{4,5},{1,2},{5,6},{2,3},{6,7},{3,11},{7,15},{11,10},{15,14},... | collective-permute-start | bytes 12582920 | tf_op jit(solution)/shard_map/ppermute | solution.py:542
  196.0 93.9 %collective-permute-start.15 = (bf16[128,128,128]{2,1,0:T(8,128)(2,1)}, bf16[128,128,128]{2,1,0:T(8,128)(2,1)}, u32[]{:S(2)}, u32[]{:S(2)}) collective-permute-start(bf16[128,128,128]{2,1,0:T(8,128)(2,1)} %collective-permute-done.9.own), channel_id=1, source_target_pairs={{1,0},{5,4},{2,1},{6,5},{3,2},{7,6},{11,3},{15,7},{10,11},{14,15},... | collective-permute-start | bytes 12582920 | tf_op jit(solution)/shard_map/ppermute | solution.py:542
  196.6 92.0 %collective-permute-start.12 = (bf16[2,128,128]{2,1,0:T(8,128)(2,1)S(1)}, bf16[2,128,128]{2,1,0:T(8,128)(2,1)S(1)}, u32[]{:S(2)}, u32[]{:S(2)}) collective-permute-start(bf16[2,128,128]{2,1,0:T(8,128)(2,1)S(1)} %collective-permute-done.6.mask), channel_id=1, source_target_pairs={{0,1},{4,5},{1,2},{5,6},{2,3},{6,7},{3,11},{7,15},{11,10},{15,14},... | collective-permute-start | bytes 196616 | tf_op jit(solution)/shard_map/ppermute | solution.py:542
  201.4 88.5 %collective-permute-start.14 = (bf16[2,128,128]{2,1,0:T(8,128)(2,1)S(1)}, bf16[2,128,128]{2,1,0:T(8,128)(2,1)S(1)}, u32[]{:S(2)}, u32[]{:S(2)}) collective-permute-start(bf16[2,128,128]{2,1,0:T(8,128)(2,1)S(1)} %collective-permute-done.8.mask), channel_id=1, source_target_pairs={{1,0},{5,4},{2,1},{6,5},{3,2},{7,6},{11,3},{15,7},{10,11},{14,15},... | collective-permute-start | bytes 196616 | tf_op jit(solution)/shard_map/ppermute | solution.py:542
  288.6 8.2 %copy-start.4 = (bf16[2,128,128]{2,1,0:T(8,128)(2,1)}, bf16[2,128,128]{2,1,0:T(8,128)(2,1)S(1)}, u32[]{:S(2)}) copy-start(bf16[2,128,128]{2,1,0:T(8,128)(2,1)S(1)} %collective-permute-done.12.mask) | copy-start | bytes 196612
  289.9 8.4 %copy-start.6 = (bf16[2,128,128]{2,1,0:T(8,128)(2,1)}, bf16[2,128,128]{2,1,0:T(8,128)(2,1)S(1)}, u32[]{:S(2)}) copy-start(bf16[2,128,128]{2,1,0:T(8,128)(2,1)S(1)} %collective-permute-done.14.mask) | copy-start | bytes 196612
  289.9 10.7 %collective-permute-start.22 = (bf16[128,128,128]{2,1,0:T(8,128)(2,1)}, bf16[128,128,128]{2,1,0:T(8,128)(2,1)}, u32[]{:S(2)}, u32[]{:S(2)}) collective-permute-start(bf16[128,128,128]{2,1,0:T(8,128)(2,1)} %collective-permute-done.13.own), channel_id=1, source_target_pairs={{0,4},{4,0},{1,5},{5,1},{2,6},{6,2},{3,7},{7,3},{11,15},{15,11},{1... | collective-permute-start | bytes 12582920 | tf_op jit(solution)/shard_map/ppermute | solution.py:581
  289.9 28.1 %collective-permute-start.21 = (bf16[128,128,128]{2,1,0:T(8,128)(2,1)}, bf16[128,128,128]{2,1,0:T(8,128)(2,1)}, u32[]{:S(2)}, u32[]{:S(2)}) collective-permute-start(bf16[128,128,128]{2,1,0:T(8,128)(2,1)} %collective-permute-done.15.own), channel_id=1, source_target_pairs={{0,4},{4,0},{1,5},{5,1},{2,6},{6,2},{3,7},{7,3},{11,15},{15,11},{1... | collective-permute-start | bytes 12582920 | tf_op jit(solution)/shard_map/ppermute | solution.py:581
  296.8 49.2 %collective-permute-start.19 = (bf16[64,128,128]{2,1,0:T(8,128)(2,1)}, bf16[64,128,128]{2,1,0:T(8,128)(2,1)}, u32[]{:S(2)}, u32[]{:S(2)}) collective-permute-start(bf16[64,128,128]{2,1,0:T(8,128)(2,1)} %slice.74), channel_id=1, source_target_pairs={{0,1},{4,5},{1,2},{5,6},{2,3},{6,7},{3,11},{7,15},{11,10},{15,14},... | collective-permute-start | bytes 6291464 | tf_op jit(solution)/shard_map/ppermute | solution.py:542
  298.2 47.7 %collective-permute-start.20 = (bf16[64,128,128]{2,1,0:T(8,128)(2,1)}, bf16[64,128,128]{2,1,0:T(8,128)(2,1)S(1)}, u32[]{:S(2)}, u32[]{:S(2)}) collective-permute-start(bf16[64,128,128]{2,1,0:T(8,128)(2,1)} %slice.75), channel_id=1, source_target_pairs={{1,0},{5,4},{2,1},{6,5},{3,2},{7,6},{11,3},{15,7},{10,11},{14,15},... | collective-permute-start | bytes 6291464 | tf_op jit(solution)/shard_map/ppermute | solution.py:542
  298.9 47.0 %collective-permute-start.18 = (bf16[2,128,128]{2,1,0:T(8,128)(2,1)}, bf16[2,128,128]{2,1,0:T(8,128)(2,1)S(1)}, u32[]{:S(2)}, u32[]{:S(2)}) collective-permute-start(bf16[2,128,128]{2,1,0:T(8,128)(2,1)} %copy-done.4), channel_id=1, source_target_pairs={{0,1},{4,5},{1,2},{5,6},{2,3},{6,7},{3,11},{7,15},{11,10},{15,14},... | collective-permute-start | bytes 196616 | tf_op jit(solution)/shard_map/ppermute | solution.py:542
  300.6 0.9 copy-start.5
  301.5 16.6 %copy-start.7 = (bf16[2,128,128]{2,1,0:T(8,128)(2,1)S(1)}, bf16[2,128,128]{2,1,0:T(8,128)(2,1)}, u32[]{:S(2)}) copy-start(bf16[2,128,128]{2,1,0:T(8,128)(2,1)} %copy-done.6) | copy-start | bytes 196612
  346.0 6.8 collective-permute-start.24
  346.0 16.7 %collective-permute-start.23 = (bf16[64,128,128]{2,1,0:T(8,128)(2,1)S(1)}, bf16[64,128,128]{2,1,0:T(8,128)(2,1)}, u32[]{:S(2)}, u32[]{:S(2)}) collective-permute-start(bf16[64,128,128]{2,1,0:T(8,128)(2,1)S(1)} %collective-permute-done.20.own), channel_id=1, source_target_pairs={{0,4},{4,0},{1,5},{5,1},{2,6},{6,2},{3,7},{7,3},{11,15},{15,11},{1... | collective-permute-start | bytes 6291464 | tf_op jit(solution)/shard_map/ppermute | solution.py:584
  393.9 20.5 %collective-permute-start.26 = (bf16[3,32,256,128]{3,2,1,0:T(8,128)(2,1)}, bf16[3,32,256,128]{3,2,1,0:T(8,128)(2,1)}, u32[]{:S(2)}, u32[]{:S(2)}) collective-permute-start(bf16[3,32,256,128]{3,2,1,0:T(8,128)(2,1)} %get-tuple-element.271), channel_id=1, source_target_pairs={{0,4},{4,0},{1,5},{5,1},{2,6},{6,2},{3,7},{7,3},{11,15},{15,11},{1... | collective-permute-start | bytes 18874376 | tf_op jit(solution)/shard_map/ppermute | solution.py:595
  394.1 32.7 %copy-start.1 = (bf16[128,128]{1,0:T(8,128)(2,1)S(1)}, bf16[128,128]{1,0:T(8,128)(2,1)}, u32[]{:S(2)}) copy-start(bf16[128,128]{1,0:T(8,128)(2,1)} %copy-done) | copy-start | bytes 98308
  413.9 10.2 %collective-permute-start.25 = (bf16[3,32,256,128]{3,2,1,0:T(8,128)(2,1)S(1)}, bf16[3,32,256,128]{3,2,1,0:T(8,128)(2,1)S(1)}, u32[]{:S(2)}, u32[]{:S(2)}) collective-permute-start(bf16[3,32,256,128]{3,2,1,0:T(8,128)(2,1)S(1)} %get-tuple-element.270), channel_id=1, source_target_pairs={{0,4},{4,0},{1,5},{5,1},{2,6},{6,2},{3,7},{7,3},{11,15},{15,11},{1... | collective-permute-start | bytes 18874376 | tf_op jit(solution)/shard_map/ppermute | solution.py:595
  424.1 2.6 copy-start.9
  675.4 24.4 %copy-start.2 = (bf16[128,128]{1,0:T(8,128)(2,1)S(1)}, bf16[128,128]{1,0:T(8,128)(2,1)}, u32[]{:S(2)}) copy-start(bf16[128,128]{1,0:T(8,128)(2,1)} %get-tuple-element.282.gate) | copy-start | bytes 98308
  675.4 24.4 %copy-start.3 = (bf16[128,128]{1,0:T(8,128)(2,1)S(1)}, bf16[128,128]{1,0:T(8,128)(2,1)}, u32[]{:S(2)}) copy-start(bf16[128,128]{1,0:T(8,128)(2,1)} %get-tuple-element.281.proj) | copy-start | bytes 98308
  692.5 7.2 %collective-permute-start.27 = (bf16[128,128,128]{2,1,0:T(8,128)(2,1)S(1)}, bf16[128,128,128]{2,1,0:T(8,128)(2,1)S(1)}, u32[]{:S(2)}, u32[]{:S(2)}) collective-permute-start(bf16[128,128,128]{2,1,0:T(8,128)(2,1)S(1)} %get-tuple-element.274), channel_id=1, source_target_pairs={{0,4},{4,0},{1,5},{5,1},{2,6},{6,2},{3,7},{7,3},{11,15},{15,11},{1... | collective-permute-start | bytes 12582920 | tf_op jit(solution)/shard_map/ppermute | solution.py:600

commit v7 on v5

--- a/solution.py
+++ b/solution.py
@@ -252,7 +252,7 @@
             send[slot, d] = sums[2 * TILE :, lanes].astype(jnp.bfloat16)
 
 
-TOGETHER = 2
+TOGETHER = 4
 PARTS = 2
 
 
@@ -369,7 +369,7 @@
     )(at, states, mask, *fixed, *parts)
 
 
-CHANNELS = 8
+CHANNELS = 16
 
 
 def incoming_kernel(at, pairs, keep, send):

time: 557 us -> 544 us (0.977)
  Pallas kernels: 299 us -> 287 us
    pallas_call x2, Pallas kernels: 41.4 us -> 33.6 us  [outgoing(): pl.pallas_call(outgoing_kernel, grid_spec=pltpu.PrefetchScalarGridSpec(nu...]
where the time goes in v7:
time: 544 us; the launch traced here: 543 us
  Pallas kernels  287 us (53%)
  waiting for transfers between devices  211 us (39%)
  local copies, waits for them, and re-layouts  21.1 us (4%)
  starting transfers between devices  20.1 us (4%)
    ppermute x15, waiting for transfers between devices, hop(): return [lax.ppermute(value, BOTH, pairs) for value in values]  182 us
    pallas_call x9, Pallas kernels, enter(): pl.pallas_call(enter_kernel, grid_spec=pltpu.PrefetchScalarGridSpec(num_s...  136 us
    pallas_call x1, Pallas kernels, middle(): pl.pallas_call(middle_kernel, grid_spec=pltpu.PrefetchScalarGridSpec(num_...  91.7 us
    pallas_call x2, Pallas kernels, outgoing(): pl.pallas_call(outgoing_kernel, grid_spec=pltpu.PrefetchScalarGridSpec(nu...  33.6 us
    ppermute x15, starting transfers between devices, hop(): return [lax.ppermute(value, BOTH, pairs) for value in values]  16.3 us
    pallas_call x1, Pallas kernels, incoming(): pl.pallas_call(incoming_kernel, grid_spec=pltpu.PrefetchScalarGridSpec(nu...  12.8 us
    pallas_call x1, Pallas kernels, leave(): pl.pallas_call(leave_kernel, grid_spec=pltpu.PrefetchScalarGridSpec(num_s...  12.4 us
  transfers between devices with their start and end apart: 28, of which 12 were waited for; matrix products, arithmetic and copies ran while one was open for 3% of the time, Pallas kernels for 26%

profile of v7, /device:TPU:0, one launch (start us, length us, event | category | flops | bytes accessed | tf_op | source)
XLA Modules:
  0.0 543.0 jit_solution(17396068567825984657)
XLA Ops:
  0.5 2.6 collective-permute-start.2
  3.0 0.8 convert_element_type.6
  4.1 0.9 fusion.10
  5.0 0.9 fusion.11
  6.4 0.8 fusion.13
  7.2 0.8 slice_bitcast_fusion
  8.7 0.8 fusion.12
  11.4 0.8 slice_bitcast_fusion.3
  12.1 0.8 slice_bitcast_fusion.2
  13.5 0.8 convert_bitcast_fusion
  14.6 1.9 collective-permute-start.1
  16.8 2.2 copy-done.6
  19.0 16.3 %enter.9 = (bf16[50,128,2048]{2,1,0:T(8,128)(2,1)}, bf16[4,32,512,128]{3,2,1,0:T(8,128)(2,1)}, bf16[4,32,512,128]{3,2,1,0:T(8,128)(2,1)}, bf16[4,64,384,128]{3,2,1,0:T(8,128)(2,1)}, bf16[4,4,128,128]{3,2,1,0:T(8,128)(2,1)S(1)}) custom-call(s32[6]{0:T(128)S(1)} %stack.240.at, bf16[128,128,128]{2,1,0:T(8,128)(2,1)S(1)} %copy-done.6, ...), custom_call_target="tpu_custom_call" | custom-call | flops 4294967296 | bytes 33554432 | tf_op jit(solution)/shard_map/enter/pallas_call | solution.py:206
  35.3 60.5 %collective-permute-done.1.mask = bf16[2,128,128]{2,1,0:T(8,128)(2,1)S(1)} collective-permute-done((bf16[2,128,128]{2,1,0:T(8,128)(2,1)S(1)}, bf16[2,128,128]{2,1,0:T(8,128)(2,1)S(1)}, u32[]{:S(2)}, u32[]{:S(2)}) %collective-permute-start.1) | collective-permute-done | bytes 65568 | tf_op jit(solution)/shard_map/ppermute | solution.py:536
  95.8 1.5 collective-permute-done.3.mask
  98.4 1.6 collective-permute-start.7
  100.6 1.6 collective-permute-start.6
  102.2 3.2 collective-permute-done.11.sib
  105.7 16.9 %enter.10 = (bf16[50,128,2048]{2,1,0:T(8,128)(2,1)}, bf16[4,32,512,128]{3,2,1,0:T(8,128)(2,1)}, bf16[4,32,512,128]{3,2,1,0:T(8,128)(2,1)}, bf16[4,64,384,128]{3,2,1,0:T(8,128)(2,1)}, bf16[4,4,128,128]{3,2,1,0:T(8,128)(2,1)S(1)}) custom-call(s32[6]{0:T(128)S(1)} %stack.255.at, ...), custom_call_target="tpu_custom_call", output_to_operand_aliasing={{0}: (8, {}), {1}: (9, {}), {2}: (10, {}), {3}: (11, {}), {... | custom-call | flops 4294967296 | bytes 33554432 | tf_op jit(solution)/shard_map/enter/pallas_call | solution.py:206
  122.6 16.9 %enter.11 = (bf16[50,128,2048]{2,1,0:T(8,128)(2,1)}, bf16[4,32,512,128]{3,2,1,0:T(8,128)(2,1)}, bf16[4,32,512,128]{3,2,1,0:T(8,128)(2,1)}, bf16[4,64,384,128]{3,2,1,0:T(8,128)(2,1)}, bf16[4,4,128,128]{3,2,1,0:T(8,128)(2,1)S(1)}) custom-call(s32[6]{0:T(128)S(1)} %stack.249.at, ...), custom_call_target="tpu_custom_call", output_to_operand_aliasing={{0}: (8, {}), {1}: (9, {}), {2}: (10, {}), {3}: (11, {}), {... | custom-call | flops 4294967296 | bytes 33554432 | tf_op jit(solution)/shard_map/enter/pallas_call | solution.py:206
  139.4 53.1 %collective-permute-done.6.mask = bf16[2,128,128]{2,1,0:T(8,128)(2,1)S(1)} collective-permute-done((bf16[2,128,128]{2,1,0:T(8,128)(2,1)S(1)}, bf16[2,128,128]{2,1,0:T(8,128)(2,1)S(1)}, u32[]{:S(2)}, u32[]{:S(2)}) %collective-permute-start.6) | collective-permute-done | bytes 65568 | tf_op jit(solution)/shard_map/ppermute | solution.py:536
  192.6 1.3 collective-permute-done.8.mask
  194.4 1.6 collective-permute-start.13
  196.6 1.6 collective-permute-start.12
  198.2 3.2 collective-permute-done.17.sib
  201.8 16.8 %enter.12 = (bf16[50,128,2048]{2,1,0:T(8,128)(2,1)}, bf16[4,32,512,128]{3,2,1,0:T(8,128)(2,1)}, bf16[4,32,512,128]{3,2,1,0:T(8,128)(2,1)}, bf16[4,64,384,128]{3,2,1,0:T(8,128)(2,1)}, bf16[4,4,128,128]{3,2,1,0:T(8,128)(2,1)S(1)}) custom-call(s32[6]{0:T(128)S(1)} %stack.267.at, ...), custom_call_target="tpu_custom_call", output_to_operand_aliasing={{0}: (8, {}), {1}: (9, {}), {2}: (10, {}), {3}: (11, {}), {... | custom-call | flops 4294967296 | bytes 33554432 | tf_op jit(solution)/shard_map/enter/pallas_call | solution.py:206
  218.7 16.6 %enter.13 = (bf16[50,128,2048]{2,1,0:T(8,128)(2,1)}, bf16[4,32,512,128]{3,2,1,0:T(8,128)(2,1)}, bf16[4,32,512,128]{3,2,1,0:T(8,128)(2,1)}, bf16[4,64,384,128]{3,2,1,0:T(8,128)(2,1)}, bf16[4,4,128,128]{3,2,1,0:T(8,128)(2,1)S(1)}) custom-call(s32[6]{0:T(128)S(1)} %stack.261.at, ...), custom_call_target="tpu_custom_call", output_to_operand_aliasing={{0}: (8, {}), {1}: (9, {}), {2}: (10, {}), {3}: (11, {}), {... | custom-call | flops 4294967296 | bytes 33554432 | tf_op jit(solution)/shard_map/enter/pallas_call | solution.py:206
  235.3 53.2 %collective-permute-done.12.mask = bf16[2,128,128]{2,1,0:T(8,128)(2,1)S(1)} collective-permute-done((bf16[2,128,128]{2,1,0:T(8,128)(2,1)S(1)}, bf16[2,128,128]{2,1,0:T(8,128)(2,1)S(1)}, u32[]{:S(2)}, u32[]{:S(2)}) %collective-permute-start.12) | collective-permute-done | bytes 65568 | tf_op jit(solution)/shard_map/ppermute | solution.py:536
  288.6 1.3 collective-permute-done.14.mask
  290.4 3.2 slice.74
  293.6 3.2 slice.75
  296.8 1.5 collective-permute-start.19
  299.0 1.7 collective-permute-start.18
  300.6 0.9 copy-done.3
  301.5 16.7 %enter.14 = (bf16[50,128,2048]{2,1,0:T(8,128)(2,1)}, bf16[4,32,512,128]{3,2,1,0:T(8,128)(2,1)}, bf16[4,32,512,128]{3,2,1,0:T(8,128)(2,1)}, bf16[4,64,384,128]{3,2,1,0:T(8,128)(2,1)}, bf16[4,4,128,128]{3,2,1,0:T(8,128)(2,1)S(1)}) custom-call(s32[6]{0:T(128)S(1)} %stack.279.at, ...), custom_call_target="tpu_custom_call", output_to_operand_aliasing={{0}: (8, {}), {1}: (9, {}), {2}: (10, {}), {3}: (11, {}), {... | custom-call | flops 4294967296 | bytes 33554432 | tf_op jit(solution)/shard_map/enter/pallas_call | solution.py:206
  318.2 16.7 %enter.15 = (bf16[50,128,2048]{2,1,0:T(8,128)(2,1)}, bf16[4,32,512,128]{3,2,1,0:T(8,128)(2,1)}, bf16[4,32,512,128]{3,2,1,0:T(8,128)(2,1)}, bf16[4,64,384,128]{3,2,1,0:T(8,128)(2,1)}, bf16[4,4,128,128]{3,2,1,0:T(8,128)(2,1)S(1)}) custom-call(s32[6]{0:T(128)S(1)} %stack.273.at, ...), custom_call_target="tpu_custom_call", output_to_operand_aliasing={{0}: (8, {}), {1}: (9, {}), {2}: (10, {}), {3}: (11, {}), {... | custom-call | flops 4294967296 | bytes 33554432 | tf_op jit(solution)/shard_map/enter/pallas_call | solution.py:206
  334.9 11.1 %collective-permute-done.18.mask = bf16[2,128,128]{2,1,0:T(8,128)(2,1)S(1)} collective-permute-done((bf16[2,128,128]{2,1,0:T(8,128)(2,1)}, bf16[2,128,128]{2,1,0:T(8,128)(2,1)S(1)}, u32[]{:S(2)}, u32[]{:S(2)}) %collective-permute-start.18) | collective-permute-done | bytes 65568 | tf_op jit(solution)/shard_map/ppermute | solution.py:536
  346.7 6.1 %collective-permute-done.24.sib = bf16[64,128,128]{2,1,0:T(8,128)(2,1)} collective-permute-done((bf16[64,128,128]{2,1,0:T(8,128)(2,1)}, bf16[64,128,128]{2,1,0:T(8,128)(2,1)}, u32[]{:S(2)}, u32[]{:S(2)}) %collective-permute-start.24) | collective-permute-done | bytes 2097184 | tf_op jit(solution)/shard_map/ppermute | solution.py:575
  352.8 10.0 %enter.16 = (bf16[50,128,2048]{2,1,0:T(8,128)(2,1)}, bf16[4,32,512,128]{3,2,1,0:T(8,128)(2,1)}, bf16[4,32,512,128]{3,2,1,0:T(8,128)(2,1)}, bf16[4,64,384,128]{3,2,1,0:T(8,128)(2,1)}, bf16[4,4,128,128]{3,2,1,0:T(8,128)(2,1)S(1)}) custom-call(s32[6]{0:T(128)S(1)} %stack.230.at, ...), custom_call_target="tpu_custom_call", output_to_operand_aliasing={{0}: (8, {}), {1}: (9, {}), {2}: (10, {}), {3}: (11, {}), {... | custom-call | flops 2147483648 | bytes 16777216 | tf_op jit(solution)/shard_map/enter/pallas_call | solution.py:206
  362.7 9.6 %enter.17 = (bf16[50,128,2048]{2,1,0:T(8,128)(2,1)}, bf16[4,32,512,128]{3,2,1,0:T(8,128)(2,1)}, bf16[4,32,512,128]{3,2,1,0:T(8,128)(2,1)}, bf16[4,64,384,128]{3,2,1,0:T(8,128)(2,1)}, bf16[4,4,128,128]{3,2,1,0:T(8,128)(2,1)S(1)}) custom-call(s32[6]{0:T(128)S(1)} %stack.230.at, ...), custom_call_target="tpu_custom_call", output_to_operand_aliasing={{0}: (8, {}), {1}: (9, {}), {2}: (10, {}), {3}: (11, {}), {... | custom-call | flops 2147483648 | bytes 16777216 | tf_op jit(solution)/shard_map/enter/pallas_call | solution.py:206
  372.3 17.7 %outgoing.3 = (bf16[3,32,256,128]{3,2,1,0:T(8,128)(2,1)S(1)}, bf16[3,32,256,128]{3,2,1,0:T(8,128)(2,1)}) custom-call(s32[2]{0:T(128)S(1)} %pad_add_fusion.1.at, bf16[4,32,512,128]{3,2,1,0:T(8,128)(2,1)} %get-tuple-element.257.left, bf16[4,64,384,128]{3,2,1,0:T(8,128)(2,1)} %get-tuple-element.255.right), custom_call_target="tpu_custom_call" | custom-call | flops 6442450944 | bytes 42598400 | tf_op jit(solution)/shard_map/outgoing/pallas_call | solution.py:266
  390.1 15.9 %outgoing.2 = (bf16[3,32,256,128]{3,2,1,0:T(8,128)(2,1)S(1)}, bf16[3,32,256,128]{3,2,1,0:T(8,128)(2,1)S(1)}) custom-call(s32[2]{0:T(128)S(1)} %pad_add_fusion.1.at, bf16[4,32,512,128]{3,2,1,0:T(8,128)(2,1)} %get-tuple-element.254.left, bf16[4,64,384,128]{3,2,1,0:T(8,128)(2,1)} %get-tuple-element.255.right), custom_call_target="tpu_custom_call" | custom-call | flops 6442450944 | bytes 42598400 | tf_op jit(solution)/shard_map/outgoing/pallas_call | solution.py:266
  406.6 9.7 %collective-permute-done.25.rest_2_ = bf16[3,32,256,128]{3,2,1,0:T(8,128)(2,1)S(1)} collective-permute-done((bf16[3,32,256,128]{3,2,1,0:T(8,128)(2,1)S(1)}, bf16[3,32,256,128]{3,2,1,0:T(8,128)(2,1)S(1)}, u32[]{:S(2)}, u32[]{:S(2)}) %collective-permute-start.25) | collective-permute-done | bytes 6291488 | tf_op jit(solution)/shard_map/ppermute | solution.py:587
  416.3 2.6 copy-done.7
  418.9 91.7 %middle.1 = (bf16[3,128,256,128]{3,2,1,0:T(8,128)(2,1)}, bf16[20,128,2048]{2,1,0:T(8,128)(2,1)}) custom-call(s32[4]{0:T(128)S(1)} %pad_add_fusion.at, bf16[50,128,2048]{2,1,0:T(8,128)(2,1)} %get-tuple-element.243.state, bf16[4,4,128,128]{3,2,1,0:T(8,128)(2,1)S(1)} %get-tuple-element.244.mask, f32[128,128]{1,0:T(8,128)S(1)} %broadcast_in_dim.55.gain.gain0, ...), custom_call_target="tpu_custom_call" | custom-call | flops 12884901888 | bytes 100663296 | tf_op jit(solution)/shard_map/middle/pallas_call | solution.py:325
  510.6 12.8 %incoming.1 = (bf16[128,128,128]{2,1,0:T(8,128)(2,1)S(1)}, bf16[128,128,128]{2,1,0:T(8,128)(2,1)S(1)}) custom-call(s32[4]{0:T(128)S(1)} %pad_add_fusion.at, bf16[3,128,256,128]{3,2,1,0:T(8,128)(2,1)} %get-tuple-element.261.pairs), custom_call_target="tpu_custom_call" | custom-call | flops 2147483648 | bytes 37748736 | tf_op jit(solution)/shard_map/incoming/pallas_call | solution.py:389
  523.9 6.8 %collective-permute-done.27.got = bf16[128,128,128]{2,1,0:T(8,128)(2,1)S(1)} collective-permute-done((bf16[128,128,128]{2,1,0:T(8,128)(2,1)S(1)}, bf16[128,128,128]{2,1,0:T(8,128)(2,1)S(1)}, u32[]{:S(2)}, u32[]{:S(2)}) %collective-permute-start.27) | collective-permute-done | bytes 4194336 | tf_op jit(solution)/shard_map/ppermute | solution.py:592
  530.7 12.4 %leave.1 = bf16[128,128,128]{2,1,0:T(8,128)(2,1)} custom-call(s32[4]{0:T(128)S(1)} %pad_add_fusion.at, bf16[128,128,128]{2,1,0:T(8,128)(2,1)S(1)} %get-tuple-element.262.kept, bf16[128,128,128]{2,1,0:T(8,128)(2,1)S(1)} %collective-permute-done.27.got, bf16[20,128,2048]{2,1,0:T(8,128)(2,1)} %get-tuple-element.264.state, ...), custom_call_target="tpu_custom_call" | custom-call | flops 1073741824 | bytes 20971520 | tf_op jit(solution)/shard_map/leave/pallas_call | solution.py:433
  (100 shorter events, 11.5 us)
Async XLA Ops:
  0.0 16.7 %collective-permute-start.5 = (bf16[128,128,128]{2,1,0:T(8,128)(2,1)}, bf16[128,128,128]{2,1,0:T(8,128)(2,1)}, u32[]{:S(2)}, u32[]{:S(2)}) collective-permute-start(bf16[128,128,128]{2,1,0:T(8,128)(2,1)} %own.1), channel_id=1, source_target_pairs={{0,4},{4,0},{1,5},{5,1},{2,6},{6,2},{3,7},{7,3},{11,15},{15,11},{1... | collective-permute-start | bytes 12582920 | tf_op jit(solution)/shard_map/ppermute | solution.py:538
  0.5 96.9 %collective-permute-start.2 = (bf16[128,128,128]{2,1,0:T(8,128)(2,1)}, bf16[128,128,128]{2,1,0:T(8,128)(2,1)}, u32[]{:S(2)}, u32[]{:S(2)}) collective-permute-start(bf16[128,128,128]{2,1,0:T(8,128)(2,1)} %own.1), channel_id=1, source_target_pairs={{0,1},{4,5},{1,2},{5,6},{2,3},{6,7},{3,11},{7,15},{11,10},{15,14},... | collective-permute-start | bytes 12582920 | tf_op jit(solution)/shard_map/ppermute | solution.py:536
  3.0 94.3 %collective-permute-start.4 = (bf16[128,128,128]{2,1,0:T(8,128)(2,1)}, bf16[128,128,128]{2,1,0:T(8,128)(2,1)}, u32[]{:S(2)}, u32[]{:S(2)}) collective-permute-start(bf16[128,128,128]{2,1,0:T(8,128)(2,1)} %own.1), channel_id=1, source_target_pairs={{1,0},{5,4},{2,1},{6,5},{3,2},{7,6},{11,3},{15,7},{10,11},{14,15},... | collective-permute-start | bytes 12582920 | tf_op jit(solution)/shard_map/ppermute | solution.py:536
  3.9 10.7 %collective-permute-start = (bf16[128,128]{1,0:T(8,128)(2,1)S(1)}, bf16[128,128]{1,0:T(8,128)(2,1)S(1)}, u32[]{:S(2)}, u32[]{:S(2)}) collective-permute-start(bf16[128,128]{1,0:T(8,128)(2,1)S(1)} %convert_element_type.6), channel_id=1, source_target_pairs={{0,4},{4,0},{1,5},{5,1},{2,6},{6,2},{3,7},{7,3},{11,15},{15,11},{1... | collective-permute-start | bytes 98312 | tf_op jit(solution)/shard_map/ppermute | solution.py:484
  14.6 81.2 %collective-permute-start.1 = (bf16[2,128,128]{2,1,0:T(8,128)(2,1)S(1)}, bf16[2,128,128]{2,1,0:T(8,128)(2,1)S(1)}, u32[]{:S(2)}, u32[]{:S(2)}) collective-permute-start(bf16[2,128,128]{2,1,0:T(8,128)(2,1)S(1)} %maximum_select_fusion.mask), channel_id=1, source_target_pairs={{0,1},{4,5},{1,2},{5,6},{2,3},{6,7},{3,11},{7,15},{11,10},{15,14},... | collective-permute-start | bytes 196616 | tf_op jit(solution)/shard_map/ppermute | solution.py:536
  16.5 80.9 %collective-permute-start.3 = (bf16[2,128,128]{2,1,0:T(8,128)(2,1)S(1)}, bf16[2,128,128]{2,1,0:T(8,128)(2,1)S(1)}, u32[]{:S(2)}, u32[]{:S(2)}) collective-permute-start(bf16[2,128,128]{2,1,0:T(8,128)(2,1)S(1)} %maximum_select_fusion.mask), channel_id=1, source_target_pairs={{1,0},{5,4},{2,1},{6,5},{3,2},{7,6},{11,3},{15,7},{10,11},{14,15},... | collective-permute-start | bytes 196616 | tf_op jit(solution)/shard_map/ppermute | solution.py:536
  16.8 2.2 copy-start.6
  97.8 7.5 %collective-permute-start.11 = (bf16[128,128,128]{2,1,0:T(8,128)(2,1)}, bf16[128,128,128]{2,1,0:T(8,128)(2,1)}, u32[]{:S(2)}, u32[]{:S(2)}) collective-permute-start(bf16[128,128,128]{2,1,0:T(8,128)(2,1)} %collective-permute-done.2.own), channel_id=1, source_target_pairs={{0,4},{4,0},{1,5},{5,1},{2,6},{6,2},{3,7},{7,3},{11,15},{15,11},{1... | collective-permute-start | bytes 12582920 | tf_op jit(solution)/shard_map/ppermute | solution.py:573
  97.9 24.7 %collective-permute-start.10 = (bf16[128,128,128]{2,1,0:T(8,128)(2,1)}, bf16[128,128,128]{2,1,0:T(8,128)(2,1)}, u32[]{:S(2)}, u32[]{:S(2)}) collective-permute-start(bf16[128,128,128]{2,1,0:T(8,128)(2,1)} %collective-permute-done.4.own), channel_id=1, source_target_pairs={{0,4},{4,0},{1,5},{5,1},{2,6},{6,2},{3,7},{7,3},{11,15},{15,11},{1... | collective-permute-start | bytes 12582920 | tf_op jit(solution)/shard_map/ppermute | solution.py:573
  98.4 95.5 %collective-permute-start.7 = (bf16[128,128,128]{2,1,0:T(8,128)(2,1)}, bf16[128,128,128]{2,1,0:T(8,128)(2,1)}, u32[]{:S(2)}, u32[]{:S(2)}) collective-permute-start(bf16[128,128,128]{2,1,0:T(8,128)(2,1)} %collective-permute-done.2.own), channel_id=1, source_target_pairs={{0,1},{4,5},{1,2},{5,6},{2,3},{6,7},{3,11},{7,15},{11,10},{15,14},... | collective-permute-start | bytes 12582920 | tf_op jit(solution)/shard_map/ppermute | solution.py:536
  100.0 93.9 %collective-permute-start.9 = (bf16[128,128,128]{2,1,0:T(8,128)(2,1)}, bf16[128,128,128]{2,1,0:T(8,128)(2,1)}, u32[]{:S(2)}, u32[]{:S(2)}) collective-permute-start(bf16[128,128,128]{2,1,0:T(8,128)(2,1)} %collective-permute-done.4.own), channel_id=1, source_target_pairs={{1,0},{5,4},{2,1},{6,5},{3,2},{7,6},{11,3},{15,7},{10,11},{14,15},... | collective-permute-start | bytes 12582920 | tf_op jit(solution)/shard_map/ppermute | solution.py:536
  100.6 92.0 %collective-permute-start.6 = (bf16[2,128,128]{2,1,0:T(8,128)(2,1)S(1)}, bf16[2,128,128]{2,1,0:T(8,128)(2,1)S(1)}, u32[]{:S(2)}, u32[]{:S(2)}) collective-permute-start(bf16[2,128,128]{2,1,0:T(8,128)(2,1)S(1)} %collective-permute-done.1.mask), channel_id=1, source_target_pairs={{0,1},{4,5},{1,2},{5,6},{2,3},{6,7},{3,11},{7,15},{11,10},{15,14},... | collective-permute-start | bytes 196616 | tf_op jit(solution)/shard_map/ppermute | solution.py:536
  105.4 88.5 %collective-permute-start.8 = (bf16[2,128,128]{2,1,0:T(8,128)(2,1)S(1)}, bf16[2,128,128]{2,1,0:T(8,128)(2,1)S(1)}, u32[]{:S(2)}, u32[]{:S(2)}) collective-permute-start(bf16[2,128,128]{2,1,0:T(8,128)(2,1)S(1)} %collective-permute-done.3.mask), channel_id=1, source_target_pairs={{1,0},{5,4},{2,1},{6,5},{3,2},{7,6},{11,3},{15,7},{10,11},{14,15},... | collective-permute-start | bytes 196616 | tf_op jit(solution)/shard_map/ppermute | solution.py:536
  193.9 7.5 %collective-permute-start.17 = (bf16[128,128,128]{2,1,0:T(8,128)(2,1)}, bf16[128,128,128]{2,1,0:T(8,128)(2,1)}, u32[]{:S(2)}, u32[]{:S(2)}) collective-permute-start(bf16[128,128,128]{2,1,0:T(8,128)(2,1)} %collective-permute-done.7.own), channel_id=1, source_target_pairs={{0,4},{4,0},{1,5},{5,1},{2,6},{6,2},{3,7},{7,3},{11,15},{15,11},{1... | collective-permute-start | bytes 12582920 | tf_op jit(solution)/shard_map/ppermute | solution.py:573
  193.9 24.8 %collective-permute-start.16 = (bf16[128,128,128]{2,1,0:T(8,128)(2,1)}, bf16[128,128,128]{2,1,0:T(8,128)(2,1)}, u32[]{:S(2)}, u32[]{:S(2)}) collective-permute-start(bf16[128,128,128]{2,1,0:T(8,128)(2,1)} %collective-permute-done.9.own), channel_id=1, source_target_pairs={{0,4},{4,0},{1,5},{5,1},{2,6},{6,2},{3,7},{7,3},{11,15},{15,11},{1... | collective-permute-start | bytes 12582920 | tf_op jit(solution)/shard_map/ppermute | solution.py:573
  194.4 95.5 %collective-permute-start.13 = (bf16[128,128,128]{2,1,0:T(8,128)(2,1)}, bf16[128,128,128]{2,1,0:T(8,128)(2,1)}, u32[]{:S(2)}, u32[]{:S(2)}) collective-permute-start(bf16[128,128,128]{2,1,0:T(8,128)(2,1)} %collective-permute-done.7.own), channel_id=1, source_target_pairs={{0,1},{4,5},{1,2},{5,6},{2,3},{6,7},{3,11},{7,15},{11,10},{15,14},... | collective-permute-start | bytes 12582920 | tf_op jit(solution)/shard_map/ppermute | solution.py:536
  196.0 93.9 %collective-permute-start.15 = (bf16[128,128,128]{2,1,0:T(8,128)(2,1)}, bf16[128,128,128]{2,1,0:T(8,128)(2,1)}, u32[]{:S(2)}, u32[]{:S(2)}) collective-permute-start(bf16[128,128,128]{2,1,0:T(8,128)(2,1)} %collective-permute-done.9.own), channel_id=1, source_target_pairs={{1,0},{5,4},{2,1},{6,5},{3,2},{7,6},{11,3},{15,7},{10,11},{14,15},... | collective-permute-start | bytes 12582920 | tf_op jit(solution)/shard_map/ppermute | solution.py:536
  196.6 92.0 %collective-permute-start.12 = (bf16[2,128,128]{2,1,0:T(8,128)(2,1)S(1)}, bf16[2,128,128]{2,1,0:T(8,128)(2,1)S(1)}, u32[]{:S(2)}, u32[]{:S(2)}) collective-permute-start(bf16[2,128,128]{2,1,0:T(8,128)(2,1)S(1)} %collective-permute-done.6.mask), channel_id=1, source_target_pairs={{0,1},{4,5},{1,2},{5,6},{2,3},{6,7},{3,11},{7,15},{11,10},{15,14},... | collective-permute-start | bytes 196616 | tf_op jit(solution)/shard_map/ppermute | solution.py:536
  201.4 88.5 %collective-permute-start.14 = (bf16[2,128,128]{2,1,0:T(8,128)(2,1)S(1)}, bf16[2,128,128]{2,1,0:T(8,128)(2,1)S(1)}, u32[]{:S(2)}, u32[]{:S(2)}) collective-permute-start(bf16[2,128,128]{2,1,0:T(8,128)(2,1)S(1)} %collective-permute-done.8.mask), channel_id=1, source_target_pairs={{1,0},{5,4},{2,1},{6,5},{3,2},{7,6},{11,3},{15,7},{10,11},{14,15},... | collective-permute-start | bytes 196616 | tf_op jit(solution)/shard_map/ppermute | solution.py:536
  288.6 8.2 %copy-start.2 = (bf16[2,128,128]{2,1,0:T(8,128)(2,1)}, bf16[2,128,128]{2,1,0:T(8,128)(2,1)S(1)}, u32[]{:S(2)}) copy-start(bf16[2,128,128]{2,1,0:T(8,128)(2,1)S(1)} %collective-permute-done.12.mask) | copy-start | bytes 196612
  289.9 8.4 %copy-start.4 = (bf16[2,128,128]{2,1,0:T(8,128)(2,1)}, bf16[2,128,128]{2,1,0:T(8,128)(2,1)S(1)}, u32[]{:S(2)}) copy-start(bf16[2,128,128]{2,1,0:T(8,128)(2,1)S(1)} %collective-permute-done.14.mask) | copy-start | bytes 196612
  289.9 10.7 %collective-permute-start.22 = (bf16[128,128,128]{2,1,0:T(8,128)(2,1)}, bf16[128,128,128]{2,1,0:T(8,128)(2,1)}, u32[]{:S(2)}, u32[]{:S(2)}) collective-permute-start(bf16[128,128,128]{2,1,0:T(8,128)(2,1)} %collective-permute-done.13.own), channel_id=1, source_target_pairs={{0,4},{4,0},{1,5},{5,1},{2,6},{6,2},{3,7},{7,3},{11,15},{15,11},{1... | collective-permute-start | bytes 12582920 | tf_op jit(solution)/shard_map/ppermute | solution.py:573
  289.9 28.2 %collective-permute-start.21 = (bf16[128,128,128]{2,1,0:T(8,128)(2,1)}, bf16[128,128,128]{2,1,0:T(8,128)(2,1)}, u32[]{:S(2)}, u32[]{:S(2)}) collective-permute-start(bf16[128,128,128]{2,1,0:T(8,128)(2,1)} %collective-permute-done.15.own), channel_id=1, source_target_pairs={{0,4},{4,0},{1,5},{5,1},{2,6},{6,2},{3,7},{7,3},{11,15},{15,11},{1... | collective-permute-start | bytes 12582920 | tf_op jit(solution)/shard_map/ppermute | solution.py:573
  296.8 49.2 %collective-permute-start.19 = (bf16[64,128,128]{2,1,0:T(8,128)(2,1)}, bf16[64,128,128]{2,1,0:T(8,128)(2,1)}, u32[]{:S(2)}, u32[]{:S(2)}) collective-permute-start(bf16[64,128,128]{2,1,0:T(8,128)(2,1)} %slice.74), channel_id=1, source_target_pairs={{0,1},{4,5},{1,2},{5,6},{2,3},{6,7},{3,11},{7,15},{11,10},{15,14},... | collective-permute-start | bytes 6291464 | tf_op jit(solution)/shard_map/ppermute | solution.py:536
  298.2 47.7 %collective-permute-start.20 = (bf16[64,128,128]{2,1,0:T(8,128)(2,1)}, bf16[64,128,128]{2,1,0:T(8,128)(2,1)S(1)}, u32[]{:S(2)}, u32[]{:S(2)}) collective-permute-start(bf16[64,128,128]{2,1,0:T(8,128)(2,1)} %slice.75), channel_id=1, source_target_pairs={{1,0},{5,4},{2,1},{6,5},{3,2},{7,6},{11,3},{15,7},{10,11},{14,15},... | collective-permute-start | bytes 6291464 | tf_op jit(solution)/shard_map/ppermute | solution.py:536
  299.0 47.0 %collective-permute-start.18 = (bf16[2,128,128]{2,1,0:T(8,128)(2,1)}, bf16[2,128,128]{2,1,0:T(8,128)(2,1)S(1)}, u32[]{:S(2)}, u32[]{:S(2)}) collective-permute-start(bf16[2,128,128]{2,1,0:T(8,128)(2,1)} %copy-done.2), channel_id=1, source_target_pairs={{0,1},{4,5},{1,2},{5,6},{2,3},{6,7},{3,11},{7,15},{11,10},{15,14},... | collective-permute-start | bytes 196616 | tf_op jit(solution)/shard_map/ppermute | solution.py:536
  300.6 0.9 copy-start.3
  301.5 16.7 %copy-start.5 = (bf16[2,128,128]{2,1,0:T(8,128)(2,1)S(1)}, bf16[2,128,128]{2,1,0:T(8,128)(2,1)}, u32[]{:S(2)}) copy-start(bf16[2,128,128]{2,1,0:T(8,128)(2,1)} %copy-done.4) | copy-start | bytes 196612
  346.0 6.8 %collective-permute-start.24 = (bf16[64,128,128]{2,1,0:T(8,128)(2,1)}, bf16[64,128,128]{2,1,0:T(8,128)(2,1)}, u32[]{:S(2)}, u32[]{:S(2)}) collective-permute-start(bf16[64,128,128]{2,1,0:T(8,128)(2,1)} %collective-permute-done.19.own), channel_id=1, source_target_pairs={{0,4},{4,0},{1,5},{5,1},{2,6},{6,2},{3,7},{7,3},{11,15},{15,11},{1... | collective-permute-start | bytes 6291464 | tf_op jit(solution)/shard_map/ppermute | solution.py:575
  346.0 16.7 %collective-permute-start.23 = (bf16[64,128,128]{2,1,0:T(8,128)(2,1)S(1)}, bf16[64,128,128]{2,1,0:T(8,128)(2,1)}, u32[]{:S(2)}, u32[]{:S(2)}) collective-permute-start(bf16[64,128,128]{2,1,0:T(8,128)(2,1)S(1)} %collective-permute-done.20.own), channel_id=1, source_target_pairs={{0,4},{4,0},{1,5},{5,1},{2,6},{6,2},{3,7},{7,3},{11,15},{15,11},{1... | collective-permute-start | bytes 6291464 | tf_op jit(solution)/shard_map/ppermute | solution.py:576
  390.0 16.6 %collective-permute-start.26 = (bf16[3,32,256,128]{3,2,1,0:T(8,128)(2,1)}, bf16[3,32,256,128]{3,2,1,0:T(8,128)(2,1)}, u32[]{:S(2)}, u32[]{:S(2)}) collective-permute-start(bf16[3,32,256,128]{3,2,1,0:T(8,128)(2,1)} %get-tuple-element.260), channel_id=1, source_target_pairs={{0,4},{4,0},{1,5},{5,1},{2,6},{6,2},{3,7},{7,3},{11,15},{15,11},{1... | collective-permute-start | bytes 18874376 | tf_op jit(solution)/shard_map/ppermute | solution.py:587
  390.1 28.8 %copy-start = (bf16[128,128]{1,0:T(8,128)(2,1)S(1)}, bf16[128,128]{1,0:T(8,128)(2,1)}, u32[]{:S(2)}) copy-start(bf16[128,128]{1,0:T(8,128)(2,1)} %fusion.5.proj) | copy-start | bytes 98308
  390.1 28.8 %copy-start.1 = (bf16[128,128]{1,0:T(8,128)(2,1)S(1)}, bf16[128,128]{1,0:T(8,128)(2,1)}, u32[]{:S(2)}) copy-start(bf16[128,128]{1,0:T(8,128)(2,1)} %multiply_bitcast_fusion.2.gate) | copy-start | bytes 98308
  406.1 10.2 %collective-permute-start.25 = (bf16[3,32,256,128]{3,2,1,0:T(8,128)(2,1)S(1)}, bf16[3,32,256,128]{3,2,1,0:T(8,128)(2,1)S(1)}, u32[]{:S(2)}, u32[]{:S(2)}) collective-permute-start(bf16[3,32,256,128]{3,2,1,0:T(8,128)(2,1)S(1)} %get-tuple-element.259), channel_id=1, source_target_pairs={{0,4},{4,0},{1,5},{5,1},{2,6},{6,2},{3,7},{7,3},{11,15},{15,11},{1... | collective-permute-start | bytes 18874376 | tf_op jit(solution)/shard_map/ppermute | solution.py:587
  416.3 2.6 copy-start.7
  523.4 7.2 %collective-permute-start.27 = (bf16[128,128,128]{2,1,0:T(8,128)(2,1)S(1)}, bf16[128,128,128]{2,1,0:T(8,128)(2,1)S(1)}, u32[]{:S(2)}, u32[]{:S(2)}) collective-permute-start(bf16[128,128,128]{2,1,0:T(8,128)(2,1)S(1)} %get-tuple-element.263), channel_id=1, source_target_pairs={{0,4},{4,0},{1,5},{5,1},{2,6},{6,2},{3,7},{7,3},{11,15},{15,11},{1... | collective-permute-start | bytes 12582920 | tf_op jit(solution)/shard_map/ppermute | solution.py:592

commit v8 on v7

--- a/solution.py
+++ b/solution.py
@@ -54,7 +54,7 @@
 TILE = 128
 SUB = 16
 BLOCKS = TILE // SUB
-CHUNK = 2
+CHUNK = 1
 PITCH = SUB + 1
 GROUPS = 2
 MIDDLE_GROUPS = 4

time: 544 us -> 549 us (level)
  Pallas kernels: 287 us -> 299 us
  waiting for transfers between devices: 211 us -> 204 us
    pallas_call x9, Pallas kernels: 136 us -> 145 us  [enter(): pl.pallas_call(enter_kernel, grid_spec=pltpu.PrefetchScalarGridSpec(num_s...]
    ppermute x15, waiting for transfers between devices: 182 us -> 175 us  [hop(): return [lax.ppermute(value, BOTH, pairs) for value in values]]
  transfers between devices with their start and end apart: 28 -> 28, of which waited for: 12 -> 12; matrix products, arithmetic and copies ran while one was open for 3% -> 3% of each run, Pallas kernels for 26% -> 27%
where the time goes in v8:
time: 549 us; the launch traced here: 548 us
  Pallas kernels  299 us (54%)
  waiting for transfers between devices  204 us (37%)
  local copies, waits for them, and re-layouts  21.1 us (4%)
  starting transfers between devices  20.1 us (4%)
    ppermute x15, waiting for transfers between devices, hop(): return [lax.ppermute(value, BOTH, pairs) for value in values]  175 us
    pallas_call x9, Pallas kernels, enter(): pl.pallas_call(enter_kernel, grid_spec=pltpu.PrefetchScalarGridSpec(num_s...  145 us
    pallas_call x1, Pallas kernels, middle(): pl.pallas_call(middle_kernel, grid_spec=pltpu.PrefetchScalarGridSpec(num_...  95.6 us
    pallas_call x2, Pallas kernels, outgoing(): pl.pallas_call(outgoing_kernel, grid_spec=pltpu.PrefetchScalarGridSpec(nu...  33.6 us
    ppermute x15, starting transfers between devices, hop(): return [lax.ppermute(value, BOTH, pairs) for value in values]  16.3 us
    pallas_call x1, Pallas kernels, incoming(): pl.pallas_call(incoming_kernel, grid_spec=pltpu.PrefetchScalarGridSpec(nu...  12.8 us
    pallas_call x1, Pallas kernels, leave(): pl.pallas_call(leave_kernel, grid_spec=pltpu.PrefetchScalarGridSpec(num_s...  12.7 us
  transfers between devices with their start and end apart: 28, of which 12 were waited for; matrix products, arithmetic and copies ran while one was open for 3% of the time, Pallas kernels for 27%

profile of v8, /device:TPU:0, one launch (start us, length us, event | category | flops | bytes accessed | tf_op | source)
XLA Modules:
  0.0 548.2 jit_solution(11492729674392825248)
XLA Ops:
  0.5 2.6 collective-permute-start.2
  3.0 0.8 convert_element_type.6
  4.1 0.9 fusion.10
  5.0 0.9 fusion.11
  6.4 0.8 fusion.13
  7.2 0.8 slice_bitcast_fusion
  7.9 0.8 slice_bitcast_fusion.1
  8.7 0.8 fusion.12
  11.4 0.8 slice_bitcast_fusion.3
  13.5 0.8 convert_bitcast_fusion
  14.6 1.9 collective-permute-start.1
  16.8 2.2 copy-done.6
  19.0 17.2 %enter.9 = (bf16[50,128,2048]{2,1,0:T(8,128)(2,1)}, bf16[4,32,512,128]{3,2,1,0:T(8,128)(2,1)}, bf16[4,32,512,128]{3,2,1,0:T(8,128)(2,1)}, bf16[4,64,384,128]{3,2,1,0:T(8,128)(2,1)}, bf16[4,4,128,128]{3,2,1,0:T(8,128)(2,1)S(1)}) custom-call(s32[6]{0:T(128)S(1)} %stack.240.at, bf16[128,128,128]{2,1,0:T(8,128)(2,1)S(1)} %copy-done.6, ...), custom_call_target="tpu_custom_call" | custom-call | flops 4294967296 | bytes 33554432 | tf_op jit(solution)/shard_map/enter/pallas_call | solution.py:206
  36.3 59.5 %collective-permute-done.1.mask = bf16[2,128,128]{2,1,0:T(8,128)(2,1)S(1)} collective-permute-done((bf16[2,128,128]{2,1,0:T(8,128)(2,1)S(1)}, bf16[2,128,128]{2,1,0:T(8,128)(2,1)S(1)}, u32[]{:S(2)}, u32[]{:S(2)}) %collective-permute-start.1) | collective-permute-done | bytes 65568 | tf_op jit(solution)/shard_map/ppermute | solution.py:536
  95.8 1.5 collective-permute-done.3.mask
  98.4 1.6 collective-permute-start.7
  100.6 1.6 collective-permute-start.6
  102.2 3.2 collective-permute-done.11.sib
  105.7 17.9 %enter.10 = (bf16[50,128,2048]{2,1,0:T(8,128)(2,1)}, bf16[4,32,512,128]{3,2,1,0:T(8,128)(2,1)}, bf16[4,32,512,128]{3,2,1,0:T(8,128)(2,1)}, bf16[4,64,384,128]{3,2,1,0:T(8,128)(2,1)}, bf16[4,4,128,128]{3,2,1,0:T(8,128)(2,1)S(1)}) custom-call(s32[6]{0:T(128)S(1)} %stack.255.at, ...), custom_call_target="tpu_custom_call", output_to_operand_aliasing={{0}: (8, {}), {1}: (9, {}), {2}: (10, {}), {3}: (11, {}), {... | custom-call | flops 4294967296 | bytes 33554432 | tf_op jit(solution)/shard_map/enter/pallas_call | solution.py:206
  123.6 17.9 %enter.11 = (bf16[50,128,2048]{2,1,0:T(8,128)(2,1)}, bf16[4,32,512,128]{3,2,1,0:T(8,128)(2,1)}, bf16[4,32,512,128]{3,2,1,0:T(8,128)(2,1)}, bf16[4,64,384,128]{3,2,1,0:T(8,128)(2,1)}, bf16[4,4,128,128]{3,2,1,0:T(8,128)(2,1)S(1)}) custom-call(s32[6]{0:T(128)S(1)} %stack.249.at, ...), custom_call_target="tpu_custom_call", output_to_operand_aliasing={{0}: (8, {}), {1}: (9, {}), {2}: (10, {}), {3}: (11, {}), {... | custom-call | flops 4294967296 | bytes 33554432 | tf_op jit(solution)/shard_map/enter/pallas_call | solution.py:206
  141.5 51.1 %collective-permute-done.6.mask = bf16[2,128,128]{2,1,0:T(8,128)(2,1)S(1)} collective-permute-done((bf16[2,128,128]{2,1,0:T(8,128)(2,1)S(1)}, bf16[2,128,128]{2,1,0:T(8,128)(2,1)S(1)}, u32[]{:S(2)}, u32[]{:S(2)}) %collective-permute-start.6) | collective-permute-done | bytes 65568 | tf_op jit(solution)/shard_map/ppermute | solution.py:536
  192.6 1.3 collective-permute-done.8.mask
  194.4 1.6 collective-permute-start.13
  196.6 1.6 collective-permute-start.12
  198.2 3.2 collective-permute-done.17.sib
  201.8 17.9 %enter.12 = (bf16[50,128,2048]{2,1,0:T(8,128)(2,1)}, bf16[4,32,512,128]{3,2,1,0:T(8,128)(2,1)}, bf16[4,32,512,128]{3,2,1,0:T(8,128)(2,1)}, bf16[4,64,384,128]{3,2,1,0:T(8,128)(2,1)}, bf16[4,4,128,128]{3,2,1,0:T(8,128)(2,1)S(1)}) custom-call(s32[6]{0:T(128)S(1)} %stack.267.at, ...), custom_call_target="tpu_custom_call", output_to_operand_aliasing={{0}: (8, {}), {1}: (9, {}), {2}: (10, {}), {3}: (11, {}), {... | custom-call | flops 4294967296 | bytes 33554432 | tf_op jit(solution)/shard_map/enter/pallas_call | solution.py:206
  219.7 17.7 %enter.13 = (bf16[50,128,2048]{2,1,0:T(8,128)(2,1)}, bf16[4,32,512,128]{3,2,1,0:T(8,128)(2,1)}, bf16[4,32,512,128]{3,2,1,0:T(8,128)(2,1)}, bf16[4,64,384,128]{3,2,1,0:T(8,128)(2,1)}, bf16[4,4,128,128]{3,2,1,0:T(8,128)(2,1)S(1)}) custom-call(s32[6]{0:T(128)S(1)} %stack.261.at, ...), custom_call_target="tpu_custom_call", output_to_operand_aliasing={{0}: (8, {}), {1}: (9, {}), {2}: (10, {}), {3}: (11, {}), {... | custom-call | flops 4294967296 | bytes 33554432 | tf_op jit(solution)/shard_map/enter/pallas_call | solution.py:206
  237.4 51.2 %collective-permute-done.12.mask = bf16[2,128,128]{2,1,0:T(8,128)(2,1)S(1)} collective-permute-done((bf16[2,128,128]{2,1,0:T(8,128)(2,1)S(1)}, bf16[2,128,128]{2,1,0:T(8,128)(2,1)S(1)}, u32[]{:S(2)}, u32[]{:S(2)}) %collective-permute-start.12) | collective-permute-done | bytes 65568 | tf_op jit(solution)/shard_map/ppermute | solution.py:536
  288.6 1.3 collective-permute-done.14.mask
  290.4 3.2 slice.74
  293.6 3.2 slice.75
  296.8 1.5 collective-permute-start.19
  299.0 1.7 collective-permute-start.18
  300.6 0.9 copy-done.3
  301.5 17.7 %enter.14 = (bf16[50,128,2048]{2,1,0:T(8,128)(2,1)}, bf16[4,32,512,128]{3,2,1,0:T(8,128)(2,1)}, bf16[4,32,512,128]{3,2,1,0:T(8,128)(2,1)}, bf16[4,64,384,128]{3,2,1,0:T(8,128)(2,1)}, bf16[4,4,128,128]{3,2,1,0:T(8,128)(2,1)S(1)}) custom-call(s32[6]{0:T(128)S(1)} %stack.279.at, ...), custom_call_target="tpu_custom_call", output_to_operand_aliasing={{0}: (8, {}), {1}: (9, {}), {2}: (10, {}), {3}: (11, {}), {... | custom-call | flops 4294967296 | bytes 33554432 | tf_op jit(solution)/shard_map/enter/pallas_call | solution.py:206
  319.2 17.8 %enter.15 = (bf16[50,128,2048]{2,1,0:T(8,128)(2,1)}, bf16[4,32,512,128]{3,2,1,0:T(8,128)(2,1)}, bf16[4,32,512,128]{3,2,1,0:T(8,128)(2,1)}, bf16[4,64,384,128]{3,2,1,0:T(8,128)(2,1)}, bf16[4,4,128,128]{3,2,1,0:T(8,128)(2,1)S(1)}) custom-call(s32[6]{0:T(128)S(1)} %stack.273.at, ...), custom_call_target="tpu_custom_call", output_to_operand_aliasing={{0}: (8, {}), {1}: (9, {}), {2}: (10, {}), {3}: (11, {}), {... | custom-call | flops 4294967296 | bytes 33554432 | tf_op jit(solution)/shard_map/enter/pallas_call | solution.py:206
  337.0 9.0 %collective-permute-done.18.mask = bf16[2,128,128]{2,1,0:T(8,128)(2,1)S(1)} collective-permute-done((bf16[2,128,128]{2,1,0:T(8,128)(2,1)}, bf16[2,128,128]{2,1,0:T(8,128)(2,1)S(1)}, u32[]{:S(2)}, u32[]{:S(2)}) %collective-permute-start.18) | collective-permute-done | bytes 65568 | tf_op jit(solution)/shard_map/ppermute | solution.py:536
  346.7 6.1 %collective-permute-done.24.sib = bf16[64,128,128]{2,1,0:T(8,128)(2,1)} collective-permute-done((bf16[64,128,128]{2,1,0:T(8,128)(2,1)}, bf16[64,128,128]{2,1,0:T(8,128)(2,1)}, u32[]{:S(2)}, u32[]{:S(2)}) %collective-permute-start.24) | collective-permute-done | bytes 2097184 | tf_op jit(solution)/shard_map/ppermute | solution.py:575
  352.8 10.5 %enter.16 = (bf16[50,128,2048]{2,1,0:T(8,128)(2,1)}, bf16[4,32,512,128]{3,2,1,0:T(8,128)(2,1)}, bf16[4,32,512,128]{3,2,1,0:T(8,128)(2,1)}, bf16[4,64,384,128]{3,2,1,0:T(8,128)(2,1)}, bf16[4,4,128,128]{3,2,1,0:T(8,128)(2,1)S(1)}) custom-call(s32[6]{0:T(128)S(1)} %stack.230.at, ...), custom_call_target="tpu_custom_call", output_to_operand_aliasing={{0}: (8, {}), {1}: (9, {}), {2}: (10, {}), {3}: (11, {}), {... | custom-call | flops 2147483648 | bytes 16777216 | tf_op jit(solution)/shard_map/enter/pallas_call | solution.py:206
  363.2 10.1 %enter.17 = (bf16[50,128,2048]{2,1,0:T(8,128)(2,1)}, bf16[4,32,512,128]{3,2,1,0:T(8,128)(2,1)}, bf16[4,32,512,128]{3,2,1,0:T(8,128)(2,1)}, bf16[4,64,384,128]{3,2,1,0:T(8,128)(2,1)}, bf16[4,4,128,128]{3,2,1,0:T(8,128)(2,1)S(1)}) custom-call(s32[6]{0:T(128)S(1)} %stack.230.at, ...), custom_call_target="tpu_custom_call", output_to_operand_aliasing={{0}: (8, {}), {1}: (9, {}), {2}: (10, {}), {3}: (11, {}), {... | custom-call | flops 2147483648 | bytes 16777216 | tf_op jit(solution)/shard_map/enter/pallas_call | solution.py:206
  373.4 17.7 %outgoing.3 = (bf16[3,32,256,128]{3,2,1,0:T(8,128)(2,1)S(1)}, bf16[3,32,256,128]{3,2,1,0:T(8,128)(2,1)}) custom-call(s32[2]{0:T(128)S(1)} %pad_add_fusion.1.at, bf16[4,32,512,128]{3,2,1,0:T(8,128)(2,1)} %get-tuple-element.257.left, bf16[4,64,384,128]{3,2,1,0:T(8,128)(2,1)} %get-tuple-element.255.right), custom_call_target="tpu_custom_call" | custom-call | flops 6442450944 | bytes 42598400 | tf_op jit(solution)/shard_map/outgoing/pallas_call | solution.py:266
  391.2 15.9 %outgoing.2 = (bf16[3,32,256,128]{3,2,1,0:T(8,128)(2,1)S(1)}, bf16[3,32,256,128]{3,2,1,0:T(8,128)(2,1)S(1)}) custom-call(s32[2]{0:T(128)S(1)} %pad_add_fusion.1.at, bf16[4,32,512,128]{3,2,1,0:T(8,128)(2,1)} %get-tuple-element.254.left, bf16[4,64,384,128]{3,2,1,0:T(8,128)(2,1)} %get-tuple-element.255.right), custom_call_target="tpu_custom_call" | custom-call | flops 6442450944 | bytes 42598400 | tf_op jit(solution)/shard_map/outgoing/pallas_call | solution.py:266
  407.6 9.7 %collective-permute-done.25.rest_2_ = bf16[3,32,256,128]{3,2,1,0:T(8,128)(2,1)S(1)} collective-permute-done((bf16[3,32,256,128]{3,2,1,0:T(8,128)(2,1)S(1)}, bf16[3,32,256,128]{3,2,1,0:T(8,128)(2,1)S(1)}, u32[]{:S(2)}, u32[]{:S(2)}) %collective-permute-start.25) | collective-permute-done | bytes 6291488 | tf_op jit(solution)/shard_map/ppermute | solution.py:587
  417.3 2.6 copy-done.7
  419.9 95.6 %middle.1 = (bf16[3,128,256,128]{3,2,1,0:T(8,128)(2,1)}, bf16[20,128,2048]{2,1,0:T(8,128)(2,1)}) custom-call(s32[4]{0:T(128)S(1)} %pad_add_fusion.at, bf16[50,128,2048]{2,1,0:T(8,128)(2,1)} %get-tuple-element.243.state, bf16[4,4,128,128]{3,2,1,0:T(8,128)(2,1)S(1)} %get-tuple-element.244.mask, f32[128,128]{1,0:T(8,128)S(1)} %broadcast_in_dim.55.gain.gain0, ...), custom_call_target="tpu_custom_call" | custom-call | flops 12884901888 | bytes 100663296 | tf_op jit(solution)/shard_map/middle/pallas_call | solution.py:325
  515.5 12.8 %incoming.1 = (bf16[128,128,128]{2,1,0:T(8,128)(2,1)S(1)}, bf16[128,128,128]{2,1,0:T(8,128)(2,1)S(1)}) custom-call(s32[4]{0:T(128)S(1)} %pad_add_fusion.at, bf16[3,128,256,128]{3,2,1,0:T(8,128)(2,1)} %get-tuple-element.261.pairs), custom_call_target="tpu_custom_call" | custom-call | flops 2147483648 | bytes 37748736 | tf_op jit(solution)/shard_map/incoming/pallas_call | solution.py:389
  528.8 6.8 %collective-permute-done.27.got = bf16[128,128,128]{2,1,0:T(8,128)(2,1)S(1)} collective-permute-done((bf16[128,128,128]{2,1,0:T(8,128)(2,1)S(1)}, bf16[128,128,128]{2,1,0:T(8,128)(2,1)S(1)}, u32[]{:S(2)}, u32[]{:S(2)}) %collective-permute-start.27) | collective-permute-done | bytes 4194336 | tf_op jit(solution)/shard_map/ppermute | solution.py:592
  535.5 12.7 %leave.1 = bf16[128,128,128]{2,1,0:T(8,128)(2,1)} custom-call(s32[4]{0:T(128)S(1)} %pad_add_fusion.at, bf16[128,128,128]{2,1,0:T(8,128)(2,1)S(1)} %get-tuple-element.262.kept, bf16[128,128,128]{2,1,0:T(8,128)(2,1)S(1)} %collective-permute-done.27.got, bf16[20,128,2048]{2,1,0:T(8,128)(2,1)} %get-tuple-element.264.state, ...), custom_call_target="tpu_custom_call" | custom-call | flops 1073741824 | bytes 20971520 | tf_op jit(solution)/shard_map/leave/pallas_call | solution.py:433
  (100 shorter events, 11.5 us)
Async XLA Ops:
  0.0 16.7 %collective-permute-start.5 = (bf16[128,128,128]{2,1,0:T(8,128)(2,1)}, bf16[128,128,128]{2,1,0:T(8,128)(2,1)}, u32[]{:S(2)}, u32[]{:S(2)}) collective-permute-start(bf16[128,128,128]{2,1,0:T(8,128)(2,1)} %own.1), channel_id=1, source_target_pairs={{0,4},{4,0},{1,5},{5,1},{2,6},{6,2},{3,7},{7,3},{11,15},{15,11},{1... | collective-permute-start | bytes 12582920 | tf_op jit(solution)/shard_map/ppermute | solution.py:538
  0.5 96.9 %collective-permute-start.2 = (bf16[128,128,128]{2,1,0:T(8,128)(2,1)}, bf16[128,128,128]{2,1,0:T(8,128)(2,1)}, u32[]{:S(2)}, u32[]{:S(2)}) collective-permute-start(bf16[128,128,128]{2,1,0:T(8,128)(2,1)} %own.1), channel_id=1, source_target_pairs={{0,1},{4,5},{1,2},{5,6},{2,3},{6,7},{3,11},{7,15},{11,10},{15,14},... | collective-permute-start | bytes 12582920 | tf_op jit(solution)/shard_map/ppermute | solution.py:536
  3.0 94.3 %collective-permute-start.4 = (bf16[128,128,128]{2,1,0:T(8,128)(2,1)}, bf16[128,128,128]{2,1,0:T(8,128)(2,1)}, u32[]{:S(2)}, u32[]{:S(2)}) collective-permute-start(bf16[128,128,128]{2,1,0:T(8,128)(2,1)} %own.1), channel_id=1, source_target_pairs={{1,0},{5,4},{2,1},{6,5},{3,2},{7,6},{11,3},{15,7},{10,11},{14,15},... | collective-permute-start | bytes 12582920 | tf_op jit(solution)/shard_map/ppermute | solution.py:536
  3.9 10.7 %collective-permute-start = (bf16[128,128]{1,0:T(8,128)(2,1)S(1)}, bf16[128,128]{1,0:T(8,128)(2,1)S(1)}, u32[]{:S(2)}, u32[]{:S(2)}) collective-permute-start(bf16[128,128]{1,0:T(8,128)(2,1)S(1)} %convert_element_type.6), channel_id=1, source_target_pairs={{0,4},{4,0},{1,5},{5,1},{2,6},{6,2},{3,7},{7,3},{11,15},{15,11},{1... | collective-permute-start | bytes 98312 | tf_op jit(solution)/shard_map/ppermute | solution.py:484
  14.6 81.2 %collective-permute-start.1 = (bf16[2,128,128]{2,1,0:T(8,128)(2,1)S(1)}, bf16[2,128,128]{2,1,0:T(8,128)(2,1)S(1)}, u32[]{:S(2)}, u32[]{:S(2)}) collective-permute-start(bf16[2,128,128]{2,1,0:T(8,128)(2,1)S(1)} %maximum_select_fusion.mask), channel_id=1, source_target_pairs={{0,1},{4,5},{1,2},{5,6},{2,3},{6,7},{3,11},{7,15},{11,10},{15,14},... | collective-permute-start | bytes 196616 | tf_op jit(solution)/shard_map/ppermute | solution.py:536
  16.5 80.9 %collective-permute-start.3 = (bf16[2,128,128]{2,1,0:T(8,128)(2,1)S(1)}, bf16[2,128,128]{2,1,0:T(8,128)(2,1)S(1)}, u32[]{:S(2)}, u32[]{:S(2)}) collective-permute-start(bf16[2,128,128]{2,1,0:T(8,128)(2,1)S(1)} %maximum_select_fusion.mask), channel_id=1, source_target_pairs={{1,0},{5,4},{2,1},{6,5},{3,2},{7,6},{11,3},{15,7},{10,11},{14,15},... | collective-permute-start | bytes 196616 | tf_op jit(solution)/shard_map/ppermute | solution.py:536
  16.8 2.2 copy-start.6
  97.8 7.5 %collective-permute-start.11 = (bf16[128,128,128]{2,1,0:T(8,128)(2,1)}, bf16[128,128,128]{2,1,0:T(8,128)(2,1)}, u32[]{:S(2)}, u32[]{:S(2)}) collective-permute-start(bf16[128,128,128]{2,1,0:T(8,128)(2,1)} %collective-permute-done.2.own), channel_id=1, source_target_pairs={{0,4},{4,0},{1,5},{5,1},{2,6},{6,2},{3,7},{7,3},{11,15},{15,11},{1... | collective-permute-start | bytes 12582920 | tf_op jit(solution)/shard_map/ppermute | solution.py:573
  97.9 25.7 %collective-permute-start.10 = (bf16[128,128,128]{2,1,0:T(8,128)(2,1)}, bf16[128,128,128]{2,1,0:T(8,128)(2,1)}, u32[]{:S(2)}, u32[]{:S(2)}) collective-permute-start(bf16[128,128,128]{2,1,0:T(8,128)(2,1)} %collective-permute-done.4.own), channel_id=1, source_target_pairs={{0,4},{4,0},{1,5},{5,1},{2,6},{6,2},{3,7},{7,3},{11,15},{15,11},{1... | collective-permute-start | bytes 12582920 | tf_op jit(solution)/shard_map/ppermute | solution.py:573
  98.4 95.5 %collective-permute-start.7 = (bf16[128,128,128]{2,1,0:T(8,128)(2,1)}, bf16[128,128,128]{2,1,0:T(8,128)(2,1)}, u32[]{:S(2)}, u32[]{:S(2)}) collective-permute-start(bf16[128,128,128]{2,1,0:T(8,128)(2,1)} %collective-permute-done.2.own), channel_id=1, source_target_pairs={{0,1},{4,5},{1,2},{5,6},{2,3},{6,7},{3,11},{7,15},{11,10},{15,14},... | collective-permute-start | bytes 12582920 | tf_op jit(solution)/shard_map/ppermute | solution.py:536
  100.0 93.9 %collective-permute-start.9 = (bf16[128,128,128]{2,1,0:T(8,128)(2,1)}, bf16[128,128,128]{2,1,0:T(8,128)(2,1)}, u32[]{:S(2)}, u32[]{:S(2)}) collective-permute-start(bf16[128,128,128]{2,1,0:T(8,128)(2,1)} %collective-permute-done.4.own), channel_id=1, source_target_pairs={{1,0},{5,4},{2,1},{6,5},{3,2},{7,6},{11,3},{15,7},{10,11},{14,15},... | collective-permute-start | bytes 12582920 | tf_op jit(solution)/shard_map/ppermute | solution.py:536
  100.6 92.0 %collective-permute-start.6 = (bf16[2,128,128]{2,1,0:T(8,128)(2,1)S(1)}, bf16[2,128,128]{2,1,0:T(8,128)(2,1)S(1)}, u32[]{:S(2)}, u32[]{:S(2)}) collective-permute-start(bf16[2,128,128]{2,1,0:T(8,128)(2,1)S(1)} %collective-permute-done.1.mask), channel_id=1, source_target_pairs={{0,1},{4,5},{1,2},{5,6},{2,3},{6,7},{3,11},{7,15},{11,10},{15,14},... | collective-permute-start | bytes 196616 | tf_op jit(solution)/shard_map/ppermute | solution.py:536
  105.4 88.5 %collective-permute-start.8 = (bf16[2,128,128]{2,1,0:T(8,128)(2,1)S(1)}, bf16[2,128,128]{2,1,0:T(8,128)(2,1)S(1)}, u32[]{:S(2)}, u32[]{:S(2)}) collective-permute-start(bf16[2,128,128]{2,1,0:T(8,128)(2,1)S(1)} %collective-permute-done.3.mask), channel_id=1, source_target_pairs={{1,0},{5,4},{2,1},{6,5},{3,2},{7,6},{11,3},{15,7},{10,11},{14,15},... | collective-permute-start | bytes 196616 | tf_op jit(solution)/shard_map/ppermute | solution.py:536
  193.9 7.5 %collective-permute-start.17 = (bf16[128,128,128]{2,1,0:T(8,128)(2,1)}, bf16[128,128,128]{2,1,0:T(8,128)(2,1)}, u32[]{:S(2)}, u32[]{:S(2)}) collective-permute-start(bf16[128,128,128]{2,1,0:T(8,128)(2,1)} %collective-permute-done.7.own), channel_id=1, source_target_pairs={{0,4},{4,0},{1,5},{5,1},{2,6},{6,2},{3,7},{7,3},{11,15},{15,11},{1... | collective-permute-start | bytes 12582920 | tf_op jit(solution)/shard_map/ppermute | solution.py:573
  193.9 25.8 %collective-permute-start.16 = (bf16[128,128,128]{2,1,0:T(8,128)(2,1)}, bf16[128,128,128]{2,1,0:T(8,128)(2,1)}, u32[]{:S(2)}, u32[]{:S(2)}) collective-permute-start(bf16[128,128,128]{2,1,0:T(8,128)(2,1)} %collective-permute-done.9.own), channel_id=1, source_target_pairs={{0,4},{4,0},{1,5},{5,1},{2,6},{6,2},{3,7},{7,3},{11,15},{15,11},{1... | collective-permute-start | bytes 12582920 | tf_op jit(solution)/shard_map/ppermute | solution.py:573
  194.4 95.5 %collective-permute-start.13 = (bf16[128,128,128]{2,1,0:T(8,128)(2,1)}, bf16[128,128,128]{2,1,0:T(8,128)(2,1)}, u32[]{:S(2)}, u32[]{:S(2)}) collective-permute-start(bf16[128,128,128]{2,1,0:T(8,128)(2,1)} %collective-permute-done.7.own), channel_id=1, source_target_pairs={{0,1},{4,5},{1,2},{5,6},{2,3},{6,7},{3,11},{7,15},{11,10},{15,14},... | collective-permute-start | bytes 12582920 | tf_op jit(solution)/shard_map/ppermute | solution.py:536
  196.0 93.9 %collective-permute-start.15 = (bf16[128,128,128]{2,1,0:T(8,128)(2,1)}, bf16[128,128,128]{2,1,0:T(8,128)(2,1)}, u32[]{:S(2)}, u32[]{:S(2)}) collective-permute-start(bf16[128,128,128]{2,1,0:T(8,128)(2,1)} %collective-permute-done.9.own), channel_id=1, source_target_pairs={{1,0},{5,4},{2,1},{6,5},{3,2},{7,6},{11,3},{15,7},{10,11},{14,15},... | collective-permute-start | bytes 12582920 | tf_op jit(solution)/shard_map/ppermute | solution.py:536
  196.6 92.0 %collective-permute-start.12 = (bf16[2,128,128]{2,1,0:T(8,128)(2,1)S(1)}, bf16[2,128,128]{2,1,0:T(8,128)(2,1)S(1)}, u32[]{:S(2)}, u32[]{:S(2)}) collective-permute-start(bf16[2,128,128]{2,1,0:T(8,128)(2,1)S(1)} %collective-permute-done.6.mask), channel_id=1, source_target_pairs={{0,1},{4,5},{1,2},{5,6},{2,3},{6,7},{3,11},{7,15},{11,10},{15,14},... | collective-permute-start | bytes 196616 | tf_op jit(solution)/shard_map/ppermute | solution.py:536
  201.4 88.5 %collective-permute-start.14 = (bf16[2,128,128]{2,1,0:T(8,128)(2,1)S(1)}, bf16[2,128,128]{2,1,0:T(8,128)(2,1)S(1)}, u32[]{:S(2)}, u32[]{:S(2)}) collective-permute-start(bf16[2,128,128]{2,1,0:T(8,128)(2,1)S(1)} %collective-permute-done.8.mask), channel_id=1, source_target_pairs={{1,0},{5,4},{2,1},{6,5},{3,2},{7,6},{11,3},{15,7},{10,11},{14,15},... | collective-permute-start | bytes 196616 | tf_op jit(solution)/shard_map/ppermute | solution.py:536
  288.6 8.2 %copy-start.2 = (bf16[2,128,128]{2,1,0:T(8,128)(2,1)}, bf16[2,128,128]{2,1,0:T(8,128)(2,1)S(1)}, u32[]{:S(2)}) copy-start(bf16[2,128,128]{2,1,0:T(8,128)(2,1)S(1)} %collective-permute-done.12.mask) | copy-start | bytes 196612
  289.9 8.4 %copy-start.4 = (bf16[2,128,128]{2,1,0:T(8,128)(2,1)}, bf16[2,128,128]{2,1,0:T(8,128)(2,1)S(1)}, u32[]{:S(2)}) copy-start(bf16[2,128,128]{2,1,0:T(8,128)(2,1)S(1)} %collective-permute-done.14.mask) | copy-start | bytes 196612
  289.9 10.7 %collective-permute-start.22 = (bf16[128,128,128]{2,1,0:T(8,128)(2,1)}, bf16[128,128,128]{2,1,0:T(8,128)(2,1)}, u32[]{:S(2)}, u32[]{:S(2)}) collective-permute-start(bf16[128,128,128]{2,1,0:T(8,128)(2,1)} %collective-permute-done.13.own), channel_id=1, source_target_pairs={{0,4},{4,0},{1,5},{5,1},{2,6},{6,2},{3,7},{7,3},{11,15},{15,11},{1... | collective-permute-start | bytes 12582920 | tf_op jit(solution)/shard_map/ppermute | solution.py:573
  289.9 29.3 %collective-permute-start.21 = (bf16[128,128,128]{2,1,0:T(8,128)(2,1)}, bf16[128,128,128]{2,1,0:T(8,128)(2,1)}, u32[]{:S(2)}, u32[]{:S(2)}) collective-permute-start(bf16[128,128,128]{2,1,0:T(8,128)(2,1)} %collective-permute-done.15.own), channel_id=1, source_target_pairs={{0,4},{4,0},{1,5},{5,1},{2,6},{6,2},{3,7},{7,3},{11,15},{15,11},{1... | collective-permute-start | bytes 12582920 | tf_op jit(solution)/shard_map/ppermute | solution.py:573
  296.8 49.2 %collective-permute-start.19 = (bf16[64,128,128]{2,1,0:T(8,128)(2,1)}, bf16[64,128,128]{2,1,0:T(8,128)(2,1)}, u32[]{:S(2)}, u32[]{:S(2)}) collective-permute-start(bf16[64,128,128]{2,1,0:T(8,128)(2,1)} %slice.74), channel_id=1, source_target_pairs={{0,1},{4,5},{1,2},{5,6},{2,3},{6,7},{3,11},{7,15},{11,10},{15,14},... | collective-permute-start | bytes 6291464 | tf_op jit(solution)/shard_map/ppermute | solution.py:536
  298.2 47.7 %collective-permute-start.20 = (bf16[64,128,128]{2,1,0:T(8,128)(2,1)}, bf16[64,128,128]{2,1,0:T(8,128)(2,1)S(1)}, u32[]{:S(2)}, u32[]{:S(2)}) collective-permute-start(bf16[64,128,128]{2,1,0:T(8,128)(2,1)} %slice.75), channel_id=1, source_target_pairs={{1,0},{5,4},{2,1},{6,5},{3,2},{7,6},{11,3},{15,7},{10,11},{14,15},... | collective-permute-start | bytes 6291464 | tf_op jit(solution)/shard_map/ppermute | solution.py:536
  299.0 47.0 %collective-permute-start.18 = (bf16[2,128,128]{2,1,0:T(8,128)(2,1)}, bf16[2,128,128]{2,1,0:T(8,128)(2,1)S(1)}, u32[]{:S(2)}, u32[]{:S(2)}) collective-permute-start(bf16[2,128,128]{2,1,0:T(8,128)(2,1)} %copy-done.2), channel_id=1, source_target_pairs={{0,1},{4,5},{1,2},{5,6},{2,3},{6,7},{3,11},{7,15},{11,10},{15,14},... | collective-permute-start | bytes 196616 | tf_op jit(solution)/shard_map/ppermute | solution.py:536
  300.6 0.9 copy-start.3
  301.5 17.7 %copy-start.5 = (bf16[2,128,128]{2,1,0:T(8,128)(2,1)S(1)}, bf16[2,128,128]{2,1,0:T(8,128)(2,1)}, u32[]{:S(2)}) copy-start(bf16[2,128,128]{2,1,0:T(8,128)(2,1)} %copy-done.4) | copy-start | bytes 196612
  346.0 6.8 %collective-permute-start.24 = (bf16[64,128,128]{2,1,0:T(8,128)(2,1)}, bf16[64,128,128]{2,1,0:T(8,128)(2,1)}, u32[]{:S(2)}, u32[]{:S(2)}) collective-permute-start(bf16[64,128,128]{2,1,0:T(8,128)(2,1)} %collective-permute-done.19.own), channel_id=1, source_target_pairs={{0,4},{4,0},{1,5},{5,1},{2,6},{6,2},{3,7},{7,3},{11,15},{15,11},{1... | collective-permute-start | bytes 6291464 | tf_op jit(solution)/shard_map/ppermute | solution.py:575
  346.0 17.2 %collective-permute-start.23 = (bf16[64,128,128]{2,1,0:T(8,128)(2,1)S(1)}, bf16[64,128,128]{2,1,0:T(8,128)(2,1)}, u32[]{:S(2)}, u32[]{:S(2)}) collective-permute-start(bf16[64,128,128]{2,1,0:T(8,128)(2,1)S(1)} %collective-permute-done.20.own), channel_id=1, source_target_pairs={{0,4},{4,0},{1,5},{5,1},{2,6},{6,2},{3,7},{7,3},{11,15},{15,11},{1... | collective-permute-start | bytes 6291464 | tf_op jit(solution)/shard_map/ppermute | solution.py:576
  391.0 16.6 %collective-permute-start.26 = (bf16[3,32,256,128]{3,2,1,0:T(8,128)(2,1)}, bf16[3,32,256,128]{3,2,1,0:T(8,128)(2,1)}, u32[]{:S(2)}, u32[]{:S(2)}) collective-permute-start(bf16[3,32,256,128]{3,2,1,0:T(8,128)(2,1)} %get-tuple-element.260), channel_id=1, source_target_pairs={{0,4},{4,0},{1,5},{5,1},{2,6},{6,2},{3,7},{7,3},{11,15},{15,11},{1... | collective-permute-start | bytes 18874376 | tf_op jit(solution)/shard_map/ppermute | solution.py:587
  391.2 28.8 %copy-start = (bf16[128,128]{1,0:T(8,128)(2,1)S(1)}, bf16[128,128]{1,0:T(8,128)(2,1)}, u32[]{:S(2)}) copy-start(bf16[128,128]{1,0:T(8,128)(2,1)} %fusion.5.proj) | copy-start | bytes 98308
  391.2 28.8 %copy-start.1 = (bf16[128,128]{1,0:T(8,128)(2,1)S(1)}, bf16[128,128]{1,0:T(8,128)(2,1)}, u32[]{:S(2)}) copy-start(bf16[128,128]{1,0:T(8,128)(2,1)} %multiply_bitcast_fusion.2.gate) | copy-start | bytes 98308
  407.1 10.3 %collective-permute-start.25 = (bf16[3,32,256,128]{3,2,1,0:T(8,128)(2,1)S(1)}, bf16[3,32,256,128]{3,2,1,0:T(8,128)(2,1)S(1)}, u32[]{:S(2)}, u32[]{:S(2)}) collective-permute-start(bf16[3,32,256,128]{3,2,1,0:T(8,128)(2,1)S(1)} %get-tuple-element.259), channel_id=1, source_target_pairs={{0,4},{4,0},{1,5},{5,1},{2,6},{6,2},{3,7},{7,3},{11,15},{15,11},{1... | collective-permute-start | bytes 18874376 | tf_op jit(solution)/shard_map/ppermute | solution.py:587
  417.3 2.6 copy-start.7
  528.3 7.2 %collective-permute-start.27 = (bf16[128,128,128]{2,1,0:T(8,128)(2,1)S(1)}, bf16[128,128,128]{2,1,0:T(8,128)(2,1)S(1)}, u32[]{:S(2)}, u32[]{:S(2)}) collective-permute-start(bf16[128,128,128]{2,1,0:T(8,128)(2,1)S(1)} %get-tuple-element.263), channel_id=1, source_target_pairs={{0,4},{4,0},{1,5},{5,1},{2,6},{6,2},{3,7},{7,3},{11,15},{15,11},{1... | collective-permute-start | bytes 12582920 | tf_op jit(solution)/shard_map/ppermute | solution.py:592
